TPU v7x, 256 devices: a whole 4x4x8 slice. The times are simulated.
256 devices in a mesh: src: 8 (over z_hi, core), tile: 32 (over y, x, z_lo).
Axes of the slice: x: 4, y: 4, z: 8 (z_hi: 4, z_lo: 2; z = z_hi * 2 + z_lo), core: 2. Of those that a mesh axis runs over, the one named last changes fastest.
Arguments:
- mask_tiles: float32 [32, 512, 512], P('tile'), may hold values from -1 to 1
- target: float32 [32, 512, 512], P('tile'), may hold values from 0 to 0.4
- pupil_gain: float32 [128, 128], replicated, may hold values from 0.5 to 1.5
- weights: float32 [32], P('src'), may hold values from 0.1 to 1
- freq_index: int32 [32, 2, 128], P('src'), may hold values from 0 to 639, as said below
Outputs:
- mask_grad: float32 [32, 512, 512], P('tile', 'src')
- weight_grad: float32 [32], P('src')
Inputs may be any that keep to these rules, and one draw needn't show every extreme that they name: freq_index[s, c, k] = (k - 64 - o) mod 640 for k = 0..127, with one integer offset o of -64 to 63 for each source s and coordinate c.
All inputs are finite; a program needn't handle non-finite values.
Results may differ from a plain program's by a relative error of at most 0.0003.
Values sent between devices are 32-bit elements; how exact they have to be, the bound alone decides.
No kernel may reach another device: no remote copies, remote signals or barrier semaphores. Data moves between devices by JAX's collectives and lax.ppermute only.
A program may use at most 128 MiB of HBM per device.

v0:
```python
import math

import jax
import jax.numpy as jnp
from jax import lax
from jax.sharding import PartitionSpec as P

A = 64
TCOLS = 8


HIGHEST = lax.Precision.HIGHEST


def passed_along(value, axis, steps):
    count = lax.axis_size(axis)
    initial, last = (max(0, -steps), min(count, count - steps))
    return lax.ppermute(value, axis, [(source, source + steps) for source in range(initial, last)])


def product(first_op, second_op):
    return jnp.dot(first_op, second_op, precision=HIGHEST, preferred_element_type=jnp.float32)


def phase_table(indices, positions, period, factor, orient):
    phases = jnp.mod(indices[:, None] * positions[None, :], period)
    angles = phases.astype(jnp.float32) * (2.0 * math.pi / period)
    return (jnp.cos(angles) * factor, orient * jnp.sin(angles) * factor)


def neighbour(piece, offset):
    return passed_along(piece, "tile", offset)


def give_back(piece, offset):
    return passed_along(piece, "tile", offset)


def fold_rims(grad_ext, pixels, column):
    from_below = give_back(grad_ext[:A], -TCOLS)
    from_above = give_back(grad_ext[pixels + A :], TCOLS)
    middle_band = grad_ext[A : A + pixels]
    middle_band = middle_band.at[pixels - A :].add(from_below)
    middle_band = middle_band.at[:A].add(from_above)
    from_right = give_back(middle_band[:, :A], -1)
    from_left = give_back(middle_band[:, pixels + A :], 1)
    inner = middle_band[:, A : A + pixels]
    inner = inner.at[:, pixels - A :].add(jnp.where(column < TCOLS - 1, from_right, 0.0))
    inner = inner.at[:, :A].add(jnp.where(column > 0, from_left, 0.0))
    return inner


def image_of(half_real, half_imag, down_real, down_imag):
    out_real = product(down_real.T, half_real) - product(down_imag.T, half_imag)
    out_imag = product(down_real.T, half_imag) + product(down_imag.T, half_real)
    return (out_real, out_imag)


def body(mask_tiles, target, pupil_gain, weights, freq_index):
    tile_now = mask_tiles[0]
    pixels = tile_now.shape[0]
    period = pixels + 2 * A
    kept_freqs = pupil_gain.shape[0]
    column = jnp.mod(lax.axis_index("tile"), TCOLS)
    left_rim = neighbour(tile_now[:, pixels - A :], 1)
    right_rim = neighbour(tile_now[:, :A], -1)
    left_rim = jnp.where(column > 0, left_rim, 0.0)
    right_rim = jnp.where(column < TCOLS - 1, right_rim, 0.0)
    middle_band = jnp.concatenate([left_rim, tile_now, right_rim], axis=1)
    upper_rim = neighbour(middle_band[pixels - A :], TCOLS)
    lower_rim = neighbour(middle_band[:A], -TCOLS)
    extended = jnp.concatenate([upper_rim, middle_band, lower_rim], axis=0)
    freq_ranks = jnp.arange(kept_freqs, dtype=jnp.int32) - kept_freqs // 2
    inside = freq_ranks[:, None] ** 2 + freq_ranks[None, :] ** 2 <= (kept_freqs // 2) ** 2
    pupil_disc = jnp.where(inside, pupil_gain, 0.0)
    down_real, down_imag = phase_table(
        jnp.mod(freq_ranks, period),
        jnp.arange(pixels, dtype=jnp.int32) + A,
        period,
        1.0 / math.sqrt(kept_freqs),
        1.0,
    )
    spread = jnp.arange(period, dtype=jnp.int32)
    count = weights.shape[0]
    tables = []
    images = []
    partial_value = jnp.zeros((pixels, pixels), jnp.float32)
    for source in range(count):
        row_real, row_imag = phase_table(
            freq_index[source, 0], spread, period, 1.0 / math.sqrt(period), -1.0
        )
        col_real, col_imag = phase_table(
            freq_index[source, 1], spread, period, 1.0 / math.sqrt(period), -1.0
        )
        upper_real = product(extended, col_real.T)
        upper_imag = product(extended, col_imag.T)
        spec_real = (product(row_real, upper_real) - product(row_imag, upper_imag)) * pupil_disc
        spec_imag = (product(row_real, upper_imag) + product(row_imag, upper_real)) * pupil_disc
        half_real = product(spec_real, down_real) - product(spec_imag, down_imag)
        half_imag = product(spec_real, down_imag) + product(spec_imag, down_real)
        out_real, out_imag = image_of(half_real, half_imag, down_real, down_imag)
        partial_value = partial_value + weights[source] * (
            out_real * out_real + out_imag * out_imag
        )
        tables.append((row_real, row_imag, col_real, col_imag))
        images.append((out_real, out_imag))
    total_sources = count * lax.axis_size("src")
    intensity = lax.psum(partial_value, "src") / total_sources
    residual = intensity - target[0]
    grad_ext = jnp.zeros((period, period), jnp.float32)
    energies = []
    for source in range(count):
        row_real, row_imag, col_real, col_imag = tables[source]
        out_real, out_imag = images[source]
        energies.append(jnp.sum(residual * (out_real * out_real + out_imag * out_imag)))
        factor = 2.0 * weights[source] * residual
        grad_real = factor * out_real
        grad_imag = factor * out_imag
        back_half_real = product(down_real, grad_real) + product(down_imag, grad_imag)
        back_half_imag = product(down_real, grad_imag) - product(down_imag, grad_real)
        back_spec_real = (
            product(back_half_real, down_real.T) + product(back_half_imag, down_imag.T)
        ) * pupil_disc
        back_spec_imag = (
            product(back_half_imag, down_real.T) - product(back_half_real, down_imag.T)
        ) * pupil_disc
        back_upper_real = product(row_real.T, back_spec_real) + product(row_imag.T, back_spec_imag)
        back_upper_imag = product(row_real.T, back_spec_imag) - product(row_imag.T, back_spec_real)
        grad_ext = (
            grad_ext + product(back_upper_real, col_real) + product(back_upper_imag, col_imag)
        )
    tile_count = lax.axis_size("tile")
    weight_grad = lax.psum(jnp.stack(energies), "tile") * (16.0 / (tile_count * pixels * pixels))
    summed = lax.psum(grad_ext, "src")
    folded = fold_rims(summed, pixels, column)
    share_rows = pixels // lax.axis_size("src")
    mask_grad = lax.dynamic_slice_in_dim(folded, lax.axis_index("src") * share_rows, share_rows, 0)
    return (mask_grad[None], weight_grad)


def solution(mesh):
    placed = (P("tile", None, None), P("tile", None, None), P(), P("src"), P("src", None, None))
    return jax.shard_map(
        body,
        mesh=mesh,
        in_specs=placed,
        out_specs=(P("tile", "src", None), P("src")),
        check_vma=False,
    )
```

profile of v0, /device:TPU:8, one launch (start us, length us, event | category | flops | bytes accessed | tf_op | source)
XLA Modules:
  0.0 544.9 jit_solution(4348239763924316394)
XLA Ops:
  8.5 5.9 %collective-permute-start.1 = (f32[512,64]{1,0:T(8,128)S(1)}, f32[512,64]{1,0:T(8,128)S(1)}, u32[]{:S(2)}, u32[]{:S(2)}) collective-permute-start(f32[512,64]{1,0:T(8,128)S(1)} %get-tuple-element.62), channel_id=1, source_target_pairs={{1,0},{2,1},{3,2},{4,3},{5,4},{6,5},{7,6},{8,7},{9,8},{10,9},{11,1... | collective-permute-start | bytes 393224 | tf_op jit(solution)/shard_map/ppermute | solution.py:18
  17.1 4.0 collective-permute-done.1
  21.1 6.0 %collective-permute-done = f32[512,64]{1,0:T(8,128)S(1)} collective-permute-done((f32[512,64]{1,0:T(8,128)S(1)}, f32[512,64]{1,0:T(8,128)S(1)}, u32[]{:S(2)}, u32[]{:S(2)}) %collective-permute-start) | collective-permute-done | bytes 131104 | tf_op jit(solution)/shard_map/ppermute | solution.py:18
  29.2 3.9 collective-permute-start.2
  36.4 2.9 fusion.77
  39.3 2.1 fusion.94
  41.4 2.9 fusion.78
  44.3 2.5 fusion.93
  51.5 2.9 fusion.65
  54.4 2.1 fusion.82
  56.5 2.9 fusion.67
  59.4 2.3 fusion.81
  66.3 2.9 fusion.69
  69.2 2.5 fusion.86
  71.7 2.9 fusion.71
  74.6 2.1 fusion.85
  81.3 2.9 fusion.73
  84.1 2.1 fusion.90
  86.2 2.9 fusion.75
  89.2 2.3 fusion.89
  102.8 2.2 fusion.350
  115.8 2.4 convolution_subtract_fusion.3
  129.0 2.2 convolution_subtract_fusion.2
  139.9 2.5 convolution_add_fusion.1
  144.5 2.1 convolution_add_fusion
  146.6 6.5 %multiply_add_fusion = (f32[512,512]{1,0:T(8,128)}, f32[512,512]{1,0:T(8,128)}) fusion(f32[]{:T(128)} %bitcast.10, f32[]{:T(128)} %bitcast.7, f32[]{:T(128)} %bitcast.4, f32[]{:T(128)} %bitcast.1, f32[512,512]{1,0:T(8,128)S(1)} %convolution_subtract_fusion.3, f32[512,512]{1,0:T(8,128)S(1)} %convolution_add_fusion.2, ...), kind=kOutput, calls=%fused_computation.71 | convolution fusion | flops 408551424 | bytes 10750480 | tf_op jit(solution)/shard_map/dot_general | solution.py:22
  155.7 75.0 %all-reduce.3.cloned.1.call-done = f32[512,512]{1,0:T(8,128)} async-done(((f32[512,512]{1,0:T(8,128)}), f32[512,512]{1,0:T(8,128)}) %all-reduce.3.cloned.1.call-update) | async-done | bytes 1048592 | tf_op jit(solution)/shard_map/psum | solution.py:108
  230.7 5.1 multiply_reduce_fusion.3
  259.0 2.2 fusion.92
  266.5 2.7 fusion.76
  283.1 2.1 convolution_subtract_fusion.5
  285.2 2.8 fusion.74
  290.0 2.7 fusion.72
  296.0 2.1 convolution_add_fusion.14
  308.3 3.2 fusion.70
  313.4 2.7 fusion.68
  331.7 2.7 fusion.64
  334.5 2.2 convolution_subtract_fusion.7
  336.6 2.8 fusion.66
  341.4 4.4 add_add_fusion
  345.8 79.1 %all-reduce.5.cloned.1.call-done = f32[640,640]{1,0:T(8,128)} async-done(((f32[640,640]{1,0:T(8,128)}), f32[640,640]{1,0:T(8,128)}) %all-reduce.5.cloned.1.call-update) | async-done | bytes 1638416 | tf_op jit(solution)/shard_map/psum | solution.py:134
  426.1 2.9 collective-permute-start.4
  429.7 2.6 pad_maximum_fusion.4
  432.3 69.4 %psum.23 = f32[4]{0:T(128)S(1)} all-reduce(f32[4]{0:T(128)S(1)} %pad_maximum_fusion.4), channel_id=1, replica_groups=mesh['src'=8,'tile'=32] {'tile'}, use_global_device_ids=true, to_apply=%region_7.8 | all-reduce | flops 4 | bytes 32 | tf_op jit(solution)/shard_map/psum | solution.py:133
  501.7 4.6 collective-permute-start.5
  506.4 13.9 %collective-permute-done.5 = f32[64,640]{1,0:T(8,128)S(1)} collective-permute-done((f32[64,640]{1,0:T(8,128)S(1)}, f32[64,640]{1,0:T(8,128)S(1)}, u32[]{:S(2)}, u32[]{:S(2)}) %collective-permute-start.5) | collective-permute-done | bytes 163872 | tf_op jit(solution)/shard_map/ppermute | solution.py:18
  523.2 3.9 collective-permute-start.7
  530.2 4.3 collective-permute-done.7
  (137 shorter events, 154.8 us)
Async XLA Ops:
  7.2 19.9 %copy-start.10 = (f32[1,512,512]{2,1,0:T(8,128)S(1)}, f32[1,512,512]{2,1,0:T(8,128)}, u32[]{:S(2)}) copy-start(f32[1,512,512]{2,1,0:T(8,128)} %param.13) | copy-start | bytes 3145732
  7.2 223.5 %all-reduce.3.cloned.1.call-start = ((), (), s32[]{:S(2)}) async-start(), calls=%async_computation | async-start | bytes 2097152 | tf_op jit(solution)/shard_map/psum | solution.py:108
  8.5 24.7 %copy-start.11 = (f32[4]{0:T(128)S(1)}, f32[4]{0:T(128)}, u32[]{:S(2)}) copy-start(f32[4]{0:T(128)} %param.16) | copy-start | bytes 52
  8.5 12.6 %collective-permute-start.1 = (f32[512,64]{1,0:T(8,128)S(1)}, f32[512,64]{1,0:T(8,128)S(1)}, u32[]{:S(2)}, u32[]{:S(2)}) collective-permute-start(f32[512,64]{1,0:T(8,128)S(1)} %get-tuple-element.62), channel_id=1, source_target_pairs={{1,0},{2,1},{3,2},{4,3},{5,4},{6,5},{7,6},{8,7},{9,8},{10,9},{11,1... | collective-permute-start | bytes 393224 | tf_op jit(solution)/shard_map/ppermute | solution.py:18
  14.4 12.7 %collective-permute-start = (f32[512,64]{1,0:T(8,128)S(1)}, f32[512,64]{1,0:T(8,128)S(1)}, u32[]{:S(2)}, u32[]{:S(2)}) collective-permute-start(f32[512,64]{1,0:T(8,128)S(1)} %get-tuple-element.61), channel_id=1, source_target_pairs={{0,1},{1,2},{2,3},{3,4},{4,5},{5,6},{6,7},{7,8},{8,9},{9,10},{10,1... | collective-permute-start | bytes 393224 | tf_op jit(solution)/shard_map/ppermute | solution.py:18
  27.3 7.2 %collective-permute-start.3 = (f32[64,640]{1,0:T(8,128)S(1)}, f32[64,640]{1,0:T(8,128)S(1)}, u32[]{:S(2)}, u32[]{:S(2)}) collective-permute-start(f32[64,640]{1,0:T(8,128)S(1)} %get-tuple-element.58), channel_id=1, source_target_pairs={{8,0},{9,1},{10,2},{11,3},{12,4},{13,5},{14,6},{15,7},{16,8},{17,9... | collective-permute-start | bytes 491528 | tf_op jit(solution)/shard_map/ppermute | solution.py:18
  29.2 7.2 %collective-permute-start.2 = (f32[64,640]{1,0:T(8,128)S(1)}, f32[64,640]{1,0:T(8,128)S(1)}, u32[]{:S(2)}, u32[]{:S(2)}) collective-permute-start(f32[64,640]{1,0:T(8,128)S(1)} %get-tuple-element.57), channel_id=1, source_target_pairs={{0,8},{1,9},{2,10},{3,11},{4,12},{5,13},{6,14},{7,15},{8,16},{9,17... | collective-permute-start | bytes 491528 | tf_op jit(solution)/shard_map/ppermute | solution.py:18
  41.4 5.4 copy-start.12
  107.1 39.5 %copy-start.4 = (f32[512,512]{1,0:T(8,128)}, f32[512,512]{1,0:T(8,128)S(1)}, u32[]{:S(2)}) copy-start(f32[512,512]{1,0:T(8,128)S(1)} %convolution_subtract_fusion) | copy-start | bytes 3145732
  118.2 28.3 %copy-start = (f32[512,512]{1,0:T(8,128)}, f32[512,512]{1,0:T(8,128)S(1)}, u32[]{:S(2)}) copy-start(f32[512,512]{1,0:T(8,128)S(1)} %convolution_subtract_fusion.3) | copy-start | bytes 3145732
  131.2 15.4 %copy-start.2 = (f32[512,512]{1,0:T(8,128)}, f32[512,512]{1,0:T(8,128)S(1)}, u32[]{:S(2)}) copy-start(f32[512,512]{1,0:T(8,128)S(1)} %convolution_subtract_fusion.2) | copy-start | bytes 3145732
  144.5 8.6 %copy-start.6 = (f32[512,512]{1,0:T(8,128)}, f32[512,512]{1,0:T(8,128)S(1)}, u32[]{:S(2)}) copy-start(f32[512,512]{1,0:T(8,128)S(1)} %convolution_subtract_fusion.1) | copy-start | bytes 3145732
  153.1 271.8 %all-reduce.5.cloned.1.call-start = ((), (), s32[]{:S(2)}) async-start(), calls=%async_computation.1 | async-start | bytes 3276800 | tf_op jit(solution)/shard_map/psum | solution.py:134
  230.7 5.1 copy-start.5
  239.6 1.9 copy-start.7
  243.3 1.9 copy-start.3
  245.2 2.1 copy-start.1
  247.2 1.9 copy-start.8
  424.9 81.4 %copy-start.9 = (f32[640,640]{1,0:T(8,128)S(1)}, f32[640,640]{1,0:T(8,128)}, u32[]{:S(2)}) copy-start(f32[640,640]{1,0:T(8,128)} %all-reduce.5.cloned.1.call-done) | copy-start | bytes 4915204
  424.9 81.4 %slice-start = ((f32[640,640]{1,0:T(8,128)}), f32[512,640]{1,0:T(8,128)S(1)}, s32[]{:S(2)}) async-start(f32[640,640]{1,0:T(8,128)} %all-reduce.5.cloned.1.call-done), calls=%async_computation.2 | async-start | bytes 2621440 | tf_op jit(solution)/shard_map/slice | solution.py:42
  426.1 80.2 %collective-permute-start.4 = (f32[64,640]{1,0:T(8,128)S(1)}, f32[64,640]{1,0:T(8,128)S(1)}, u32[]{:S(2)}, u32[]{:S(2)}) collective-permute-start(f32[64,640]{1,0:T(8,128)S(1)} %get-tuple-element.56), channel_id=1, source_target_pairs={{8,0},{9,1},{10,2},{11,3},{12,4},{13,5},{14,6},{15,7},{16,8},{17,9... | collective-permute-start | bytes 491528 | tf_op jit(solution)/shard_map/ppermute | solution.py:18
  501.7 18.6 %collective-permute-start.5 = (f32[64,640]{1,0:T(8,128)S(1)}, f32[64,640]{1,0:T(8,128)S(1)}, u32[]{:S(2)}, u32[]{:S(2)}) collective-permute-start(f32[64,640]{1,0:T(8,128)S(1)} %get-tuple-element.55), channel_id=1, source_target_pairs={{0,8},{1,9},{2,10},{3,11},{4,12},{5,13},{6,14},{7,15},{8,16},{9,17... | collective-permute-start | bytes 491528 | tf_op jit(solution)/shard_map/ppermute | solution.py:18
  520.5 8.3 %collective-permute-start.6 = (f32[512,64]{1,0:T(8,128)S(1)}, f32[512,64]{1,0:T(8,128)S(1)}, u32[]{:S(2)}, u32[]{:S(2)}) collective-permute-start(f32[512,64]{1,0:T(8,128)S(1)} %get-tuple-element.60), channel_id=1, source_target_pairs={{1,0},{2,1},{3,2},{4,3},{5,4},{6,5},{7,6},{8,7},{9,8},{10,9},{11,1... | collective-permute-start | bytes 393224 | tf_op jit(solution)/shard_map/ppermute | solution.py:18
  523.2 11.3 %collective-permute-start.7 = (f32[512,64]{1,0:T(8,128)S(1)}, f32[512,64]{1,0:T(8,128)S(1)}, u32[]{:S(2)}, u32[]{:S(2)}) collective-permute-start(f32[512,64]{1,0:T(8,128)S(1)} %get-tuple-element.59), channel_id=1, source_target_pairs={{0,1},{1,2},{2,3},{3,4},{4,5},{5,6},{6,7},{7,8},{8,9},{9,10},{10,1... | collective-permute-start | bytes 393224 | tf_op jit(solution)/shard_map/ppermute | solution.py:18
Sparse Core Ops, SparseCore 0:
  153.3 77.3 all-reduce.2
  345.9 78.9 all-reduce.4
where the time goes:
time: 552 us; the launch traced here: 545 us
  matrix products  226 us (41%)
  waiting for transfers between devices  186 us (34%)
  blocking collectives  69.4 us (13%)
  starting transfers between devices  27.2 us (5%)
  between operations  17.9 us (3%)
  other arithmetic  9.88 us (2%)
  local copies, waits for them, and re-layouts  8.43 us (2%)
    dot_general x112, matrix products, product(): jnp.dot(first_op, second_op, precision=HIGHEST, preferred_element_type=jn...  226 us
    psum x1, waiting for transfers between devices, body(): summed = lax.psum(grad_ext, 'src')  79.1 us
    psum x1, waiting for transfers between devices, body(): intensity = lax.psum(partial_value, 'src') / total_sources  75 us
    psum x1, blocking collectives, body(): lax.psum(jnp.stack(energies), 'tile')  69.4 us
    ppermute x8, waiting for transfers between devices, passed_along(): lax.ppermute(value, axis, [(source, source + steps) for source in range(i...  32.3 us
    ppermute x8, starting transfers between devices, passed_along(): lax.ppermute(value, axis, [(source, source + steps) for source in range(i...  27.1 us
  transfers between devices with their start and end apart: 10, of which 9 were waited for; matrix products, arithmetic and copies ran while one was open for 1% of the time, Pallas kernels for 0%

commit v1 on v0

v1 whole, which is shorter than its diff:
```python
import functools
import math

import jax
import jax.numpy as jnp
import ml_dtypes
import numpy as np
from jax import lax
from jax.experimental import pallas as pl
from jax.experimental.pallas import tpu as pltpu
from jax.sharding import PartitionSpec as P

A = 64
TROWS = 4
TCOLS = 8
PIX = 512
N = PIX + 2 * A
K = 128
W = 256
SOURCES = 4
BF = jnp.bfloat16
F32 = jnp.float32
BOTH = ("src", "tile")


def two_terms(table):
    first = table.astype(np.float32).astype(ml_dtypes.bfloat16)
    rest = (table - first.astype(np.float64)).astype(np.float32)
    return np.stack([first, rest.astype(ml_dtypes.bfloat16)])


def real_basis():
    angles = 2.0 * np.pi / N * np.mod(np.outer(np.arange(N), np.arange(K)), N)
    return np.concatenate([np.cos(angles), np.sin(angles)], axis=1) / math.sqrt(N)


def fold_table():
    ranks = np.arange(W) - K
    parts = np.arange(K)
    same = np.abs(ranks)[None, :] == parts[:, None]
    return np.concatenate([same * 1.0, same * np.sign(ranks)[None, :]], axis=0)


def coarse_table():
    ranks = np.arange(K) - K // 2
    angles = 2.0 * np.pi / W * np.mod(np.outer(ranks, np.arange(W)), W)
    down_real, down_imag = np.cos(angles) / math.sqrt(K), np.sin(angles) / math.sqrt(K)
    return np.block([[down_real, down_imag], [-down_imag, down_real]])


def interpolation():
    ranks = np.arange(1, K)
    shift = (np.arange(PIX) + A)[:, None] / N - np.arange(W)[None, :] / W
    return (1.0 + 2.0 * np.cos(2.0 * np.pi * shift[..., None] * ranks).sum(-1)) / W


def make_tables():
    basis = real_basis()
    fold = fold_table()
    coarse = coarse_table()
    spread = interpolation()
    rims = np.concatenate([basis[:A], basis[N - A :]])
    bf16 = ml_dtypes.bfloat16
    return {
        "mid": two_terms(basis[A : N - A]),
        "mid_t": two_terms(basis[A : N - A].T),
        "all_t": two_terms(basis.T),
        "rims": two_terms(rims),
        "rims_t": two_terms(rims.T),
        "fold": fold.astype(bf16),
        "fold_t": np.ascontiguousarray(fold.T).astype(bf16),
        "coarse": two_terms(coarse),
        "coarse_t": two_terms(coarse.T),
        "spread": two_terms(spread),
        "spread_t": two_terms(spread.T),
        "gram": two_terms(spread.T @ spread),
        "blocks": np.ascontiguousarray(two_terms(basis[A : N - A]).reshape(2, 4, K, W).swapaxes(0, 1)),
        "outer": np.stack([two_terms(basis[N - A :])] * 2 + [two_terms(basis[:A])] * 2),
        "sides_t": np.stack([two_terms(basis[:A].T), two_terms(basis[N - A :].T)]),
    }


def terms(value):
    first = value.astype(BF)
    return first, (value - first.astype(F32)).astype(BF)


def dot(first_op, second_op):
    return jnp.dot(first_op, second_op, preferred_element_type=F32)


def product(first_op, second_op):
    first_hi, first_lo = first_op
    second_hi, second_lo = second_op
    return dot(first_hi, second_hi) + (dot(first_hi, second_lo) + dot(first_lo, second_hi))


def pair_of(ref):
    return ref[0], ref[1]


def exact_left(table, value):
    high, low = terms(value)
    return dot(table, high) + dot(table, low)


def exact_right(value, table):
    high, low = terms(value)
    return dot(high, table) + dot(low, table)


def call(kernel, outs, ins, name, flops, scratch=(), smem=()):
    specs = [
        pl.BlockSpec(memory_space=pltpu.SMEM if at in smem else pltpu.VMEM) for at in range(len(ins))
    ]
    shapes = [jax.ShapeDtypeStruct(shape, F32) for shape in outs]
    moved = 4 * sum(math.prod(shape) for shape in outs) + sum(one.size * one.dtype.itemsize for one in ins)
    return pl.pallas_call(
        kernel,
        out_shape=shapes,
        in_specs=specs,
        out_specs=[pl.BlockSpec(memory_space=pltpu.VMEM) for _ in outs],
        scratch_shapes=list(scratch),
        compiler_params=pltpu.CompilerParams(vmem_limit_bytes=40 * 1024 * 1024),
        cost_estimate=pl.CostEstimate(flops=flops, bytes_accessed=moved, transcendentals=0),
        name=name,
    )(*ins)


def own_kernel(tile_ref, target_ref, mid_ref, mid_t_ref, spread_ref, spread_t_ref, basis_ref, wanted_ref):
    upper = product(terms(tile_ref[0]), pair_of(mid_ref))
    basis_ref[...] = product(pair_of(mid_t_ref), terms(upper))
    upper = product(terms(target_ref[0]), pair_of(spread_ref))
    wanted_ref[...] = product(pair_of(spread_t_ref), terms(upper))


def pack_kernel(at_ref, left_ref, right_ref, mine_ref, other_ref, out_ref):
    first = at_ref[1] == 0
    mine, other = mine_ref[...], other_ref[...]
    up = jnp.where(first, mine, other)
    down = jnp.where(first, other, mine)

    def chosen(left, right):
        return jnp.where(first, right[:, K - A :], left[:, :A])

    up_part = chosen(up[:, :K], up[:, PIX - K :])
    down_part = chosen(down[:, :K], down[:, PIX - K :])
    middle = chosen(left_ref[0], right_ref[0])
    half = N // 2
    top = jnp.concatenate([up_part, middle[: half - A]], axis=0)
    bottom = jnp.concatenate([middle[half - A :], down_part], axis=0)
    out_ref[...] = jnp.concatenate([top, bottom], axis=1)


def rows_kernel(at_ref, basis_ref, mine_ref, other_ref, mid_ref, rims_t_ref, out_ref):
    first = at_ref[1] == 0
    mine, other = mine_ref[...], other_ref[...]
    rim = jnp.concatenate([jnp.where(first, mine, other), jnp.where(first, other, mine)], axis=0)
    upper = product(terms(rim), pair_of(mid_ref))
    out_ref[...] = basis_ref[...] + product(pair_of(rims_t_ref), terms(upper))


def halves(value, core):
    top, bottom = value[:K], value[K:]
    return jnp.where(core == 0, top, bottom), jnp.where(core == 0, bottom, top)


def joined(mine, other, core):
    return jnp.concatenate(
        [jnp.where(core == 0, mine, other), jnp.where(core == 0, other, mine)], axis=0
    )


def disc_of(gain):
    rows = lax.broadcasted_iota(jnp.int32, (K, K), 0) - K // 2
    columns = lax.broadcasted_iota(jnp.int32, (K, K), 1) - K // 2
    return jnp.where(rows * rows + columns * columns <= (K // 2) ** 2, gain, 0.0)


def window_starts(index_ref, source):
    def start(coordinate):
        return jnp.clip(lax.rem(index_ref[source, coordinate, 0] + K, N), 0, K)

    return start(0), start(1)


def image_kernel(
    at_ref,
    index_ref,
    weights_ref,
    basis_ref,
    mine_ref,
    other_ref,
    gain_ref,
    rims_ref,
    all_t_ref,
    fold_ref,
    fold_t_ref,
    coarse_ref,
    coarse_t_ref,
    field_ref,
    keep_ref,
    send_ref,
    real_ref,
    imag_ref,
):
    core = at_ref[1]
    first = core == 0
    mine, other = mine_ref[...], other_ref[...]
    left = jnp.where(first, mine, other)
    right = jnp.where(first, other, mine)
    rim = jnp.concatenate(
        [
            jnp.concatenate([left[:, :A], right[:, :A]], axis=1),
            jnp.concatenate([left[:, A:], right[:, A:]], axis=1),
        ],
        axis=0,
    )
    upper = product(terms(rim), pair_of(rims_ref))
    basis = basis_ref[...] + product(pair_of(all_t_ref), terms(upper))
    zero = jnp.zeros((K, K), F32)
    even = jnp.concatenate(
        [
            jnp.concatenate([basis[:K, :K], zero], axis=1),
            jnp.concatenate([zero, -basis[K:, K:]], axis=1),
        ],
        axis=0,
    )
    odd = jnp.concatenate(
        [
            jnp.concatenate([zero, -basis[:K, K:]], axis=1),
            jnp.concatenate([-basis[K:, :K], zero], axis=1),
        ],
        axis=0,
    )
    fold, fold_t = fold_ref[...], fold_t_ref[...]
    for ref, part in ((real_ref, even), (imag_ref, odd)):
        plane = exact_right(exact_left(fold_t, part), fold)
        ref[0] = plane[:, :K]
        ref[1] = plane[:, K:]
    disc = disc_of(gain_ref[...])
    total = jnp.zeros((W, W), F32)
    for source in range(SOURCES):
        row, column = window_starts(index_ref, source)

        def window(ref):
            rows = jnp.concatenate([ref[0, pl.ds(row, K), :], ref[1, pl.ds(row, K), :]], axis=1)
            return pltpu.roll(rows, lax.rem(W - column, W), 1)[:, :K] * disc

        spec = jnp.concatenate([window(real_ref), window(imag_ref)], axis=1)
        half = product(terms(spec), pair_of(coarse_ref))
        half = jnp.concatenate([half[:, :W], half[:, W:]], axis=0)
        field = product(pair_of(coarse_t_ref), terms(half))
        field_ref[source] = field
        real, imag = field[:W], field[W:]
        total = total + weights_ref[source] * (real * real + imag * imag)
    keep, send = halves(total, core)
    keep_ref[...] = keep
    send_ref[...] = send


def adjoint_kernel(
    at_ref,
    index_ref,
    weights_ref,
    mine_ref,
    other_ref,
    wanted_ref,
    field_ref,
    gain_ref,
    gram_ref,
    fold_ref,
    fold_t_ref,
    coarse_ref,
    coarse_t_ref,
    keep_ref,
    send_ref,
    energy_ref,
    real_ref,
    imag_ref,
):
    core = at_ref[1]
    bright = joined(mine_ref[...], other_ref[...], core)
    gram = pair_of(gram_ref)
    value = product(terms(product(gram, terms(bright))), gram)
    residual = value * (1.0 / (8 * SOURCES)) - wanted_ref[...]
    disc = disc_of(gain_ref[...])
    sides = []
    lanes = lax.broadcasted_iota(jnp.int32, (8, K), 1)
    energies = jnp.zeros((8, K), F32)
    for source in range(SOURCES):
        field = field_ref[source]
        real, imag = field[:W], field[W:]
        scaled = jnp.concatenate([residual * real, residual * imag], axis=1)
        energy = jnp.sum(scaled[:, :W] * real + scaled[:, W:] * imag)
        energies = jnp.where(lanes == source, energy, energies)
        back = product(terms(scaled), pair_of(coarse_t_ref))
        sides.append(jnp.concatenate([back[:, :K], back[:, K:]], axis=0))
    energy_ref[...] = energies
    real_ref[...] = jnp.zeros((2, W, K), F32)
    imag_ref[...] = jnp.zeros((2, W, K), F32)
    pad = jnp.zeros((K, K), F32)
    for couple in range(SOURCES // 2):
        spec = product(pair_of(coarse_ref), terms(jnp.concatenate(sides[2 * couple : 2 * couple + 2], axis=1)))
        for place in range(2):
            source = 2 * couple + place
            row, column = window_starts(index_ref, source)
            scale = disc * (2.0 * weights_ref[source])
            for ref, part in ((real_ref, spec[:K]), (imag_ref, spec[K:])):
                part = part[:, place * K : place * K + K] * scale
                wide = pltpu.roll(jnp.concatenate([part, pad], axis=1), column, 1)
                for side in range(2):
                    ref[side, pl.ds(row, K), :] += wide[:, side * K : side * K + K]
    fold, fold_t = fold_ref[...], fold_t_ref[...]

    def folded(ref):
        return exact_right(exact_left(fold, jnp.concatenate([ref[0], ref[1]], axis=1)), fold_t)

    even, odd = folded(real_ref), folded(imag_ref)
    top = jnp.concatenate([even[:K, :K], -odd[:K, K:]], axis=1)
    bottom = jnp.concatenate([-odd[K:, :K], -even[K:, K:]], axis=1)
    keep_ref[...] = jnp.where(core == 0, top, bottom)
    send_ref[...] = jnp.where(core == 0, bottom, top)


def lines_kernel(at_ref, mine_ref, other_ref, block_ref, outer_ref, lines_ref, rim_ref):
    spectrum = terms(joined(mine_ref[...], other_ref[...], at_ref[1]))
    lines_ref[...] = product((block_ref[0, 0], block_ref[0, 1]), spectrum)
    rim_ref[...] = product((outer_ref[0, 0], outer_ref[0, 1]), spectrum)


def pixels_kernel(at_ref, lines_ref, rim_ref, mid_t_ref, sides_ref, inner_ref, side_ref):
    place, core = at_ref[0], at_ref[1]
    rim = rim_ref[...]
    lines = lines_ref[...]
    top = lines[:A] + jnp.where(place == 0, rim, 0.0)
    bottom = lines[A:] + jnp.where(place == 3, rim, 0.0)
    table = (sides_ref[0, 0], sides_ref[0, 1])
    side_ref[...] = jnp.concatenate([product(terms(top), table), product(terms(bottom), table)], axis=1)
    own = jnp.where(core == 0, top, bottom)
    inner_ref[...] = product(terms(own), pair_of(mid_t_ref))


def join_kernel(at_ref, inner_ref, mine_ref, other_ref, out_ref):
    first = at_ref[1] == 0
    mine, other = mine_ref[...], other_ref[...]
    left = jnp.where(first, other[:, :A], mine[:, A:])
    right = jnp.where(first, mine[:, :A], other[:, A:])
    inner = inner_ref[...]
    pad = jnp.zeros((A, A), F32)
    out_ref[0, :, :K] = inner[:, :K] + jnp.concatenate([left, pad], axis=1)
    out_ref[0, :, K : PIX - K] = inner[:, K : PIX - K]
    out_ref[0, :, PIX - K :] = inner[:, PIX - K :] + jnp.concatenate([pad, right], axis=1)


def swap_cores(value):
    return lax.ppermute(value, "src", [(at, at ^ 1) for at in range(8)])


def swap_chips(value, partner):
    return lax.ppermute(value, "src", [(at, 2 * partner(at // 2) + at % 2) for at in range(8)])


def all_sum(keep, send):
    value = keep + swap_cores(send)
    value = value + swap_chips(value, lambda chip: chip ^ 1)
    value = value + swap_chips(value, lambda chip: 3 - chip)
    return value, swap_cores(value)


def tile_move(value, shift_of):
    pairs = []
    for source in range(8):
        shift = shift_of(source)
        if shift is None:
            continue
        for row in range(TROWS):
            for column in range(TCOLS):
                to_row, to_column = row + shift[0], column + shift[1]
                if 0 <= to_row < TROWS and 0 <= to_column < TCOLS:
                    pairs.append(
                        (source * 32 + row * TCOLS + column, source * 32 + to_row * TCOLS + to_column)
                    )
    return lax.ppermute(value, BOTH, pairs)


def tile_sum(value):
    for bit in (1, 2, 4, 8, 16):
        value = value + lax.ppermute(value, "tile", [(at, at ^ bit) for at in range(TROWS * TCOLS)])
    return value


def body(tables, mask_tiles, target, pupil_gain, weights, freq_index):
    group = lax.axis_index("src").astype(jnp.int32)
    chip, core = group // 2, group % 2
    at = jnp.stack([chip, core])

    edge = jnp.where(core == 0, mask_tiles[0, PIX - A :], mask_tiles[0, :A])
    mine = tile_move(edge, lambda source: (1, 0) if source % 2 == 0 else (-1, 0))
    basis, wanted = call(
        own_kernel,
        [(W, W), (W, W)],
        [mask_tiles, target, tables["mid"], tables["mid_t"], tables["spread"], tables["spread_t"]],
        "own",
        2 * 3 * 2 * (PIX * PIX * W + W * PIX * W),
    )
    other = swap_cores(mine)
    whole = pl.BlockSpec(memory_space=pltpu.VMEM)
    packed = pl.pallas_call(
        pack_kernel,
        out_shape=jax.ShapeDtypeStruct((N // 2, K), F32),
        grid=(1,),
        in_specs=[
            pl.BlockSpec(memory_space=pltpu.SMEM),
            pl.BlockSpec((1, PIX, K), lambda step: (0, 0, 0)),
            pl.BlockSpec((1, PIX, K), lambda step: (0, 0, PIX // K - 1)),
            whole,
            whole,
        ],
        out_specs=whole,
        name="pack",
    )(at, mask_tiles, mask_tiles, mine, other)
    my_side = tile_move(packed, lambda source: (0, 1) if source % 2 == 0 else (0, -1))
    (basis,) = call(
        rows_kernel,
        [(W, W)],
        [at, basis, mine, other, tables["mid"], tables["rims_t"]],
        "rows",
        3 * 2 * (K * PIX * W + W * K * W),
        smem=(0,),
    )
    other_side = swap_cores(my_side)
    plane = pltpu.VMEM((2, W, K), F32)
    field, keep, send = call(
        image_kernel,
        [(SOURCES, 2 * W, W), (K, W), (K, W)],
        [
            at,
            freq_index,
            weights,
            basis,
            my_side,
            other_side,
            pupil_gain,
            tables["rims"],
            tables["all_t"],
            tables["fold"],
            tables["fold_t"],
            tables["coarse"],
            tables["coarse_t"],
        ],
        "image",
        1_500_000_000,
        scratch=(plane, plane),
        smem=(0, 1, 2),
    )
    mine, other = all_sum(keep, send)
    keep, send, energies = call(
        adjoint_kernel,
        [(K, W), (K, W), (8, K)],
        [
            at,
            freq_index,
            weights,
            mine,
            other,
            wanted,
            field,
            pupil_gain,
            tables["gram"],
            tables["fold"],
            tables["fold_t"],
            tables["coarse"],
            tables["coarse_t"],
        ],
        "adjoint",
        1_700_000_000,
        scratch=(plane, plane),
        smem=(0, 1, 2),
    )
    energies = tile_sum(energies)
    mine, other = all_sum(keep, send)
    lines, rim = pl.pallas_call(
        lines_kernel,
        out_shape=[jax.ShapeDtypeStruct((K, W), F32), jax.ShapeDtypeStruct((A, W), F32)],
        grid_spec=pltpu.PrefetchScalarGridSpec(
            num_scalar_prefetch=1,
            grid=(1,),
            in_specs=[
                whole,
                whole,
                pl.BlockSpec((1, 2, K, W), lambda step, at: (at[0], 0, 0, 0)),
                pl.BlockSpec((1, 2, A, W), lambda step, at: (at[0], 0, 0, 0)),
            ],
            out_specs=[whole, whole],
        ),
        name="lines",
    )(at, mine, other, tables["blocks"], tables["outer"])
    from_rows = tile_move(rim, lambda source: {0: (1, 0), 3: (-1, 0)}.get(source // 2))
    inner, side = pl.pallas_call(
        pixels_kernel,
        out_shape=[jax.ShapeDtypeStruct((A, PIX), F32), jax.ShapeDtypeStruct((A, K), F32)],
        grid_spec=pltpu.PrefetchScalarGridSpec(
            num_scalar_prefetch=1,
            grid=(1,),
            in_specs=[
                whole,
                whole,
                whole,
                pl.BlockSpec((1, 2, W, A), lambda step, at: (at[1], 0, 0, 0)),
            ],
            out_specs=[whole, whole],
        ),
        name="pixels",
    )(at, lines, from_rows, tables["mid_t"], tables["sides_t"])
    my_side = tile_move(side, lambda source: (0, -1) if source % 2 == 0 else (0, 1))
    other_side = swap_cores(my_side)
    (mask_grad,) = call(
        join_kernel,
        [(1, A, PIX)],
        [at, inner, my_side, other_side],
        "join",
        A * PIX,
        smem=(0,),
    )
    weight_grad = energies[0, :SOURCES] * (16.0 / (TROWS * TCOLS * PIX * PIX))
    return mask_grad, weight_grad


def solution(mesh):
    placed = (P("tile", None, None), P("tile", None, None), P(), P("src"), P("src", None, None))
    return jax.shard_map(
        functools.partial(body, make_tables()),
        mesh=mesh,
        in_specs=placed,
        out_specs=(P("tile", "src", None), P("src")),
        check_vma=False,
    )
```

time: 552 us -> 123 us (0.22)
  the two profiles are of different devices: /device:TPU:8 before, /device:TPU:1 now
where the time goes in v1:
time: 123 us; the launch traced here: 122 us
  waiting for transfers between devices  46.3 us (38%)
  starting transfers between devices  45.6 us (37%)
  Pallas kernels  20.6 us (17%)
  local copies, waits for them, and re-layouts  6.24 us (5%)
  other arithmetic  2.4 us (2%)
    ppermute x4, waiting for transfers between devices, swap_chips(): lax.ppermute(value, 'src', [(at, 2 * partner(at // 2) + at % 2) for at in...  23.8 us
    pallas_call x5, Pallas kernels, call(): pl.pallas_call(kernel, out_shape=shapes, in_specs=specs, out_specs=[pl.Bl...  13.1 us
    ppermute x7, starting transfers between devices, swap_cores(): return lax.ppermute(value, 'src', [(at, at ^ 1) for at in range(8)])  13 us
    ppermute x5, starting transfers between devices, tile_sum(): lax.ppermute(value, 'tile', [(at, at ^ bit) for at in range(TROWS * TCOLS)])  12.4 us
    ppermute x4, waiting for transfers between devices, tile_move(): return lax.ppermute(value, BOTH, pairs)  12 us
    ppermute x4, starting transfers between devices, tile_move(): return lax.ppermute(value, BOTH, pairs)  10.6 us
    ppermute x4, starting transfers between devices, swap_chips(): lax.ppermute(value, 'src', [(at, 2 * partner(at // 2) + at % 2) for at in...  9.66 us
    unnamed x54, local copies, waits for them, and re-layouts  6.24 us
  transfers between devices with their start and end apart: 20, of which 18 were waited for; matrix products, arithmetic and copies ran while one was open for 1% of the time, Pallas kernels for 3%

profile of v1, /device:TPU:1, one launch (start us, length us, event | category | flops | bytes accessed | tf_op | source)
XLA Modules:
  0.0 122.0 jit_solution(3629250267333489216)
XLA Ops:
  0.7 1.1 select_bitcast_fusion
  1.8 1.3 %collective-permute-start = (f32[64,512]{1,0:T(8,128)S(1)}, f32[64,512]{1,0:T(8,128)S(1)}, u32[]{:S(2)}, u32[]{:S(2)}) collective-permute-start(f32[64,512]{1,0:T(8,128)S(1)} %select_bitcast_fusion), channel_id=1, source_target_pairs={{0,8},{1,9},{2,10},{3,11},{4,12},{5,13},{6,14},{7,15},{8,16},{9,17... | collective-permute-start | bytes 393224 | tf_op jit(solution)/shard_map/ppermute | solution.py:384
  3.1 5.1 %collective-permute-done.mine_ref = f32[64,512]{1,0:T(8,128)S(1)} collective-permute-done((f32[64,512]{1,0:T(8,128)S(1)}, f32[64,512]{1,0:T(8,128)S(1)}, u32[]{:S(2)}, u32[]{:S(2)}) %collective-permute-start) | collective-permute-done | bytes 131104 | tf_op jit(solution)/shard_map/ppermute | solution.py:384
  8.2 1.1 collective-permute-start.1
  10.3 0.7 copy-done.5
  11.0 2.1 %pack.1 = f32[320,128]{1,0:T(8,128)} custom-call(s32[2]{0:T(128)} %pad_add_fusion.at_ref, f32[1,512,512]{2,1,0:T(8,128)} %right_ref.1, f32[1,512,512]{2,1,0:T(8,128)} %right_ref.1, f32[64,512]{1,0:T(8,128)} %copy-done.3, f32[64,512]{1,0:T(8,128)} %copy-done.5), custom_call_target="tpu_custom_call" | custom-call | tf_op jit(solution)/shard_map/pack/pallas_call | solution.py:409
  13.1 1.4 %collective-permute-start.2 = (f32[320,128]{1,0:T(8,128)}, f32[320,128]{1,0:T(8,128)S(1)}, u32[]{:S(2)}, u32[]{:S(2)}) collective-permute-start(f32[320,128]{1,0:T(8,128)} %pack.1), channel_id=1, source_target_pairs={{0,1},{1,2},{2,3},{3,4},{4,5},{5,6},{6,7},{8,9},{9,10},{10,11},{11... | collective-permute-start | bytes 491528 | tf_op jit(solution)/shard_map/ppermute | solution.py:384
  14.5 5.3 %collective-permute-done.2.mine_ref = f32[320,128]{1,0:T(8,128)S(1)} collective-permute-done((f32[320,128]{1,0:T(8,128)}, f32[320,128]{1,0:T(8,128)S(1)}, u32[]{:S(2)}, u32[]{:S(2)}) %collective-permute-start.2) | collective-permute-done | bytes 163872 | tf_op jit(solution)/shard_map/ppermute | solution.py:384
  19.8 0.7 collective-permute-start.3
  20.5 1.2 copy-done.11
  21.8 1.0 copy-done.18
  22.8 1.0 copy-done.19
  23.9 2.7 %own.1 = (f32[256,256]{1,0:T(8,128)S(1)}, f32[256,256]{1,0:T(8,128)S(1)}) custom-call(f32[1,512,512]{2,1,0:T(8,128)S(1)} %copy-done, f32[1,512,512]{2,1,0:T(8,128)S(1)} %copy-done.11, bf16[2,512,256]{2,1,0:T(8,128)(2,1)S(1)} %copy-done.2, bf16[2,256,512]{2,1,0:T(8,128)(2,1)S(1)} %copy-done.1, bf16[2,512,256]{2,1,0:T(8,128)(2,1)S(1)} %copy-done.19, ...), custom_call_target="tpu_custom_call" | custom-call | flops 1207959552 | bytes 4718592 | tf_op jit(solution)/shard_map/own/pallas_call | solution.py:118
  26.6 1.2 rows.1.basis_ref
  27.9 4.3 %image.1 = (f32[4,512,256]{2,1,0:T(8,128)S(1)}, f32[128,256]{1,0:T(8,128)S(1)}, f32[128,256]{1,0:T(8,128)S(1)}) custom-call(s32[2]{0:T(128)S(1)} %copy-done.9, s32[4,2,128]{2,1,0:T(2,128)S(1)} %copy-done.13, f32[4]{0:T(128)S(1)} %copy-done.14, f32[256,256]{1,0:T(8,128)S(1)} %rows.1.basis_ref, f32[320,128]{1,0:T(8,128)S(1)} %collective-permute-done.2.mine_ref, ...), custom_call_target="tpu_custom_call" | custom-call | flops 1500000000 | bytes 5115928 | tf_op jit(solution)/shard_map/image/pallas_call | solution.py:118
  32.4 1.3 %collective-permute-done.4 = f32[128,256]{1,0:T(8,128)S(1)} collective-permute-done((f32[128,256]{1,0:T(8,128)S(1)}, f32[128,256]{1,0:T(8,128)S(1)}, u32[]{:S(2)}, u32[]{:S(2)}) %collective-permute-start.4) | collective-permute-done | bytes 131104 | tf_op jit(solution)/shard_map/ppermute | solution.py:357
  33.7 3.1 %collective-permute-start.5 = (f32[128,256]{1,0:T(8,128)S(1)}, f32[128,256]{1,0:T(8,128)S(1)}, u32[]{:S(2)}, u32[]{:S(2)}) collective-permute-start(f32[128,256]{1,0:T(8,128)S(1)} %add.39), channel_id=1, source_target_pairs={{0,64},{32,96},{64,0},{96,32},{128,192},{160,224},{192,128},{224,1... | collective-permute-start | bytes 393224 | tf_op jit(solution)/shard_map/ppermute | solution.py:361
  36.8 6.5 %collective-permute-done.5 = f32[128,256]{1,0:T(8,128)S(1)} collective-permute-done((f32[128,256]{1,0:T(8,128)S(1)}, f32[128,256]{1,0:T(8,128)S(1)}, u32[]{:S(2)}, u32[]{:S(2)}) %collective-permute-start.5) | collective-permute-done | bytes 131104 | tf_op jit(solution)/shard_map/ppermute | solution.py:361
  43.3 1.3 %collective-permute-start.6 = (f32[128,256]{1,0:T(8,128)S(1)}, f32[128,256]{1,0:T(8,128)S(1)}, u32[]{:S(2)}, u32[]{:S(2)}) collective-permute-start(f32[128,256]{1,0:T(8,128)S(1)} %add.40), channel_id=1, source_target_pairs={{0,192},{32,224},{64,128},{96,160},{128,64},{160,96},{192,0},{224,... | collective-permute-start | bytes 393224 | tf_op jit(solution)/shard_map/ppermute | solution.py:361
  44.7 5.2 %collective-permute-done.6 = f32[128,256]{1,0:T(8,128)S(1)} collective-permute-done((f32[128,256]{1,0:T(8,128)S(1)}, f32[128,256]{1,0:T(8,128)S(1)}, u32[]{:S(2)}, u32[]{:S(2)}) %collective-permute-start.6) | collective-permute-done | bytes 131104 | tf_op jit(solution)/shard_map/ppermute | solution.py:361
  49.9 1.8 %collective-permute-start.7 = (f32[128,256]{1,0:T(8,128)S(1)}, f32[128,256]{1,0:T(8,128)S(1)}, u32[]{:S(2)}, u32[]{:S(2)}) collective-permute-start(f32[128,256]{1,0:T(8,128)S(1)} %add.41.mine_ref), channel_id=1, source_target_pairs={{0,32},{32,0},{64,96},{96,64},{128,160},{160,128},{192,224},{224,1... | collective-permute-start | bytes 393224 | tf_op jit(solution)/shard_map/ppermute | solution.py:357
  51.7 1.0 collective-permute-done.7.other_ref
  52.7 3.5 %adjoint.1 = (f32[128,256]{1,0:T(8,128)S(1)}, f32[128,256]{1,0:T(8,128)S(1)}, f32[8,128]{1,0:T(8,128)S(1)}) custom-call(s32[2]{0:T(128)S(1)} %copy-done.9, s32[4,2,128]{2,1,0:T(2,128)S(1)} %copy-done.13, f32[4]{0:T(128)S(1)} %copy-done.14, f32[128,256]{1,0:T(8,128)S(1)} %add.41.mine_ref, f32[128,256]{1,0:T(8,128)S(1)} %collective-permute-done.7.other_ref, ...), custom_call_target="tpu_custom_call" | custom-call | flops 1700000000 | bytes 4530200 | tf_op jit(solution)/shard_map/adjoint/pallas_call | solution.py:118
  56.6 1.0 collective-permute-done.8
  57.6 4.4 %collective-permute-start.9 = (f32[128,256]{1,0:T(8,128)S(1)}, f32[128,256]{1,0:T(8,128)S(1)}, u32[]{:S(2)}, u32[]{:S(2)}) collective-permute-start(f32[128,256]{1,0:T(8,128)S(1)} %add.42), channel_id=1, source_target_pairs={{0,64},{32,96},{64,0},{96,32},{128,192},{160,224},{192,128},{224,1... | collective-permute-start | bytes 393224 | tf_op jit(solution)/shard_map/ppermute | solution.py:361
  62.0 6.4 %collective-permute-done.9 = f32[128,256]{1,0:T(8,128)S(1)} collective-permute-done((f32[128,256]{1,0:T(8,128)S(1)}, f32[128,256]{1,0:T(8,128)S(1)}, u32[]{:S(2)}, u32[]{:S(2)}) %collective-permute-start.9) | collective-permute-done | bytes 131104 | tf_op jit(solution)/shard_map/ppermute | solution.py:361
  68.4 0.9 collective-permute-start.10
  69.3 5.7 %collective-permute-done.10 = f32[128,256]{1,0:T(8,128)S(1)} collective-permute-done((f32[128,256]{1,0:T(8,128)S(1)}, f32[128,256]{1,0:T(8,128)S(1)}, u32[]{:S(2)}, u32[]{:S(2)}) %collective-permute-start.10) | collective-permute-done | bytes 131104 | tf_op jit(solution)/shard_map/ppermute | solution.py:361
  75.1 1.9 %collective-permute-start.11 = (f32[128,256]{1,0:T(8,128)S(1)}, f32[128,256]{1,0:T(8,128)S(1)}, u32[]{:S(2)}, u32[]{:S(2)}) collective-permute-start(f32[128,256]{1,0:T(8,128)S(1)} %add.44.mine_ref), channel_id=1, source_target_pairs={{0,32},{32,0},{64,96},{96,64},{128,160},{160,128},{192,224},{224,1... | collective-permute-start | bytes 393224 | tf_op jit(solution)/shard_map/ppermute | solution.py:357
  77.0 1.0 collective-permute-done.11.other_ref
  78.6 2.6 %lines.1 = (f32[128,256]{1,0:T(8,128)}, f32[64,256]{1,0:T(8,128)}) custom-call(s32[2]{0:T(128)} %pad_add_fusion.at_ref, f32[128,256]{1,0:T(8,128)} %copy-done.24, f32[128,256]{1,0:T(8,128)} %copy-done.25, bf16[4,2,128,256]{3,2,1,0:T(8,128)(2,1)} %constant.75.clone.block_ref, bf16[4,2,64,256]{3,2,1,0:T(8,128)(2,1)} %constant.76.clone.outer_ref), custom_call_target="tpu_custom_call" | custom-call | tf_op jit(solution)/shard_map/lines/pallas_call | solution.py:483
  81.2 4.1 %collective-permute-start.12 = (f32[64,256]{1,0:T(8,128)}, f32[64,256]{1,0:T(8,128)S(1)}, u32[]{:S(2)}, u32[]{:S(2)}) collective-permute-start(f32[64,256]{1,0:T(8,128)} %get-tuple-element.22), channel_id=1, source_target_pairs={{0,8},{1,9},{2,10},{3,11},{4,12},{5,13},{6,14},{7,15},{8,16},{9,17... | collective-permute-start | bytes 196616 | tf_op jit(solution)/shard_map/ppermute | solution.py:384
  85.3 1.6 %collective-permute-done.12.rim_ref = f32[64,256]{1,0:T(8,128)S(1)} collective-permute-done((f32[64,256]{1,0:T(8,128)}, f32[64,256]{1,0:T(8,128)S(1)}, u32[]{:S(2)}, u32[]{:S(2)}) %collective-permute-start.12) | collective-permute-done | bytes 65568 | tf_op jit(solution)/shard_map/ppermute | solution.py:384
  87.6 2.8 %pixels.1 = (f32[64,512]{1,0:T(8,128)}, f32[64,128]{1,0:T(8,128)}) custom-call(s32[2]{0:T(128)} %pad_add_fusion.at_ref, f32[128,256]{1,0:T(8,128)} %get-tuple-element.21.lines_ref, f32[64,256]{1,0:T(8,128)} %copy-done.26, bf16[2,256,512]{2,1,0:T(8,128)(2,1)} %constant.64.clone.mid_t_ref, bf16[2,2,256,64]{3,2,1,0:T(8,128)(2,1)} %constant.77.clone.sides_ref), custom_call_target="tpu_custom_call" | custom-call | tf_op jit(solution)/shard_map/pixels/pallas_call | solution.py:500
  90.4 3.8 %collective-permute-start.13 = (f32[64,128]{1,0:T(8,128)}, f32[64,128]{1,0:T(8,128)S(1)}, u32[]{:S(2)}, u32[]{:S(2)}) collective-permute-start(f32[64,128]{1,0:T(8,128)} %get-tuple-element.24), channel_id=1, source_target_pairs={{1,0},{2,1},{3,2},{4,3},{5,4},{6,5},{7,6},{9,8},{10,9},{11,10},{12... | collective-permute-start | bytes 98312 | tf_op jit(solution)/shard_map/ppermute | solution.py:384
  94.1 3.2 %collective-permute-start.15 = (f32[8,128]{1,0:T(8,128)S(1)}, f32[8,128]{1,0:T(8,128)S(1)}, u32[]{:S(2)}, u32[]{:S(2)}) collective-permute-start(f32[8,128]{1,0:T(8,128)S(1)} %get-tuple-element.25), channel_id=1, source_target_pairs={{0,1},{1,0},{2,3},{3,2},{4,5},{5,4},{6,7},{7,6},{8,9},{9,8},{10,11... | collective-permute-start | bytes 12296 | tf_op jit(solution)/shard_map/ppermute | solution.py:389
  97.3 1.4 %collective-permute-done.15 = f32[8,128]{1,0:T(8,128)S(1)} collective-permute-done((f32[8,128]{1,0:T(8,128)S(1)}, f32[8,128]{1,0:T(8,128)S(1)}, u32[]{:S(2)}, u32[]{:S(2)}) %collective-permute-start.15) | collective-permute-done | bytes 4128 | tf_op jit(solution)/shard_map/ppermute | solution.py:389
  98.8 1.4 %collective-permute-start.16 = (f32[8,128]{1,0:T(8,128)S(1)}, f32[8,128]{1,0:T(8,128)S(1)}, u32[]{:S(2)}, u32[]{:S(2)}) collective-permute-start(f32[8,128]{1,0:T(8,128)S(1)} %add.45), channel_id=1, source_target_pairs={{0,2},{1,3},{2,0},{3,1},{4,6},{5,7},{6,4},{7,5},{8,10},{9,11},{10,... | collective-permute-start | bytes 12296 | tf_op jit(solution)/shard_map/ppermute | solution.py:389
  100.2 1.0 collective-permute-done.16
  101.2 3.0 %collective-permute-start.17 = (f32[8,128]{1,0:T(8,128)S(1)}, f32[8,128]{1,0:T(8,128)S(1)}, u32[]{:S(2)}, u32[]{:S(2)}) collective-permute-start(f32[8,128]{1,0:T(8,128)S(1)} %add.46), channel_id=1, source_target_pairs={{0,4},{1,5},{2,6},{3,7},{4,0},{5,1},{6,2},{7,3},{8,12},{9,13},{10,... | collective-permute-start | bytes 12296 | tf_op jit(solution)/shard_map/ppermute | solution.py:389
  104.2 1.0 collective-permute-done.17
  105.2 1.7 %collective-permute-start.18 = (f32[8,128]{1,0:T(8,128)S(1)}, f32[8,128]{1,0:T(8,128)S(1)}, u32[]{:S(2)}, u32[]{:S(2)}) collective-permute-start(f32[8,128]{1,0:T(8,128)S(1)} %add.47), channel_id=1, source_target_pairs={{0,8},{1,9},{2,10},{3,11},{4,12},{5,13},{6,14},{7,15},{8,0},{9,1},... | collective-permute-start | bytes 12296 | tf_op jit(solution)/shard_map/ppermute | solution.py:389
  106.9 1.0 collective-permute-done.18
  107.9 3.1 %collective-permute-start.19 = (f32[8,128]{1,0:T(8,128)S(1)}, f32[8,128]{1,0:T(8,128)S(1)}, u32[]{:S(2)}, u32[]{:S(2)}) collective-permute-start(f32[8,128]{1,0:T(8,128)S(1)} %add.48), channel_id=1, source_target_pairs={{0,16},{1,17},{2,18},{3,19},{4,20},{5,21},{6,22},{7,23},{8,24},{9,... | collective-permute-start | bytes 12296 | tf_op jit(solution)/shard_map/ppermute | solution.py:389
  111.0 1.0 collective-permute-done.19
  112.0 6.9 %collective-permute-start.14 = (f32[64,128]{1,0:T(8,128)S(1)}, f32[64,128]{1,0:T(8,128)S(1)}, u32[]{:S(2)}, u32[]{:S(2)}) collective-permute-start(f32[64,128]{1,0:T(8,128)S(1)} %collective-permute-done.13.mine_ref), channel_id=1, source_target_pairs={{0,32},{32,0},{64,96},{96,64},{128,160},{160,128},{192,224},{224,1... | collective-permute-start | bytes 98312 | tf_op jit(solution)/shard_map/ppermute | solution.py:357
  119.8 0.9 copy-done.7
  120.7 1.3 %join.1 = f32[1,64,512]{2,1,0:T(8,128)} custom-call(s32[2]{0:T(128)S(1)} %copy-done.10, f32[64,512]{1,0:T(8,128)S(1)} %copy-done.7, f32[64,128]{1,0:T(8,128)S(1)} %collective-permute-done.13.mine_ref, f32[64,128]{1,0:T(8,128)S(1)} %collective-permute-done.14.other_ref), custom_call_target="tpu_custom_call" | custom-call | flops 32768 | bytes 327688 | tf_op jit(solution)/shard_map/join/pallas_call | solution.py:118
  (68 shorter events, 3.9 us)
Async XLA Ops:
  0.6 19.9 %copy-start.1 = (bf16[2,256,512]{2,1,0:T(8,128)(2,1)S(1)}, bf16[2,256,512]{2,1,0:T(8,128)(2,1)}, u32[]{:S(2)}) copy-start(bf16[2,256,512]{2,1,0:T(8,128)(2,1)} %constant.64.clone.mid_t_ref) | copy-start | bytes 1572868
  0.6 19.9 %copy-start.2 = (bf16[2,512,256]{2,1,0:T(8,128)(2,1)S(1)}, bf16[2,512,256]{2,1,0:T(8,128)(2,1)}, u32[]{:S(2)}) copy-start(bf16[2,512,256]{2,1,0:T(8,128)(2,1)} %constant.63.clone.mid_ref) | copy-start | bytes 1572868
  0.7 19.9 %copy-start = (f32[1,512,512]{2,1,0:T(8,128)S(1)}, f32[1,512,512]{2,1,0:T(8,128)}, u32[]{:S(2)}) copy-start(f32[1,512,512]{2,1,0:T(8,128)} %right_ref.1) | copy-start | bytes 3145732
  1.8 6.4 %collective-permute-start = (f32[64,512]{1,0:T(8,128)S(1)}, f32[64,512]{1,0:T(8,128)S(1)}, u32[]{:S(2)}, u32[]{:S(2)}) collective-permute-start(f32[64,512]{1,0:T(8,128)S(1)} %select_bitcast_fusion), channel_id=1, source_target_pairs={{0,8},{1,9},{2,10},{3,11},{4,12},{5,13},{6,14},{7,15},{8,16},{9,17... | collective-permute-start | bytes 393224 | tf_op jit(solution)/shard_map/ppermute | solution.py:384
  8.2 2.1 %copy-start.3 = (f32[64,512]{1,0:T(8,128)}, f32[64,512]{1,0:T(8,128)S(1)}, u32[]{:S(2)}) copy-start(f32[64,512]{1,0:T(8,128)S(1)} %collective-permute-done.mine_ref) | copy-start | bytes 393220
  8.2 2.1 %collective-permute-start.1 = (f32[64,512]{1,0:T(8,128)S(1)}, f32[64,512]{1,0:T(8,128)S(1)}, u32[]{:S(2)}, u32[]{:S(2)}) collective-permute-start(f32[64,512]{1,0:T(8,128)S(1)} %collective-permute-done.mine_ref), channel_id=1, source_target_pairs={{0,32},{32,0},{64,96},{96,64},{128,160},{160,128},{192,224},{224,1... | collective-permute-start | bytes 393224 | tf_op jit(solution)/shard_map/ppermute | solution.py:357
  10.3 0.7 copy-start.5
  11.0 16.9 %copy-start.12 = (f32[128,128]{1,0:T(8,128)S(1)}, f32[128,128]{1,0:T(8,128)}, u32[]{:S(2)}) copy-start(f32[128,128]{1,0:T(8,128)} %gain_ref.3) | copy-start | bytes 196612
  11.0 16.9 %copy-start.13 = (s32[4,2,128]{2,1,0:T(2,128)S(1)}, s32[4,2,128]{2,1,0:T(2,128)}, u32[]{:S(2)}) copy-start(s32[4,2,128]{2,1,0:T(2,128)} %index_ref.3) | copy-start | bytes 12292
  11.0 16.9 %copy-start.14 = (f32[4]{0:T(128)S(1)}, f32[4]{0:T(128)}, u32[]{:S(2)}) copy-start(f32[4]{0:T(128)} %weights_ref.3) | copy-start | bytes 52
  11.0 16.9 %copy-start.15 = (bf16[2,256,640]{2,1,0:T(8,128)(2,1)S(1)}, bf16[2,256,640]{2,1,0:T(8,128)(2,1)}, u32[]{:S(2)}) copy-start(bf16[2,256,640]{2,1,0:T(8,128)(2,1)} %constant.69.clone.all_t_ref) | copy-start | bytes 1966084
  11.0 16.9 %copy-start.21 = (bf16[256,256]{1,0:T(8,128)(2,1)S(1)}, bf16[256,256]{1,0:T(8,128)(2,1)}, u32[]{:S(2)}) copy-start(bf16[256,256]{1,0:T(8,128)(2,1)} %constant.71.clone.fold_t_ref) | copy-start | bytes 393220
  13.0 13.5 %copy-start.4 = (f32[64,512]{1,0:T(8,128)S(1)}, f32[64,512]{1,0:T(8,128)}, u32[]{:S(2)}) copy-start(f32[64,512]{1,0:T(8,128)} %copy-done.3) | copy-start | bytes 393220
  13.0 13.5 %copy-start.6 = (f32[64,512]{1,0:T(8,128)S(1)}, f32[64,512]{1,0:T(8,128)}, u32[]{:S(2)}) copy-start(f32[64,512]{1,0:T(8,128)} %copy-done.5) | copy-start | bytes 393220
  13.1 13.5 %copy-start.8 = (bf16[2,256,128]{2,1,0:T(8,128)(2,1)S(1)}, bf16[2,256,128]{2,1,0:T(8,128)(2,1)}, u32[]{:S(2)}) copy-start(bf16[2,256,128]{2,1,0:T(8,128)(2,1)} %constant.67.clone.rims_t_ref) | copy-start | bytes 393220
  13.1 13.5 %copy-start.9 = (s32[2]{0:T(128)S(1)}, s32[2]{0:T(128)}, u32[]{:S(2)}) copy-start(s32[2]{0:T(128)} %pad_add_fusion.at_ref) | copy-start | bytes 28
  13.1 6.7 %collective-permute-start.2 = (f32[320,128]{1,0:T(8,128)}, f32[320,128]{1,0:T(8,128)S(1)}, u32[]{:S(2)}, u32[]{:S(2)}) collective-permute-start(f32[320,128]{1,0:T(8,128)} %pack.1), channel_id=1, source_target_pairs={{0,1},{1,2},{2,3},{3,4},{4,5},{5,6},{6,7},{8,9},{9,10},{10,11},{11... | collective-permute-start | bytes 491528 | tf_op jit(solution)/shard_map/ppermute | solution.py:384
  19.8 8.0 %collective-permute-start.3 = (f32[320,128]{1,0:T(8,128)S(1)}, f32[320,128]{1,0:T(8,128)S(1)}, u32[]{:S(2)}, u32[]{:S(2)}) collective-permute-start(f32[320,128]{1,0:T(8,128)S(1)} %collective-permute-done.2.mine_ref), channel_id=1, source_target_pairs={{0,32},{32,0},{64,96},{96,64},{128,160},{160,128},{192,224},{224,1... | collective-permute-start | bytes 491528 | tf_op jit(solution)/shard_map/ppermute | solution.py:357
  20.5 1.2 %copy-start.11 = (f32[1,512,512]{2,1,0:T(8,128)S(1)}, f32[1,512,512]{2,1,0:T(8,128)}, u32[]{:S(2)}) copy-start(f32[1,512,512]{2,1,0:T(8,128)} %target_ref.1) | copy-start | bytes 3145732
  21.8 1.0 copy-start.18
  22.8 1.0 copy-start.19
  23.8 4.0 %copy-start.16 = (bf16[2,512,256]{2,1,0:T(8,128)(2,1)S(1)}, bf16[2,512,256]{2,1,0:T(8,128)(2,1)}, u32[]{:S(2)}) copy-start(bf16[2,512,256]{2,1,0:T(8,128)(2,1)} %constant.73.clone.coarse_t_ref) | copy-start | bytes 1572868
  23.8 4.0 %copy-start.17 = (bf16[2,256,512]{2,1,0:T(8,128)(2,1)S(1)}, bf16[2,256,512]{2,1,0:T(8,128)(2,1)}, u32[]{:S(2)}) copy-start(bf16[2,256,512]{2,1,0:T(8,128)(2,1)} %constant.72.clone.coarse_ref) | copy-start | bytes 1572868
  23.8 4.0 %copy-start.22 = (bf16[256,256]{1,0:T(8,128)(2,1)S(1)}, bf16[256,256]{1,0:T(8,128)(2,1)}, u32[]{:S(2)}) copy-start(bf16[256,256]{1,0:T(8,128)(2,1)} %constant.70.clone.fold_ref) | copy-start | bytes 393220
  23.8 4.1 %copy-start.23 = (bf16[2,128,256]{2,1,0:T(8,128)(2,1)S(1)}, bf16[2,128,256]{2,1,0:T(8,128)(2,1)}, u32[]{:S(2)}) copy-start(bf16[2,128,256]{2,1,0:T(8,128)(2,1)} %constant.68.clone.rims_ref) | copy-start | bytes 393220
  27.8 24.9 %copy-start.20 = (bf16[2,256,256]{2,1,0:T(8,128)(2,1)S(1)}, bf16[2,256,256]{2,1,0:T(8,128)(2,1)}, u32[]{:S(2)}) copy-start(bf16[2,256,256]{2,1,0:T(8,128)(2,1)} %constant.74.clone.gram_ref) | copy-start | bytes 786436
  32.3 1.4 %collective-permute-start.4 = (f32[128,256]{1,0:T(8,128)S(1)}, f32[128,256]{1,0:T(8,128)S(1)}, u32[]{:S(2)}, u32[]{:S(2)}) collective-permute-start(f32[128,256]{1,0:T(8,128)S(1)} %get-tuple-element.16), channel_id=1, source_target_pairs={{0,32},{32,0},{64,96},{96,64},{128,160},{160,128},{192,224},{224,1... | collective-permute-start | bytes 393224 | tf_op jit(solution)/shard_map/ppermute | solution.py:357
  33.7 9.6 %collective-permute-start.5 = (f32[128,256]{1,0:T(8,128)S(1)}, f32[128,256]{1,0:T(8,128)S(1)}, u32[]{:S(2)}, u32[]{:S(2)}) collective-permute-start(f32[128,256]{1,0:T(8,128)S(1)} %add.39), channel_id=1, source_target_pairs={{0,64},{32,96},{64,0},{96,32},{128,192},{160,224},{192,128},{224,1... | collective-permute-start | bytes 393224 | tf_op jit(solution)/shard_map/ppermute | solution.py:361
  43.3 6.5 %collective-permute-start.6 = (f32[128,256]{1,0:T(8,128)S(1)}, f32[128,256]{1,0:T(8,128)S(1)}, u32[]{:S(2)}, u32[]{:S(2)}) collective-permute-start(f32[128,256]{1,0:T(8,128)S(1)} %add.40), channel_id=1, source_target_pairs={{0,192},{32,224},{64,128},{96,160},{128,64},{160,96},{192,0},{224,... | collective-permute-start | bytes 393224 | tf_op jit(solution)/shard_map/ppermute | solution.py:361
  49.9 2.8 %collective-permute-start.7 = (f32[128,256]{1,0:T(8,128)S(1)}, f32[128,256]{1,0:T(8,128)S(1)}, u32[]{:S(2)}, u32[]{:S(2)}) collective-permute-start(f32[128,256]{1,0:T(8,128)S(1)} %add.41.mine_ref), channel_id=1, source_target_pairs={{0,32},{32,0},{64,96},{96,64},{128,160},{160,128},{192,224},{224,1... | collective-permute-start | bytes 393224 | tf_op jit(solution)/shard_map/ppermute | solution.py:357
  56.2 63.6 %copy-start.10 = (s32[2]{0:T(128)S(1)}, s32[2]{0:T(128)}, u32[]{:S(2)}) copy-start(s32[2]{0:T(128)} %pad_add_fusion.at_ref) | copy-start | bytes 28
  56.2 1.4 %collective-permute-start.8 = (f32[128,256]{1,0:T(8,128)S(1)}, f32[128,256]{1,0:T(8,128)S(1)}, u32[]{:S(2)}, u32[]{:S(2)}) collective-permute-start(f32[128,256]{1,0:T(8,128)S(1)} %get-tuple-element.20), channel_id=1, source_target_pairs={{0,32},{32,0},{64,96},{96,64},{128,160},{160,128},{192,224},{224,1... | collective-permute-start | bytes 393224 | tf_op jit(solution)/shard_map/ppermute | solution.py:357
  57.6 10.8 %collective-permute-start.9 = (f32[128,256]{1,0:T(8,128)S(1)}, f32[128,256]{1,0:T(8,128)S(1)}, u32[]{:S(2)}, u32[]{:S(2)}) collective-permute-start(f32[128,256]{1,0:T(8,128)S(1)} %add.42), channel_id=1, source_target_pairs={{0,64},{32,96},{64,0},{96,32},{128,192},{160,224},{192,128},{224,1... | collective-permute-start | bytes 393224 | tf_op jit(solution)/shard_map/ppermute | solution.py:361
  68.4 6.6 %collective-permute-start.10 = (f32[128,256]{1,0:T(8,128)S(1)}, f32[128,256]{1,0:T(8,128)S(1)}, u32[]{:S(2)}, u32[]{:S(2)}) collective-permute-start(f32[128,256]{1,0:T(8,128)S(1)} %add.43), channel_id=1, source_target_pairs={{0,192},{32,224},{64,128},{96,160},{128,64},{160,96},{192,0},{224,... | collective-permute-start | bytes 393224 | tf_op jit(solution)/shard_map/ppermute | solution.py:361
  75.1 2.9 %copy-start.24 = (f32[128,256]{1,0:T(8,128)}, f32[128,256]{1,0:T(8,128)S(1)}, u32[]{:S(2)}) copy-start(f32[128,256]{1,0:T(8,128)S(1)} %add.44.mine_ref) | copy-start | bytes 393220
  75.1 2.9 %collective-permute-start.11 = (f32[128,256]{1,0:T(8,128)S(1)}, f32[128,256]{1,0:T(8,128)S(1)}, u32[]{:S(2)}, u32[]{:S(2)}) collective-permute-start(f32[128,256]{1,0:T(8,128)S(1)} %add.44.mine_ref), channel_id=1, source_target_pairs={{0,32},{32,0},{64,96},{96,64},{128,160},{160,128},{192,224},{224,1... | collective-permute-start | bytes 393224 | tf_op jit(solution)/shard_map/ppermute | solution.py:357
  77.9 0.7 copy-start.25
  81.2 5.7 %collective-permute-start.12 = (f32[64,256]{1,0:T(8,128)}, f32[64,256]{1,0:T(8,128)S(1)}, u32[]{:S(2)}, u32[]{:S(2)}) collective-permute-start(f32[64,256]{1,0:T(8,128)} %get-tuple-element.22), channel_id=1, source_target_pairs={{0,8},{1,9},{2,10},{3,11},{4,12},{5,13},{6,14},{7,15},{8,16},{9,17... | collective-permute-start | bytes 196616 | tf_op jit(solution)/shard_map/ppermute | solution.py:384
  86.9 0.6 copy-start.26
  90.4 21.7 %collective-permute-start.13 = (f32[64,128]{1,0:T(8,128)}, f32[64,128]{1,0:T(8,128)S(1)}, u32[]{:S(2)}, u32[]{:S(2)}) collective-permute-start(f32[64,128]{1,0:T(8,128)} %get-tuple-element.24), channel_id=1, source_target_pairs={{1,0},{2,1},{3,2},{4,3},{5,4},{6,5},{7,6},{9,8},{10,9},{11,10},{12... | collective-permute-start | bytes 98312 | tf_op jit(solution)/shard_map/ppermute | solution.py:384
  94.1 4.6 %collective-permute-start.15 = (f32[8,128]{1,0:T(8,128)S(1)}, f32[8,128]{1,0:T(8,128)S(1)}, u32[]{:S(2)}, u32[]{:S(2)}) collective-permute-start(f32[8,128]{1,0:T(8,128)S(1)} %get-tuple-element.25), channel_id=1, source_target_pairs={{0,1},{1,0},{2,3},{3,2},{4,5},{5,4},{6,7},{7,6},{8,9},{9,8},{10,11... | collective-permute-start | bytes 12296 | tf_op jit(solution)/shard_map/ppermute | solution.py:389
  98.8 2.5 %collective-permute-start.16 = (f32[8,128]{1,0:T(8,128)S(1)}, f32[8,128]{1,0:T(8,128)S(1)}, u32[]{:S(2)}, u32[]{:S(2)}) collective-permute-start(f32[8,128]{1,0:T(8,128)S(1)} %add.45), channel_id=1, source_target_pairs={{0,2},{1,3},{2,0},{3,1},{4,6},{5,7},{6,4},{7,5},{8,10},{9,11},{10,... | collective-permute-start | bytes 12296 | tf_op jit(solution)/shard_map/ppermute | solution.py:389
  101.2 4.0 %collective-permute-start.17 = (f32[8,128]{1,0:T(8,128)S(1)}, f32[8,128]{1,0:T(8,128)S(1)}, u32[]{:S(2)}, u32[]{:S(2)}) collective-permute-start(f32[8,128]{1,0:T(8,128)S(1)} %add.46), channel_id=1, source_target_pairs={{0,4},{1,5},{2,6},{3,7},{4,0},{5,1},{6,2},{7,3},{8,12},{9,13},{10,... | collective-permute-start | bytes 12296 | tf_op jit(solution)/shard_map/ppermute | solution.py:389
  105.2 2.7 %collective-permute-start.18 = (f32[8,128]{1,0:T(8,128)S(1)}, f32[8,128]{1,0:T(8,128)S(1)}, u32[]{:S(2)}, u32[]{:S(2)}) collective-permute-start(f32[8,128]{1,0:T(8,128)S(1)} %add.47), channel_id=1, source_target_pairs={{0,8},{1,9},{2,10},{3,11},{4,12},{5,13},{6,14},{7,15},{8,0},{9,1},... | collective-permute-start | bytes 12296 | tf_op jit(solution)/shard_map/ppermute | solution.py:389
  107.9 4.1 %collective-permute-start.19 = (f32[8,128]{1,0:T(8,128)S(1)}, f32[8,128]{1,0:T(8,128)S(1)}, u32[]{:S(2)}, u32[]{:S(2)}) collective-permute-start(f32[8,128]{1,0:T(8,128)S(1)} %add.48), channel_id=1, source_target_pairs={{0,16},{1,17},{2,18},{3,19},{4,20},{5,21},{6,22},{7,23},{8,24},{9,... | collective-permute-start | bytes 12296 | tf_op jit(solution)/shard_map/ppermute | solution.py:389
  112.0 7.8 %collective-permute-start.14 = (f32[64,128]{1,0:T(8,128)S(1)}, f32[64,128]{1,0:T(8,128)S(1)}, u32[]{:S(2)}, u32[]{:S(2)}) collective-permute-start(f32[64,128]{1,0:T(8,128)S(1)} %collective-permute-done.13.mine_ref), channel_id=1, source_target_pairs={{0,32},{32,0},{64,96},{96,64},{128,160},{160,128},{192,224},{224,1... | collective-permute-start | bytes 98312 | tf_op jit(solution)/shard_map/ppermute | solution.py:357
  119.8 0.9 copy-start.7

commit v2 on v1

--- a/solution.py
+++ b/solution.py
@@ -64,7 +64,6 @@
     return {
         "mid": two_terms(basis[A : N - A]),
         "mid_t": two_terms(basis[A : N - A].T),
-        "all_t": two_terms(basis.T),
         "rims": two_terms(rims),
         "rims_t": two_terms(rims.T),
         "fold": fold.astype(bf16),
@@ -75,7 +74,7 @@
         "spread_t": two_terms(spread.T),
         "gram": two_terms(spread.T @ spread),
         "blocks": np.ascontiguousarray(two_terms(basis[A : N - A]).reshape(2, 4, K, W).swapaxes(0, 1)),
-        "outer": np.stack([two_terms(basis[N - A :])] * 2 + [two_terms(basis[:A])] * 2),
+        "outer": np.stack([two_terms(basis[N - A :]), two_terms(basis[:A])]),
         "sides_t": np.stack([two_terms(basis[:A].T), two_terms(basis[N - A :].T)]),
     }
 
@@ -109,10 +108,9 @@
     return dot(high, table) + dot(low, table)
 
 
-def call(kernel, outs, ins, name, flops, scratch=(), smem=()):
-    specs = [
-        pl.BlockSpec(memory_space=pltpu.SMEM if at in smem else pltpu.VMEM) for at in range(len(ins))
-    ]
+def call(kernel, outs, ins, name, flops, scratch=(), smem=(), hbm=()):
+    spaces = dict.fromkeys(smem, pltpu.SMEM) | dict.fromkeys(hbm, pltpu.HBM)
+    specs = [pl.BlockSpec(memory_space=spaces.get(at, pltpu.VMEM)) for at in range(len(ins))]
     shapes = [jax.ShapeDtypeStruct(shape, F32) for shape in outs]
     moved = 4 * sum(math.prod(shape) for shape in outs) + sum(one.size * one.dtype.itemsize for one in ins)
     return pl.pallas_call(
@@ -127,37 +125,57 @@
     )(*ins)
 
 
-def own_kernel(tile_ref, target_ref, mid_ref, mid_t_ref, spread_ref, spread_t_ref, basis_ref, wanted_ref):
-    upper = product(terms(tile_ref[0]), pair_of(mid_ref))
-    basis_ref[...] = product(pair_of(mid_t_ref), terms(upper))
-    upper = product(terms(target_ref[0]), pair_of(spread_ref))
+def my_place():
+    group = lax.axis_index("src")
+    return group // 2, group % 2
+
+
+def own_kernel(tile_hbm, table_hbm, rows_ref, tile_ref, table_ref, done_ref):
+    table_copy = pltpu.make_async_copy(table_hbm, table_ref, done_ref.at[0])
+    table_copy.start()
+    chunks = []
+    for chunk in range(PIX // K):
+        part = pl.ds(chunk * K, K)
+        chunks.append(pltpu.make_async_copy(tile_hbm.at[0, part], tile_ref.at[part], done_ref.at[1 + chunk]))
+        chunks[-1].start()
+    table_copy.wait()
+    total = jnp.zeros((W, PIX), F32)
+    for chunk, copy in enumerate(chunks):
+        copy.wait()
+        part = slice(chunk * K, chunk * K + K)
+        total = total + product((table_ref[0, :, part], table_ref[1, :, part]), terms(tile_ref[part]))
+    rows_ref[...] = total
+
+
+def wanted_kernel(
+    target_hbm, spread_hbm, spread_t_hbm, wanted_ref, target_ref, spread_ref, spread_t_ref, done_ref
+):
+    copies = [
+        pltpu.make_async_copy(spread_hbm, spread_ref, done_ref.at[0]),
+        pltpu.make_async_copy(target_hbm.at[0], target_ref, done_ref.at[1]),
+        pltpu.make_async_copy(spread_t_hbm, spread_t_ref, done_ref.at[2]),
+    ]
+    for copy in copies:
+        copy.start()
+    for copy in copies:
+        copy.wait()
+    upper = product(terms(target_ref[...]), pair_of(spread_ref))
     wanted_ref[...] = product(pair_of(spread_t_ref), terms(upper))
 
 
-def pack_kernel(at_ref, left_ref, right_ref, mine_ref, other_ref, out_ref):
-    first = at_ref[1] == 0
-    mine, other = mine_ref[...], other_ref[...]
-    up = jnp.where(first, mine, other)
-    down = jnp.where(first, other, mine)
-
-    def chosen(left, right):
-        return jnp.where(first, right[:, K - A :], left[:, :A])
-
-    up_part = chosen(up[:, :K], up[:, PIX - K :])
-    down_part = chosen(down[:, :K], down[:, PIX - K :])
-    middle = chosen(left_ref[0], right_ref[0])
-    half = N // 2
-    top = jnp.concatenate([up_part, middle[: half - A]], axis=0)
-    bottom = jnp.concatenate([middle[half - A :], down_part], axis=0)
-    out_ref[...] = jnp.concatenate([top, bottom], axis=1)
-
-
-def rows_kernel(at_ref, basis_ref, mine_ref, other_ref, mid_ref, rims_t_ref, out_ref):
-    first = at_ref[1] == 0
+def rows_kernel(rows_ref, mine_ref, other_ref, rims_t_ref, all_ref, side_ref):
+    _, core = my_place()
+    first = core == 0
     mine, other = mine_ref[...], other_ref[...]
     rim = jnp.concatenate([jnp.where(first, mine, other), jnp.where(first, other, mine)], axis=0)
-    upper = product(terms(rim), pair_of(mid_ref))
-    out_ref[...] = basis_ref[...] + product(pair_of(rims_t_ref), terms(upper))
+    rows = rows_ref[...] + product(pair_of(rims_t_ref), terms(rim))
+    all_ref[...] = rows
+    side = jnp.where(first, rows[:, PIX - A :], rows[:, :A])
+    side_ref[...] = jnp.concatenate([side[:K], side[K:]], axis=1)
+
+
+def columns_kernel(rows_ref, mid_ref, basis_ref):
+    basis_ref[...] = product(terms(rows_ref[...]), pair_of(mid_ref))
 
 
 def halves(value, core):
@@ -185,7 +203,6 @@
 
 
 def image_kernel(
-    at_ref,
     index_ref,
     weights_ref,
     basis_ref,
@@ -193,7 +210,6 @@
     other_ref,
     gain_ref,
     rims_ref,
-    all_t_ref,
     fold_ref,
     fold_t_ref,
     coarse_ref,
@@ -204,7 +220,7 @@
     real_ref,
     imag_ref,
 ):
-    core = at_ref[1]
+    _, core = my_place()
     first = core == 0
     mine, other = mine_ref[...], other_ref[...]
     left = jnp.where(first, mine, other)
@@ -216,8 +232,7 @@
         ],
         axis=0,
     )
-    upper = product(terms(rim), pair_of(rims_ref))
-    basis = basis_ref[...] + product(pair_of(all_t_ref), terms(upper))
+    basis = basis_ref[...] + product(terms(rim), pair_of(rims_ref))
     zero = jnp.zeros((K, K), F32)
     even = jnp.concatenate(
         [
@@ -259,44 +274,47 @@
     send_ref[...] = send
 
 
+def residual_kernel(mine_ref, other_ref, wanted_ref, field_ref, gram_ref, residual_ref, energy_ref):
+    _, core = my_place()
+    bright = joined(mine_ref[...], other_ref[...], core)
+    gram = pair_of(gram_ref)
+    value = product(terms(product(gram, terms(bright))), gram)
+    residual = value * (1.0 / (8 * SOURCES)) - wanted_ref[...]
+    residual_ref[...] = residual
+    lanes = lax.broadcasted_iota(jnp.int32, (8, K), 1)
+    energies = jnp.zeros((8, K), F32)
+    for source in range(SOURCES):
+        real, imag = field_ref[source, :W], field_ref[source, W:]
+        energy = jnp.sum(residual * (real * real + imag * imag))
+        energies = jnp.where(lanes == source, energy, energies)
+    energy_ref[...] = energies
+
+
 def adjoint_kernel(
-    at_ref,
     index_ref,
     weights_ref,
-    mine_ref,
-    other_ref,
-    wanted_ref,
+    residual_ref,
     field_ref,
     gain_ref,
-    gram_ref,
     fold_ref,
     fold_t_ref,
     coarse_ref,
     coarse_t_ref,
     keep_ref,
     send_ref,
-    energy_ref,
     real_ref,
     imag_ref,
 ):
-    core = at_ref[1]
-    bright = joined(mine_ref[...], other_ref[...], core)
-    gram = pair_of(gram_ref)
-    value = product(terms(product(gram, terms(bright))), gram)
-    residual = value * (1.0 / (8 * SOURCES)) - wanted_ref[...]
+    _, core = my_place()
+    residual = residual_ref[...]
     disc = disc_of(gain_ref[...])
     sides = []
-    lanes = lax.broadcasted_iota(jnp.int32, (8, K), 1)
-    energies = jnp.zeros((8, K), F32)
     for source in range(SOURCES):
         field = field_ref[source]
         real, imag = field[:W], field[W:]
         scaled = jnp.concatenate([residual * real, residual * imag], axis=1)
-        energy = jnp.sum(scaled[:, :W] * real + scaled[:, W:] * imag)
-        energies = jnp.where(lanes == source, energy, energies)
         back = product(terms(scaled), pair_of(coarse_t_ref))
         sides.append(jnp.concatenate([back[:, :K], back[:, K:]], axis=0))
-    energy_ref[...] = energies
     real_ref[...] = jnp.zeros((2, W, K), F32)
     imag_ref[...] = jnp.zeros((2, W, K), F32)
     pad = jnp.zeros((K, K), F32)
@@ -323,26 +341,28 @@
     send_ref[...] = jnp.where(core == 0, bottom, top)
 
 
-def lines_kernel(at_ref, mine_ref, other_ref, block_ref, outer_ref, lines_ref, rim_ref):
-    spectrum = terms(joined(mine_ref[...], other_ref[...], at_ref[1]))
-    lines_ref[...] = product((block_ref[0, 0], block_ref[0, 1]), spectrum)
-    rim_ref[...] = product((outer_ref[0, 0], outer_ref[0, 1]), spectrum)
-
-
-def pixels_kernel(at_ref, lines_ref, rim_ref, mid_t_ref, sides_ref, inner_ref, side_ref):
-    place, core = at_ref[0], at_ref[1]
+def lines_kernel(mine_ref, other_ref, block_ref, outer_ref, lines_ref, rim_ref):
+    chip, core = my_place()
+    spectrum = terms(joined(mine_ref[...], other_ref[...], core))
+    lines_ref[...] = product((block_ref[chip, 0], block_ref[chip, 1]), spectrum)
+    rim_ref[...] = product((outer_ref[chip // 2, 0], outer_ref[chip // 2, 1]), spectrum)
+
+
+def pixels_kernel(lines_ref, rim_ref, mid_t_ref, sides_ref, inner_ref, side_ref):
+    chip, core = my_place()
     rim = rim_ref[...]
     lines = lines_ref[...]
-    top = lines[:A] + jnp.where(place == 0, rim, 0.0)
-    bottom = lines[A:] + jnp.where(place == 3, rim, 0.0)
-    table = (sides_ref[0, 0], sides_ref[0, 1])
+    top = lines[:A] + jnp.where(chip == 0, rim, 0.0)
+    bottom = lines[A:] + jnp.where(chip == 3, rim, 0.0)
+    table = (sides_ref[core, 0], sides_ref[core, 1])
     side_ref[...] = jnp.concatenate([product(terms(top), table), product(terms(bottom), table)], axis=1)
     own = jnp.where(core == 0, top, bottom)
     inner_ref[...] = product(terms(own), pair_of(mid_t_ref))
 
 
-def join_kernel(at_ref, inner_ref, mine_ref, other_ref, out_ref):
-    first = at_ref[1] == 0
+def join_kernel(inner_ref, mine_ref, other_ref, out_ref):
+    _, core = my_place()
+    first = core == 0
     mine, other = mine_ref[...], other_ref[...]
     left = jnp.where(first, other[:, :A], mine[:, A:])
     right = jnp.where(first, mine[:, :A], other[:, A:])
@@ -357,15 +377,12 @@
     return lax.ppermute(value, "src", [(at, at ^ 1) for at in range(8)])
 
 
-def swap_chips(value, partner):
-    return lax.ppermute(value, "src", [(at, 2 * partner(at // 2) + at % 2) for at in range(8)])
-
-
-def all_sum(keep, send):
-    value = keep + swap_cores(send)
-    value = value + swap_chips(value, lambda chip: chip ^ 1)
-    value = value + swap_chips(value, lambda chip: 3 - chip)
-    return value, swap_cores(value)
+def swap_chips(value, turn):
+    def partner(at):
+        chip, core = at // 2, at % 2
+        return 2 * (chip ^ 1 if core == turn else 3 - chip) + core
+
+    return lax.ppermute(value, "src", [(at, partner(at)) for at in range(8)])
 
 
 def tile_move(value, shift_of):
@@ -384,58 +401,59 @@
     return lax.ppermute(value, BOTH, pairs)
 
 
-def tile_sum(value):
-    for bit in (1, 2, 4, 8, 16):
-        value = value + lax.ppermute(value, "tile", [(at, at ^ bit) for at in range(TROWS * TCOLS)])
-    return value
+def tile_move_all(value, step):
+    def partner(at):
+        y, x, z = at // TCOLS, at // 2 % 4, at % 2
+        if step == 0:
+            z = 1 - z
+        elif step < 3:
+            x = x ^ 1 if step == 1 else 3 - x
+        else:
+            y = y ^ 1 if step == 3 else 3 - y
+        return y * TCOLS + x * 2 + z
+
+    return lax.ppermute(value, "tile", [(at, partner(at)) for at in range(TROWS * TCOLS)])
+
+
+def tile_pass(value, step):
+    return value + tile_move_all(value, step)
+
+
+def tied(*values):
+    return lax.optimization_barrier(values)
 
 
 def body(tables, mask_tiles, target, pupil_gain, weights, freq_index):
-    group = lax.axis_index("src").astype(jnp.int32)
-    chip, core = group // 2, group % 2
-    at = jnp.stack([chip, core])
-
+    core = lax.axis_index("src") % 2
     edge = jnp.where(core == 0, mask_tiles[0, PIX - A :], mask_tiles[0, :A])
     mine = tile_move(edge, lambda source: (1, 0) if source % 2 == 0 else (-1, 0))
-    basis, wanted = call(
+    (rows,) = call(
         own_kernel,
-        [(W, W), (W, W)],
-        [mask_tiles, target, tables["mid"], tables["mid_t"], tables["spread"], tables["spread_t"]],
+        [(W, PIX)],
+        [mask_tiles, tables["mid_t"]],
         "own",
-        2 * 3 * 2 * (PIX * PIX * W + W * PIX * W),
-    )
+        400_000_000,
+        scratch=(
+            pltpu.VMEM((PIX, PIX), F32),
+            pltpu.VMEM((2, W, PIX), BF),
+            pltpu.SemaphoreType.DMA((1 + PIX // K,)),
+        ),
+        hbm=(0, 1),
+    )
+    mine, rows = tied(mine, rows)
     other = swap_cores(mine)
-    whole = pl.BlockSpec(memory_space=pltpu.VMEM)
-    packed = pl.pallas_call(
-        pack_kernel,
-        out_shape=jax.ShapeDtypeStruct((N // 2, K), F32),
-        grid=(1,),
-        in_specs=[
-            pl.BlockSpec(memory_space=pltpu.SMEM),
-            pl.BlockSpec((1, PIX, K), lambda step: (0, 0, 0)),
-            pl.BlockSpec((1, PIX, K), lambda step: (0, 0, PIX // K - 1)),
-            whole,
-            whole,
-        ],
-        out_specs=whole,
-        name="pack",
-    )(at, mask_tiles, mask_tiles, mine, other)
-    my_side = tile_move(packed, lambda source: (0, 1) if source % 2 == 0 else (0, -1))
-    (basis,) = call(
-        rows_kernel,
-        [(W, W)],
-        [at, basis, mine, other, tables["mid"], tables["rims_t"]],
-        "rows",
-        3 * 2 * (K * PIX * W + W * K * W),
-        smem=(0,),
-    )
+    rows, side = call(
+        rows_kernel, [(W, PIX), (K, K)], [rows, mine, other, tables["rims_t"]], "rows", 100_000_000
+    )
+    my_side = tile_move(side, lambda source: (0, 1) if source % 2 == 0 else (0, -1))
+    (basis,) = call(columns_kernel, [(W, W)], [rows, tables["mid"]], "columns", 200_000_000)
+    my_side, basis = tied(my_side, basis)
     other_side = swap_cores(my_side)
     plane = pltpu.VMEM((2, W, K), F32)
     field, keep, send = call(
         image_kernel,
         [(SOURCES, 2 * W, W), (K, W), (K, W)],
         [
-            at,
             freq_index,
             weights,
             basis,
@@ -443,7 +461,6 @@
             other_side,
             pupil_gain,
             tables["rims"],
-            tables["all_t"],
             tables["fold"],
             tables["fold_t"],
             tables["coarse"],
@@ -452,77 +469,81 @@
         "image",
         1_500_000_000,
         scratch=(plane, plane),
-        smem=(0, 1, 2),
-    )
-    mine, other = all_sum(keep, send)
-    keep, send, energies = call(
+        smem=(0, 1),
+    )
+    value = keep + swap_cores(send)
+    moved = swap_chips(value, 0)
+    (wanted,) = call(
+        wanted_kernel,
+        [(W, W)],
+        [target, tables["spread"], tables["spread_t"]],
+        "wanted",
+        600_000_000,
+        scratch=(
+            pltpu.VMEM((PIX, PIX), F32),
+            pltpu.VMEM((2, PIX, W), BF),
+            pltpu.VMEM((2, W, PIX), BF),
+            pltpu.SemaphoreType.DMA((3,)),
+        ),
+        hbm=(0, 1, 2),
+    )
+    value, wanted = tied(value + moved, wanted)
+    mine = value + swap_chips(value, 1)
+    other = swap_cores(mine)
+    residual, energies = call(
+        residual_kernel, [(W, W), (8, K)], [mine, other, wanted, field, tables["gram"]], "residual", 300_000_000
+    )
+    arrived = tile_move_all(energies, 3)
+    keep, send = call(
         adjoint_kernel,
-        [(K, W), (K, W), (8, K)],
+        [(K, W), (K, W)],
         [
-            at,
             freq_index,
             weights,
-            mine,
-            other,
-            wanted,
+            residual,
             field,
             pupil_gain,
-            tables["gram"],
             tables["fold"],
             tables["fold_t"],
             tables["coarse"],
             tables["coarse_t"],
         ],
         "adjoint",
-        1_700_000_000,
+        1_500_000_000,
         scratch=(plane, plane),
-        smem=(0, 1, 2),
-    )
-    energies = tile_sum(energies)
-    mine, other = all_sum(keep, send)
-    lines, rim = pl.pallas_call(
+        smem=(0, 1),
+    )
+    keep, send, energies = tied(keep, send, energies + arrived)
+    value = keep + swap_cores(send)
+    moved = swap_chips(value, 0)
+    energies = tile_pass(energies, 1)
+    value, energies = tied(value + moved, energies)
+    moved = swap_chips(value, 1)
+    energies = tile_pass(energies, 4)
+    mine, energies = tied(value + moved, energies)
+    other = swap_cores(mine)
+    lines, rim = call(
         lines_kernel,
-        out_shape=[jax.ShapeDtypeStruct((K, W), F32), jax.ShapeDtypeStruct((A, W), F32)],
-        grid_spec=pltpu.PrefetchScalarGridSpec(
-            num_scalar_prefetch=1,
-            grid=(1,),
-            in_specs=[
-                whole,
-                whole,
-                pl.BlockSpec((1, 2, K, W), lambda step, at: (at[0], 0, 0, 0)),
-                pl.BlockSpec((1, 2, A, W), lambda step, at: (at[0], 0, 0, 0)),
-            ],
-            out_specs=[whole, whole],
-        ),
-        name="lines",
-    )(at, mine, other, tables["blocks"], tables["outer"])
+        [(K, W), (A, W)],
+        [mine, other, tables["blocks"], tables["outer"]],
+        "lines",
+        100_000_000,
+    )
     from_rows = tile_move(rim, lambda source: {0: (1, 0), 3: (-1, 0)}.get(source // 2))
-    inner, side = pl.pallas_call(
+    energies = tile_pass(energies, 0)
+    from_rows, energies = tied(from_rows, energies)
+    inner, side = call(
         pixels_kernel,
-        out_shape=[jax.ShapeDtypeStruct((A, PIX), F32), jax.ShapeDtypeStruct((A, K), F32)],
-        grid_spec=pltpu.PrefetchScalarGridSpec(
-            num_scalar_prefetch=1,
-            grid=(1,),
-            in_specs=[
-                whole,
-                whole,
-                whole,
-                pl.BlockSpec((1, 2, W, A), lambda step, at: (at[1], 0, 0, 0)),
-            ],
-            out_specs=[whole, whole],
-        ),
-        name="pixels",
-    )(at, lines, from_rows, tables["mid_t"], tables["sides_t"])
+        [(A, PIX), (A, K)],
+        [lines, from_rows, tables["mid_t"], tables["sides_t"]],
+        "pixels",
+        100_000_000,
+    )
     my_side = tile_move(side, lambda source: (0, -1) if source % 2 == 0 else (0, 1))
+    energies = tile_pass(energies, 2)
+    my_side, energies = tied(my_side, energies)
     other_side = swap_cores(my_side)
-    (mask_grad,) = call(
-        join_kernel,
-        [(1, A, PIX)],
-        [at, inner, my_side, other_side],
-        "join",
-        A * PIX,
-        smem=(0,),
-    )
+    (mask_grad,) = call(join_kernel, [(1, A, PIX)], [inner, my_side, other_side], "join", A * PIX)
     weight_grad = energies[0, :SOURCES] * (16.0 / (TROWS * TCOLS * PIX * PIX))
     return mask_grad, weight_grad
 

time: 123 us -> 83 us (0.67)
  waiting for transfers between devices: 46.3 us -> 21.9 us
  Pallas kernels: 20.6 us -> 12 us
  local copies, waits for them, and re-layouts: 6.24 us -> 2.37 us
  starting transfers between devices: 45.6 us -> 43.6 us
    ppermute x9, waiting for transfers between devices: 29.3 us -> 10.8 us  [the longest x4 5.71 us: swap_chips(): return lax.ppermute(value, 'src', [(at, partner(at)) for at in range(8)])]
    pallas_call x3 -> x0, Pallas kernels: 7.49 us -> none  [the longest x1 2.8 us: body(): pl.pallas_call(pixels_kernel, out_shape=[jax.ShapeDtypeStruct((A, PIX), F...]
    ppermute x4, waiting for transfers between devices: 12 us -> 4.97 us  [tile_move(): return lax.ppermute(value, BOTH, pairs)]
    unnamed x54 -> x40, local copies, waits for them, and re-layouts: 6.24 us -> 2.37 us
    ppermute x9, starting transfers between devices: 22.1 us -> 25.5 us  [the longest x5 13.3 us: tile_move_all(): lax.ppermute(value, 'tile', [(at, partner(at)) for at in range(TROWS * TC...]
    ppermute x4, starting transfers between devices: 10.6 us -> 7.6 us  [tile_move(): return lax.ppermute(value, BOTH, pairs)]
    ppermute x7, starting transfers between devices: 13 us -> 10.5 us  [swap_cores(): return lax.ppermute(value, 'src', [(at, at ^ 1) for at in range(8)])]
    pallas_call x5 -> x10, Pallas kernels: 13.1 us -> 12 us  [call(): pl.pallas_call(kernel, out_shape=shapes, in_specs=specs, out_specs=[pl.Bl...]
  transfers between devices with their start and end apart: 20 -> 20, of which waited for: 18 -> 16; matrix products, arithmetic and copies ran while one was open for 1% -> 1% of each run, Pallas kernels for 3% -> 7%
where the time goes in v2:
time: 83 us; the launch traced here: 82.6 us
  starting transfers between devices  43.6 us (53%)
  waiting for transfers between devices  21.9 us (26%)
  Pallas kernels  12 us (14%)
  local copies, waits for them, and re-layouts  2.37 us (3%)
  other arithmetic  1.66 us (2%)
  between operations  0.96 us (1%)
    ppermute x5, starting transfers between devices, tile_move_all(): lax.ppermute(value, 'tile', [(at, partner(at)) for at in range(TROWS * TC...  13.3 us
    ppermute x4, starting transfers between devices, swap_chips(): return lax.ppermute(value, 'src', [(at, partner(at)) for at in range(8)])  12.2 us
    pallas_call x10, Pallas kernels, call(): pl.pallas_call(kernel, out_shape=shapes, in_specs=specs, out_specs=[pl.Bl...  12 us
    ppermute x7, starting transfers between devices, swap_cores(): return lax.ppermute(value, 'src', [(at, at ^ 1) for at in range(8)])  10.5 us
    ppermute x4, starting transfers between devices, tile_move(): return lax.ppermute(value, BOTH, pairs)  7.6 us
    ppermute x7, waiting for transfers between devices, swap_cores(): return lax.ppermute(value, 'src', [(at, at ^ 1) for at in range(8)])  6.19 us
    ppermute x4, waiting for transfers between devices, swap_chips(): return lax.ppermute(value, 'src', [(at, partner(at)) for at in range(8)])  5.71 us
    ppermute x5, waiting for transfers between devices, tile_move_all(): lax.ppermute(value, 'tile', [(at, partner(at)) for at in range(TROWS * TC...  5.05 us
  transfers between devices with their start and end apart: 20, of which 16 were waited for; matrix products, arithmetic and copies ran while one was open for 1% of the time, Pallas kernels for 7%

profile of v2, /device:TPU:1, one launch (start us, length us, event | category | flops | bytes accessed | tf_op | source)
XLA Modules:
  0.0 82.6 jit_solution(2178998685172026859)
XLA Ops:
  0.7 1.0 %select_bitcast_fusion = f32[64,512]{1,0:T(8,128)S(1)} fusion(f32[1,512,512]{2,1,0:T(8,128)} %tile_hbm.1, pred[]{:T(512)S(6)} %eq.5), kind=kLoop, calls=%fused_computation | loop fusion | flops 32768 | bytes 393217 | tf_op jit(solution)/shard_map/jit(_where)/select_n | solution.py:428
  1.7 1.3 %collective-permute-start = (f32[64,512]{1,0:T(8,128)S(1)}, f32[64,512]{1,0:T(8,128)S(1)}, u32[]{:S(2)}, u32[]{:S(2)}) collective-permute-start(f32[64,512]{1,0:T(8,128)S(1)} %select_bitcast_fusion), channel_id=1, source_target_pairs={{0,8},{1,9},{2,10},{3,11},{4,12},{5,13},{6,14},{7,15},{8,16},{9,17... | collective-permute-start | bytes 393224 | tf_op jit(solution)/shard_map/ppermute | solution.py:401
  3.0 1.0 %copy-done = bf16[2,256,512]{2,1,0:T(8,128)(2,1)S(1)} copy-done((bf16[2,256,512]{2,1,0:T(8,128)(2,1)S(1)}, bf16[2,256,512]{2,1,0:T(8,128)(2,1)}, u32[]{:S(2)}) %copy-start) | copy-done | bytes 524312
  4.0 1.2 %copy-done.2 = f32[1,512,512]{2,1,0:T(8,128)S(1)} copy-done((f32[1,512,512]{2,1,0:T(8,128)S(1)}, f32[1,512,512]{2,1,0:T(8,128)}, u32[]{:S(2)}) %copy-start.2) | copy-done | bytes 1048600
  5.3 1.2 %own.1.rows_ref = f32[256,512]{1,0:T(8,128)S(1)} custom-call(f32[1,512,512]{2,1,0:T(8,128)S(1)} %copy-done.2, bf16[2,256,512]{2,1,0:T(8,128)(2,1)S(1)} %copy-done), custom_call_target="tpu_custom_call" | custom-call | flops 400000000 | bytes 2097152 | tf_op jit(solution)/shard_map/own/pallas_call | solution.py:116
  6.6 1.5 %collective-permute-done.mine_ref = f32[64,512]{1,0:T(8,128)S(1)} collective-permute-done((f32[64,512]{1,0:T(8,128)S(1)}, f32[64,512]{1,0:T(8,128)S(1)}, u32[]{:S(2)}, u32[]{:S(2)}) %collective-permute-start) | collective-permute-done | bytes 131104 | tf_op jit(solution)/shard_map/ppermute | solution.py:401
  8.1 2.3 %collective-permute-start.1 = (f32[64,512]{1,0:T(8,128)S(1)}, f32[64,512]{1,0:T(8,128)S(1)}, u32[]{:S(2)}, u32[]{:S(2)}) collective-permute-start(f32[64,512]{1,0:T(8,128)S(1)} %collective-permute-done.mine_ref), channel_id=1, source_target_pairs={{0,32},{32,0},{64,96},{96,64},{128,160},{160,128},{192,224},{224,1... | collective-permute-start | bytes 393224 | tf_op jit(solution)/shard_map/ppermute | solution.py:377
  10.4 1.0 %collective-permute-done.1.other_ref = f32[64,512]{1,0:T(8,128)S(1)} collective-permute-done((f32[64,512]{1,0:T(8,128)S(1)}, f32[64,512]{1,0:T(8,128)S(1)}, u32[]{:S(2)}, u32[]{:S(2)}) %collective-permute-start.1) | collective-permute-done | bytes 131104 | tf_op jit(solution)/shard_map/ppermute | solution.py:377
  11.3 0.5 rows.1
  11.8 1.3 %collective-permute-start.2 = (f32[128,128]{1,0:T(8,128)S(1)}, f32[128,128]{1,0:T(8,128)S(1)}, u32[]{:S(2)}, u32[]{:S(2)}) collective-permute-start(f32[128,128]{1,0:T(8,128)S(1)} %get-tuple-element.34), channel_id=1, source_target_pairs={{0,1},{1,2},{2,3},{3,4},{4,5},{5,6},{6,7},{8,9},{9,10},{10,11},{11... | collective-permute-start | bytes 196616 | tf_op jit(solution)/shard_map/ppermute | solution.py:401
  13.1 0.4 columns.1.basis_ref
  13.6 3.5 %collective-permute-done.2.mine_ref = f32[128,128]{1,0:T(8,128)S(1)} collective-permute-done((f32[128,128]{1,0:T(8,128)S(1)}, f32[128,128]{1,0:T(8,128)S(1)}, u32[]{:S(2)}, u32[]{:S(2)}) %collective-permute-start.2) | collective-permute-done | bytes 65568 | tf_op jit(solution)/shard_map/ppermute | solution.py:401
  17.0 0.9 %collective-permute-start.3 = (f32[128,128]{1,0:T(8,128)S(1)}, f32[128,128]{1,0:T(8,128)S(1)}, u32[]{:S(2)}, u32[]{:S(2)}) collective-permute-start(f32[128,128]{1,0:T(8,128)S(1)} %collective-permute-done.2.mine_ref), channel_id=1, source_target_pairs={{0,32},{32,0},{64,96},{96,64},{128,160},{160,128},{192,224},{224,1... | collective-permute-start | bytes 196616 | tf_op jit(solution)/shard_map/ppermute | solution.py:377
  17.9 0.9 %collective-permute-done.3.other_ref = f32[128,128]{1,0:T(8,128)S(1)} collective-permute-done((f32[128,128]{1,0:T(8,128)S(1)}, f32[128,128]{1,0:T(8,128)S(1)}, u32[]{:S(2)}, u32[]{:S(2)}) %collective-permute-start.3) | collective-permute-done | bytes 65568 | tf_op jit(solution)/shard_map/ppermute | solution.py:377
  18.9 3.4 %image.1 = (f32[4,512,256]{2,1,0:T(8,128)S(1)}, f32[128,256]{1,0:T(8,128)S(1)}, f32[128,256]{1,0:T(8,128)S(1)}) custom-call(s32[4,2,128]{2,1,0:T(2,128)S(1)} %copy-done.13, f32[4]{0:T(128)S(1)} %copy-done.14, f32[256,256]{1,0:T(8,128)S(1)} %columns.1.basis_ref, f32[128,128]{1,0:T(8,128)S(1)} %collective-permute-done.2.mine_ref, ...), custom_call_target="tpu_custom_call" | custom-call | flops 1500000000 | bytes 4263952 | tf_op jit(solution)/shard_map/image/pallas_call | solution.py:116
  22.3 0.4 collective-permute-start.4
  22.7 1.0 %collective-permute-done.4 = f32[128,256]{1,0:T(8,128)S(1)} collective-permute-done((f32[128,256]{1,0:T(8,128)S(1)}, f32[128,256]{1,0:T(8,128)S(1)}, u32[]{:S(2)}, u32[]{:S(2)}) %collective-permute-start.4) | collective-permute-done | bytes 131104 | tf_op jit(solution)/shard_map/ppermute | solution.py:377
  23.8 5.4 %collective-permute-start.5 = (f32[128,256]{1,0:T(8,128)S(1)}, f32[128,256]{1,0:T(8,128)S(1)}, u32[]{:S(2)}, u32[]{:S(2)}) collective-permute-start(f32[128,256]{1,0:T(8,128)S(1)} %add.38), channel_id=1, source_target_pairs={{0,64},{32,224},{64,0},{96,160},{128,192},{160,96},{192,128},{224,... | collective-permute-start | bytes 393224 | tf_op jit(solution)/shard_map/ppermute | solution.py:385
  29.2 1.4 %wanted.1.wanted_ref = f32[256,256]{1,0:T(8,128)S(1)} custom-call(f32[1,512,512]{2,1,0:T(8,128)S(1)} %copy-done.3, bf16[2,512,256]{2,1,0:T(8,128)(2,1)S(1)} %copy-done.6, bf16[2,256,512]{2,1,0:T(8,128)(2,1)S(1)} %copy-done.7), custom_call_target="tpu_custom_call" | custom-call | flops 600000000 | bytes 2359296 | tf_op jit(solution)/shard_map/wanted/pallas_call | solution.py:116
  30.6 1.0 %collective-permute-done.5 = f32[128,256]{1,0:T(8,128)S(1)} collective-permute-done((f32[128,256]{1,0:T(8,128)S(1)}, f32[128,256]{1,0:T(8,128)S(1)}, u32[]{:S(2)}, u32[]{:S(2)}) %collective-permute-start.5) | collective-permute-done | bytes 131104 | tf_op jit(solution)/shard_map/ppermute | solution.py:385
  31.6 2.2 %collective-permute-start.6 = (f32[128,256]{1,0:T(8,128)S(1)}, f32[128,256]{1,0:T(8,128)S(1)}, u32[]{:S(2)}, u32[]{:S(2)}) collective-permute-start(f32[128,256]{1,0:T(8,128)S(1)} %add.39), channel_id=1, source_target_pairs={{0,192},{32,96},{64,128},{96,32},{128,64},{160,224},{192,0},{224,1... | collective-permute-start | bytes 393224 | tf_op jit(solution)/shard_map/ppermute | solution.py:385
  33.8 2.6 %collective-permute-done.6 = f32[128,256]{1,0:T(8,128)S(1)} collective-permute-done((f32[128,256]{1,0:T(8,128)S(1)}, f32[128,256]{1,0:T(8,128)S(1)}, u32[]{:S(2)}, u32[]{:S(2)}) %collective-permute-start.6) | collective-permute-done | bytes 131104 | tf_op jit(solution)/shard_map/ppermute | solution.py:385
  36.4 2.3 %collective-permute-start.7 = (f32[128,256]{1,0:T(8,128)S(1)}, f32[128,256]{1,0:T(8,128)S(1)}, u32[]{:S(2)}, u32[]{:S(2)}) collective-permute-start(f32[128,256]{1,0:T(8,128)S(1)} %add.40.mine_ref), channel_id=1, source_target_pairs={{0,32},{32,0},{64,96},{96,64},{128,160},{160,128},{192,224},{224,1... | collective-permute-start | bytes 393224 | tf_op jit(solution)/shard_map/ppermute | solution.py:377
  38.7 1.0 %collective-permute-done.7.other_ref = f32[128,256]{1,0:T(8,128)S(1)} collective-permute-done((f32[128,256]{1,0:T(8,128)S(1)}, f32[128,256]{1,0:T(8,128)S(1)}, u32[]{:S(2)}, u32[]{:S(2)}) %collective-permute-start.7) | collective-permute-done | bytes 131104 | tf_op jit(solution)/shard_map/ppermute | solution.py:377
  39.7 0.8 residual.1
  40.5 1.4 %collective-permute-start.8 = (f32[8,128]{1,0:T(8,128)S(1)}, f32[8,128]{1,0:T(8,128)S(1)}, u32[]{:S(2)}, u32[]{:S(2)}) collective-permute-start(f32[8,128]{1,0:T(8,128)S(1)} %get-tuple-element.46), channel_id=1, source_target_pairs={{0,8},{1,9},{2,10},{3,11},{4,12},{5,13},{6,14},{7,15},{8,0},{9,1},... | collective-permute-start | bytes 12296 | tf_op jit(solution)/shard_map/ppermute | solution.py:415
  41.9 2.9 %adjoint.1 = (f32[128,256]{1,0:T(8,128)S(1)}, f32[128,256]{1,0:T(8,128)S(1)}) custom-call(s32[4,2,128]{2,1,0:T(2,128)S(1)} %copy-done.13, f32[4]{0:T(128)S(1)} %copy-done.14, f32[256,256]{1,0:T(8,128)S(1)} %get-tuple-element.43.residual_ref, f32[4,512,256]{2,1,0:T(8,128)S(1)} %get-tuple-element.42.field_ref, f32[128,128]{1,0:T(8,128)S(1)} %copy-done.12, ...), custom_call_target="tpu_custom_call" | custom-call | flops 1500000000 | bytes 4001808 | tf_op jit(solution)/shard_map/adjoint/pallas_call | solution.py:116
  44.8 0.7 collective-permute-start.9
  45.6 1.0 %collective-permute-done.9 = f32[128,256]{1,0:T(8,128)S(1)} collective-permute-done((f32[128,256]{1,0:T(8,128)S(1)}, f32[128,256]{1,0:T(8,128)S(1)}, u32[]{:S(2)}, u32[]{:S(2)}) %collective-permute-start.9) | collective-permute-done | bytes 131104 | tf_op jit(solution)/shard_map/ppermute | solution.py:377
  46.6 4.0 %collective-permute-start.10 = (f32[128,256]{1,0:T(8,128)S(1)}, f32[128,256]{1,0:T(8,128)S(1)}, u32[]{:S(2)}, u32[]{:S(2)}) collective-permute-start(f32[128,256]{1,0:T(8,128)S(1)} %add.42), channel_id=1, source_target_pairs={{0,64},{32,224},{64,0},{96,160},{128,192},{160,96},{192,128},{224,... | collective-permute-start | bytes 393224 | tf_op jit(solution)/shard_map/ppermute | solution.py:385
  50.6 4.9 %collective-permute-start.11 = (f32[8,128]{1,0:T(8,128)S(1)}, f32[8,128]{1,0:T(8,128)S(1)}, u32[]{:S(2)}, u32[]{:S(2)}) collective-permute-start(f32[8,128]{1,0:T(8,128)S(1)} %add.41), channel_id=1, source_target_pairs={{0,2},{1,3},{2,0},{3,1},{4,6},{5,7},{6,4},{7,5},{8,10},{9,11},{10,... | collective-permute-start | bytes 12296 | tf_op jit(solution)/shard_map/ppermute | solution.py:415
  55.5 1.0 %collective-permute-done.11 = f32[8,128]{1,0:T(8,128)S(1)} collective-permute-done((f32[8,128]{1,0:T(8,128)S(1)}, f32[8,128]{1,0:T(8,128)S(1)}, u32[]{:S(2)}, u32[]{:S(2)}) %collective-permute-start.11) | collective-permute-done | bytes 4128 | tf_op jit(solution)/shard_map/ppermute | solution.py:415
  56.6 0.6 collective-permute-start.12
  57.2 1.6 %collective-permute-start.13 = (f32[8,128]{1,0:T(8,128)S(1)}, f32[8,128]{1,0:T(8,128)S(1)}, u32[]{:S(2)}, u32[]{:S(2)}) collective-permute-start(f32[8,128]{1,0:T(8,128)S(1)} %add.44), channel_id=1, source_target_pairs={{0,24},{1,25},{2,26},{3,27},{4,28},{5,29},{6,30},{7,31},{8,16},{9,... | collective-permute-start | bytes 12296 | tf_op jit(solution)/shard_map/ppermute | solution.py:415
  58.8 2.1 %collective-permute-done.13 = f32[8,128]{1,0:T(8,128)S(1)} collective-permute-done((f32[8,128]{1,0:T(8,128)S(1)}, f32[8,128]{1,0:T(8,128)S(1)}, u32[]{:S(2)}, u32[]{:S(2)}) %collective-permute-start.13) | collective-permute-done | bytes 4128 | tf_op jit(solution)/shard_map/ppermute | solution.py:415
  60.8 2.0 %collective-permute-done.12 = f32[128,256]{1,0:T(8,128)S(1)} collective-permute-done((f32[128,256]{1,0:T(8,128)S(1)}, f32[128,256]{1,0:T(8,128)S(1)}, u32[]{:S(2)}, u32[]{:S(2)}) %collective-permute-start.12) | collective-permute-done | bytes 131104 | tf_op jit(solution)/shard_map/ppermute | solution.py:385
  62.9 1.0 %collective-permute-start.14 = (f32[128,256]{1,0:T(8,128)S(1)}, f32[128,256]{1,0:T(8,128)S(1)}, u32[]{:S(2)}, u32[]{:S(2)}) collective-permute-start(f32[128,256]{1,0:T(8,128)S(1)} %add.45.mine_ref), channel_id=1, source_target_pairs={{0,32},{32,0},{64,96},{96,64},{128,160},{160,128},{192,224},{224,1... | collective-permute-start | bytes 393224 | tf_op jit(solution)/shard_map/ppermute | solution.py:377
  63.9 1.0 %collective-permute-done.14.other_ref = f32[128,256]{1,0:T(8,128)S(1)} collective-permute-done((f32[128,256]{1,0:T(8,128)S(1)}, f32[128,256]{1,0:T(8,128)S(1)}, u32[]{:S(2)}, u32[]{:S(2)}) %collective-permute-start.14) | collective-permute-done | bytes 131104 | tf_op jit(solution)/shard_map/ppermute | solution.py:377
  65.2 1.7 %collective-permute-start.15 = (f32[64,256]{1,0:T(8,128)S(1)}, f32[64,256]{1,0:T(8,128)S(1)}, u32[]{:S(2)}, u32[]{:S(2)}) collective-permute-start(f32[64,256]{1,0:T(8,128)S(1)} %get-tuple-element.54), channel_id=1, source_target_pairs={{0,8},{1,9},{2,10},{3,11},{4,12},{5,13},{6,14},{7,15},{8,16},{9,17... | collective-permute-start | bytes 196616 | tf_op jit(solution)/shard_map/ppermute | solution.py:401
  66.8 2.6 %collective-permute-start.16 = (f32[8,128]{1,0:T(8,128)S(1)}, f32[8,128]{1,0:T(8,128)S(1)}, u32[]{:S(2)}, u32[]{:S(2)}) collective-permute-start(f32[8,128]{1,0:T(8,128)S(1)} %add.46), channel_id=1, source_target_pairs={{0,1},{1,0},{2,3},{3,2},{4,5},{5,4},{6,7},{7,6},{8,9},{9,8},{10,11... | collective-permute-start | bytes 12296 | tf_op jit(solution)/shard_map/ppermute | solution.py:415
  69.4 1.0 %collective-permute-done.16 = f32[8,128]{1,0:T(8,128)S(1)} collective-permute-done((f32[8,128]{1,0:T(8,128)S(1)}, f32[8,128]{1,0:T(8,128)S(1)}, u32[]{:S(2)}, u32[]{:S(2)}) %collective-permute-start.16) | collective-permute-done | bytes 4128 | tf_op jit(solution)/shard_map/ppermute | solution.py:415
  70.8 3.4 %collective-permute-start.17 = (f32[64,128]{1,0:T(8,128)S(1)}, f32[64,128]{1,0:T(8,128)S(1)}, u32[]{:S(2)}, u32[]{:S(2)}) collective-permute-start(f32[64,128]{1,0:T(8,128)S(1)} %get-tuple-element.58), channel_id=1, source_target_pairs={{1,0},{2,1},{3,2},{4,3},{5,4},{6,5},{7,6},{9,8},{10,9},{11,10},{12... | collective-permute-start | bytes 98312 | tf_op jit(solution)/shard_map/ppermute | solution.py:401
  74.1 2.9 %collective-permute-start.18 = (f32[8,128]{1,0:T(8,128)S(1)}, f32[8,128]{1,0:T(8,128)S(1)}, u32[]{:S(2)}, u32[]{:S(2)}) collective-permute-start(f32[8,128]{1,0:T(8,128)S(1)} %add.47), channel_id=1, source_target_pairs={{0,6},{1,7},{2,4},{3,5},{4,2},{5,3},{6,0},{7,1},{8,14},{9,15},{10,... | collective-permute-start | bytes 12296 | tf_op jit(solution)/shard_map/ppermute | solution.py:415
  77.0 1.0 %collective-permute-done.18 = f32[8,128]{1,0:T(8,128)S(1)} collective-permute-done((f32[8,128]{1,0:T(8,128)S(1)}, f32[8,128]{1,0:T(8,128)S(1)}, u32[]{:S(2)}, u32[]{:S(2)}) %collective-permute-start.18) | collective-permute-done | bytes 4128 | tf_op jit(solution)/shard_map/ppermute | solution.py:415
  78.0 2.9 %collective-permute-start.19 = (f32[64,128]{1,0:T(8,128)S(1)}, f32[64,128]{1,0:T(8,128)S(1)}, u32[]{:S(2)}, u32[]{:S(2)}) collective-permute-start(f32[64,128]{1,0:T(8,128)S(1)} %collective-permute-done.17.mine_ref), channel_id=1, source_target_pairs={{0,32},{32,0},{64,96},{96,64},{128,160},{160,128},{192,224},{224,1... | collective-permute-start | bytes 98312 | tf_op jit(solution)/shard_map/ppermute | solution.py:377
  80.9 0.5 multiply_bitcast_fusion
  81.4 0.3 collective-permute-done.19.other_ref
  81.8 0.8 join.1
  (55 shorter events, 0.9 us)
Async XLA Ops:
  0.6 10.7 %copy-start.11 = (bf16[2,256,128]{2,1,0:T(8,128)(2,1)S(1)}, bf16[2,256,128]{2,1,0:T(8,128)(2,1)}, u32[]{:S(2)}) copy-start(bf16[2,256,128]{2,1,0:T(8,128)(2,1)} %constant.51.clone.rims_t_ref) | copy-start | bytes 393220
  1.7 6.4 %collective-permute-start = (f32[64,512]{1,0:T(8,128)S(1)}, f32[64,512]{1,0:T(8,128)S(1)}, u32[]{:S(2)}, u32[]{:S(2)}) collective-permute-start(f32[64,512]{1,0:T(8,128)S(1)} %select_bitcast_fusion), channel_id=1, source_target_pairs={{0,8},{1,9},{2,10},{3,11},{4,12},{5,13},{6,14},{7,15},{8,16},{9,17... | collective-permute-start | bytes 393224 | tf_op jit(solution)/shard_map/ppermute | solution.py:401
  3.0 1.0 %copy-start = (bf16[2,256,512]{2,1,0:T(8,128)(2,1)S(1)}, bf16[2,256,512]{2,1,0:T(8,128)(2,1)}, u32[]{:S(2)}) copy-start(bf16[2,256,512]{2,1,0:T(8,128)(2,1)} %constant.50.clone.table_hbm.mid_t_ref) | copy-start | bytes 1572868
  4.0 1.2 %copy-start.2 = (f32[1,512,512]{2,1,0:T(8,128)S(1)}, f32[1,512,512]{2,1,0:T(8,128)}, u32[]{:S(2)}) copy-start(f32[1,512,512]{2,1,0:T(8,128)} %tile_hbm.1) | copy-start | bytes 3145732
  5.3 7.9 %copy-start.5 = (bf16[2,512,256]{2,1,0:T(8,128)(2,1)S(1)}, bf16[2,512,256]{2,1,0:T(8,128)(2,1)}, u32[]{:S(2)}) copy-start(bf16[2,512,256]{2,1,0:T(8,128)(2,1)} %constant.52.clone.mid_ref) | copy-start | bytes 1572868
  5.3 13.5 %copy-start.12 = (f32[128,128]{1,0:T(8,128)S(1)}, f32[128,128]{1,0:T(8,128)}, u32[]{:S(2)}) copy-start(f32[128,128]{1,0:T(8,128)} %gain_ref.3) | copy-start | bytes 196612
  5.3 13.5 %copy-start.13 = (s32[4,2,128]{2,1,0:T(2,128)S(1)}, s32[4,2,128]{2,1,0:T(2,128)}, u32[]{:S(2)}) copy-start(s32[4,2,128]{2,1,0:T(2,128)} %index_ref.3) | copy-start | bytes 12292
  5.3 13.5 %copy-start.14 = (f32[4]{0:T(128)S(1)}, f32[4]{0:T(128)}, u32[]{:S(2)}) copy-start(f32[4]{0:T(128)} %weights_ref.3) | copy-start | bytes 52
  5.3 13.5 %copy-start.15 = (bf16[2,256,512]{2,1,0:T(8,128)(2,1)S(1)}, bf16[2,256,512]{2,1,0:T(8,128)(2,1)}, u32[]{:S(2)}) copy-start(bf16[2,256,512]{2,1,0:T(8,128)(2,1)} %constant.56.clone.coarse_ref) | copy-start | bytes 1572868
  5.3 13.5 %copy-start.16 = (bf16[2,512,256]{2,1,0:T(8,128)(2,1)S(1)}, bf16[2,512,256]{2,1,0:T(8,128)(2,1)}, u32[]{:S(2)}) copy-start(bf16[2,512,256]{2,1,0:T(8,128)(2,1)} %constant.57.clone.coarse_t_ref) | copy-start | bytes 1572868
  5.3 13.5 %copy-start.17 = (bf16[256,256]{1,0:T(8,128)(2,1)S(1)}, bf16[256,256]{1,0:T(8,128)(2,1)}, u32[]{:S(2)}) copy-start(bf16[256,256]{1,0:T(8,128)(2,1)} %constant.54.clone.fold_ref) | copy-start | bytes 393220
  5.3 13.5 %copy-start.18 = (bf16[256,256]{1,0:T(8,128)(2,1)S(1)}, bf16[256,256]{1,0:T(8,128)(2,1)}, u32[]{:S(2)}) copy-start(bf16[256,256]{1,0:T(8,128)(2,1)} %constant.55.clone.fold_t_ref) | copy-start | bytes 393220
  5.3 13.5 %copy-start.19 = (bf16[2,128,256]{2,1,0:T(8,128)(2,1)S(1)}, bf16[2,128,256]{2,1,0:T(8,128)(2,1)}, u32[]{:S(2)}) copy-start(bf16[2,128,256]{2,1,0:T(8,128)(2,1)} %constant.53.clone.rims_ref) | copy-start | bytes 393220
  8.1 3.3 %collective-permute-start.1 = (f32[64,512]{1,0:T(8,128)S(1)}, f32[64,512]{1,0:T(8,128)S(1)}, u32[]{:S(2)}, u32[]{:S(2)}) collective-permute-start(f32[64,512]{1,0:T(8,128)S(1)} %collective-permute-done.mine_ref), channel_id=1, source_target_pairs={{0,32},{32,0},{64,96},{96,64},{128,160},{160,128},{192,224},{224,1... | collective-permute-start | bytes 393224 | tf_op jit(solution)/shard_map/ppermute | solution.py:377
  11.8 5.2 %collective-permute-start.2 = (f32[128,128]{1,0:T(8,128)S(1)}, f32[128,128]{1,0:T(8,128)S(1)}, u32[]{:S(2)}, u32[]{:S(2)}) collective-permute-start(f32[128,128]{1,0:T(8,128)S(1)} %get-tuple-element.34), channel_id=1, source_target_pairs={{0,1},{1,2},{2,3},{3,4},{4,5},{5,6},{6,7},{8,9},{9,10},{10,11},{11... | collective-permute-start | bytes 196616 | tf_op jit(solution)/shard_map/ppermute | solution.py:401
  13.5 15.6 %copy-start.3 = (f32[1,512,512]{2,1,0:T(8,128)S(1)}, f32[1,512,512]{2,1,0:T(8,128)}, u32[]{:S(2)}) copy-start(f32[1,512,512]{2,1,0:T(8,128)} %target_hbm.1) | copy-start | bytes 3145732
  13.5 15.6 %copy-start.6 = (bf16[2,512,256]{2,1,0:T(8,128)(2,1)S(1)}, bf16[2,512,256]{2,1,0:T(8,128)(2,1)}, u32[]{:S(2)}) copy-start(bf16[2,512,256]{2,1,0:T(8,128)(2,1)} %constant.58.clone.spread_hbm) | copy-start | bytes 1572868
  13.5 15.6 %copy-start.7 = (bf16[2,256,512]{2,1,0:T(8,128)(2,1)S(1)}, bf16[2,256,512]{2,1,0:T(8,128)(2,1)}, u32[]{:S(2)}) copy-start(bf16[2,256,512]{2,1,0:T(8,128)(2,1)} %constant.59.clone.spread_t_hbm) | copy-start | bytes 1572868
  17.0 1.8 %collective-permute-start.3 = (f32[128,128]{1,0:T(8,128)S(1)}, f32[128,128]{1,0:T(8,128)S(1)}, u32[]{:S(2)}, u32[]{:S(2)}) collective-permute-start(f32[128,128]{1,0:T(8,128)S(1)} %collective-permute-done.2.mine_ref), channel_id=1, source_target_pairs={{0,32},{32,0},{64,96},{96,64},{128,160},{160,128},{192,224},{224,1... | collective-permute-start | bytes 196616 | tf_op jit(solution)/shard_map/ppermute | solution.py:377
  22.3 17.4 %copy-start.9 = (bf16[2,256,256]{2,1,0:T(8,128)(2,1)S(1)}, bf16[2,256,256]{2,1,0:T(8,128)(2,1)}, u32[]{:S(2)}) copy-start(bf16[2,256,256]{2,1,0:T(8,128)(2,1)} %constant.60.clone.gram_ref) | copy-start | bytes 786436
  22.3 1.4 %collective-permute-start.4 = (f32[128,256]{1,0:T(8,128)S(1)}, f32[128,256]{1,0:T(8,128)S(1)}, u32[]{:S(2)}, u32[]{:S(2)}) collective-permute-start(f32[128,256]{1,0:T(8,128)S(1)} %get-tuple-element.39), channel_id=1, source_target_pairs={{0,32},{32,0},{64,96},{96,64},{128,160},{160,128},{192,224},{224,1... | collective-permute-start | bytes 393224 | tf_op jit(solution)/shard_map/ppermute | solution.py:377
  23.8 7.8 %collective-permute-start.5 = (f32[128,256]{1,0:T(8,128)S(1)}, f32[128,256]{1,0:T(8,128)S(1)}, u32[]{:S(2)}, u32[]{:S(2)}) collective-permute-start(f32[128,256]{1,0:T(8,128)S(1)} %add.38), channel_id=1, source_target_pairs={{0,64},{32,224},{64,0},{96,160},{128,192},{160,96},{192,128},{224,... | collective-permute-start | bytes 393224 | tf_op jit(solution)/shard_map/ppermute | solution.py:385
  31.6 4.8 %collective-permute-start.6 = (f32[128,256]{1,0:T(8,128)S(1)}, f32[128,256]{1,0:T(8,128)S(1)}, u32[]{:S(2)}, u32[]{:S(2)}) collective-permute-start(f32[128,256]{1,0:T(8,128)S(1)} %add.39), channel_id=1, source_target_pairs={{0,192},{32,96},{64,128},{96,32},{128,64},{160,224},{192,0},{224,1... | collective-permute-start | bytes 393224 | tf_op jit(solution)/shard_map/ppermute | solution.py:385
  36.4 3.3 %collective-permute-start.7 = (f32[128,256]{1,0:T(8,128)S(1)}, f32[128,256]{1,0:T(8,128)S(1)}, u32[]{:S(2)}, u32[]{:S(2)}) collective-permute-start(f32[128,256]{1,0:T(8,128)S(1)} %add.40.mine_ref), channel_id=1, source_target_pairs={{0,32},{32,0},{64,96},{96,64},{128,160},{160,128},{192,224},{224,1... | collective-permute-start | bytes 393224 | tf_op jit(solution)/shard_map/ppermute | solution.py:377
  40.5 4.3 %collective-permute-start.8 = (f32[8,128]{1,0:T(8,128)S(1)}, f32[8,128]{1,0:T(8,128)S(1)}, u32[]{:S(2)}, u32[]{:S(2)}) collective-permute-start(f32[8,128]{1,0:T(8,128)S(1)} %get-tuple-element.46), channel_id=1, source_target_pairs={{0,8},{1,9},{2,10},{3,11},{4,12},{5,13},{6,14},{7,15},{8,0},{9,1},... | collective-permute-start | bytes 12296 | tf_op jit(solution)/shard_map/ppermute | solution.py:415
  41.9 23.0 %copy-start.4 = (bf16[4,2,128,256]{3,2,1,0:T(8,128)(2,1)S(1)}, bf16[4,2,128,256]{3,2,1,0:T(8,128)(2,1)}, u32[]{:S(2)}) copy-start(bf16[4,2,128,256]{3,2,1,0:T(8,128)(2,1)} %constant.61.clone.block_ref) | copy-start | bytes 1572868
  41.9 23.0 %copy-start.10 = (bf16[2,2,64,256]{3,2,1,0:T(8,128)(2,1)S(1)}, bf16[2,2,64,256]{3,2,1,0:T(8,128)(2,1)}, u32[]{:S(2)}) copy-start(bf16[2,2,64,256]{3,2,1,0:T(8,128)(2,1)} %constant.62.clone.outer_ref) | copy-start | bytes 393220
  44.8 25.6 %copy-start.1 = (bf16[2,256,512]{2,1,0:T(8,128)(2,1)S(1)}, bf16[2,256,512]{2,1,0:T(8,128)(2,1)}, u32[]{:S(2)}) copy-start(bf16[2,256,512]{2,1,0:T(8,128)(2,1)} %constant.50.clone.table_hbm.mid_t_ref) | copy-start | bytes 1572868
  44.8 25.6 %copy-start.8 = (bf16[2,2,256,64]{3,2,1,0:T(8,128)(2,1)S(1)}, bf16[2,2,256,64]{3,2,1,0:T(8,128)(2,1)}, u32[]{:S(2)}) copy-start(bf16[2,2,256,64]{3,2,1,0:T(8,128)(2,1)} %constant.63.clone.sides_ref) | copy-start | bytes 393220
  44.8 1.7 %collective-permute-start.9 = (f32[128,256]{1,0:T(8,128)S(1)}, f32[128,256]{1,0:T(8,128)S(1)}, u32[]{:S(2)}, u32[]{:S(2)}) collective-permute-start(f32[128,256]{1,0:T(8,128)S(1)} %get-tuple-element.48), channel_id=1, source_target_pairs={{0,32},{32,0},{64,96},{96,64},{128,160},{160,128},{192,224},{224,1... | collective-permute-start | bytes 393224 | tf_op jit(solution)/shard_map/ppermute | solution.py:377
  46.6 9.9 %collective-permute-start.10 = (f32[128,256]{1,0:T(8,128)S(1)}, f32[128,256]{1,0:T(8,128)S(1)}, u32[]{:S(2)}, u32[]{:S(2)}) collective-permute-start(f32[128,256]{1,0:T(8,128)S(1)} %add.42), channel_id=1, source_target_pairs={{0,64},{32,224},{64,0},{96,160},{128,192},{160,96},{192,128},{224,... | collective-permute-start | bytes 393224 | tf_op jit(solution)/shard_map/ppermute | solution.py:385
  50.6 5.9 %collective-permute-start.11 = (f32[8,128]{1,0:T(8,128)S(1)}, f32[8,128]{1,0:T(8,128)S(1)}, u32[]{:S(2)}, u32[]{:S(2)}) collective-permute-start(f32[8,128]{1,0:T(8,128)S(1)} %add.41), channel_id=1, source_target_pairs={{0,2},{1,3},{2,0},{3,1},{4,6},{5,7},{6,4},{7,5},{8,10},{9,11},{10,... | collective-permute-start | bytes 12296 | tf_op jit(solution)/shard_map/ppermute | solution.py:415
  56.6 6.3 %collective-permute-start.12 = (f32[128,256]{1,0:T(8,128)S(1)}, f32[128,256]{1,0:T(8,128)S(1)}, u32[]{:S(2)}, u32[]{:S(2)}) collective-permute-start(f32[128,256]{1,0:T(8,128)S(1)} %add.43), channel_id=1, source_target_pairs={{0,192},{32,96},{64,128},{96,32},{128,64},{160,224},{192,0},{224,1... | collective-permute-start | bytes 393224 | tf_op jit(solution)/shard_map/ppermute | solution.py:385
  57.2 3.7 %collective-permute-start.13 = (f32[8,128]{1,0:T(8,128)S(1)}, f32[8,128]{1,0:T(8,128)S(1)}, u32[]{:S(2)}, u32[]{:S(2)}) collective-permute-start(f32[8,128]{1,0:T(8,128)S(1)} %add.44), channel_id=1, source_target_pairs={{0,24},{1,25},{2,26},{3,27},{4,28},{5,29},{6,30},{7,31},{8,16},{9,... | collective-permute-start | bytes 12296 | tf_op jit(solution)/shard_map/ppermute | solution.py:415
  62.9 2.0 %collective-permute-start.14 = (f32[128,256]{1,0:T(8,128)S(1)}, f32[128,256]{1,0:T(8,128)S(1)}, u32[]{:S(2)}, u32[]{:S(2)}) collective-permute-start(f32[128,256]{1,0:T(8,128)S(1)} %add.45.mine_ref), channel_id=1, source_target_pairs={{0,32},{32,0},{64,96},{96,64},{128,160},{160,128},{192,224},{224,1... | collective-permute-start | bytes 393224 | tf_op jit(solution)/shard_map/ppermute | solution.py:377
  65.2 5.2 %collective-permute-start.15 = (f32[64,256]{1,0:T(8,128)S(1)}, f32[64,256]{1,0:T(8,128)S(1)}, u32[]{:S(2)}, u32[]{:S(2)}) collective-permute-start(f32[64,256]{1,0:T(8,128)S(1)} %get-tuple-element.54), channel_id=1, source_target_pairs={{0,8},{1,9},{2,10},{3,11},{4,12},{5,13},{6,14},{7,15},{8,16},{9,17... | collective-permute-start | bytes 196616 | tf_op jit(solution)/shard_map/ppermute | solution.py:401
  66.8 3.6 %collective-permute-start.16 = (f32[8,128]{1,0:T(8,128)S(1)}, f32[8,128]{1,0:T(8,128)S(1)}, u32[]{:S(2)}, u32[]{:S(2)}) collective-permute-start(f32[8,128]{1,0:T(8,128)S(1)} %add.46), channel_id=1, source_target_pairs={{0,1},{1,0},{2,3},{3,2},{4,5},{5,4},{6,7},{7,6},{8,9},{9,8},{10,11... | collective-permute-start | bytes 12296 | tf_op jit(solution)/shard_map/ppermute | solution.py:415
  70.8 7.2 %collective-permute-start.17 = (f32[64,128]{1,0:T(8,128)S(1)}, f32[64,128]{1,0:T(8,128)S(1)}, u32[]{:S(2)}, u32[]{:S(2)}) collective-permute-start(f32[64,128]{1,0:T(8,128)S(1)} %get-tuple-element.58), channel_id=1, source_target_pairs={{1,0},{2,1},{3,2},{4,3},{5,4},{6,5},{7,6},{9,8},{10,9},{11,10},{12... | collective-permute-start | bytes 98312 | tf_op jit(solution)/shard_map/ppermute | solution.py:401
  74.1 3.9 %collective-permute-start.18 = (f32[8,128]{1,0:T(8,128)S(1)}, f32[8,128]{1,0:T(8,128)S(1)}, u32[]{:S(2)}, u32[]{:S(2)}) collective-permute-start(f32[8,128]{1,0:T(8,128)S(1)} %add.47), channel_id=1, source_target_pairs={{0,6},{1,7},{2,4},{3,5},{4,2},{5,3},{6,0},{7,1},{8,14},{9,15},{10,... | collective-permute-start | bytes 12296 | tf_op jit(solution)/shard_map/ppermute | solution.py:415
  78.0 3.8 %collective-permute-start.19 = (f32[64,128]{1,0:T(8,128)S(1)}, f32[64,128]{1,0:T(8,128)S(1)}, u32[]{:S(2)}, u32[]{:S(2)}) collective-permute-start(f32[64,128]{1,0:T(8,128)S(1)} %collective-permute-done.17.mine_ref), channel_id=1, source_target_pairs={{0,32},{32,0},{64,96},{96,64},{128,160},{160,128},{192,224},{224,1... | collective-permute-start | bytes 98312 | tf_op jit(solution)/shard_map/ppermute | solution.py:377

commit v3 on v2

v3 whole, which is shorter than its diff:
```python
import functools
import math

import jax
import jax.numpy as jnp
import ml_dtypes
import numpy as np
from jax import lax
from jax.experimental import pallas as pl
from jax.experimental.pallas import tpu as pltpu
from jax.sharding import PartitionSpec as P

A = 64
TROWS = 4
TCOLS = 8
PIX = 512
N = PIX + 2 * A
K = 128
W = 256
SOURCES = 4
CHIPS = 4
BF = jnp.bfloat16
F32 = jnp.float32
BOTH = ("src", "tile")


def two_terms(table):
    first = table.astype(np.float32).astype(ml_dtypes.bfloat16)
    rest = (table - first.astype(np.float64)).astype(np.float32)
    return np.stack([first, rest.astype(ml_dtypes.bfloat16)])


def real_basis():
    angles = 2.0 * np.pi / N * np.mod(np.outer(np.arange(N), np.arange(K)), N)
    return np.concatenate([np.cos(angles), np.sin(angles)], axis=1) / math.sqrt(N)


def fold_table():
    ranks = np.arange(W) - K
    parts = np.arange(K)
    same = np.abs(ranks)[None, :] == parts[:, None]
    return np.concatenate([same * 1.0, same * np.sign(ranks)[None, :]], axis=0)


def coarse_table():
    ranks = np.arange(K) - K // 2
    angles = 2.0 * np.pi / W * np.mod(np.outer(ranks, np.arange(W)), W)
    down_real, down_imag = np.cos(angles) / math.sqrt(K), np.sin(angles) / math.sqrt(K)
    return np.block([[down_real, down_imag], [-down_imag, down_real]])


def interpolation():
    ranks = np.arange(1, K)
    shift = (np.arange(PIX) + A)[:, None] / N - np.arange(W)[None, :] / W
    return (1.0 + 2.0 * np.cos(2.0 * np.pi * shift[..., None] * ranks).sum(-1)) / W


ROWS = 64


def packed(entries):
    spots, pieces, at = {}, [], 0
    for name, tables in entries.items():
        spots[name] = []
        for table in tables:
            count = table.shape[0] // ROWS
            spots[name].append((at, count))
            pieces.append(table.reshape(count, ROWS, W))
            at += count
    return np.concatenate(pieces), spots


def two_halves(table):
    return [half for term in two_terms(table) for half in (term[:, :W], term[:, W:])]


def make_tables():
    basis = real_basis()
    coarse = coarse_table()
    spread = interpolation()
    fold = fold_table().astype(ml_dtypes.bfloat16)
    middle = basis[A : N - A]
    rims = np.concatenate([basis[:A], basis[N - A :]])
    sides = [two_terms(basis[:A].T), two_terms(basis[N - A :].T)]
    early = packed(
        {
            "mid": two_terms(middle),
            "mid_t": two_halves(middle.T),
            "rims": two_terms(rims),
            "rims_t": [np.concatenate(list(two_terms(rims.T)), axis=1)],
            "sides": [np.concatenate([term for pair in sides for term in pair], axis=1)],
        }
    )
    late = packed(
        {
            "coarse": two_halves(coarse),
            "coarse_t": two_terms(coarse.T),
            "fold": [fold],
            "fold_t": [np.ascontiguousarray(fold.T)],
            "spread": two_terms(spread),
            "spread_t": two_halves(spread.T),
            "gram": two_terms(spread.T @ spread),
        }
    )
    return early, late


(EARLY, EARLY_AT), (LATE, LATE_AT) = make_tables()
SPOTS = EARLY_AT | LATE_AT


def stored(ref, name, at=0):
    start, count = SPOTS[name][at]
    return ref[start : start + count].reshape(count * ROWS, W)


def narrow(ref, name):
    return stored(ref, name, 0), stored(ref, name, 1)


def wide(ref, name):
    return tuple(
        jnp.concatenate([stored(ref, name, at), stored(ref, name, at + 1)], axis=1) for at in (0, 2)
    )


def terms(value):
    first = value.astype(BF)
    return first, (value - first.astype(F32)).astype(BF)


def dot(first_op, second_op):
    return jnp.dot(first_op, second_op, preferred_element_type=F32)


def product(first_op, second_op):
    first_hi, first_lo = first_op
    second_hi, second_lo = second_op
    return dot(
        jnp.concatenate([first_hi, first_hi, first_lo], axis=1),
        jnp.concatenate([second_hi, second_lo, second_hi], axis=0),
    )


def exact_left(table, value):
    high, low = terms(value)
    return dot(table, high) + dot(table, low)


def exact_right(value, table):
    high, low = terms(value)
    return dot(high, table) + dot(low, table)


def call(kernel, outs, ins, name, flops, scratch=(), smem=(), bf16=(), grant=20):
    specs = [
        pl.BlockSpec(memory_space=pltpu.SMEM if at in smem else pltpu.VMEM) for at in range(len(ins))
    ]
    shapes = [jax.ShapeDtypeStruct(shape, BF if at in bf16 else F32) for at, shape in enumerate(outs)]
    moved = 4 * sum(math.prod(shape) for shape in outs) + sum(one.size * one.dtype.itemsize for one in ins)
    return pl.pallas_call(
        kernel,
        out_shape=shapes,
        in_specs=specs,
        out_specs=[pl.BlockSpec(memory_space=pltpu.VMEM) for _ in outs],
        scratch_shapes=list(scratch),
        compiler_params=pltpu.CompilerParams(vmem_limit_bytes=40 * 1024 * 1024),
        cost_estimate=pl.CostEstimate(flops=flops, bytes_accessed=moved, transcendentals=0),
        name=name,
    )(*ins)


def my_place():
    group = lax.axis_index("src")
    return group // 2, group % 2


def own_kernel(tile_ref, early_ref, rows_ref, table_ref):
    rows_ref[...] = product(wide(early_ref, "mid_t"), terms(tile_ref[0]))
    table_ref[...] = stored(early_ref, "rims_t")


def wanted_kernel(target_ref, late_ref, wanted_ref):
    upper = product(terms(target_ref[0]), narrow(late_ref, "spread"))
    wanted_ref[...] = product(wide(late_ref, "spread_t"), terms(upper))


def rows_kernel(rows_ref, mine_ref, other_ref, table_ref, all_ref, side_ref):
    _, core = my_place()
    first = core == 0
    mine, other = mine_ref[...], other_ref[...]
    rim = jnp.concatenate([jnp.where(first, mine, other), jnp.where(first, other, mine)], axis=0)
    table = table_ref[...]
    rows = rows_ref[...] + product((table[:, :K], table[:, K:]), terms(rim))
    all_ref[...] = rows
    side = jnp.where(first, rows[:, PIX - A :], rows[:, :A])
    side_ref[...] = jnp.concatenate([side[:K], side[K:]], axis=1)


def columns_kernel(rows_ref, early_ref, _, basis_ref):
    basis_ref[...] = product(terms(rows_ref[...]), narrow(early_ref, "mid"))


def disc_of(gain):
    rows = lax.broadcasted_iota(jnp.int32, (K, K), 0) - K // 2
    columns = lax.broadcasted_iota(jnp.int32, (K, K), 1) - K // 2
    return jnp.where(rows * rows + columns * columns <= (K // 2) ** 2, gain, 0.0)


def window_starts(info_refs, source):
    ref = info_refs[min(source // SOURCES, 2)]
    at = source % SOURCES + (SOURCES if source // SOURCES == 3 else 0)

    def start(coordinate):
        index = ref[at, coordinate, 0].astype(jnp.int32)
        return jnp.clip(lax.rem(index + K, N), 0, K)

    return start(0), start(1)


def weight_of(info_refs, source):
    ref = info_refs[min(source // SOURCES, 2)]
    return ref[source % SOURCES + (SOURCES if source // SOURCES == 3 else 0), 0, 1]


def image_of(info_refs, chips, planes, disc, late_ref, field_ref):
    coarse, coarse_t = wide(late_ref, "coarse"), narrow(late_ref, "coarse_t")
    total = jnp.zeros((W, W), F32)
    for chip in chips:
        specs = []
        for source in range(chip * SOURCES, chip * SOURCES + SOURCES):
            row, column = window_starts(info_refs, source)

            def window(ref):
                rows = jnp.concatenate([ref[0, pl.ds(row, K), :], ref[1, pl.ds(row, K), :]], axis=1)
                return pltpu.roll(rows, lax.rem(W - column, W), 1)[:, :K] * disc

            specs.append(jnp.concatenate([window(ref) for ref in planes], axis=1))
        stacked = product(terms(jnp.concatenate(specs, axis=0)), coarse)
        for at in range(SOURCES):
            half = stacked[at * K : at * K + K]
            half = jnp.concatenate([half[:, :W], half[:, W:]], axis=0)
            field = product(coarse_t, terms(half))
            field_ref[(chip - chips[0]) * SOURCES + at] = field
            real, imag = field[:W], field[W:]
            weight = weight_of(info_refs, chip * SOURCES + at)
            total = total + weight * (real * real + imag * imag)
    return total


def image_kernel(
    info_ref,
    basis_ref,
    mine_ref,
    other_ref,
    gain_ref,
    early_ref,
    late_ref,
    field_ref,
    total_ref,
    real_ref,
    imag_ref,
):
    _, core = my_place()
    first = core == 0
    mine, other = mine_ref[...], other_ref[...]
    left = jnp.where(first, mine, other)
    right = jnp.where(first, other, mine)
    rim = jnp.concatenate(
        [
            jnp.concatenate([left[:, :A], right[:, :A]], axis=1),
            jnp.concatenate([left[:, A:], right[:, A:]], axis=1),
        ],
        axis=0,
    )
    basis = basis_ref[...] + product(terms(rim), narrow(early_ref, "rims"))
    zero = jnp.zeros((K, K), F32)
    even = jnp.concatenate(
        [
            jnp.concatenate([basis[:K, :K], zero], axis=1),
            jnp.concatenate([zero, -basis[K:, K:]], axis=1),
        ],
        axis=0,
    )
    odd = jnp.concatenate(
        [
            jnp.concatenate([zero, -basis[:K, K:]], axis=1),
            jnp.concatenate([-basis[K:, :K], zero], axis=1),
        ],
        axis=0,
    )
    fold, fold_t = stored(late_ref, "fold"), stored(late_ref, "fold_t")
    for ref, part in ((real_ref, even), (imag_ref, odd)):
        plane = exact_right(exact_left(fold_t, part), fold)
        ref[0] = plane[:, :K]
        ref[1] = plane[:, K:]
    disc = disc_of(gain_ref[...])
    total_ref[...] = image_of((info_ref,), (0,), (real_ref, imag_ref), disc, late_ref, field_ref)


def others_kernel(
    near_ref, far_ref, gain_ref, late_ref, real_ref, imag_ref, before_ref, field_ref, total_ref
):
    info_refs = (None, near_ref, far_ref)
    disc = disc_of(gain_ref[...])
    total_ref[...] = before_ref[...] + image_of(
        info_refs, (1, 2, 3), (real_ref, imag_ref), disc, late_ref, field_ref
    )


def residual_kernel(mine_ref, other_ref, wanted_ref, field_ref, late_ref, residual_ref, energy_ref):
    bright = mine_ref[...] + other_ref[...]
    gram = narrow(late_ref, "gram")
    value = product(terms(product(gram, terms(bright))), gram)
    residual = value * (1.0 / (8 * SOURCES)) - wanted_ref[...]
    residual_ref[...] = residual
    lanes = lax.broadcasted_iota(jnp.int32, (8, K), 1)
    energies = jnp.zeros((8, K), F32)
    for source in range(SOURCES):
        real, imag = field_ref[source, :W], field_ref[source, W:]
        energy = jnp.sum(residual * (real * real + imag * imag))
        energies = jnp.where(lanes == source, energy, energies)
    energy_ref[...] = energies


def adjoint_kernel(
    chip,
    info_ref,
    residual_ref,
    field_ref,
    gain_ref,
    late_ref,
    real_in,
    imag_in,
    *outs,
):
    info_refs = (info_ref,) * 3
    first_field = SOURCES if chip else 0
    coarse, coarse_t = wide(late_ref, "coarse"), narrow(late_ref, "coarse_t")
    _, core = my_place()
    last = chip == CHIPS - 1
    real_ref, imag_ref = outs[2:] if last else outs
    residual = residual_ref[...]
    disc = disc_of(gain_ref[...])
    real_ref[...] = jnp.zeros((2, W, K), F32) if chip == 0 else real_in[...]
    imag_ref[...] = jnp.zeros((2, W, K), F32) if chip == 0 else imag_in[...]
    pad = jnp.zeros((K, K), F32)
    for couple in range(chip * SOURCES, chip * SOURCES + SOURCES, 2):
        sides = []
        for source in (couple, couple + 1):
            field = field_ref.at[source - first_field]
            real, imag = field[:W], field[W:]
            scaled = jnp.concatenate([residual * real, residual * imag], axis=1)
            back = product(terms(scaled), coarse_t)
            sides.append(jnp.concatenate([back[:, :K], back[:, K:]], axis=0))
        spec = product(coarse, terms(jnp.concatenate(sides, axis=1)))
        for place in range(2):
            source = couple + place
            row, column = window_starts(info_refs, source)
            scale = disc * (2.0 * weight_of(info_refs, source))
            for ref, part in ((real_ref, spec[:K]), (imag_ref, spec[K:])):
                part = part[:, place * K : place * K + K] * scale
                spread = pltpu.roll(jnp.concatenate([part, pad], axis=1), column, 1)
                for side in range(2):
                    ref[side, pl.ds(row, K), :] += spread[:, side * K : side * K + K]
    if not last:
        return
    keep_ref, send_ref = outs[:2]
    fold, fold_t = stored(late_ref, "fold"), stored(late_ref, "fold_t")

    def folded(ref):
        return exact_right(exact_left(fold, jnp.concatenate([ref[0], ref[1]], axis=1)), fold_t)

    even, odd = folded(real_ref), folded(imag_ref)
    left = jnp.concatenate([even[:K, :K], -odd[K:, :K]], axis=0)
    right = jnp.concatenate([-odd[:K, K:], -even[K:, K:]], axis=0)
    keep_ref[...] = jnp.where(core == 0, left, right)
    send_ref[...] = jnp.where(core == 0, right, left)


def lines_kernel(mine_ref, early_ref, lines_ref, rim_ref):
    chip, _ = my_place()
    spectrum = terms(mine_ref[...])
    lines = [early_ref[pl.ds(SPOTS["mid"][at][0] + 2 * chip, 2)].reshape(K, W) for at in range(2)]
    lines_ref[...] = product(lines, spectrum)
    outer = [early_ref[SPOTS["rims"][at][0] + 1 - chip // 2] for at in range(2)]
    rim_ref[...] = product(outer, spectrum)


def rim_kernel(lines_ref, rim_ref, energy_ref, out_ref):
    chip, _ = my_place()
    rim = rim_ref[...]
    out_ref[:A] = lines_ref[:A] + jnp.where(chip == 0, rim, 0.0)
    out_ref[A:K] = lines_ref[A:] + jnp.where(chip == 3, rim, 0.0)
    out_ref[K:] = energy_ref[...]


def pixels_kernel(mine_ref, other_ref, early_ref, inner_ref, side_ref):
    _, core = my_place()
    first = core == 0
    mine, other = mine_ref[...], other_ref[...]
    lines = jnp.concatenate([jnp.where(first, mine, other), jnp.where(first, other, mine)], axis=1)
    top, bottom = lines[:A], lines[A:K]
    table = stored(early_ref, "sides")
    table = jnp.where(first, table[:, :K], table[:, K:])
    table = (table[:, :A], table[:, A:])
    side_ref[:A] = jnp.concatenate([product(terms(top), table), product(terms(bottom), table)], axis=1)
    lanes = lax.broadcasted_iota(jnp.int32, (8, K), 1)
    side_ref[A:] = jnp.where(lanes < A, lines[K:, :K], pltpu.roll(lines[K:, K:], A, 1))
    own = jnp.where(first, top, bottom)
    inner_ref[...] = product(terms(own), wide(early_ref, "mid_t"))


def join_kernel(inner_ref, before_ref, mine_ref, other_ref, out_ref, energy_ref):
    _, core = my_place()
    first = core == 0
    mine, other = mine_ref[...], other_ref[...]
    left = jnp.where(first, other[:A, :A], mine[:A, A:])
    right = jnp.where(first, mine[:A, :A], other[:A, A:])
    inner = inner_ref[...]
    pad = jnp.zeros((A, A), F32)
    out_ref[0, :, :K] = inner[:, :K] + jnp.concatenate([left, pad], axis=1)
    out_ref[0, :, K : PIX - K] = inner[:, K : PIX - K]
    out_ref[0, :, PIX - K :] = inner[:, PIX - K :] + jnp.concatenate([pad, right], axis=1)
    odd = lax.rem(lax.axis_index("tile"), 2)
    total = before_ref[A : A + 1] + jnp.where(core == odd, mine[A : A + 1], other[A : A + 1])
    total = pltpu.roll(total, core * A, 1) * (16.0 / (TROWS * TCOLS * PIX * PIX))
    energy_ref[...] = total[0, :SOURCES]


def swap_cores(value):
    return lax.ppermute(value, "src", [(at, at ^ 1) for at in range(8)])


def next_chip(value, steps):
    return lax.ppermute(
        value, "src", [(at, (at // 2 + steps) % CHIPS * 2 + at % 2) for at in range(2 * CHIPS)]
    )


def tile_move(value, shift_of):
    pairs = []
    for source in range(8):
        shift = shift_of(source)
        if shift is None:
            continue
        for row in range(TROWS):
            for column in range(TCOLS):
                to_row, to_column = row + shift[0], column + shift[1]
                if 0 <= to_row < TROWS and 0 <= to_column < TCOLS:
                    pairs.append(
                        (source * 32 + row * TCOLS + column, source * 32 + to_row * TCOLS + to_column)
                    )
    return lax.ppermute(value, BOTH, pairs)


def tile_swap(value, step):
    def partner(at):
        y, x, z = at // TCOLS, at // 2 % 4, at % 2
        if step == 0:
            z = 1 - z
        elif step < 3:
            x = x ^ 1 if step == 1 else 3 - x
        else:
            y = y ^ 1 if step == 3 else 3 - y
        return y * TCOLS + x * 2 + z

    return lax.ppermute(value, "tile", [(at, partner(at)) for at in range(TROWS * TCOLS)])


def tied(*values):
    return lax.optimization_barrier(values)


def body(mask_tiles, target, pupil_gain, weights, freq_index):
    core = lax.axis_index("src") % 2
    edge = jnp.where(core == 0, mask_tiles[0, PIX - A :], mask_tiles[0, :A])
    mine = tile_move(edge, lambda source: (1, 0) if source % 2 == 0 else (-1, 0))
    rows, rim_table = call(own_kernel, [(W, PIX), (W, W)], [mask_tiles, EARLY], "own", 400_000_000, bf16=(1,))
    mine, rows, weights, freq_index = tied(mine, rows, weights, freq_index)
    other = swap_cores(mine)
    lanes = lax.broadcasted_iota(jnp.int32, freq_index.shape, 2)
    info = jnp.where(lanes == 1, weights[:, None, None], freq_index.astype(F32))
    near = next_chip(info, 1)
    rows, side = call(
        rows_kernel, [(W, PIX), (K, K)], [rows, mine, other, rim_table], "rows", 100_000_000
    )
    my_side = tile_move(side, lambda source: (0, 1) if source % 2 == 0 else (0, -1))
    (basis,) = call(columns_kernel, [(W, W)], [rows, EARLY, LATE], "columns", 200_000_000)
    far = next_chip(jnp.concatenate([info, near]), 2)
    my_side, basis = tied(my_side, basis)
    other_side = swap_cores(my_side)
    own_field, total, real, imag = call(
        image_kernel,
        [(SOURCES, 2 * W, W), (W, W), (2, W, K), (2, W, K)],
        [info, basis, my_side, other_side, pupil_gain, EARLY, LATE],
        "image",
        2_000_000_000,
        smem=(0,),
    )
    field, mine = call(
        others_kernel,
        [((CHIPS - 1) * SOURCES, 2 * W, W), (W, W)],
        [near, far, pupil_gain, LATE, real, imag, total],
        "others",
        5_000_000_000,
        smem=(0, 1),
    )
    other = swap_cores(mine)
    (wanted,) = call(wanted_kernel, [(W, W)], [target, LATE], "wanted", 600_000_000)
    other, wanted = tied(other, wanted)
    residual, energies = call(
        residual_kernel, [(W, W), (8, K)], [mine, other, wanted, own_field, LATE], "residual", 300_000_000
    )
    plane = pltpu.VMEM((2, W, K), F32)
    planes = (jnp.zeros((8, K), F32),) * 2
    for chip in range(CHIPS):
        arrived = tile_swap(energies, (3, 1, 4, 2)[chip])
        last = chip == CHIPS - 1
        outs = call(
            functools.partial(adjoint_kernel, chip),
            [(W, K), (W, K)] if last else [(2, W, K), (2, W, K)],
            [(info, near, far, far)[chip], residual, field if chip else own_field, pupil_gain, LATE, *planes],
            "adjoint",
            1_500_000_000,
            scratch=(plane, plane) if last else (),
            smem=(0,),
        )
        planes = outs[:2]
        *planes, energies = tied(*planes, energies + arrived)
    keep, send = planes
    mine = keep + swap_cores(send)
    lines, rim = call(
        lines_kernel,
        [(K, K), (A, K)],
        [mine, EARLY],
        "lines",
        100_000_000,
    )
    from_rows = tile_move(rim, lambda source: {0: (1, 0), 3: (-1, 0)}.get(source // 2))
    (mine,) = call(rim_kernel, [(K + 8, K)], [lines, from_rows, energies], "rim", K * K)
    other = swap_cores(mine)
    inner, side = call(
        pixels_kernel,
        [(A, PIX), (A + 8, K)],
        [mine, other, EARLY],
        "pixels",
        100_000_000,
    )
    my_side = tile_move(side, lambda source: (0, -1) if source % 2 == 0 else (0, 1))
    other_side = swap_cores(my_side)
    mask_grad, weight_grad = call(
        join_kernel, [(1, A, PIX), (SOURCES,)], [inner, side, my_side, other_side], "join", A * PIX
    )
    return mask_grad, weight_grad


def solution(mesh):
    placed = (P("tile", None, None), P("tile", None, None), P(), P("src"), P("src", None, None))
    return jax.shard_map(
        body,
        mesh=mesh,
        in_specs=placed,
        out_specs=(P("tile", "src", None), P("src")),
        check_vma=False,
    )
```

time: 83 us -> 74.3 us (0.90)
  waiting for transfers between devices: 21.9 us -> 7.71 us
  Pallas kernels: 12 us -> 24.7 us
  starting transfers between devices: 43.6 us -> 35 us
  local copies, waits for them, and re-layouts: 2.37 us -> 3.98 us
    pallas_call x10 -> x15, Pallas kernels: 12 us -> 24.7 us  [call(): pl.pallas_call(kernel, out_shape=shapes, in_specs=specs, out_specs=[pl.Bl...]
    ppermute x9 -> x6, starting transfers between devices: 25.5 us -> 14.2 us  [the longest x2 7.31 us: next_chip(): lax.ppermute(value, 'src', [(at, (at // 2 + steps) % CHIPS * 2 + at % 2)...]
    ppermute x9 -> x6, waiting for transfers between devices: 10.8 us -> 0.02 us  [the longest x4 0.01 us: tile_swap(): lax.ppermute(value, 'tile', [(at, partner(at)) for at in range(TROWS * TC...]
    ppermute x7 -> x6, waiting for transfers between devices: 6.19 us -> 3.74 us  [swap_cores(): return lax.ppermute(value, 'src', [(at, at ^ 1) for at in range(8)])]
    ppermute x7 -> x6, starting transfers between devices: 10.5 us -> 12.9 us  [swap_cores(): return lax.ppermute(value, 'src', [(at, at ^ 1) for at in range(8)])]
    unnamed x40 -> x18, local copies, waits for them, and re-layouts: 2.37 us -> 3.98 us
    ppermute x4, waiting for transfers between devices: 4.97 us -> 3.95 us  [tile_move(): return lax.ppermute(value, BOTH, pairs)]
  transfers between devices with their start and end apart: 20 -> 16, of which waited for: 16 -> 7; matrix products, arithmetic and copies ran while one was open for 1% -> 0% of each run, Pallas kernels for 7% -> 23%
where the time goes in v3:
time: 74.3 us; the launch traced here: 73.6 us
  starting transfers between devices  35 us (47%)
  Pallas kernels  24.7 us (33%)
  waiting for transfers between devices  7.71 us (10%)
  local copies, waits for them, and re-layouts  3.98 us (5%)
  other arithmetic  1.26 us (2%)
  between operations  0.93 us (1%)
    pallas_call x15, Pallas kernels, call(): pl.pallas_call(kernel, out_shape=shapes, in_specs=specs, out_specs=[pl.Bl...  24.7 us
    ppermute x6, starting transfers between devices, swap_cores(): return lax.ppermute(value, 'src', [(at, at ^ 1) for at in range(8)])  12.9 us
    ppermute x4, starting transfers between devices, tile_move(): return lax.ppermute(value, BOTH, pairs)  7.97 us
    ppermute x2, starting transfers between devices, next_chip(): lax.ppermute(value, 'src', [(at, (at // 2 + steps) % CHIPS * 2 + at % 2)...  7.31 us
    ppermute x4, starting transfers between devices, tile_swap(): lax.ppermute(value, 'tile', [(at, partner(at)) for at in range(TROWS * TC...  6.85 us
    unnamed x18, local copies, waits for them, and re-layouts  3.98 us
    ppermute x4, waiting for transfers between devices, tile_move(): return lax.ppermute(value, BOTH, pairs)  3.95 us
    ppermute x6, waiting for transfers between devices, swap_cores(): return lax.ppermute(value, 'src', [(at, at ^ 1) for at in range(8)])  3.74 us
  transfers between devices with their start and end apart: 16, of which 7 were waited for; matrix products, arithmetic and copies ran while one was open for 0% of the time, Pallas kernels for 23%

profile of v3, /device:TPU:1, one launch (start us, length us, event | category | flops | bytes accessed | tf_op | source)
XLA Modules:
  0.0 73.6 jit_solution(10060540063229501265)
XLA Ops:
  0.6 0.0 copy-start
  0.7 1.1 %select_bitcast_fusion = f32[64,512]{1,0:T(8,128)S(1)} fusion(f32[1,512,512]{2,1,0:T(8,128)} %tile_ref.1, pred[]{:T(512)S(6)} %eq.14), kind=kLoop, calls=%fused_computation | loop fusion | flops 32768 | bytes 393217 | tf_op jit(solution)/shard_map/jit(_where)/select_n | solution.py:477
  1.8 1.3 %collective-permute-start = (f32[64,512]{1,0:T(8,128)S(1)}, f32[64,512]{1,0:T(8,128)S(1)}, u32[]{:S(2)}, u32[]{:S(2)}) collective-permute-start(f32[64,512]{1,0:T(8,128)S(1)} %select_bitcast_fusion), channel_id=1, source_target_pairs={{0,8},{1,9},{2,10},{3,11},{4,12},{5,13},{6,14},{7,15},{8,16},{9,17... | collective-permute-start | bytes 393224 | tf_op jit(solution)/shard_map/ppermute | solution.py:454
  3.1 0.0 copy-start.1
  3.1 1.4 %copy-done.1 = bf16[44,64,256]{2,1,0:T(8,128)(2,1)S(1)} copy-done((bf16[44,64,256]{2,1,0:T(8,128)(2,1)S(1)}, bf16[44,64,256]{2,1,0:T(8,128)(2,1)}, u32[]{:S(2)}) %copy-start.1) | copy-done | bytes 1441816
  4.5 1.2 %copy-done.4 = f32[1,512,512]{2,1,0:T(8,128)S(1)} copy-done((f32[1,512,512]{2,1,0:T(8,128)S(1)}, f32[1,512,512]{2,1,0:T(8,128)}, u32[]{:S(2)}) %copy-start.4) | copy-done | bytes 1048600
  5.7 0.6 own.1
  6.3 1.9 %collective-permute-done.mine_ref = f32[64,512]{1,0:T(8,128)S(1)} collective-permute-done((f32[64,512]{1,0:T(8,128)S(1)}, f32[64,512]{1,0:T(8,128)S(1)}, u32[]{:S(2)}, u32[]{:S(2)}) %collective-permute-start) | collective-permute-done | bytes 131104 | tf_op jit(solution)/shard_map/ppermute | solution.py:454
  8.2 1.9 %collective-permute-start.3 = (f32[64,512]{1,0:T(8,128)S(1)}, f32[64,512]{1,0:T(8,128)S(1)}, u32[]{:S(2)}, u32[]{:S(2)}) collective-permute-start(f32[64,512]{1,0:T(8,128)S(1)} %collective-permute-done.mine_ref), channel_id=1, source_target_pairs={{0,32},{32,0},{64,96},{96,64},{128,160},{160,128},{192,224},{224,1... | collective-permute-start | bytes 393224 | tf_op jit(solution)/shard_map/ppermute | solution.py:432
  10.1 1.0 %collective-permute-done.3.other_ref = f32[64,512]{1,0:T(8,128)S(1)} collective-permute-done((f32[64,512]{1,0:T(8,128)S(1)}, f32[64,512]{1,0:T(8,128)S(1)}, u32[]{:S(2)}, u32[]{:S(2)}) %collective-permute-start.3) | collective-permute-done | bytes 131104 | tf_op jit(solution)/shard_map/ppermute | solution.py:432
  11.1 0.4 rows.1
  11.5 1.3 %collective-permute-start.4 = (f32[128,128]{1,0:T(8,128)S(1)}, f32[128,128]{1,0:T(8,128)S(1)}, u32[]{:S(2)}, u32[]{:S(2)}) collective-permute-start(f32[128,128]{1,0:T(8,128)S(1)} %get-tuple-element.52), channel_id=1, source_target_pairs={{0,1},{1,2},{2,3},{3,4},{4,5},{5,6},{6,7},{8,9},{9,10},{10,11},{11... | collective-permute-start | bytes 196616 | tf_op jit(solution)/shard_map/ppermute | solution.py:454
  12.8 0.1 convert_select_fusion.info_ref
  12.9 3.0 %collective-permute-start.1 = (f32[4,2,128]{2,1,0:T(2,128)S(1)}, f32[4,2,128]{2,1,0:T(2,128)S(1)}, u32[]{:S(2)}, u32[]{:S(2)}) collective-permute-start(f32[4,2,128]{2,1,0:T(2,128)S(1)} %convert_select_fusion.info_ref), channel_id=1, source_target_pairs={{0,64},{32,96},{64,128},{96,160},{128,192},{160,224},{192,0},{224,... | collective-permute-start | bytes 12296 | tf_op jit(solution)/shard_map/ppermute | solution.py:436
  15.9 1.4 %copy-done.2 = bf16[44,64,256]{2,1,0:T(8,128)(2,1)S(1)} copy-done((bf16[44,64,256]{2,1,0:T(8,128)(2,1)S(1)}, bf16[44,64,256]{2,1,0:T(8,128)(2,1)}, u32[]{:S(2)}) %copy-start.2) | copy-done | bytes 1441816
  17.3 0.4 columns.1.basis_ref
  17.6 0.0 collective-permute-done.4.mine_ref
  17.6 3.3 %collective-permute-start.5 = (f32[128,128]{1,0:T(8,128)S(1)}, f32[128,128]{1,0:T(8,128)S(1)}, u32[]{:S(2)}, u32[]{:S(2)}) collective-permute-start(f32[128,128]{1,0:T(8,128)S(1)} %collective-permute-done.4.mine_ref), channel_id=1, source_target_pairs={{0,32},{32,0},{64,96},{96,64},{128,160},{160,128},{192,224},{224,1... | collective-permute-start | bytes 196616 | tf_op jit(solution)/shard_map/ppermute | solution.py:432
  20.9 4.3 %collective-permute-start.2 = (f32[8,2,128]{2,1,0:T(2,128)S(1)}, f32[8,2,128]{2,1,0:T(2,128)S(1)}, u32[]{:S(2)}, u32[]{:S(2)}) collective-permute-start(f32[8,2,128]{2,1,0:T(2,128)S(1)} %pad_maximum_fusion), channel_id=1, source_target_pairs={{0,128},{32,160},{64,192},{96,224},{128,0},{160,32},{192,64},{224,... | collective-permute-start | bytes 24584 | tf_op jit(solution)/shard_map/ppermute | solution.py:436
  25.2 3.0 %image.1 = (f32[4,512,256]{2,1,0:T(8,128)S(1)}, f32[256,256]{1,0:T(8,128)S(1)}, f32[2,256,128]{2,1,0:T(8,128)S(1)}, f32[2,256,128]{2,1,0:T(8,128)S(1)}) custom-call(f32[4,2,128]{2,1,0:T(2,128)S(1)} %convert_select_fusion.info_ref, f32[256,256]{1,0:T(8,128)S(1)} %columns.1.basis_ref, f32[128,128]{1,0:T(8,128)S(1)} %collective-permute-done.4.mine_ref, ...), custom_call_target="tpu_custom_call" | custom-call | flops 2000000000 | bytes 7409664 | tf_op jit(solution)/shard_map/image/pallas_call | solution.py:161
  28.3 0.0 collective-permute-done.2.far_ref.info_ref
  28.3 0.0 copy-start.5
  28.3 5.0 %others.1 = (f32[12,512,256]{2,1,0:T(8,128)S(1)}, f32[256,256]{1,0:T(8,128)S(1)}) custom-call(f32[4,2,128]{2,1,0:T(2,128)S(1)} %collective-permute-done.1.near_ref.info_ref, f32[8,2,128]{2,1,0:T(2,128)S(1)} %collective-permute-done.2.far_ref.info_ref, f32[128,128]{1,0:T(8,128)S(1)} %copy-done.6, bf16[80,64,256]{2,1,0:T(8,128)(2,1)S(1)} %copy-done, ...), custom_call_target="tpu_custom_call" | custom-call | flops 5000000000 | bytes 10039296 | tf_op jit(solution)/shard_map/others/pallas_call | solution.py:161
  33.3 2.7 %collective-permute-start.6 = (f32[256,256]{1,0:T(8,128)S(1)}, f32[256,256]{1,0:T(8,128)S(1)}, u32[]{:S(2)}, u32[]{:S(2)}) collective-permute-start(f32[256,256]{1,0:T(8,128)S(1)} %get-tuple-element.59.mine_ref), channel_id=1, source_target_pairs={{0,32},{32,0},{64,96},{96,64},{128,160},{160,128},{192,224},{224,1... | collective-permute-start | bytes 786440 | tf_op jit(solution)/shard_map/ppermute | solution.py:432
  36.0 1.2 %wanted.1.wanted_ref = f32[256,256]{1,0:T(8,128)S(1)} custom-call(f32[1,512,512]{2,1,0:T(8,128)S(1)} %copy-done.5, bf16[80,64,256]{2,1,0:T(8,128)(2,1)S(1)} %copy-done), custom_call_target="tpu_custom_call" | custom-call | flops 600000000 | bytes 3932160 | tf_op jit(solution)/shard_map/wanted/pallas_call | solution.py:161
  37.3 0.8 %residual.1 = (f32[256,256]{1,0:T(8,128)S(1)}, f32[8,128]{1,0:T(8,128)S(1)}) custom-call(f32[256,256]{1,0:T(8,128)S(1)} %get-tuple-element.59.mine_ref, f32[256,256]{1,0:T(8,128)S(1)} %collective-permute-done.6.other_ref, f32[256,256]{1,0:T(8,128)S(1)} %wanted.1.wanted_ref, f32[4,512,256]{2,1,0:T(8,128)S(1)} %get-tuple-element.62.field_ref, ...), custom_call_target="tpu_custom_call" | custom-call | flops 300000000 | bytes 5771264 | tf_op jit(solution)/shard_map/residual/pallas_call | solution.py:161
  38.1 1.6 %collective-permute-start.7 = (f32[8,128]{1,0:T(8,128)S(1)}, f32[8,128]{1,0:T(8,128)S(1)}, u32[]{:S(2)}, u32[]{:S(2)}) collective-permute-start(f32[8,128]{1,0:T(8,128)S(1)} %get-tuple-element.67), channel_id=1, source_target_pairs={{0,8},{1,9},{2,10},{3,11},{4,12},{5,13},{6,14},{7,15},{8,0},{9,1},... | collective-permute-start | bytes 12296 | tf_op jit(solution)/shard_map/ppermute | solution.py:468
  39.7 2.8 %adjoint.4 = (f32[2,256,128]{2,1,0:T(8,128)S(1)}, f32[2,256,128]{2,1,0:T(8,128)S(1)}) custom-call(f32[4,2,128]{2,1,0:T(2,128)S(1)} %convert_select_fusion.info_ref, f32[256,256]{1,0:T(8,128)S(1)} %get-tuple-element.63.residual_ref, f32[4,512,256]{2,1,0:T(8,128)S(1)} %get-tuple-element.62.field_ref, f32[128,128]{1,0:T(8,128)S(1)} %copy-done.6, ...), custom_call_target="tpu_custom_call" | custom-call | flops 1500000000 | bytes 5582848 | tf_op jit(solution)/shard_map/adjoint/pallas_call | solution.py:161
  42.5 1.3 %collective-permute-start.8 = (f32[8,128]{1,0:T(8,128)S(1)}, f32[8,128]{1,0:T(8,128)S(1)}, u32[]{:S(2)}, u32[]{:S(2)}) collective-permute-start(f32[8,128]{1,0:T(8,128)S(1)} %add.20), channel_id=1, source_target_pairs={{0,2},{1,3},{2,0},{3,1},{4,6},{5,7},{6,4},{7,5},{8,10},{9,11},{10,... | collective-permute-start | bytes 12296 | tf_op jit(solution)/shard_map/ppermute | solution.py:468
  43.8 2.8 %adjoint.5 = (f32[2,256,128]{2,1,0:T(8,128)S(1)}, f32[2,256,128]{2,1,0:T(8,128)S(1)}) custom-call(f32[4,2,128]{2,1,0:T(2,128)S(1)} %collective-permute-done.1.near_ref.info_ref, f32[256,256]{1,0:T(8,128)S(1)} %get-tuple-element.63.residual_ref, f32[12,512,256]{2,1,0:T(8,128)S(1)} %get-tuple-element.64.field_ref, f32[128,128]{1,0:T(8,128)S(1)} %copy-done.6, ...), custom_call_target="tpu_custom_call" | custom-call | flops 1500000000 | bytes 10293248 | tf_op jit(solution)/shard_map/adjoint/pallas_call | solution.py:161
  46.6 2.0 %collective-permute-start.9 = (f32[8,128]{1,0:T(8,128)S(1)}, f32[8,128]{1,0:T(8,128)S(1)}, u32[]{:S(2)}, u32[]{:S(2)}) collective-permute-start(f32[8,128]{1,0:T(8,128)S(1)} %add.21), channel_id=1, source_target_pairs={{0,24},{1,25},{2,26},{3,27},{4,28},{5,29},{6,30},{7,31},{8,16},{9,... | collective-permute-start | bytes 12296 | tf_op jit(solution)/shard_map/ppermute | solution.py:468
  48.6 2.9 %adjoint.6 = (f32[2,256,128]{2,1,0:T(8,128)S(1)}, f32[2,256,128]{2,1,0:T(8,128)S(1)}) custom-call(f32[8,2,128]{2,1,0:T(2,128)S(1)} %collective-permute-done.2.far_ref.info_ref, f32[256,256]{1,0:T(8,128)S(1)} %get-tuple-element.63.residual_ref, f32[12,512,256]{2,1,0:T(8,128)S(1)} %get-tuple-element.64.field_ref, f32[128,128]{1,0:T(8,128)S(1)} %copy-done.6, ...), custom_call_target="tpu_custom_call" | custom-call | flops 1500000000 | bytes 10297344 | tf_op jit(solution)/shard_map/adjoint/pallas_call | solution.py:161
  51.5 1.9 %collective-permute-start.10 = (f32[8,128]{1,0:T(8,128)S(1)}, f32[8,128]{1,0:T(8,128)S(1)}, u32[]{:S(2)}, u32[]{:S(2)}) collective-permute-start(f32[8,128]{1,0:T(8,128)S(1)} %add.22), channel_id=1, source_target_pairs={{0,6},{1,7},{2,4},{3,5},{4,2},{5,3},{6,0},{7,1},{8,14},{9,15},{10,... | collective-permute-start | bytes 12296 | tf_op jit(solution)/shard_map/ppermute | solution.py:468
  53.4 3.5 %adjoint.7 = (f32[256,128]{1,0:T(8,128)S(1)}, f32[256,128]{1,0:T(8,128)S(1)}) custom-call(f32[8,2,128]{2,1,0:T(2,128)S(1)} %collective-permute-done.2.far_ref.info_ref, f32[256,256]{1,0:T(8,128)S(1)} %get-tuple-element.63.residual_ref, f32[12,512,256]{2,1,0:T(8,128)S(1)} %get-tuple-element.64.field_ref, f32[128,128]{1,0:T(8,128)S(1)} %copy-done.6, ...), custom_call_target="tpu_custom_call" | custom-call | flops 1500000000 | bytes 10035200 | tf_op jit(solution)/shard_map/adjoint/pallas_call | solution.py:161
  56.9 0.0 copy-start.3
  56.9 1.6 %collective-permute-start.11 = (f32[256,128]{1,0:T(8,128)S(1)}, f32[256,128]{1,0:T(8,128)S(1)}, u32[]{:S(2)}, u32[]{:S(2)}) collective-permute-start(f32[256,128]{1,0:T(8,128)S(1)} %get-tuple-element.84), channel_id=1, source_target_pairs={{0,32},{32,0},{64,96},{96,64},{128,160},{160,128},{192,224},{224,1... | collective-permute-start | bytes 393224 | tf_op jit(solution)/shard_map/ppermute | solution.py:432
  58.6 1.0 %collective-permute-done.11 = f32[256,128]{1,0:T(8,128)S(1)} collective-permute-done((f32[256,128]{1,0:T(8,128)S(1)}, f32[256,128]{1,0:T(8,128)S(1)}, u32[]{:S(2)}, u32[]{:S(2)}) %collective-permute-start.11) | collective-permute-done | bytes 131104 | tf_op jit(solution)/shard_map/ppermute | solution.py:432
  59.6 0.2 lines.1
  59.8 2.3 %collective-permute-start.12 = (f32[64,128]{1,0:T(8,128)S(1)}, f32[64,128]{1,0:T(8,128)S(1)}, u32[]{:S(2)}, u32[]{:S(2)}) collective-permute-start(f32[64,128]{1,0:T(8,128)S(1)} %get-tuple-element.86), channel_id=1, source_target_pairs={{0,8},{1,9},{2,10},{3,11},{4,12},{5,13},{6,14},{7,15},{8,16},{9,17... | collective-permute-start | bytes 98312 | tf_op jit(solution)/shard_map/ppermute | solution.py:454
  62.1 1.0 %collective-permute-done.12.rim_ref = f32[64,128]{1,0:T(8,128)S(1)} collective-permute-done((f32[64,128]{1,0:T(8,128)S(1)}, f32[64,128]{1,0:T(8,128)S(1)}, u32[]{:S(2)}, u32[]{:S(2)}) %collective-permute-start.12) | collective-permute-done | bytes 32800 | tf_op jit(solution)/shard_map/ppermute | solution.py:454
  63.1 1.3 %collective-permute-start.13 = (f32[136,128]{1,0:T(8,128)S(1)}, f32[136,128]{1,0:T(8,128)S(1)}, u32[]{:S(2)}, u32[]{:S(2)}) collective-permute-start(f32[136,128]{1,0:T(8,128)S(1)} %rim.1.mine_ref), channel_id=1, source_target_pairs={{0,32},{32,0},{64,96},{96,64},{128,160},{160,128},{192,224},{224,1... | collective-permute-start | bytes 208904 | tf_op jit(solution)/shard_map/ppermute | solution.py:432
  64.4 0.9 %collective-permute-done.13.other_ref = f32[136,128]{1,0:T(8,128)S(1)} collective-permute-done((f32[136,128]{1,0:T(8,128)S(1)}, f32[136,128]{1,0:T(8,128)S(1)}, u32[]{:S(2)}, u32[]{:S(2)}) %collective-permute-start.13) | collective-permute-done | bytes 69664 | tf_op jit(solution)/shard_map/ppermute | solution.py:432
  65.3 0.4 pixels.1
  65.7 3.1 %collective-permute-start.14 = (f32[72,128]{1,0:T(8,128)S(1)}, f32[72,128]{1,0:T(8,128)S(1)}, u32[]{:S(2)}, u32[]{:S(2)}) collective-permute-start(f32[72,128]{1,0:T(8,128)S(1)} %get-tuple-element.89.before_ref), channel_id=1, source_target_pairs={{1,0},{2,1},{3,2},{4,3},{5,4},{6,5},{7,6},{9,8},{10,9},{11,10},{12... | collective-permute-start | bytes 110600 | tf_op jit(solution)/shard_map/ppermute | solution.py:454
  68.8 1.0 %collective-permute-done.14.mine_ref = f32[72,128]{1,0:T(8,128)S(1)} collective-permute-done((f32[72,128]{1,0:T(8,128)S(1)}, f32[72,128]{1,0:T(8,128)S(1)}, u32[]{:S(2)}, u32[]{:S(2)}) %collective-permute-start.14) | collective-permute-done | bytes 36896 | tf_op jit(solution)/shard_map/ppermute | solution.py:454
  69.9 2.1 %collective-permute-start.15 = (f32[72,128]{1,0:T(8,128)S(1)}, f32[72,128]{1,0:T(8,128)S(1)}, u32[]{:S(2)}, u32[]{:S(2)}) collective-permute-start(f32[72,128]{1,0:T(8,128)S(1)} %collective-permute-done.14.mine_ref), channel_id=1, source_target_pairs={{0,32},{32,0},{64,96},{96,64},{128,160},{160,128},{192,224},{224,1... | collective-permute-start | bytes 110600 | tf_op jit(solution)/shard_map/ppermute | solution.py:432
  71.9 0.9 %collective-permute-done.15.other_ref = f32[72,128]{1,0:T(8,128)S(1)} collective-permute-done((f32[72,128]{1,0:T(8,128)S(1)}, f32[72,128]{1,0:T(8,128)S(1)}, u32[]{:S(2)}, u32[]{:S(2)}) %collective-permute-start.15) | collective-permute-done | bytes 36896 | tf_op jit(solution)/shard_map/ppermute | solution.py:432
  72.8 0.8 %join.1 = (f32[1,64,512]{2,1,0:T(8,128)}, f32[4]{0:T(128)}) custom-call(f32[64,512]{1,0:T(8,128)S(1)} %get-tuple-element.88.inner_ref, f32[72,128]{1,0:T(8,128)S(1)} %get-tuple-element.89.before_ref, f32[72,128]{1,0:T(8,128)S(1)} %collective-permute-done.14.mine_ref, f32[72,128]{1,0:T(8,128)S(1)} %collective-permute-done.15.other_ref), custom_call_target="tpu_custom_call" | custom-call | flops 32768 | bytes 372752 | tf_op jit(solution)/shard_map/join/pallas_call | solution.py:161
  (27 shorter events, 0.1 us)
Async XLA Ops:
  0.6 15.3 %copy-start = (bf16[80,64,256]{2,1,0:T(8,128)(2,1)S(1)}, bf16[80,64,256]{2,1,0:T(8,128)(2,1)}, u32[]{:S(2)}) copy-start(bf16[80,64,256]{2,1,0:T(8,128)(2,1)} %constant.28.clone._.late_ref) | copy-start | bytes 7864324
  1.8 6.4 %collective-permute-start = (f32[64,512]{1,0:T(8,128)S(1)}, f32[64,512]{1,0:T(8,128)S(1)}, u32[]{:S(2)}, u32[]{:S(2)}) collective-permute-start(f32[64,512]{1,0:T(8,128)S(1)} %select_bitcast_fusion), channel_id=1, source_target_pairs={{0,8},{1,9},{2,10},{3,11},{4,12},{5,13},{6,14},{7,15},{8,16},{9,17... | collective-permute-start | bytes 393224 | tf_op jit(solution)/shard_map/ppermute | solution.py:454
  3.1 1.4 %copy-start.1 = (bf16[44,64,256]{2,1,0:T(8,128)(2,1)S(1)}, bf16[44,64,256]{2,1,0:T(8,128)(2,1)}, u32[]{:S(2)}) copy-start(bf16[44,64,256]{2,1,0:T(8,128)(2,1)} %constant.27.clone.early_ref) | copy-start | bytes 4325380
  4.5 1.2 %copy-start.4 = (f32[1,512,512]{2,1,0:T(8,128)S(1)}, f32[1,512,512]{2,1,0:T(8,128)}, u32[]{:S(2)}) copy-start(f32[1,512,512]{2,1,0:T(8,128)} %tile_ref.1) | copy-start | bytes 3145732
  5.7 7.1 %copy-start.7 = (s32[4,2,128]{2,1,0:T(2,128)S(1)}, s32[4,2,128]{2,1,0:T(2,128)}, u32[]{:S(2)}) copy-start(s32[4,2,128]{2,1,0:T(2,128)} %param.11) | copy-start | bytes 12292
  5.7 7.1 %copy-start.8 = (f32[4]{0:T(128)S(1)}, f32[4]{0:T(128)}, u32[]{:S(2)}) copy-start(f32[4]{0:T(128)} %param.10) | copy-start | bytes 52
  8.2 2.9 %collective-permute-start.3 = (f32[64,512]{1,0:T(8,128)S(1)}, f32[64,512]{1,0:T(8,128)S(1)}, u32[]{:S(2)}, u32[]{:S(2)}) collective-permute-start(f32[64,512]{1,0:T(8,128)S(1)} %collective-permute-done.mine_ref), channel_id=1, source_target_pairs={{0,32},{32,0},{64,96},{96,64},{128,160},{160,128},{192,224},{224,1... | collective-permute-start | bytes 393224 | tf_op jit(solution)/shard_map/ppermute | solution.py:432
  11.1 14.2 %copy-start.6 = (f32[128,128]{1,0:T(8,128)S(1)}, f32[128,128]{1,0:T(8,128)}, u32[]{:S(2)}) copy-start(f32[128,128]{1,0:T(8,128)} %gain_ref.11) | copy-start | bytes 196612
  11.5 6.1 %collective-permute-start.4 = (f32[128,128]{1,0:T(8,128)S(1)}, f32[128,128]{1,0:T(8,128)S(1)}, u32[]{:S(2)}, u32[]{:S(2)}) collective-permute-start(f32[128,128]{1,0:T(8,128)S(1)} %get-tuple-element.52), channel_id=1, source_target_pairs={{0,1},{1,2},{2,3},{3,4},{4,5},{5,6},{6,7},{8,9},{9,10},{10,11},{11... | collective-permute-start | bytes 196616 | tf_op jit(solution)/shard_map/ppermute | solution.py:454
  12.9 8.0 %collective-permute-start.1 = (f32[4,2,128]{2,1,0:T(2,128)S(1)}, f32[4,2,128]{2,1,0:T(2,128)S(1)}, u32[]{:S(2)}, u32[]{:S(2)}) collective-permute-start(f32[4,2,128]{2,1,0:T(2,128)S(1)} %convert_select_fusion.info_ref), channel_id=1, source_target_pairs={{0,64},{32,96},{64,128},{96,160},{128,192},{160,224},{192,0},{224,... | collective-permute-start | bytes 12296 | tf_op jit(solution)/shard_map/ppermute | solution.py:436
  15.9 1.4 %copy-start.2 = (bf16[44,64,256]{2,1,0:T(8,128)(2,1)S(1)}, bf16[44,64,256]{2,1,0:T(8,128)(2,1)}, u32[]{:S(2)}) copy-start(bf16[44,64,256]{2,1,0:T(8,128)(2,1)} %constant.27.clone.early_ref) | copy-start | bytes 4325380
  17.6 7.6 %collective-permute-start.5 = (f32[128,128]{1,0:T(8,128)S(1)}, f32[128,128]{1,0:T(8,128)S(1)}, u32[]{:S(2)}, u32[]{:S(2)}) collective-permute-start(f32[128,128]{1,0:T(8,128)S(1)} %collective-permute-done.4.mine_ref), channel_id=1, source_target_pairs={{0,32},{32,0},{64,96},{96,64},{128,160},{160,128},{192,224},{224,1... | collective-permute-start | bytes 196616 | tf_op jit(solution)/shard_map/ppermute | solution.py:432
  20.9 7.4 %collective-permute-start.2 = (f32[8,2,128]{2,1,0:T(2,128)S(1)}, f32[8,2,128]{2,1,0:T(2,128)S(1)}, u32[]{:S(2)}, u32[]{:S(2)}) collective-permute-start(f32[8,2,128]{2,1,0:T(2,128)S(1)} %pad_maximum_fusion), channel_id=1, source_target_pairs={{0,128},{32,160},{64,192},{96,224},{128,0},{160,32},{192,64},{224,... | collective-permute-start | bytes 24584 | tf_op jit(solution)/shard_map/ppermute | solution.py:436
  28.3 7.7 %copy-start.5 = (f32[1,512,512]{2,1,0:T(8,128)S(1)}, f32[1,512,512]{2,1,0:T(8,128)}, u32[]{:S(2)}) copy-start(f32[1,512,512]{2,1,0:T(8,128)} %target_ref.1) | copy-start | bytes 3145732
  33.3 3.9 %collective-permute-start.6 = (f32[256,256]{1,0:T(8,128)S(1)}, f32[256,256]{1,0:T(8,128)S(1)}, u32[]{:S(2)}, u32[]{:S(2)}) collective-permute-start(f32[256,256]{1,0:T(8,128)S(1)} %get-tuple-element.59.mine_ref), channel_id=1, source_target_pairs={{0,32},{32,0},{64,96},{96,64},{128,160},{160,128},{192,224},{224,1... | collective-permute-start | bytes 786440 | tf_op jit(solution)/shard_map/ppermute | solution.py:432
  38.1 4.4 %collective-permute-start.7 = (f32[8,128]{1,0:T(8,128)S(1)}, f32[8,128]{1,0:T(8,128)S(1)}, u32[]{:S(2)}, u32[]{:S(2)}) collective-permute-start(f32[8,128]{1,0:T(8,128)S(1)} %get-tuple-element.67), channel_id=1, source_target_pairs={{0,8},{1,9},{2,10},{3,11},{4,12},{5,13},{6,14},{7,15},{8,0},{9,1},... | collective-permute-start | bytes 12296 | tf_op jit(solution)/shard_map/ppermute | solution.py:468
  42.5 4.1 %collective-permute-start.8 = (f32[8,128]{1,0:T(8,128)S(1)}, f32[8,128]{1,0:T(8,128)S(1)}, u32[]{:S(2)}, u32[]{:S(2)}) collective-permute-start(f32[8,128]{1,0:T(8,128)S(1)} %add.20), channel_id=1, source_target_pairs={{0,2},{1,3},{2,0},{3,1},{4,6},{5,7},{6,4},{7,5},{8,10},{9,11},{10,... | collective-permute-start | bytes 12296 | tf_op jit(solution)/shard_map/ppermute | solution.py:468
  46.6 4.8 %collective-permute-start.9 = (f32[8,128]{1,0:T(8,128)S(1)}, f32[8,128]{1,0:T(8,128)S(1)}, u32[]{:S(2)}, u32[]{:S(2)}) collective-permute-start(f32[8,128]{1,0:T(8,128)S(1)} %add.21), channel_id=1, source_target_pairs={{0,24},{1,25},{2,26},{3,27},{4,28},{5,29},{6,30},{7,31},{8,16},{9,... | collective-permute-start | bytes 12296 | tf_op jit(solution)/shard_map/ppermute | solution.py:468
  51.5 5.4 %collective-permute-start.10 = (f32[8,128]{1,0:T(8,128)S(1)}, f32[8,128]{1,0:T(8,128)S(1)}, u32[]{:S(2)}, u32[]{:S(2)}) collective-permute-start(f32[8,128]{1,0:T(8,128)S(1)} %add.22), channel_id=1, source_target_pairs={{0,6},{1,7},{2,4},{3,5},{4,2},{5,3},{6,0},{7,1},{8,14},{9,15},{10,... | collective-permute-start | bytes 12296 | tf_op jit(solution)/shard_map/ppermute | solution.py:468
  56.9 8.5 %copy-start.3 = (bf16[44,64,256]{2,1,0:T(8,128)(2,1)S(1)}, bf16[44,64,256]{2,1,0:T(8,128)(2,1)}, u32[]{:S(2)}) copy-start(bf16[44,64,256]{2,1,0:T(8,128)(2,1)} %constant.27.clone.early_ref) | copy-start | bytes 4325380
  56.9 2.6 %collective-permute-start.11 = (f32[256,128]{1,0:T(8,128)S(1)}, f32[256,128]{1,0:T(8,128)S(1)}, u32[]{:S(2)}, u32[]{:S(2)}) collective-permute-start(f32[256,128]{1,0:T(8,128)S(1)} %get-tuple-element.84), channel_id=1, source_target_pairs={{0,32},{32,0},{64,96},{96,64},{128,160},{160,128},{192,224},{224,1... | collective-permute-start | bytes 393224 | tf_op jit(solution)/shard_map/ppermute | solution.py:432
  59.8 3.3 %collective-permute-start.12 = (f32[64,128]{1,0:T(8,128)S(1)}, f32[64,128]{1,0:T(8,128)S(1)}, u32[]{:S(2)}, u32[]{:S(2)}) collective-permute-start(f32[64,128]{1,0:T(8,128)S(1)} %get-tuple-element.86), channel_id=1, source_target_pairs={{0,8},{1,9},{2,10},{3,11},{4,12},{5,13},{6,14},{7,15},{8,16},{9,17... | collective-permute-start | bytes 98312 | tf_op jit(solution)/shard_map/ppermute | solution.py:454
  63.1 2.2 %collective-permute-start.13 = (f32[136,128]{1,0:T(8,128)S(1)}, f32[136,128]{1,0:T(8,128)S(1)}, u32[]{:S(2)}, u32[]{:S(2)}) collective-permute-start(f32[136,128]{1,0:T(8,128)S(1)} %rim.1.mine_ref), channel_id=1, source_target_pairs={{0,32},{32,0},{64,96},{96,64},{128,160},{160,128},{192,224},{224,1... | collective-permute-start | bytes 208904 | tf_op jit(solution)/shard_map/ppermute | solution.py:432
  65.7 4.1 %collective-permute-start.14 = (f32[72,128]{1,0:T(8,128)S(1)}, f32[72,128]{1,0:T(8,128)S(1)}, u32[]{:S(2)}, u32[]{:S(2)}) collective-permute-start(f32[72,128]{1,0:T(8,128)S(1)} %get-tuple-element.89.before_ref), channel_id=1, source_target_pairs={{1,0},{2,1},{3,2},{4,3},{5,4},{6,5},{7,6},{9,8},{10,9},{11,10},{12... | collective-permute-start | bytes 110600 | tf_op jit(solution)/shard_map/ppermute | solution.py:454
  69.9 2.9 %collective-permute-start.15 = (f32[72,128]{1,0:T(8,128)S(1)}, f32[72,128]{1,0:T(8,128)S(1)}, u32[]{:S(2)}, u32[]{:S(2)}) collective-permute-start(f32[72,128]{1,0:T(8,128)S(1)} %collective-permute-done.14.mine_ref), channel_id=1, source_target_pairs={{0,32},{32,0},{64,96},{96,64},{128,160},{160,128},{192,224},{224,1... | collective-permute-start | bytes 110600 | tf_op jit(solution)/shard_map/ppermute | solution.py:432

commit v4 on v3

--- a/solution.py
+++ b/solution.py
@@ -82,17 +82,13 @@
     middle = basis[A : N - A]
     rims = np.concatenate([basis[:A], basis[N - A :]])
     sides = [two_terms(basis[:A].T), two_terms(basis[N - A :].T)]
-    early = packed(
+    return packed(
         {
             "mid": two_terms(middle),
             "mid_t": two_halves(middle.T),
             "rims": two_terms(rims),
             "rims_t": [np.concatenate(list(two_terms(rims.T)), axis=1)],
             "sides": [np.concatenate([term for pair in sides for term in pair], axis=1)],
-        }
-    )
-    late = packed(
-        {
             "coarse": two_halves(coarse),
             "coarse_t": two_terms(coarse.T),
             "fold": [fold],
@@ -102,11 +98,9 @@
             "gram": two_terms(spread.T @ spread),
         }
     )
-    return early, late
-
-
-(EARLY, EARLY_AT), (LATE, LATE_AT) = make_tables()
-SPOTS = EARLY_AT | LATE_AT
+
+
+TABLES, SPOTS = make_tables()
 
 
 def stored(ref, name, at=0):
@@ -175,14 +169,14 @@
     return group // 2, group % 2
 
 
-def own_kernel(tile_ref, early_ref, rows_ref, table_ref):
-    rows_ref[...] = product(wide(early_ref, "mid_t"), terms(tile_ref[0]))
-    table_ref[...] = stored(early_ref, "rims_t")
-
-
-def wanted_kernel(target_ref, late_ref, wanted_ref):
-    upper = product(terms(target_ref[0]), narrow(late_ref, "spread"))
-    wanted_ref[...] = product(wide(late_ref, "spread_t"), terms(upper))
+def own_kernel(tile_ref, table_ref, rows_ref, rims_ref):
+    rows_ref[...] = product(wide(table_ref, "mid_t"), terms(tile_ref[0]))
+    rims_ref[...] = stored(table_ref, "rims_t")
+
+
+def wanted_kernel(target_ref, table_ref, wanted_ref):
+    upper = product(terms(target_ref[0]), narrow(table_ref, "spread"))
+    wanted_ref[...] = product(wide(table_ref, "spread_t"), terms(upper)).T
 
 
 def rows_kernel(rows_ref, mine_ref, other_ref, table_ref, all_ref, side_ref):
@@ -197,8 +191,8 @@
     side_ref[...] = jnp.concatenate([side[:K], side[K:]], axis=1)
 
 
-def columns_kernel(rows_ref, early_ref, _, basis_ref):
-    basis_ref[...] = product(terms(rows_ref[...]), narrow(early_ref, "mid"))
+def columns_kernel(rows_ref, table_ref, basis_ref):
+    basis_ref[...] = product(terms(rows_ref[...]), narrow(table_ref, "mid"))
 
 
 def disc_of(gain):
@@ -223,8 +217,8 @@
     return ref[source % SOURCES + (SOURCES if source // SOURCES == 3 else 0), 0, 1]
 
 
-def image_of(info_refs, chips, planes, disc, late_ref, field_ref):
-    coarse, coarse_t = wide(late_ref, "coarse"), narrow(late_ref, "coarse_t")
+def image_of(info_refs, chips, planes, disc, table_ref, field_ref):
+    coarse = wide(table_ref, "coarse")
     total = jnp.zeros((W, W), F32)
     for chip in chips:
         specs = []
@@ -238,11 +232,11 @@
             specs.append(jnp.concatenate([window(ref) for ref in planes], axis=1))
         stacked = product(terms(jnp.concatenate(specs, axis=0)), coarse)
         for at in range(SOURCES):
-            half = stacked[at * K : at * K + K]
-            half = jnp.concatenate([half[:, :W], half[:, W:]], axis=0)
-            field = product(coarse_t, terms(half))
+            half = stacked[at * K : at * K + K].T
+            half = jnp.concatenate([half[:W], half[W:]], axis=1)
+            field = product(terms(half), coarse)
             field_ref[(chip - chips[0]) * SOURCES + at] = field
-            real, imag = field[:W], field[W:]
+            real, imag = field[:, :W], field[:, W:]
             weight = weight_of(info_refs, chip * SOURCES + at)
             total = total + weight * (real * real + imag * imag)
     return total
@@ -254,8 +248,7 @@
     mine_ref,
     other_ref,
     gain_ref,
-    early_ref,
-    late_ref,
+    table_ref,
     field_ref,
     total_ref,
     real_ref,
@@ -273,7 +266,7 @@
         ],
         axis=0,
     )
-    basis = basis_ref[...] + product(terms(rim), narrow(early_ref, "rims"))
+    basis = basis_ref[...] + product(terms(rim), narrow(table_ref, "rims"))
     zero = jnp.zeros((K, K), F32)
     even = jnp.concatenate(
         [
@@ -289,35 +282,35 @@
         ],
         axis=0,
     )
-    fold, fold_t = stored(late_ref, "fold"), stored(late_ref, "fold_t")
+    fold, fold_t = stored(table_ref, "fold"), stored(table_ref, "fold_t")
     for ref, part in ((real_ref, even), (imag_ref, odd)):
         plane = exact_right(exact_left(fold_t, part), fold)
         ref[0] = plane[:, :K]
         ref[1] = plane[:, K:]
     disc = disc_of(gain_ref[...])
-    total_ref[...] = image_of((info_ref,), (0,), (real_ref, imag_ref), disc, late_ref, field_ref)
+    total_ref[...] = image_of((info_ref,), (0,), (real_ref, imag_ref), disc, table_ref, field_ref)
 
 
 def others_kernel(
-    near_ref, far_ref, gain_ref, late_ref, real_ref, imag_ref, before_ref, field_ref, total_ref
+    near_ref, far_ref, gain_ref, table_ref, real_ref, imag_ref, before_ref, field_ref, total_ref
 ):
     info_refs = (None, near_ref, far_ref)
     disc = disc_of(gain_ref[...])
     total_ref[...] = before_ref[...] + image_of(
-        info_refs, (1, 2, 3), (real_ref, imag_ref), disc, late_ref, field_ref
-    )
-
-
-def residual_kernel(mine_ref, other_ref, wanted_ref, field_ref, late_ref, residual_ref, energy_ref):
+        info_refs, (1, 2, 3), (real_ref, imag_ref), disc, table_ref, field_ref
+    )
+
+
+def residual_kernel(mine_ref, other_ref, wanted_ref, field_ref, table_ref, residual_ref, energy_ref):
     bright = mine_ref[...] + other_ref[...]
-    gram = narrow(late_ref, "gram")
+    gram = narrow(table_ref, "gram")
     value = product(terms(product(gram, terms(bright))), gram)
     residual = value * (1.0 / (8 * SOURCES)) - wanted_ref[...]
     residual_ref[...] = residual
     lanes = lax.broadcasted_iota(jnp.int32, (8, K), 1)
     energies = jnp.zeros((8, K), F32)
     for source in range(SOURCES):
-        real, imag = field_ref[source, :W], field_ref[source, W:]
+        real, imag = field_ref[source, :, :W], field_ref[source, :, W:]
         energy = jnp.sum(residual * (real * real + imag * imag))
         energies = jnp.where(lanes == source, energy, energies)
     energy_ref[...] = energies
@@ -329,86 +322,80 @@
     residual_ref,
     field_ref,
     gain_ref,
-    late_ref,
+    table_ref,
     real_in,
     imag_in,
     *outs,
 ):
     info_refs = (info_ref,) * 3
     first_field = SOURCES if chip else 0
-    coarse, coarse_t = wide(late_ref, "coarse"), narrow(late_ref, "coarse_t")
-    _, core = my_place()
+    coarse_t = narrow(table_ref, "coarse_t")
     last = chip == CHIPS - 1
-    real_ref, imag_ref = outs[2:] if last else outs
+    real_ref, imag_ref = outs[1:] if last else outs
     residual = residual_ref[...]
     disc = disc_of(gain_ref[...])
     real_ref[...] = jnp.zeros((2, W, K), F32) if chip == 0 else real_in[...]
     imag_ref[...] = jnp.zeros((2, W, K), F32) if chip == 0 else imag_in[...]
     pad = jnp.zeros((K, K), F32)
-    for couple in range(chip * SOURCES, chip * SOURCES + SOURCES, 2):
-        sides = []
-        for source in (couple, couple + 1):
-            field = field_ref.at[source - first_field]
-            real, imag = field[:W], field[W:]
-            scaled = jnp.concatenate([residual * real, residual * imag], axis=1)
-            back = product(terms(scaled), coarse_t)
-            sides.append(jnp.concatenate([back[:, :K], back[:, K:]], axis=0))
-        spec = product(coarse, terms(jnp.concatenate(sides, axis=1)))
-        for place in range(2):
-            source = couple + place
-            row, column = window_starts(info_refs, source)
-            scale = disc * (2.0 * weight_of(info_refs, source))
-            for ref, part in ((real_ref, spec[:K]), (imag_ref, spec[K:])):
-                part = part[:, place * K : place * K + K] * scale
-                spread = pltpu.roll(jnp.concatenate([part, pad], axis=1), column, 1)
-                for side in range(2):
-                    ref[side, pl.ds(row, K), :] += spread[:, side * K : side * K + K]
+    first = chip * SOURCES
+    halves = []
+    for source in range(first, first + SOURCES):
+        field = field_ref.at[source - first_field]
+        scaled = jnp.concatenate([residual * field[:, :W], residual * field[:, W:]], axis=1)
+        half = product(terms(scaled), coarse_t).T
+        halves.append(jnp.concatenate([half[:K], half[K:]], axis=1))
+    spec = product(terms(jnp.concatenate(halves, axis=0)), coarse_t)
+    for source in range(first, first + SOURCES):
+        row, column = window_starts(info_refs, source)
+        scale = disc * (2.0 * weight_of(info_refs, source))
+        own = spec[(source - first) * K : (source - first) * K + K]
+        for ref, part in ((real_ref, own[:, :K]), (imag_ref, own[:, K:])):
+            spread = pltpu.roll(jnp.concatenate([part * scale, pad], axis=1), column, 1)
+            for side in range(2):
+                ref[side, pl.ds(row, K), :] += spread[:, side * K : side * K + K]
     if not last:
         return
-    keep_ref, send_ref = outs[:2]
-    fold, fold_t = stored(late_ref, "fold"), stored(late_ref, "fold_t")
+    fold, fold_t = stored(table_ref, "fold"), stored(table_ref, "fold_t")
 
     def folded(ref):
         return exact_right(exact_left(fold, jnp.concatenate([ref[0], ref[1]], axis=1)), fold_t)
 
     even, odd = folded(real_ref), folded(imag_ref)
-    left = jnp.concatenate([even[:K, :K], -odd[K:, :K]], axis=0)
-    right = jnp.concatenate([-odd[:K, K:], -even[K:, K:]], axis=0)
-    keep_ref[...] = jnp.where(core == 0, left, right)
-    send_ref[...] = jnp.where(core == 0, right, left)
-
-
-def lines_kernel(mine_ref, early_ref, lines_ref, rim_ref):
+    outs[0][:K] = jnp.concatenate([even[:K, :K], -odd[:K, K:]], axis=1)
+    outs[0][K:] = jnp.concatenate([-odd[K:, :K], -even[K:, K:]], axis=1)
+
+
+def lines_kernel(mine_ref, table_ref, lines_ref, rim_ref):
     chip, _ = my_place()
     spectrum = terms(mine_ref[...])
-    lines = [early_ref[pl.ds(SPOTS["mid"][at][0] + 2 * chip, 2)].reshape(K, W) for at in range(2)]
+    lines = [table_ref[pl.ds(SPOTS["mid"][at][0] + 2 * chip, 2)].reshape(K, W) for at in range(2)]
     lines_ref[...] = product(lines, spectrum)
-    outer = [early_ref[SPOTS["rims"][at][0] + 1 - chip // 2] for at in range(2)]
+    outer = [table_ref[SPOTS["rims"][at][0] + 1 - chip // 2] for at in range(2)]
     rim_ref[...] = product(outer, spectrum)
 
 
 def rim_kernel(lines_ref, rim_ref, energy_ref, out_ref):
-    chip, _ = my_place()
+    chip, core = my_place()
     rim = rim_ref[...]
     out_ref[:A] = lines_ref[:A] + jnp.where(chip == 0, rim, 0.0)
     out_ref[A:K] = lines_ref[A:] + jnp.where(chip == 3, rim, 0.0)
-    out_ref[K:] = energy_ref[...]
-
-
-def pixels_kernel(mine_ref, other_ref, early_ref, inner_ref, side_ref):
+    energy = energy_ref[...]
+    out_ref[K:] = jnp.concatenate([jnp.where(core == at, energy, 0.0) for at in range(2)], axis=1)
+
+
+def pixels_kernel(mine_ref, other_ref, table_ref, inner_ref, side_ref):
     _, core = my_place()
     first = core == 0
-    mine, other = mine_ref[...], other_ref[...]
-    lines = jnp.concatenate([jnp.where(first, mine, other), jnp.where(first, other, mine)], axis=1)
+    lines = mine_ref[...] + other_ref[...]
     top, bottom = lines[:A], lines[A:K]
-    table = stored(early_ref, "sides")
+    table = stored(table_ref, "sides")
     table = jnp.where(first, table[:, :K], table[:, K:])
     table = (table[:, :A], table[:, A:])
     side_ref[:A] = jnp.concatenate([product(terms(top), table), product(terms(bottom), table)], axis=1)
     lanes = lax.broadcasted_iota(jnp.int32, (8, K), 1)
     side_ref[A:] = jnp.where(lanes < A, lines[K:, :K], pltpu.roll(lines[K:, K:], A, 1))
     own = jnp.where(first, top, bottom)
-    inner_ref[...] = product(terms(own), wide(early_ref, "mid_t"))
+    inner_ref[...] = product(terms(own), wide(table_ref, "mid_t"))
 
 
 def join_kernel(inner_ref, before_ref, mine_ref, other_ref, out_ref, energy_ref):
@@ -432,10 +419,14 @@
     return lax.ppermute(value, "src", [(at, at ^ 1) for at in range(8)])
 
 
-def next_chip(value, steps):
-    return lax.ppermute(
-        value, "src", [(at, (at // 2 + steps) % CHIPS * 2 + at % 2) for at in range(2 * CHIPS)]
-    )
+def chip_swap(value, low):
+    pairs = []
+    for source in range(2 * CHIPS):
+        for tile in range(TROWS * TCOLS):
+            step = 1 if tile % 2 == low else -1
+            partner = (source // 2 + step) % CHIPS * 2 + source % 2
+            pairs.append((source * 32 + tile, partner * 32 + (tile ^ 1)))
+    return lax.ppermute(value, BOTH, pairs)
 
 
 def tile_move(value, shift_of):
@@ -476,41 +467,42 @@
     core = lax.axis_index("src") % 2
     edge = jnp.where(core == 0, mask_tiles[0, PIX - A :], mask_tiles[0, :A])
     mine = tile_move(edge, lambda source: (1, 0) if source % 2 == 0 else (-1, 0))
-    rows, rim_table = call(own_kernel, [(W, PIX), (W, W)], [mask_tiles, EARLY], "own", 400_000_000, bf16=(1,))
-    mine, rows, weights, freq_index = tied(mine, rows, weights, freq_index)
+    rows, rim_table = call(own_kernel, [(W, PIX), (W, W)], [mask_tiles, TABLES], "own", 400_000_000, bf16=(1,))
+    rows, weights, freq_index = tied(rows, weights, freq_index)
+    mine, rows = tied(mine, rows)
     other = swap_cores(mine)
     lanes = lax.broadcasted_iota(jnp.int32, freq_index.shape, 2)
     info = jnp.where(lanes == 1, weights[:, None, None], freq_index.astype(F32))
-    near = next_chip(info, 1)
+    near = chip_swap(info, 1)
     rows, side = call(
         rows_kernel, [(W, PIX), (K, K)], [rows, mine, other, rim_table], "rows", 100_000_000
     )
     my_side = tile_move(side, lambda source: (0, 1) if source % 2 == 0 else (0, -1))
-    (basis,) = call(columns_kernel, [(W, W)], [rows, EARLY, LATE], "columns", 200_000_000)
-    far = next_chip(jnp.concatenate([info, near]), 2)
+    (basis,) = call(columns_kernel, [(W, W)], [rows, TABLES], "columns", 200_000_000)
+    far = chip_swap(jnp.concatenate([info, near]), 0)
     my_side, basis = tied(my_side, basis)
     other_side = swap_cores(my_side)
     own_field, total, real, imag = call(
         image_kernel,
-        [(SOURCES, 2 * W, W), (W, W), (2, W, K), (2, W, K)],
-        [info, basis, my_side, other_side, pupil_gain, EARLY, LATE],
+        [(SOURCES, W, 2 * W), (W, W), (2, W, K), (2, W, K)],
+        [info, basis, my_side, other_side, pupil_gain, TABLES],
         "image",
         2_000_000_000,
         smem=(0,),
     )
     field, mine = call(
         others_kernel,
-        [((CHIPS - 1) * SOURCES, 2 * W, W), (W, W)],
-        [near, far, pupil_gain, LATE, real, imag, total],
+        [((CHIPS - 1) * SOURCES, W, 2 * W), (W, W)],
+        [near, far, pupil_gain, TABLES, real, imag, total],
         "others",
         5_000_000_000,
         smem=(0, 1),
     )
     other = swap_cores(mine)
-    (wanted,) = call(wanted_kernel, [(W, W)], [target, LATE], "wanted", 600_000_000)
+    (wanted,) = call(wanted_kernel, [(W, W)], [target, TABLES], "wanted", 600_000_000)
     other, wanted = tied(other, wanted)
     residual, energies = call(
-        residual_kernel, [(W, W), (8, K)], [mine, other, wanted, own_field, LATE], "residual", 300_000_000
+        residual_kernel, [(W, W), (8, K)], [mine, other, wanted, own_field, TABLES], "residual", 300_000_000
     )
     plane = pltpu.VMEM((2, W, K), F32)
     planes = (jnp.zeros((8, K), F32),) * 2
@@ -519,31 +511,29 @@
         last = chip == CHIPS - 1
         outs = call(
             functools.partial(adjoint_kernel, chip),
-            [(W, K), (W, K)] if last else [(2, W, K), (2, W, K)],
-            [(info, near, far, far)[chip], residual, field if chip else own_field, pupil_gain, LATE, *planes],
+            [(W, W)] if last else [(2, W, K), (2, W, K)],
+            [(info, near, far, far)[chip], residual, field if chip else own_field, pupil_gain, TABLES, *planes],
             "adjoint",
             1_500_000_000,
             scratch=(plane, plane) if last else (),
             smem=(0,),
         )
-        planes = outs[:2]
+        planes = outs
         *planes, energies = tied(*planes, energies + arrived)
-    keep, send = planes
-    mine = keep + swap_cores(send)
     lines, rim = call(
         lines_kernel,
-        [(K, K), (A, K)],
-        [mine, EARLY],
+        [(K, W), (A, W)],
+        [planes[0], TABLES],
         "lines",
         100_000_000,
     )
     from_rows = tile_move(rim, lambda source: {0: (1, 0), 3: (-1, 0)}.get(source // 2))
-    (mine,) = call(rim_kernel, [(K + 8, K)], [lines, from_rows, energies], "rim", K * K)
+    (mine,) = call(rim_kernel, [(K + 8, W)], [lines, from_rows, energies], "rim", K * K)
     other = swap_cores(mine)
     inner, side = call(
         pixels_kernel,
         [(A, PIX), (A + 8, K)],
-        [mine, other, EARLY],
+        [mine, other, TABLES],
         "pixels",
         100_000_000,
     )

time: 74.3 us -> 70.3 us (0.946)
  starting transfers between devices: 35 us -> 33 us
  Pallas kernels: 24.7 us -> 23.7 us
  waiting for transfers between devices: 7.71 us -> 6.87 us
    ppermute x6 -> x5, starting transfers between devices: 12.9 us -> 11.2 us  [swap_cores(): return lax.ppermute(value, 'src', [(at, at ^ 1) for at in range(8)])]
    pallas_call x15, Pallas kernels: 24.7 us -> 23.7 us  [call(): pl.pallas_call(kernel, out_shape=shapes, in_specs=specs, out_specs=[pl.Bl...]
    ppermute x6 -> x5, waiting for transfers between devices: 3.74 us -> 2.96 us  [swap_cores(): return lax.ppermute(value, 'src', [(at, at ^ 1) for at in range(8)])]
    unnamed x18 -> x14, local copies, waits for them, and re-layouts: 3.98 us -> 3.39 us
  transfers between devices with their start and end apart: 16 -> 15, of which waited for: 7 -> 8; matrix products, arithmetic and copies ran while one was open for 0% -> 0% of each run, Pallas kernels for 23% -> 23%
where the time goes in v4:
time: 70.3 us; the launch traced here: 69 us
  starting transfers between devices  33 us (47%)
  Pallas kernels  23.7 us (34%)
  waiting for transfers between devices  6.87 us (10%)
  local copies, waits for them, and re-layouts  3.39 us (5%)
  other arithmetic  1.09 us (2%)
  between operations  0.91 us (1%)
    pallas_call x15, Pallas kernels, call(): pl.pallas_call(kernel, out_shape=shapes, in_specs=specs, out_specs=[pl.Bl...  23.7 us
    ppermute x5, starting transfers between devices, swap_cores(): return lax.ppermute(value, 'src', [(at, at ^ 1) for at in range(8)])  11.2 us
    ppermute x4, starting transfers between devices, tile_move(): return lax.ppermute(value, BOTH, pairs)  7.86 us
    ppermute x2, starting transfers between devices, chip_swap(): return lax.ppermute(value, BOTH, pairs)  7.73 us
    ppermute x4, starting transfers between devices, tile_swap(): lax.ppermute(value, 'tile', [(at, partner(at)) for at in range(TROWS * TC...  6.21 us
    ppermute x4, waiting for transfers between devices, tile_move(): return lax.ppermute(value, BOTH, pairs)  3.46 us
    unnamed x14, local copies, waits for them, and re-layouts  3.39 us
    ppermute x5, waiting for transfers between devices, swap_cores(): return lax.ppermute(value, 'src', [(at, at ^ 1) for at in range(8)])  2.96 us
  transfers between devices with their start and end apart: 15, of which 8 were waited for; matrix products, arithmetic and copies ran while one was open for 0% of the time, Pallas kernels for 23%

profile of v4, /device:TPU:1, one launch (start us, length us, event | category | flops | bytes accessed | tf_op | source)
XLA Modules:
  0.0 69.0 jit_solution(3339915894073574337)
XLA Ops:
  0.7 1.0 %select_bitcast_fusion = f32[64,512]{1,0:T(8,128)S(1)} fusion(f32[1,512,512]{2,1,0:T(8,128)} %tile_ref.1, pred[]{:T(512)S(6)} %eq.14), kind=kLoop, calls=%fused_computation | loop fusion | flops 32768 | bytes 393217 | tf_op jit(solution)/shard_map/jit(_where)/select_n | solution.py:468
  1.7 1.3 %collective-permute-start.2 = (f32[64,512]{1,0:T(8,128)S(1)}, f32[64,512]{1,0:T(8,128)S(1)}, u32[]{:S(2)}, u32[]{:S(2)}) collective-permute-start(f32[64,512]{1,0:T(8,128)S(1)} %select_bitcast_fusion), channel_id=1, source_target_pairs={{0,8},{1,9},{2,10},{3,11},{4,12},{5,13},{6,14},{7,15},{8,16},{9,17... | collective-permute-start | bytes 393224 | tf_op jit(solution)/shard_map/ppermute | solution.py:445
  3.0 0.0 copy-start
  3.0 2.1 %copy-done = bf16[124,64,256]{2,1,0:T(8,128)(2,1)S(1)} copy-done((bf16[124,64,256]{2,1,0:T(8,128)(2,1)S(1)}, bf16[124,64,256]{2,1,0:T(8,128)(2,1)}, u32[]{:S(2)}) %copy-start) | copy-done | bytes 4063256
  5.1 1.2 %copy-done.2 = f32[1,512,512]{2,1,0:T(8,128)S(1)} copy-done((f32[1,512,512]{2,1,0:T(8,128)S(1)}, f32[1,512,512]{2,1,0:T(8,128)}, u32[]{:S(2)}) %copy-start.2) | copy-done | bytes 1048600
  6.3 0.6 own.1
  6.9 0.0 copy-start.3
  6.9 1.1 %collective-permute-done.2.mine_ref = f32[64,512]{1,0:T(8,128)S(1)} collective-permute-done((f32[64,512]{1,0:T(8,128)S(1)}, f32[64,512]{1,0:T(8,128)S(1)}, u32[]{:S(2)}, u32[]{:S(2)}) %collective-permute-start.2) | collective-permute-done | bytes 131104 | tf_op jit(solution)/shard_map/ppermute | solution.py:445
  8.0 2.7 %collective-permute-start.3 = (f32[64,512]{1,0:T(8,128)S(1)}, f32[64,512]{1,0:T(8,128)S(1)}, u32[]{:S(2)}, u32[]{:S(2)}) collective-permute-start(f32[64,512]{1,0:T(8,128)S(1)} %collective-permute-done.2.mine_ref), channel_id=1, source_target_pairs={{0,32},{32,0},{64,96},{96,64},{128,160},{160,128},{192,224},{224,1... | collective-permute-start | bytes 393224 | tf_op jit(solution)/shard_map/ppermute | solution.py:419
  10.7 1.0 %collective-permute-done.3.other_ref = f32[64,512]{1,0:T(8,128)S(1)} collective-permute-done((f32[64,512]{1,0:T(8,128)S(1)}, f32[64,512]{1,0:T(8,128)S(1)}, u32[]{:S(2)}, u32[]{:S(2)}) %collective-permute-start.3) | collective-permute-done | bytes 131104 | tf_op jit(solution)/shard_map/ppermute | solution.py:419
  11.7 0.4 rows.1
  12.1 1.3 %collective-permute-start.4 = (f32[128,128]{1,0:T(8,128)S(1)}, f32[128,128]{1,0:T(8,128)S(1)}, u32[]{:S(2)}, u32[]{:S(2)}) collective-permute-start(f32[128,128]{1,0:T(8,128)S(1)} %get-tuple-element.51), channel_id=1, source_target_pairs={{0,1},{1,2},{2,3},{3,4},{4,5},{5,6},{6,7},{8,9},{9,10},{10,11},{11... | collective-permute-start | bytes 196616 | tf_op jit(solution)/shard_map/ppermute | solution.py:445
  13.5 0.1 convert_select_fusion.info_ref
  13.5 7.0 %collective-permute-start = (f32[4,2,128]{2,1,0:T(2,128)S(1)}, f32[4,2,128]{2,1,0:T(2,128)S(1)}, u32[]{:S(2)}, u32[]{:S(2)}) collective-permute-start(f32[4,2,128]{2,1,0:T(2,128)S(1)} %convert_select_fusion.info_ref), channel_id=1, source_target_pairs={{0,193},{1,64},{2,195},{3,66},{4,197},{5,68},{6,199},{7,70},{8,201... | collective-permute-start | bytes 12296 | tf_op jit(solution)/shard_map/ppermute | solution.py:429
  20.5 0.4 columns.1.basis_ref
  20.9 0.0 collective-permute-done.4.mine_ref
  20.9 1.9 %collective-permute-start.5 = (f32[128,128]{1,0:T(8,128)S(1)}, f32[128,128]{1,0:T(8,128)S(1)}, u32[]{:S(2)}, u32[]{:S(2)}) collective-permute-start(f32[128,128]{1,0:T(8,128)S(1)} %collective-permute-done.4.mine_ref), channel_id=1, source_target_pairs={{0,32},{32,0},{64,96},{96,64},{128,160},{160,128},{192,224},{224,1... | collective-permute-start | bytes 196616 | tf_op jit(solution)/shard_map/ppermute | solution.py:419
  22.8 0.0 collective-permute-done.near_ref.info_ref
  22.8 0.8 %collective-permute-start.1 = (f32[8,2,128]{2,1,0:T(2,128)S(1)}, f32[8,2,128]{2,1,0:T(2,128)S(1)}, u32[]{:S(2)}, u32[]{:S(2)}) collective-permute-start(f32[8,2,128]{2,1,0:T(2,128)S(1)} %pad_maximum_fusion), channel_id=1, source_target_pairs={{0,65},{1,192},{2,67},{3,194},{4,69},{5,196},{6,71},{7,198},{8,73}... | collective-permute-start | bytes 24584 | tf_op jit(solution)/shard_map/ppermute | solution.py:429
  23.6 0.1 collective-permute-done.5.other_ref
  23.7 3.1 %image.1 = (f32[4,256,512]{2,1,0:T(8,128)S(1)}, f32[256,256]{1,0:T(8,128)S(1)}, f32[2,256,128]{2,1,0:T(8,128)S(1)}, f32[2,256,128]{2,1,0:T(8,128)S(1)}) custom-call(f32[4,2,128]{2,1,0:T(2,128)S(1)} %convert_select_fusion.info_ref, f32[256,256]{1,0:T(8,128)S(1)} %columns.1.basis_ref, f32[128,128]{1,0:T(8,128)S(1)} %collective-permute-done.4.mine_ref, ...), custom_call_target="tpu_custom_call" | custom-call | flops 2000000000 | bytes 7409664 | tf_op jit(solution)/shard_map/image/pallas_call | solution.py:155
  26.8 0.4 collective-permute-done.1.far_ref.info_ref
  27.3 5.2 %others.1 = (f32[12,256,512]{2,1,0:T(8,128)S(1)}, f32[256,256]{1,0:T(8,128)S(1)}) custom-call(f32[4,2,128]{2,1,0:T(2,128)S(1)} %collective-permute-done.near_ref.info_ref, f32[8,2,128]{2,1,0:T(2,128)S(1)} %collective-permute-done.1.far_ref.info_ref, f32[128,128]{1,0:T(8,128)S(1)} %copy-done.3, bf16[124,64,256]{2,1,0:T(8,128)(2,1)S(1)} %copy-done.1, ...), custom_call_target="tpu_custom_call" | custom-call | flops 5000000000 | bytes 11481088 | tf_op jit(solution)/shard_map/others/pallas_call | solution.py:155
  32.5 2.2 %collective-permute-start.6 = (f32[256,256]{1,0:T(8,128)S(1)}, f32[256,256]{1,0:T(8,128)S(1)}, u32[]{:S(2)}, u32[]{:S(2)}) collective-permute-start(f32[256,256]{1,0:T(8,128)S(1)} %get-tuple-element.58.mine_ref), channel_id=1, source_target_pairs={{0,32},{32,0},{64,96},{96,64},{128,160},{160,128},{192,224},{224,1... | collective-permute-start | bytes 786440 | tf_op jit(solution)/shard_map/ppermute | solution.py:419
  34.7 1.3 %wanted.1.wanted_ref = f32[256,256]{1,0:T(8,128)S(1)} custom-call(f32[1,512,512]{2,1,0:T(8,128)S(1)} %copy-done.4, bf16[124,64,256]{2,1,0:T(8,128)(2,1)S(1)} %copy-done.1), custom_call_target="tpu_custom_call" | custom-call | flops 600000000 | bytes 5373952 | tf_op jit(solution)/shard_map/wanted/pallas_call | solution.py:155
  36.0 0.0 collective-permute-done.6.other_ref
  36.0 0.8 %residual.1 = (f32[256,256]{1,0:T(8,128)S(1)}, f32[8,128]{1,0:T(8,128)S(1)}) custom-call(f32[256,256]{1,0:T(8,128)S(1)} %get-tuple-element.58.mine_ref, f32[256,256]{1,0:T(8,128)S(1)} %collective-permute-done.6.other_ref, f32[256,256]{1,0:T(8,128)S(1)} %wanted.1.wanted_ref, f32[4,256,512]{2,1,0:T(8,128)S(1)} %get-tuple-element.61.field_ref, ...), custom_call_target="tpu_custom_call" | custom-call | flops 300000000 | bytes 7213056 | tf_op jit(solution)/shard_map/residual/pallas_call | solution.py:155
  36.8 1.6 %collective-permute-start.7 = (f32[8,128]{1,0:T(8,128)S(1)}, f32[8,128]{1,0:T(8,128)S(1)}, u32[]{:S(2)}, u32[]{:S(2)}) collective-permute-start(f32[8,128]{1,0:T(8,128)S(1)} %get-tuple-element.66), channel_id=1, source_target_pairs={{0,8},{1,9},{2,10},{3,11},{4,12},{5,13},{6,14},{7,15},{8,0},{9,1},... | collective-permute-start | bytes 12296 | tf_op jit(solution)/shard_map/ppermute | solution.py:459
  38.4 2.3 %adjoint.4 = (f32[2,256,128]{2,1,0:T(8,128)S(1)}, f32[2,256,128]{2,1,0:T(8,128)S(1)}) custom-call(f32[4,2,128]{2,1,0:T(2,128)S(1)} %convert_select_fusion.info_ref, f32[256,256]{1,0:T(8,128)S(1)} %get-tuple-element.62.residual_ref, f32[4,256,512]{2,1,0:T(8,128)S(1)} %get-tuple-element.61.field_ref, f32[128,128]{1,0:T(8,128)S(1)} %copy-done.3, ...), custom_call_target="tpu_custom_call" | custom-call | flops 1500000000 | bytes 7024640 | tf_op jit(solution)/shard_map/adjoint/pallas_call | solution.py:155
  40.8 1.3 %collective-permute-start.8 = (f32[8,128]{1,0:T(8,128)S(1)}, f32[8,128]{1,0:T(8,128)S(1)}, u32[]{:S(2)}, u32[]{:S(2)}) collective-permute-start(f32[8,128]{1,0:T(8,128)S(1)} %add.17), channel_id=1, source_target_pairs={{0,2},{1,3},{2,0},{3,1},{4,6},{5,7},{6,4},{7,5},{8,10},{9,11},{10,... | collective-permute-start | bytes 12296 | tf_op jit(solution)/shard_map/ppermute | solution.py:459
  42.1 2.3 %adjoint.5 = (f32[2,256,128]{2,1,0:T(8,128)S(1)}, f32[2,256,128]{2,1,0:T(8,128)S(1)}) custom-call(f32[4,2,128]{2,1,0:T(2,128)S(1)} %collective-permute-done.near_ref.info_ref, f32[256,256]{1,0:T(8,128)S(1)} %get-tuple-element.62.residual_ref, f32[12,256,512]{2,1,0:T(8,128)S(1)} %get-tuple-element.63.field_ref, f32[128,128]{1,0:T(8,128)S(1)} %copy-done.3, ...), custom_call_target="tpu_custom_call" | custom-call | flops 1500000000 | bytes 11735040 | tf_op jit(solution)/shard_map/adjoint/pallas_call | solution.py:155
  44.4 0.0 collective-permute-done.8
  44.4 1.7 %collective-permute-start.9 = (f32[8,128]{1,0:T(8,128)S(1)}, f32[8,128]{1,0:T(8,128)S(1)}, u32[]{:S(2)}, u32[]{:S(2)}) collective-permute-start(f32[8,128]{1,0:T(8,128)S(1)} %add.18), channel_id=1, source_target_pairs={{0,24},{1,25},{2,26},{3,27},{4,28},{5,29},{6,30},{7,31},{8,16},{9,... | collective-permute-start | bytes 12296 | tf_op jit(solution)/shard_map/ppermute | solution.py:459
  46.1 2.4 %adjoint.6 = (f32[2,256,128]{2,1,0:T(8,128)S(1)}, f32[2,256,128]{2,1,0:T(8,128)S(1)}) custom-call(f32[8,2,128]{2,1,0:T(2,128)S(1)} %collective-permute-done.1.far_ref.info_ref, f32[256,256]{1,0:T(8,128)S(1)} %get-tuple-element.62.residual_ref, f32[12,256,512]{2,1,0:T(8,128)S(1)} %get-tuple-element.63.field_ref, f32[128,128]{1,0:T(8,128)S(1)} %copy-done.3, ...), custom_call_target="tpu_custom_call" | custom-call | flops 1500000000 | bytes 11739136 | tf_op jit(solution)/shard_map/adjoint/pallas_call | solution.py:155
  48.5 1.7 %collective-permute-start.10 = (f32[8,128]{1,0:T(8,128)S(1)}, f32[8,128]{1,0:T(8,128)S(1)}, u32[]{:S(2)}, u32[]{:S(2)}) collective-permute-start(f32[8,128]{1,0:T(8,128)S(1)} %add.19), channel_id=1, source_target_pairs={{0,6},{1,7},{2,4},{3,5},{4,2},{5,3},{6,0},{7,1},{8,14},{9,15},{10,... | collective-permute-start | bytes 12296 | tf_op jit(solution)/shard_map/ppermute | solution.py:459
  50.1 3.4 %adjoint.7.mine_ref = f32[256,256]{1,0:T(8,128)S(1)} custom-call(f32[8,2,128]{2,1,0:T(2,128)S(1)} %collective-permute-done.1.far_ref.info_ref, f32[256,256]{1,0:T(8,128)S(1)} %get-tuple-element.62.residual_ref, f32[12,256,512]{2,1,0:T(8,128)S(1)} %get-tuple-element.63.field_ref, f32[128,128]{1,0:T(8,128)S(1)} %copy-done.3, ...), custom_call_target="tpu_custom_call" | custom-call | flops 1500000000 | bytes 11476992 | tf_op jit(solution)/shard_map/adjoint/pallas_call | solution.py:155
  53.6 0.0 collective-permute-done.10
  53.6 0.3 lines.1
  53.9 1.9 %collective-permute-start.11 = (f32[64,256]{1,0:T(8,128)S(1)}, f32[64,256]{1,0:T(8,128)S(1)}, u32[]{:S(2)}, u32[]{:S(2)}) collective-permute-start(f32[64,256]{1,0:T(8,128)S(1)} %get-tuple-element.82), channel_id=1, source_target_pairs={{0,8},{1,9},{2,10},{3,11},{4,12},{5,13},{6,14},{7,15},{8,16},{9,17... | collective-permute-start | bytes 196616 | tf_op jit(solution)/shard_map/ppermute | solution.py:445
  55.8 1.3 %collective-permute-done.11.rim_ref = f32[64,256]{1,0:T(8,128)S(1)} collective-permute-done((f32[64,256]{1,0:T(8,128)S(1)}, f32[64,256]{1,0:T(8,128)S(1)}, u32[]{:S(2)}, u32[]{:S(2)}) %collective-permute-start.11) | collective-permute-done | bytes 65568 | tf_op jit(solution)/shard_map/ppermute | solution.py:445
  57.1 2.6 %collective-permute-start.12 = (f32[136,256]{1,0:T(8,128)S(1)}, f32[136,256]{1,0:T(8,128)S(1)}, u32[]{:S(2)}, u32[]{:S(2)}) collective-permute-start(f32[136,256]{1,0:T(8,128)S(1)} %rim.1.mine_ref), channel_id=1, source_target_pairs={{0,32},{32,0},{64,96},{96,64},{128,160},{160,128},{192,224},{224,1... | collective-permute-start | bytes 417800 | tf_op jit(solution)/shard_map/ppermute | solution.py:419
  59.7 1.0 %collective-permute-done.12.other_ref = f32[136,256]{1,0:T(8,128)S(1)} collective-permute-done((f32[136,256]{1,0:T(8,128)S(1)}, f32[136,256]{1,0:T(8,128)S(1)}, u32[]{:S(2)}, u32[]{:S(2)}) %collective-permute-start.12) | collective-permute-done | bytes 139296 | tf_op jit(solution)/shard_map/ppermute | solution.py:419
  60.7 0.4 pixels.1
  61.1 3.4 %collective-permute-start.13 = (f32[72,128]{1,0:T(8,128)S(1)}, f32[72,128]{1,0:T(8,128)S(1)}, u32[]{:S(2)}, u32[]{:S(2)}) collective-permute-start(f32[72,128]{1,0:T(8,128)S(1)} %get-tuple-element.85.before_ref), channel_id=1, source_target_pairs={{1,0},{2,1},{3,2},{4,3},{5,4},{6,5},{7,6},{9,8},{10,9},{11,10},{12... | collective-permute-start | bytes 110600 | tf_op jit(solution)/shard_map/ppermute | solution.py:445
  64.5 1.0 %collective-permute-done.13.mine_ref = f32[72,128]{1,0:T(8,128)S(1)} collective-permute-done((f32[72,128]{1,0:T(8,128)S(1)}, f32[72,128]{1,0:T(8,128)S(1)}, u32[]{:S(2)}, u32[]{:S(2)}) %collective-permute-start.13) | collective-permute-done | bytes 36896 | tf_op jit(solution)/shard_map/ppermute | solution.py:445
  65.5 1.8 %collective-permute-start.14 = (f32[72,128]{1,0:T(8,128)S(1)}, f32[72,128]{1,0:T(8,128)S(1)}, u32[]{:S(2)}, u32[]{:S(2)}) collective-permute-start(f32[72,128]{1,0:T(8,128)S(1)} %collective-permute-done.13.mine_ref), channel_id=1, source_target_pairs={{0,32},{32,0},{64,96},{96,64},{128,160},{160,128},{192,224},{224,1... | collective-permute-start | bytes 110600 | tf_op jit(solution)/shard_map/ppermute | solution.py:419
  67.3 0.9 %collective-permute-done.14.other_ref = f32[72,128]{1,0:T(8,128)S(1)} collective-permute-done((f32[72,128]{1,0:T(8,128)S(1)}, f32[72,128]{1,0:T(8,128)S(1)}, u32[]{:S(2)}, u32[]{:S(2)}) %collective-permute-start.14) | collective-permute-done | bytes 36896 | tf_op jit(solution)/shard_map/ppermute | solution.py:419
  68.2 0.8 %join.1 = (f32[1,64,512]{2,1,0:T(8,128)}, f32[4]{0:T(128)}) custom-call(f32[64,512]{1,0:T(8,128)S(1)} %get-tuple-element.84.inner_ref, f32[72,128]{1,0:T(8,128)S(1)} %get-tuple-element.85.before_ref, f32[72,128]{1,0:T(8,128)S(1)} %collective-permute-done.13.mine_ref, f32[72,128]{1,0:T(8,128)S(1)} %collective-permute-done.14.other_ref), custom_call_target="tpu_custom_call" | custom-call | flops 32768 | bytes 372752 | tf_op jit(solution)/shard_map/join/pallas_call | solution.py:155
  (20 shorter events, 0.1 us)
Async XLA Ops:
  0.6 12.8 %copy-start.5 = (s32[4,2,128]{2,1,0:T(2,128)S(1)}, s32[4,2,128]{2,1,0:T(2,128)}, u32[]{:S(2)}) copy-start(s32[4,2,128]{2,1,0:T(2,128)} %param.10) | copy-start | bytes 12292
  0.6 12.8 %copy-start.6 = (f32[4]{0:T(128)S(1)}, f32[4]{0:T(128)}, u32[]{:S(2)}) copy-start(f32[4]{0:T(128)} %param.9) | copy-start | bytes 52
  1.7 6.4 %collective-permute-start.2 = (f32[64,512]{1,0:T(8,128)S(1)}, f32[64,512]{1,0:T(8,128)S(1)}, u32[]{:S(2)}, u32[]{:S(2)}) collective-permute-start(f32[64,512]{1,0:T(8,128)S(1)} %select_bitcast_fusion), channel_id=1, source_target_pairs={{0,8},{1,9},{2,10},{3,11},{4,12},{5,13},{6,14},{7,15},{8,16},{9,17... | collective-permute-start | bytes 393224 | tf_op jit(solution)/shard_map/ppermute | solution.py:445
  3.0 2.2 %copy-start = (bf16[124,64,256]{2,1,0:T(8,128)(2,1)S(1)}, bf16[124,64,256]{2,1,0:T(8,128)(2,1)}, u32[]{:S(2)}) copy-start(bf16[124,64,256]{2,1,0:T(8,128)(2,1)} %constant.25.clone.table_ref) | copy-start | bytes 12189700
  5.1 1.2 %copy-start.2 = (f32[1,512,512]{2,1,0:T(8,128)S(1)}, f32[1,512,512]{2,1,0:T(8,128)}, u32[]{:S(2)}) copy-start(f32[1,512,512]{2,1,0:T(8,128)} %tile_ref.1) | copy-start | bytes 3145732
  6.3 14.2 %copy-start.1 = (bf16[124,64,256]{2,1,0:T(8,128)(2,1)S(1)}, bf16[124,64,256]{2,1,0:T(8,128)(2,1)}, u32[]{:S(2)}) copy-start(bf16[124,64,256]{2,1,0:T(8,128)(2,1)} %constant.25.clone.table_ref) | copy-start | bytes 12189700
  6.9 16.8 %copy-start.3 = (f32[128,128]{1,0:T(8,128)S(1)}, f32[128,128]{1,0:T(8,128)}, u32[]{:S(2)}) copy-start(f32[128,128]{1,0:T(8,128)} %gain_ref.11) | copy-start | bytes 196612
  8.0 3.7 %collective-permute-start.3 = (f32[64,512]{1,0:T(8,128)S(1)}, f32[64,512]{1,0:T(8,128)S(1)}, u32[]{:S(2)}, u32[]{:S(2)}) collective-permute-start(f32[64,512]{1,0:T(8,128)S(1)} %collective-permute-done.2.mine_ref), channel_id=1, source_target_pairs={{0,32},{32,0},{64,96},{96,64},{128,160},{160,128},{192,224},{224,1... | collective-permute-start | bytes 393224 | tf_op jit(solution)/shard_map/ppermute | solution.py:419
  12.1 8.7 %collective-permute-start.4 = (f32[128,128]{1,0:T(8,128)S(1)}, f32[128,128]{1,0:T(8,128)S(1)}, u32[]{:S(2)}, u32[]{:S(2)}) collective-permute-start(f32[128,128]{1,0:T(8,128)S(1)} %get-tuple-element.51), channel_id=1, source_target_pairs={{0,1},{1,2},{2,3},{3,4},{4,5},{5,6},{6,7},{8,9},{9,10},{10,11},{11... | collective-permute-start | bytes 196616 | tf_op jit(solution)/shard_map/ppermute | solution.py:445
  13.5 9.3 %collective-permute-start = (f32[4,2,128]{2,1,0:T(2,128)S(1)}, f32[4,2,128]{2,1,0:T(2,128)S(1)}, u32[]{:S(2)}, u32[]{:S(2)}) collective-permute-start(f32[4,2,128]{2,1,0:T(2,128)S(1)} %convert_select_fusion.info_ref), channel_id=1, source_target_pairs={{0,193},{1,64},{2,195},{3,66},{4,197},{5,68},{6,199},{7,70},{8,201... | collective-permute-start | bytes 12296 | tf_op jit(solution)/shard_map/ppermute | solution.py:429
  20.9 2.8 %collective-permute-start.5 = (f32[128,128]{1,0:T(8,128)S(1)}, f32[128,128]{1,0:T(8,128)S(1)}, u32[]{:S(2)}, u32[]{:S(2)}) collective-permute-start(f32[128,128]{1,0:T(8,128)S(1)} %collective-permute-done.4.mine_ref), channel_id=1, source_target_pairs={{0,32},{32,0},{64,96},{96,64},{128,160},{160,128},{192,224},{224,1... | collective-permute-start | bytes 196616 | tf_op jit(solution)/shard_map/ppermute | solution.py:419
  22.8 4.4 %collective-permute-start.1 = (f32[8,2,128]{2,1,0:T(2,128)S(1)}, f32[8,2,128]{2,1,0:T(2,128)S(1)}, u32[]{:S(2)}, u32[]{:S(2)}) collective-permute-start(f32[8,2,128]{2,1,0:T(2,128)S(1)} %pad_maximum_fusion), channel_id=1, source_target_pairs={{0,65},{1,192},{2,67},{3,194},{4,69},{5,196},{6,71},{7,198},{8,73}... | collective-permute-start | bytes 24584 | tf_op jit(solution)/shard_map/ppermute | solution.py:429
  27.3 7.5 %copy-start.4 = (f32[1,512,512]{2,1,0:T(8,128)S(1)}, f32[1,512,512]{2,1,0:T(8,128)}, u32[]{:S(2)}) copy-start(f32[1,512,512]{2,1,0:T(8,128)} %target_ref.1) | copy-start | bytes 3145732
  32.5 3.5 %collective-permute-start.6 = (f32[256,256]{1,0:T(8,128)S(1)}, f32[256,256]{1,0:T(8,128)S(1)}, u32[]{:S(2)}, u32[]{:S(2)}) collective-permute-start(f32[256,256]{1,0:T(8,128)S(1)} %get-tuple-element.58.mine_ref), channel_id=1, source_target_pairs={{0,32},{32,0},{64,96},{96,64},{128,160},{160,128},{192,224},{224,1... | collective-permute-start | bytes 786440 | tf_op jit(solution)/shard_map/ppermute | solution.py:419
  36.8 3.9 %collective-permute-start.7 = (f32[8,128]{1,0:T(8,128)S(1)}, f32[8,128]{1,0:T(8,128)S(1)}, u32[]{:S(2)}, u32[]{:S(2)}) collective-permute-start(f32[8,128]{1,0:T(8,128)S(1)} %get-tuple-element.66), channel_id=1, source_target_pairs={{0,8},{1,9},{2,10},{3,11},{4,12},{5,13},{6,14},{7,15},{8,0},{9,1},... | collective-permute-start | bytes 12296 | tf_op jit(solution)/shard_map/ppermute | solution.py:459
  40.8 3.6 %collective-permute-start.8 = (f32[8,128]{1,0:T(8,128)S(1)}, f32[8,128]{1,0:T(8,128)S(1)}, u32[]{:S(2)}, u32[]{:S(2)}) collective-permute-start(f32[8,128]{1,0:T(8,128)S(1)} %add.17), channel_id=1, source_target_pairs={{0,2},{1,3},{2,0},{3,1},{4,6},{5,7},{6,4},{7,5},{8,10},{9,11},{10,... | collective-permute-start | bytes 12296 | tf_op jit(solution)/shard_map/ppermute | solution.py:459
  44.4 4.1 %collective-permute-start.9 = (f32[8,128]{1,0:T(8,128)S(1)}, f32[8,128]{1,0:T(8,128)S(1)}, u32[]{:S(2)}, u32[]{:S(2)}) collective-permute-start(f32[8,128]{1,0:T(8,128)S(1)} %add.18), channel_id=1, source_target_pairs={{0,24},{1,25},{2,26},{3,27},{4,28},{5,29},{6,30},{7,31},{8,16},{9,... | collective-permute-start | bytes 12296 | tf_op jit(solution)/shard_map/ppermute | solution.py:459
  48.5 5.1 %collective-permute-start.10 = (f32[8,128]{1,0:T(8,128)S(1)}, f32[8,128]{1,0:T(8,128)S(1)}, u32[]{:S(2)}, u32[]{:S(2)}) collective-permute-start(f32[8,128]{1,0:T(8,128)S(1)} %add.19), channel_id=1, source_target_pairs={{0,6},{1,7},{2,4},{3,5},{4,2},{5,3},{6,0},{7,1},{8,14},{9,15},{10,... | collective-permute-start | bytes 12296 | tf_op jit(solution)/shard_map/ppermute | solution.py:459
  53.9 3.2 %collective-permute-start.11 = (f32[64,256]{1,0:T(8,128)S(1)}, f32[64,256]{1,0:T(8,128)S(1)}, u32[]{:S(2)}, u32[]{:S(2)}) collective-permute-start(f32[64,256]{1,0:T(8,128)S(1)} %get-tuple-element.82), channel_id=1, source_target_pairs={{0,8},{1,9},{2,10},{3,11},{4,12},{5,13},{6,14},{7,15},{8,16},{9,17... | collective-permute-start | bytes 196616 | tf_op jit(solution)/shard_map/ppermute | solution.py:445
  57.1 3.6 %collective-permute-start.12 = (f32[136,256]{1,0:T(8,128)S(1)}, f32[136,256]{1,0:T(8,128)S(1)}, u32[]{:S(2)}, u32[]{:S(2)}) collective-permute-start(f32[136,256]{1,0:T(8,128)S(1)} %rim.1.mine_ref), channel_id=1, source_target_pairs={{0,32},{32,0},{64,96},{96,64},{128,160},{160,128},{192,224},{224,1... | collective-permute-start | bytes 417800 | tf_op jit(solution)/shard_map/ppermute | solution.py:419
  61.1 4.4 %collective-permute-start.13 = (f32[72,128]{1,0:T(8,128)S(1)}, f32[72,128]{1,0:T(8,128)S(1)}, u32[]{:S(2)}, u32[]{:S(2)}) collective-permute-start(f32[72,128]{1,0:T(8,128)S(1)} %get-tuple-element.85.before_ref), channel_id=1, source_target_pairs={{1,0},{2,1},{3,2},{4,3},{5,4},{6,5},{7,6},{9,8},{10,9},{11,10},{12... | collective-permute-start | bytes 110600 | tf_op jit(solution)/shard_map/ppermute | solution.py:445
  65.5 2.7 %collective-permute-start.14 = (f32[72,128]{1,0:T(8,128)S(1)}, f32[72,128]{1,0:T(8,128)S(1)}, u32[]{:S(2)}, u32[]{:S(2)}) collective-permute-start(f32[72,128]{1,0:T(8,128)S(1)} %collective-permute-done.13.mine_ref), channel_id=1, source_target_pairs={{0,32},{32,0},{64,96},{96,64},{128,160},{160,128},{192,224},{224,1... | collective-permute-start | bytes 110600 | tf_op jit(solution)/shard_map/ppermute | solution.py:419

commit v5 on v4

--- a/solution.py
+++ b/solution.py
@@ -169,6 +169,11 @@
     return group // 2, group % 2
 
 
+def my_tile():
+    tile = lax.axis_index("tile")
+    return tile // TCOLS, lax.rem(tile, TCOLS)
+
+
 def own_kernel(tile_ref, table_ref, rows_ref, rims_ref):
     rows_ref[...] = product(wide(table_ref, "mid_t"), terms(tile_ref[0]))
     rims_ref[...] = stored(table_ref, "rims_t")
@@ -183,7 +188,10 @@
     _, core = my_place()
     first = core == 0
     mine, other = mine_ref[...], other_ref[...]
-    rim = jnp.concatenate([jnp.where(first, mine, other), jnp.where(first, other, mine)], axis=0)
+    row, _ = my_tile()
+    upper = jnp.where(row > 0, jnp.where(first, mine, other), 0.0)
+    lower = jnp.where(row < TROWS - 1, jnp.where(first, other, mine), 0.0)
+    rim = jnp.concatenate([upper, lower], axis=0)
     table = table_ref[...]
     rows = rows_ref[...] + product((table[:, :K], table[:, K:]), terms(rim))
     all_ref[...] = rows
@@ -257,8 +265,9 @@
     _, core = my_place()
     first = core == 0
     mine, other = mine_ref[...], other_ref[...]
-    left = jnp.where(first, mine, other)
-    right = jnp.where(first, other, mine)
+    _, column = my_tile()
+    left = jnp.where(column > 0, jnp.where(first, mine, other), 0.0)
+    right = jnp.where(column < TCOLS - 1, jnp.where(first, other, mine), 0.0)
     rim = jnp.concatenate(
         [
             jnp.concatenate([left[:, :A], right[:, :A]], axis=1),
@@ -376,9 +385,10 @@
 
 def rim_kernel(lines_ref, rim_ref, energy_ref, out_ref):
     chip, core = my_place()
+    row, _ = my_tile()
     rim = rim_ref[...]
-    out_ref[:A] = lines_ref[:A] + jnp.where(chip == 0, rim, 0.0)
-    out_ref[A:K] = lines_ref[A:] + jnp.where(chip == 3, rim, 0.0)
+    out_ref[:A] = lines_ref[:A] + jnp.where((chip == 0) & (row > 0), rim, 0.0)
+    out_ref[A:K] = lines_ref[A:] + jnp.where((chip == 3) & (row < TROWS - 1), rim, 0.0)
     energy = energy_ref[...]
     out_ref[K:] = jnp.concatenate([jnp.where(core == at, energy, 0.0) for at in range(2)], axis=1)
 
@@ -402,14 +412,15 @@
     _, core = my_place()
     first = core == 0
     mine, other = mine_ref[...], other_ref[...]
-    left = jnp.where(first, other[:A, :A], mine[:A, A:])
-    right = jnp.where(first, mine[:A, :A], other[:A, A:])
+    _, column = my_tile()
+    left = jnp.where(column > 0, jnp.where(first, other[:A, :A], mine[:A, A:]), 0.0)
+    right = jnp.where(column < TCOLS - 1, jnp.where(first, mine[:A, :A], other[:A, A:]), 0.0)
     inner = inner_ref[...]
     pad = jnp.zeros((A, A), F32)
     out_ref[0, :, :K] = inner[:, :K] + jnp.concatenate([left, pad], axis=1)
     out_ref[0, :, K : PIX - K] = inner[:, K : PIX - K]
     out_ref[0, :, PIX - K :] = inner[:, PIX - K :] + jnp.concatenate([pad, right], axis=1)
-    odd = lax.rem(lax.axis_index("tile"), 2)
+    odd = lax.rem(column, 2)
     total = before_ref[A : A + 1] + jnp.where(core == odd, mine[A : A + 1], other[A : A + 1])
     total = pltpu.roll(total, core * A, 1) * (16.0 / (TROWS * TCOLS * PIX * PIX))
     energy_ref[...] = total[0, :SOURCES]
@@ -431,17 +442,12 @@
 
 def tile_move(value, shift_of):
     pairs = []
-    for source in range(8):
-        shift = shift_of(source)
-        if shift is None:
-            continue
+    for source in range(2 * CHIPS):
+        down, right = shift_of(source)
         for row in range(TROWS):
             for column in range(TCOLS):
-                to_row, to_column = row + shift[0], column + shift[1]
-                if 0 <= to_row < TROWS and 0 <= to_column < TCOLS:
-                    pairs.append(
-                        (source * 32 + row * TCOLS + column, source * 32 + to_row * TCOLS + to_column)
-                    )
+                to = (row + down) % TROWS * TCOLS + (column + right) % TCOLS
+                pairs.append((source * 32 + row * TCOLS + column, source * 32 + to))
     return lax.ppermute(value, BOTH, pairs)
 
 
@@ -527,7 +533,7 @@
         "lines",
         100_000_000,
     )
-    from_rows = tile_move(rim, lambda source: {0: (1, 0), 3: (-1, 0)}.get(source // 2))
+    from_rows = tile_move(rim, lambda source: (1, 0) if source < CHIPS else (-1, 0))
     (mine,) = call(rim_kernel, [(K + 8, W)], [lines, from_rows, energies], "rim", K * K)
     other = swap_cores(mine)
     inner, side = call(

time: 70.3 us -> 66.7 us (0.949); the launches traced: 69 us -> 66.5 us
  starting transfers between devices: 33 us -> 26.3 us
  waiting for transfers between devices: 6.87 us -> 11.1 us
    ppermute x4, waiting for transfers between devices: 3.46 us -> 7.91 us  [tile_move(): return lax.ppermute(value, BOTH, pairs)]
    ppermute x5, starting transfers between devices: 11.2 us -> 7.83 us  [swap_cores(): return lax.ppermute(value, 'src', [(at, at ^ 1) for at in range(8)])]
    ppermute x2, starting transfers between devices: 7.73 us -> 5.21 us  [chip_swap(): return lax.ppermute(value, BOTH, pairs)]
    ppermute x4, starting transfers between devices: 6.21 us -> 5.37 us  [tile_swap(): lax.ppermute(value, 'tile', [(at, partner(at)) for at in range(TROWS * TC...]
  transfers between devices with their start and end apart: 15 -> 15, of which waited for: 8 -> 5; matrix products, arithmetic and copies ran while one was open for 0% -> 0% of each run, Pallas kernels for 23% -> 24%
where the time goes in v5:
time: 66.7 us; the launch traced here: 66.5 us
  starting transfers between devices  26.3 us (39%)
  Pallas kernels  23.7 us (36%)
  waiting for transfers between devices  11.1 us (17%)
  local copies, waits for them, and re-layouts  3.4 us (5%)
  other arithmetic  1.09 us (2%)
  between operations  0.89 us (1%)
    pallas_call x15, Pallas kernels, call(): pl.pallas_call(kernel, out_shape=shapes, in_specs=specs, out_specs=[pl.Bl...  23.7 us
    ppermute x4, waiting for transfers between devices, tile_move(): return lax.ppermute(value, BOTH, pairs)  7.91 us
    ppermute x4, starting transfers between devices, tile_move(): return lax.ppermute(value, BOTH, pairs)  7.86 us
    ppermute x5, starting transfers between devices, swap_cores(): return lax.ppermute(value, 'src', [(at, at ^ 1) for at in range(8)])  7.83 us
    ppermute x4, starting transfers between devices, tile_swap(): lax.ppermute(value, 'tile', [(at, partner(at)) for at in range(TROWS * TC...  5.37 us
    ppermute x2, starting transfers between devices, chip_swap(): return lax.ppermute(value, BOTH, pairs)  5.21 us
    unnamed x14, local copies, waits for them, and re-layouts  3.4 us
    ppermute x5, waiting for transfers between devices, swap_cores(): return lax.ppermute(value, 'src', [(at, at ^ 1) for at in range(8)])  3.19 us
  transfers between devices with their start and end apart: 15, of which 5 were waited for; matrix products, arithmetic and copies ran while one was open for 0% of the time, Pallas kernels for 24%

profile of v5, /device:TPU:1, one launch (start us, length us, event | category | flops | bytes accessed | tf_op | source)
XLA Modules:
  0.0 66.5 jit_solution(17078697547658114526)
XLA Ops:
  0.7 1.0 %select_bitcast_fusion = f32[64,512]{1,0:T(8,128)S(1)} fusion(f32[1,512,512]{2,1,0:T(8,128)} %tile_ref.1, pred[]{:T(512)S(6)} %eq.14), kind=kLoop, calls=%fused_computation | loop fusion | flops 32768 | bytes 393217 | tf_op jit(solution)/shard_map/jit(_where)/select_n | solution.py:474
  1.7 3.6 %collective-permute-start.2 = (f32[64,512]{1,0:T(8,128)S(1)}, f32[64,512]{1,0:T(8,128)S(1)}, u32[]{:S(2)}, u32[]{:S(2)}) collective-permute-start(f32[64,512]{1,0:T(8,128)S(1)} %select_bitcast_fusion), channel_id=1, source_target_pairs={{0,8},{1,9},{2,10},{3,11},{4,12},{5,13},{6,14},{7,15},{8,16},{9,17... | collective-permute-start | bytes 393224 | tf_op jit(solution)/shard_map/ppermute | solution.py:451
  5.3 2.1 %copy-done = bf16[124,64,256]{2,1,0:T(8,128)(2,1)S(1)} copy-done((bf16[124,64,256]{2,1,0:T(8,128)(2,1)S(1)}, bf16[124,64,256]{2,1,0:T(8,128)(2,1)}, u32[]{:S(2)}) %copy-start) | copy-done | bytes 4063256
  7.4 1.2 %copy-done.2 = f32[1,512,512]{2,1,0:T(8,128)S(1)} copy-done((f32[1,512,512]{2,1,0:T(8,128)S(1)}, f32[1,512,512]{2,1,0:T(8,128)}, u32[]{:S(2)}) %copy-start.2) | copy-done | bytes 1048600
  8.7 0.6 own.1
  9.3 0.0 copy-start.3
  9.3 0.0 collective-permute-done.2.mine_ref
  9.3 1.9 %collective-permute-start.3 = (f32[64,512]{1,0:T(8,128)S(1)}, f32[64,512]{1,0:T(8,128)S(1)}, u32[]{:S(2)}, u32[]{:S(2)}) collective-permute-start(f32[64,512]{1,0:T(8,128)S(1)} %collective-permute-done.2.mine_ref), channel_id=1, source_target_pairs={{0,32},{32,0},{64,96},{96,64},{128,160},{160,128},{192,224},{224,1... | collective-permute-start | bytes 393224 | tf_op jit(solution)/shard_map/ppermute | solution.py:430
  11.2 1.0 %collective-permute-done.3.other_ref = f32[64,512]{1,0:T(8,128)S(1)} collective-permute-done((f32[64,512]{1,0:T(8,128)S(1)}, f32[64,512]{1,0:T(8,128)S(1)}, u32[]{:S(2)}, u32[]{:S(2)}) %collective-permute-start.3) | collective-permute-done | bytes 131104 | tf_op jit(solution)/shard_map/ppermute | solution.py:430
  12.1 0.4 rows.1
  12.6 2.5 %collective-permute-start.4 = (f32[128,128]{1,0:T(8,128)S(1)}, f32[128,128]{1,0:T(8,128)S(1)}, u32[]{:S(2)}, u32[]{:S(2)}) collective-permute-start(f32[128,128]{1,0:T(8,128)S(1)} %get-tuple-element.51), channel_id=1, source_target_pairs={{0,1},{1,2},{2,3},{3,4},{4,5},{5,6},{6,7},{7,0},{8,9},{9,10},{10,1... | collective-permute-start | bytes 196616 | tf_op jit(solution)/shard_map/ppermute | solution.py:451
  15.1 0.1 convert_select_fusion.info_ref
  15.1 2.5 %collective-permute-start = (f32[4,2,128]{2,1,0:T(2,128)S(1)}, f32[4,2,128]{2,1,0:T(2,128)S(1)}, u32[]{:S(2)}, u32[]{:S(2)}) collective-permute-start(f32[4,2,128]{2,1,0:T(2,128)S(1)} %convert_select_fusion.info_ref), channel_id=1, source_target_pairs={{0,193},{1,64},{2,195},{3,66},{4,197},{5,68},{6,199},{7,70},{8,201... | collective-permute-start | bytes 12296 | tf_op jit(solution)/shard_map/ppermute | solution.py:440
  17.6 0.4 columns.1.basis_ref
  18.0 0.0 collective-permute-done.4.mine_ref
  18.1 1.7 %collective-permute-start.5 = (f32[128,128]{1,0:T(8,128)S(1)}, f32[128,128]{1,0:T(8,128)S(1)}, u32[]{:S(2)}, u32[]{:S(2)}) collective-permute-start(f32[128,128]{1,0:T(8,128)S(1)} %collective-permute-done.4.mine_ref), channel_id=1, source_target_pairs={{0,32},{32,0},{64,96},{96,64},{128,160},{160,128},{192,224},{224,1... | collective-permute-start | bytes 196616 | tf_op jit(solution)/shard_map/ppermute | solution.py:430
  19.8 0.0 collective-permute-done.near_ref.info_ref
  19.8 2.7 %collective-permute-start.1 = (f32[8,2,128]{2,1,0:T(2,128)S(1)}, f32[8,2,128]{2,1,0:T(2,128)S(1)}, u32[]{:S(2)}, u32[]{:S(2)}) collective-permute-start(f32[8,2,128]{2,1,0:T(2,128)S(1)} %pad_maximum_fusion), channel_id=1, source_target_pairs={{0,65},{1,192},{2,67},{3,194},{4,69},{5,196},{6,71},{7,198},{8,73}... | collective-permute-start | bytes 24584 | tf_op jit(solution)/shard_map/ppermute | solution.py:440
  22.5 0.0 collective-permute-done.5.other_ref
  22.5 3.1 %image.1 = (f32[4,256,512]{2,1,0:T(8,128)S(1)}, f32[256,256]{1,0:T(8,128)S(1)}, f32[2,256,128]{2,1,0:T(8,128)S(1)}, f32[2,256,128]{2,1,0:T(8,128)S(1)}) custom-call(f32[4,2,128]{2,1,0:T(2,128)S(1)} %convert_select_fusion.info_ref, f32[256,256]{1,0:T(8,128)S(1)} %columns.1.basis_ref, f32[128,128]{1,0:T(8,128)S(1)} %collective-permute-done.4.mine_ref, ...), custom_call_target="tpu_custom_call" | custom-call | flops 2000000000 | bytes 7409664 | tf_op jit(solution)/shard_map/image/pallas_call | solution.py:155
  25.6 0.0 collective-permute-done.1.far_ref.info_ref
  25.6 0.0 copy-start.4
  25.6 5.2 %others.1 = (f32[12,256,512]{2,1,0:T(8,128)S(1)}, f32[256,256]{1,0:T(8,128)S(1)}) custom-call(f32[4,2,128]{2,1,0:T(2,128)S(1)} %collective-permute-done.near_ref.info_ref, f32[8,2,128]{2,1,0:T(2,128)S(1)} %collective-permute-done.1.far_ref.info_ref, f32[128,128]{1,0:T(8,128)S(1)} %copy-done.3, bf16[124,64,256]{2,1,0:T(8,128)(2,1)S(1)} %copy-done.1, ...), custom_call_target="tpu_custom_call" | custom-call | flops 5000000000 | bytes 11481088 | tf_op jit(solution)/shard_map/others/pallas_call | solution.py:155
  30.8 1.0 %collective-permute-start.6 = (f32[256,256]{1,0:T(8,128)S(1)}, f32[256,256]{1,0:T(8,128)S(1)}, u32[]{:S(2)}, u32[]{:S(2)}) collective-permute-start(f32[256,256]{1,0:T(8,128)S(1)} %get-tuple-element.58.mine_ref), channel_id=1, source_target_pairs={{0,32},{32,0},{64,96},{96,64},{128,160},{160,128},{192,224},{224,1... | collective-permute-start | bytes 786440 | tf_op jit(solution)/shard_map/ppermute | solution.py:430
  31.8 1.3 %wanted.1.wanted_ref = f32[256,256]{1,0:T(8,128)S(1)} custom-call(f32[1,512,512]{2,1,0:T(8,128)S(1)} %copy-done.4, bf16[124,64,256]{2,1,0:T(8,128)(2,1)S(1)} %copy-done.1), custom_call_target="tpu_custom_call" | custom-call | flops 600000000 | bytes 5373952 | tf_op jit(solution)/shard_map/wanted/pallas_call | solution.py:155
  33.1 0.0 collective-permute-done.6.other_ref
  33.1 0.8 %residual.1 = (f32[256,256]{1,0:T(8,128)S(1)}, f32[8,128]{1,0:T(8,128)S(1)}) custom-call(f32[256,256]{1,0:T(8,128)S(1)} %get-tuple-element.58.mine_ref, f32[256,256]{1,0:T(8,128)S(1)} %collective-permute-done.6.other_ref, f32[256,256]{1,0:T(8,128)S(1)} %wanted.1.wanted_ref, f32[4,256,512]{2,1,0:T(8,128)S(1)} %get-tuple-element.61.field_ref, ...), custom_call_target="tpu_custom_call" | custom-call | flops 300000000 | bytes 7213056 | tf_op jit(solution)/shard_map/residual/pallas_call | solution.py:155
  34.0 0.8 %collective-permute-start.7 = (f32[8,128]{1,0:T(8,128)S(1)}, f32[8,128]{1,0:T(8,128)S(1)}, u32[]{:S(2)}, u32[]{:S(2)}) collective-permute-start(f32[8,128]{1,0:T(8,128)S(1)} %get-tuple-element.66), channel_id=1, source_target_pairs={{0,8},{1,9},{2,10},{3,11},{4,12},{5,13},{6,14},{7,15},{8,0},{9,1},... | collective-permute-start | bytes 12296 | tf_op jit(solution)/shard_map/ppermute | solution.py:465
  34.7 2.3 %adjoint.4 = (f32[2,256,128]{2,1,0:T(8,128)S(1)}, f32[2,256,128]{2,1,0:T(8,128)S(1)}) custom-call(f32[4,2,128]{2,1,0:T(2,128)S(1)} %convert_select_fusion.info_ref, f32[256,256]{1,0:T(8,128)S(1)} %get-tuple-element.62.residual_ref, f32[4,256,512]{2,1,0:T(8,128)S(1)} %get-tuple-element.61.field_ref, f32[128,128]{1,0:T(8,128)S(1)} %copy-done.3, ...), custom_call_target="tpu_custom_call" | custom-call | flops 1500000000 | bytes 7024640 | tf_op jit(solution)/shard_map/adjoint/pallas_call | solution.py:155
  37.0 0.0 collective-permute-done.7
  37.1 1.3 %collective-permute-start.8 = (f32[8,128]{1,0:T(8,128)S(1)}, f32[8,128]{1,0:T(8,128)S(1)}, u32[]{:S(2)}, u32[]{:S(2)}) collective-permute-start(f32[8,128]{1,0:T(8,128)S(1)} %add.17), channel_id=1, source_target_pairs={{0,2},{1,3},{2,0},{3,1},{4,6},{5,7},{6,4},{7,5},{8,10},{9,11},{10,... | collective-permute-start | bytes 12296 | tf_op jit(solution)/shard_map/ppermute | solution.py:465
  38.4 2.3 %adjoint.5 = (f32[2,256,128]{2,1,0:T(8,128)S(1)}, f32[2,256,128]{2,1,0:T(8,128)S(1)}) custom-call(f32[4,2,128]{2,1,0:T(2,128)S(1)} %collective-permute-done.near_ref.info_ref, f32[256,256]{1,0:T(8,128)S(1)} %get-tuple-element.62.residual_ref, f32[12,256,512]{2,1,0:T(8,128)S(1)} %get-tuple-element.63.field_ref, f32[128,128]{1,0:T(8,128)S(1)} %copy-done.3, ...), custom_call_target="tpu_custom_call" | custom-call | flops 1500000000 | bytes 11735040 | tf_op jit(solution)/shard_map/adjoint/pallas_call | solution.py:155
  40.7 0.0 collective-permute-done.8
  40.7 1.7 %collective-permute-start.9 = (f32[8,128]{1,0:T(8,128)S(1)}, f32[8,128]{1,0:T(8,128)S(1)}, u32[]{:S(2)}, u32[]{:S(2)}) collective-permute-start(f32[8,128]{1,0:T(8,128)S(1)} %add.18), channel_id=1, source_target_pairs={{0,24},{1,25},{2,26},{3,27},{4,28},{5,29},{6,30},{7,31},{8,16},{9,... | collective-permute-start | bytes 12296 | tf_op jit(solution)/shard_map/ppermute | solution.py:465
  42.4 2.4 %adjoint.6 = (f32[2,256,128]{2,1,0:T(8,128)S(1)}, f32[2,256,128]{2,1,0:T(8,128)S(1)}) custom-call(f32[8,2,128]{2,1,0:T(2,128)S(1)} %collective-permute-done.1.far_ref.info_ref, f32[256,256]{1,0:T(8,128)S(1)} %get-tuple-element.62.residual_ref, f32[12,256,512]{2,1,0:T(8,128)S(1)} %get-tuple-element.63.field_ref, f32[128,128]{1,0:T(8,128)S(1)} %copy-done.3, ...), custom_call_target="tpu_custom_call" | custom-call | flops 1500000000 | bytes 11739136 | tf_op jit(solution)/shard_map/adjoint/pallas_call | solution.py:155
  44.8 1.6 %collective-permute-start.10 = (f32[8,128]{1,0:T(8,128)S(1)}, f32[8,128]{1,0:T(8,128)S(1)}, u32[]{:S(2)}, u32[]{:S(2)}) collective-permute-start(f32[8,128]{1,0:T(8,128)S(1)} %add.19), channel_id=1, source_target_pairs={{0,6},{1,7},{2,4},{3,5},{4,2},{5,3},{6,0},{7,1},{8,14},{9,15},{10,... | collective-permute-start | bytes 12296 | tf_op jit(solution)/shard_map/ppermute | solution.py:465
  46.4 3.4 %adjoint.7.mine_ref = f32[256,256]{1,0:T(8,128)S(1)} custom-call(f32[8,2,128]{2,1,0:T(2,128)S(1)} %collective-permute-done.1.far_ref.info_ref, f32[256,256]{1,0:T(8,128)S(1)} %get-tuple-element.62.residual_ref, f32[12,256,512]{2,1,0:T(8,128)S(1)} %get-tuple-element.63.field_ref, f32[128,128]{1,0:T(8,128)S(1)} %copy-done.3, ...), custom_call_target="tpu_custom_call" | custom-call | flops 1500000000 | bytes 11476992 | tf_op jit(solution)/shard_map/adjoint/pallas_call | solution.py:155
  49.8 0.0 collective-permute-done.10
  49.9 0.3 lines.1
  50.1 0.1 collective-permute-start.11
  50.2 4.3 %collective-permute-done.11.rim_ref = f32[64,256]{1,0:T(8,128)S(1)} collective-permute-done((f32[64,256]{1,0:T(8,128)S(1)}, f32[64,256]{1,0:T(8,128)S(1)}, u32[]{:S(2)}, u32[]{:S(2)}) %collective-permute-start.11) | collective-permute-done | bytes 65568 | tf_op jit(solution)/shard_map/ppermute | solution.py:451
  54.6 3.3 %collective-permute-start.12 = (f32[136,256]{1,0:T(8,128)S(1)}, f32[136,256]{1,0:T(8,128)S(1)}, u32[]{:S(2)}, u32[]{:S(2)}) collective-permute-start(f32[136,256]{1,0:T(8,128)S(1)} %rim.1.mine_ref), channel_id=1, source_target_pairs={{0,32},{32,0},{64,96},{96,64},{128,160},{160,128},{192,224},{224,1... | collective-permute-start | bytes 417800 | tf_op jit(solution)/shard_map/ppermute | solution.py:430
  57.8 1.0 %collective-permute-done.12.other_ref = f32[136,256]{1,0:T(8,128)S(1)} collective-permute-done((f32[136,256]{1,0:T(8,128)S(1)}, f32[136,256]{1,0:T(8,128)S(1)}, u32[]{:S(2)}, u32[]{:S(2)}) %collective-permute-start.12) | collective-permute-done | bytes 139296 | tf_op jit(solution)/shard_map/ppermute | solution.py:430
  58.8 0.4 pixels.1
  59.2 1.6 %collective-permute-start.13 = (f32[72,128]{1,0:T(8,128)S(1)}, f32[72,128]{1,0:T(8,128)S(1)}, u32[]{:S(2)}, u32[]{:S(2)}) collective-permute-start(f32[72,128]{1,0:T(8,128)S(1)} %get-tuple-element.85.before_ref), channel_id=1, source_target_pairs={{0,7},{1,0},{2,1},{3,2},{4,3},{5,4},{6,5},{7,6},{8,15},{9,8},{10,9... | collective-permute-start | bytes 110600 | tf_op jit(solution)/shard_map/ppermute | solution.py:451
  60.9 3.6 %collective-permute-done.13.mine_ref = f32[72,128]{1,0:T(8,128)S(1)} collective-permute-done((f32[72,128]{1,0:T(8,128)S(1)}, f32[72,128]{1,0:T(8,128)S(1)}, u32[]{:S(2)}, u32[]{:S(2)}) %collective-permute-start.13) | collective-permute-done | bytes 36896 | tf_op jit(solution)/shard_map/ppermute | solution.py:451
  64.5 1.2 %collective-permute-done.14.other_ref = f32[72,128]{1,0:T(8,128)S(1)} collective-permute-done((f32[72,128]{1,0:T(8,128)S(1)}, f32[72,128]{1,0:T(8,128)S(1)}, u32[]{:S(2)}, u32[]{:S(2)}) %collective-permute-start.14) | collective-permute-done | bytes 36896 | tf_op jit(solution)/shard_map/ppermute | solution.py:430
  65.7 0.8 %join.1 = (f32[1,64,512]{2,1,0:T(8,128)}, f32[4]{0:T(128)}) custom-call(f32[64,512]{1,0:T(8,128)S(1)} %get-tuple-element.84.inner_ref, f32[72,128]{1,0:T(8,128)S(1)} %get-tuple-element.85.before_ref, f32[72,128]{1,0:T(8,128)S(1)} %collective-permute-done.13.mine_ref, f32[72,128]{1,0:T(8,128)S(1)} %collective-permute-done.14.other_ref), custom_call_target="tpu_custom_call" | custom-call | flops 32768 | bytes 372752 | tf_op jit(solution)/shard_map/join/pallas_call | solution.py:155
  (20 shorter events, 0.1 us)
Async XLA Ops:
  0.6 14.4 %copy-start.5 = (s32[4,2,128]{2,1,0:T(2,128)S(1)}, s32[4,2,128]{2,1,0:T(2,128)}, u32[]{:S(2)}) copy-start(s32[4,2,128]{2,1,0:T(2,128)} %param.10) | copy-start | bytes 12292
  0.6 14.4 %copy-start.6 = (f32[4]{0:T(128)S(1)}, f32[4]{0:T(128)}, u32[]{:S(2)}) copy-start(f32[4]{0:T(128)} %param.9) | copy-start | bytes 52
  1.7 7.6 %collective-permute-start.2 = (f32[64,512]{1,0:T(8,128)S(1)}, f32[64,512]{1,0:T(8,128)S(1)}, u32[]{:S(2)}, u32[]{:S(2)}) collective-permute-start(f32[64,512]{1,0:T(8,128)S(1)} %select_bitcast_fusion), channel_id=1, source_target_pairs={{0,8},{1,9},{2,10},{3,11},{4,12},{5,13},{6,14},{7,15},{8,16},{9,17... | collective-permute-start | bytes 393224 | tf_op jit(solution)/shard_map/ppermute | solution.py:451
  5.3 2.2 %copy-start = (bf16[124,64,256]{2,1,0:T(8,128)(2,1)S(1)}, bf16[124,64,256]{2,1,0:T(8,128)(2,1)}, u32[]{:S(2)}) copy-start(bf16[124,64,256]{2,1,0:T(8,128)(2,1)} %constant.25.clone.table_ref) | copy-start | bytes 12189700
  7.4 1.2 %copy-start.2 = (f32[1,512,512]{2,1,0:T(8,128)S(1)}, f32[1,512,512]{2,1,0:T(8,128)}, u32[]{:S(2)}) copy-start(f32[1,512,512]{2,1,0:T(8,128)} %tile_ref.1) | copy-start | bytes 3145732
  8.7 9.0 %copy-start.1 = (bf16[124,64,256]{2,1,0:T(8,128)(2,1)S(1)}, bf16[124,64,256]{2,1,0:T(8,128)(2,1)}, u32[]{:S(2)}) copy-start(bf16[124,64,256]{2,1,0:T(8,128)(2,1)} %constant.25.clone.table_ref) | copy-start | bytes 12189700
  9.3 13.2 %copy-start.3 = (f32[128,128]{1,0:T(8,128)S(1)}, f32[128,128]{1,0:T(8,128)}, u32[]{:S(2)}) copy-start(f32[128,128]{1,0:T(8,128)} %gain_ref.11) | copy-start | bytes 196612
  9.3 2.9 %collective-permute-start.3 = (f32[64,512]{1,0:T(8,128)S(1)}, f32[64,512]{1,0:T(8,128)S(1)}, u32[]{:S(2)}, u32[]{:S(2)}) collective-permute-start(f32[64,512]{1,0:T(8,128)S(1)} %collective-permute-done.2.mine_ref), channel_id=1, source_target_pairs={{0,32},{32,0},{64,96},{96,64},{128,160},{160,128},{192,224},{224,1... | collective-permute-start | bytes 393224 | tf_op jit(solution)/shard_map/ppermute | solution.py:430
  12.6 5.5 %collective-permute-start.4 = (f32[128,128]{1,0:T(8,128)S(1)}, f32[128,128]{1,0:T(8,128)S(1)}, u32[]{:S(2)}, u32[]{:S(2)}) collective-permute-start(f32[128,128]{1,0:T(8,128)S(1)} %get-tuple-element.51), channel_id=1, source_target_pairs={{0,1},{1,2},{2,3},{3,4},{4,5},{5,6},{6,7},{7,0},{8,9},{9,10},{10,1... | collective-permute-start | bytes 196616 | tf_op jit(solution)/shard_map/ppermute | solution.py:451
  15.1 4.6 %collective-permute-start = (f32[4,2,128]{2,1,0:T(2,128)S(1)}, f32[4,2,128]{2,1,0:T(2,128)S(1)}, u32[]{:S(2)}, u32[]{:S(2)}) collective-permute-start(f32[4,2,128]{2,1,0:T(2,128)S(1)} %convert_select_fusion.info_ref), channel_id=1, source_target_pairs={{0,193},{1,64},{2,195},{3,66},{4,197},{5,68},{6,199},{7,70},{8,201... | collective-permute-start | bytes 12296 | tf_op jit(solution)/shard_map/ppermute | solution.py:440
  18.1 4.4 %collective-permute-start.5 = (f32[128,128]{1,0:T(8,128)S(1)}, f32[128,128]{1,0:T(8,128)S(1)}, u32[]{:S(2)}, u32[]{:S(2)}) collective-permute-start(f32[128,128]{1,0:T(8,128)S(1)} %collective-permute-done.4.mine_ref), channel_id=1, source_target_pairs={{0,32},{32,0},{64,96},{96,64},{128,160},{160,128},{192,224},{224,1... | collective-permute-start | bytes 196616 | tf_op jit(solution)/shard_map/ppermute | solution.py:430
  19.8 5.8 %collective-permute-start.1 = (f32[8,2,128]{2,1,0:T(2,128)S(1)}, f32[8,2,128]{2,1,0:T(2,128)S(1)}, u32[]{:S(2)}, u32[]{:S(2)}) collective-permute-start(f32[8,2,128]{2,1,0:T(2,128)S(1)} %pad_maximum_fusion), channel_id=1, source_target_pairs={{0,65},{1,192},{2,67},{3,194},{4,69},{5,196},{6,71},{7,198},{8,73}... | collective-permute-start | bytes 24584 | tf_op jit(solution)/shard_map/ppermute | solution.py:440
  25.6 6.3 %copy-start.4 = (f32[1,512,512]{2,1,0:T(8,128)S(1)}, f32[1,512,512]{2,1,0:T(8,128)}, u32[]{:S(2)}) copy-start(f32[1,512,512]{2,1,0:T(8,128)} %target_ref.1) | copy-start | bytes 3145732
  30.8 2.3 %collective-permute-start.6 = (f32[256,256]{1,0:T(8,128)S(1)}, f32[256,256]{1,0:T(8,128)S(1)}, u32[]{:S(2)}, u32[]{:S(2)}) collective-permute-start(f32[256,256]{1,0:T(8,128)S(1)} %get-tuple-element.58.mine_ref), channel_id=1, source_target_pairs={{0,32},{32,0},{64,96},{96,64},{128,160},{160,128},{192,224},{224,1... | collective-permute-start | bytes 786440 | tf_op jit(solution)/shard_map/ppermute | solution.py:430
  34.0 3.1 %collective-permute-start.7 = (f32[8,128]{1,0:T(8,128)S(1)}, f32[8,128]{1,0:T(8,128)S(1)}, u32[]{:S(2)}, u32[]{:S(2)}) collective-permute-start(f32[8,128]{1,0:T(8,128)S(1)} %get-tuple-element.66), channel_id=1, source_target_pairs={{0,8},{1,9},{2,10},{3,11},{4,12},{5,13},{6,14},{7,15},{8,0},{9,1},... | collective-permute-start | bytes 12296 | tf_op jit(solution)/shard_map/ppermute | solution.py:465
  37.1 3.6 %collective-permute-start.8 = (f32[8,128]{1,0:T(8,128)S(1)}, f32[8,128]{1,0:T(8,128)S(1)}, u32[]{:S(2)}, u32[]{:S(2)}) collective-permute-start(f32[8,128]{1,0:T(8,128)S(1)} %add.17), channel_id=1, source_target_pairs={{0,2},{1,3},{2,0},{3,1},{4,6},{5,7},{6,4},{7,5},{8,10},{9,11},{10,... | collective-permute-start | bytes 12296 | tf_op jit(solution)/shard_map/ppermute | solution.py:465
  40.7 4.1 %collective-permute-start.9 = (f32[8,128]{1,0:T(8,128)S(1)}, f32[8,128]{1,0:T(8,128)S(1)}, u32[]{:S(2)}, u32[]{:S(2)}) collective-permute-start(f32[8,128]{1,0:T(8,128)S(1)} %add.18), channel_id=1, source_target_pairs={{0,24},{1,25},{2,26},{3,27},{4,28},{5,29},{6,30},{7,31},{8,16},{9,... | collective-permute-start | bytes 12296 | tf_op jit(solution)/shard_map/ppermute | solution.py:465
  44.8 5.0 %collective-permute-start.10 = (f32[8,128]{1,0:T(8,128)S(1)}, f32[8,128]{1,0:T(8,128)S(1)}, u32[]{:S(2)}, u32[]{:S(2)}) collective-permute-start(f32[8,128]{1,0:T(8,128)S(1)} %add.19), channel_id=1, source_target_pairs={{0,6},{1,7},{2,4},{3,5},{4,2},{5,3},{6,0},{7,1},{8,14},{9,15},{10,... | collective-permute-start | bytes 12296 | tf_op jit(solution)/shard_map/ppermute | solution.py:465
  50.1 4.4 %collective-permute-start.11 = (f32[64,256]{1,0:T(8,128)S(1)}, f32[64,256]{1,0:T(8,128)S(1)}, u32[]{:S(2)}, u32[]{:S(2)}) collective-permute-start(f32[64,256]{1,0:T(8,128)S(1)} %get-tuple-element.82), channel_id=1, source_target_pairs={{0,8},{1,9},{2,10},{3,11},{4,12},{5,13},{6,14},{7,15},{8,16},{9,17... | collective-permute-start | bytes 196616 | tf_op jit(solution)/shard_map/ppermute | solution.py:451
  54.6 4.3 %collective-permute-start.12 = (f32[136,256]{1,0:T(8,128)S(1)}, f32[136,256]{1,0:T(8,128)S(1)}, u32[]{:S(2)}, u32[]{:S(2)}) collective-permute-start(f32[136,256]{1,0:T(8,128)S(1)} %rim.1.mine_ref), channel_id=1, source_target_pairs={{0,32},{32,0},{64,96},{96,64},{128,160},{160,128},{192,224},{224,1... | collective-permute-start | bytes 417800 | tf_op jit(solution)/shard_map/ppermute | solution.py:430
  59.2 5.2 %collective-permute-start.13 = (f32[72,128]{1,0:T(8,128)S(1)}, f32[72,128]{1,0:T(8,128)S(1)}, u32[]{:S(2)}, u32[]{:S(2)}) collective-permute-start(f32[72,128]{1,0:T(8,128)S(1)} %get-tuple-element.85.before_ref), channel_id=1, source_target_pairs={{0,7},{1,0},{2,1},{3,2},{4,3},{5,4},{6,5},{7,6},{8,15},{9,8},{10,9... | collective-permute-start | bytes 110600 | tf_op jit(solution)/shard_map/ppermute | solution.py:451
  64.5 1.2 %collective-permute-start.14 = (f32[72,128]{1,0:T(8,128)S(1)}, f32[72,128]{1,0:T(8,128)S(1)}, u32[]{:S(2)}, u32[]{:S(2)}) collective-permute-start(f32[72,128]{1,0:T(8,128)S(1)} %collective-permute-done.13.mine_ref), channel_id=1, source_target_pairs={{0,32},{32,0},{64,96},{96,64},{128,160},{160,128},{192,224},{224,1... | collective-permute-start | bytes 110600 | tf_op jit(solution)/shard_map/ppermute | solution.py:430

commit v6 on v5

--- a/solution.py
+++ b/solution.py
@@ -82,13 +82,17 @@
     middle = basis[A : N - A]
     rims = np.concatenate([basis[:A], basis[N - A :]])
     sides = [two_terms(basis[:A].T), two_terms(basis[N - A :].T)]
-    return packed(
+    early = packed(
         {
             "mid": two_terms(middle),
             "mid_t": two_halves(middle.T),
             "rims": two_terms(rims),
             "rims_t": [np.concatenate(list(two_terms(rims.T)), axis=1)],
             "sides": [np.concatenate([term for pair in sides for term in pair], axis=1)],
+        }
+    )
+    late = packed(
+        {
             "coarse": two_halves(coarse),
             "coarse_t": two_terms(coarse.T),
             "fold": [fold],
@@ -98,9 +102,11 @@
             "gram": two_terms(spread.T @ spread),
         }
     )
-
-
-TABLES, SPOTS = make_tables()
+    return early, late
+
+
+(EARLY, EARLY_AT), (LATE, LATE_AT) = make_tables()
+SPOTS = EARLY_AT | LATE_AT
 
 
 def stored(ref, name, at=0):
@@ -199,7 +205,7 @@
     side_ref[...] = jnp.concatenate([side[:K], side[K:]], axis=1)
 
 
-def columns_kernel(rows_ref, table_ref, basis_ref):
+def columns_kernel(rows_ref, table_ref, _, basis_ref):
     basis_ref[...] = product(terms(rows_ref[...]), narrow(table_ref, "mid"))
 
 
@@ -256,6 +262,7 @@
     mine_ref,
     other_ref,
     gain_ref,
+    early_ref,
     table_ref,
     field_ref,
     total_ref,
@@ -275,7 +282,7 @@
         ],
         axis=0,
     )
-    basis = basis_ref[...] + product(terms(rim), narrow(table_ref, "rims"))
+    basis = basis_ref[...] + product(terms(rim), narrow(early_ref, "rims"))
     zero = jnp.zeros((K, K), F32)
     even = jnp.concatenate(
         [
@@ -332,6 +339,7 @@
     field_ref,
     gain_ref,
     table_ref,
+    early_ref,
     real_in,
     imag_in,
     *outs,
@@ -340,7 +348,7 @@
     first_field = SOURCES if chip else 0
     coarse_t = narrow(table_ref, "coarse_t")
     last = chip == CHIPS - 1
-    real_ref, imag_ref = outs[1:] if last else outs
+    real_ref, imag_ref = outs[2:] if last else outs
     residual = residual_ref[...]
     disc = disc_of(gain_ref[...])
     real_ref[...] = jnp.zeros((2, W, K), F32) if chip == 0 else real_in[...]
@@ -365,21 +373,17 @@
     if not last:
         return
     fold, fold_t = stored(table_ref, "fold"), stored(table_ref, "fold_t")
-
-    def folded(ref):
-        return exact_right(exact_left(fold, jnp.concatenate([ref[0], ref[1]], axis=1)), fold_t)
-
-    even, odd = folded(real_ref), folded(imag_ref)
-    outs[0][:K] = jnp.concatenate([even[:K, :K], -odd[:K, K:]], axis=1)
-    outs[0][K:] = jnp.concatenate([-odd[K:, :K], -even[K:, K:]], axis=1)
-
-
-def lines_kernel(mine_ref, table_ref, lines_ref, rim_ref):
-    chip, _ = my_place()
-    spectrum = terms(mine_ref[...])
-    lines = [table_ref[pl.ds(SPOTS["mid"][at][0] + 2 * chip, 2)].reshape(K, W) for at in range(2)]
+    real, imag = (
+        exact_left(fold, jnp.concatenate([ref[0], ref[1]], axis=1)) for ref in (real_ref, imag_ref)
+    )
+    cosines = exact_right(jnp.concatenate([real[:K], -imag[K:]], axis=0), fold_t[:, :K])
+    sines = exact_right(jnp.concatenate([-imag[:K], -real[K:]], axis=0), fold_t[:, K:])
+    spectrum = terms(jnp.concatenate([cosines, sines], axis=1))
+    lines_ref, rim_ref = outs[:2]
+    place, _ = my_place()
+    lines = [early_ref[pl.ds(SPOTS["mid"][at][0] + 2 * place, 2)].reshape(K, W) for at in range(2)]
     lines_ref[...] = product(lines, spectrum)
-    outer = [table_ref[SPOTS["rims"][at][0] + 1 - chip // 2] for at in range(2)]
+    outer = [early_ref[SPOTS["rims"][at][0] + 1 - place // 2] for at in range(2)]
     rim_ref[...] = product(outer, spectrum)
 
 
@@ -444,10 +448,14 @@
     pairs = []
     for source in range(2 * CHIPS):
         down, right = shift_of(source)
+        turns = shift_of(source ^ 1) == (-down, -right)
         for row in range(TROWS):
             for column in range(TCOLS):
-                to = (row + down) % TROWS * TCOLS + (column + right) % TCOLS
-                pairs.append((source * 32 + row * TCOLS + column, source * 32 + to))
+                to_row, to_column = row + down, column + right
+                inside = 0 <= to_row < TROWS and 0 <= to_column < TCOLS
+                to = to_row % TROWS * TCOLS + to_column % TCOLS
+                to = source * 32 + to if inside or not turns else (source ^ 1) * 32 + row * TCOLS + column
+                pairs.append((source * 32 + row * TCOLS + column, to))
     return lax.ppermute(value, BOTH, pairs)
 
 
@@ -473,7 +481,7 @@
     core = lax.axis_index("src") % 2
     edge = jnp.where(core == 0, mask_tiles[0, PIX - A :], mask_tiles[0, :A])
     mine = tile_move(edge, lambda source: (1, 0) if source % 2 == 0 else (-1, 0))
-    rows, rim_table = call(own_kernel, [(W, PIX), (W, W)], [mask_tiles, TABLES], "own", 400_000_000, bf16=(1,))
+    rows, rim_table = call(own_kernel, [(W, PIX), (W, W)], [mask_tiles, EARLY], "own", 400_000_000, bf16=(1,))
     rows, weights, freq_index = tied(rows, weights, freq_index)
     mine, rows = tied(mine, rows)
     other = swap_cores(mine)
@@ -484,14 +492,14 @@
         rows_kernel, [(W, PIX), (K, K)], [rows, mine, other, rim_table], "rows", 100_000_000
     )
     my_side = tile_move(side, lambda source: (0, 1) if source % 2 == 0 else (0, -1))
-    (basis,) = call(columns_kernel, [(W, W)], [rows, TABLES], "columns", 200_000_000)
+    (basis,) = call(columns_kernel, [(W, W)], [rows, EARLY, LATE], "columns", 200_000_000)
     far = chip_swap(jnp.concatenate([info, near]), 0)
     my_side, basis = tied(my_side, basis)
     other_side = swap_cores(my_side)
     own_field, total, real, imag = call(
         image_kernel,
         [(SOURCES, W, 2 * W), (W, W), (2, W, K), (2, W, K)],
-        [info, basis, my_side, other_side, pupil_gain, TABLES],
+        [info, basis, my_side, other_side, pupil_gain, EARLY, LATE],
         "image",
         2_000_000_000,
         smem=(0,),
@@ -499,16 +507,16 @@
     field, mine = call(
         others_kernel,
         [((CHIPS - 1) * SOURCES, W, 2 * W), (W, W)],
-        [near, far, pupil_gain, TABLES, real, imag, total],
+        [near, far, pupil_gain, LATE, real, imag, total],
         "others",
         5_000_000_000,
         smem=(0, 1),
     )
     other = swap_cores(mine)
-    (wanted,) = call(wanted_kernel, [(W, W)], [target, TABLES], "wanted", 600_000_000)
+    (wanted,) = call(wanted_kernel, [(W, W)], [target, LATE], "wanted", 600_000_000)
     other, wanted = tied(other, wanted)
     residual, energies = call(
-        residual_kernel, [(W, W), (8, K)], [mine, other, wanted, own_field, TABLES], "residual", 300_000_000
+        residual_kernel, [(W, W), (8, K)], [mine, other, wanted, own_field, LATE], "residual", 300_000_000
     )
     plane = pltpu.VMEM((2, W, K), F32)
     planes = (jnp.zeros((8, K), F32),) * 2
@@ -517,8 +525,8 @@
         last = chip == CHIPS - 1
         outs = call(
             functools.partial(adjoint_kernel, chip),
-            [(W, W)] if last else [(2, W, K), (2, W, K)],
-            [(info, near, far, far)[chip], residual, field if chip else own_field, pupil_gain, TABLES, *planes],
+            [(K, W), (A, W)] if last else [(2, W, K), (2, W, K)],
+            [(info, near, far, far)[chip], residual, field if chip else own_field, pupil_gain, LATE, EARLY, *planes],
             "adjoint",
             1_500_000_000,
             scratch=(plane, plane) if last else (),
@@ -526,20 +534,14 @@
         )
         planes = outs
         *planes, energies = tied(*planes, energies + arrived)
-    lines, rim = call(
-        lines_kernel,
-        [(K, W), (A, W)],
-        [planes[0], TABLES],
-        "lines",
-        100_000_000,
-    )
+    lines, rim = planes
     from_rows = tile_move(rim, lambda source: (1, 0) if source < CHIPS else (-1, 0))
     (mine,) = call(rim_kernel, [(K + 8, W)], [lines, from_rows, energies], "rim", K * K)
     other = swap_cores(mine)
     inner, side = call(
         pixels_kernel,
         [(A, PIX), (A + 8, K)],
-        [mine, other, TABLES],
+        [mine, other, EARLY],
         "pixels",
         100_000_000,
     )

time: 66.7 us -> 65.1 us (0.976)
  waiting for transfers between devices: 11.1 us -> 8.73 us
    ppermute x4, waiting for transfers between devices: 7.91 us -> 4.99 us  [tile_move(): return lax.ppermute(value, BOTH, pairs)]
    ppermute x4, starting transfers between devices: 7.86 us -> 5.25 us  [tile_move(): return lax.ppermute(value, BOTH, pairs)]
    ppermute x4, starting transfers between devices: 5.37 us -> 6.65 us  [tile_swap(): lax.ppermute(value, 'tile', [(at, partner(at)) for at in range(TROWS * TC...]
    ppermute x2, starting transfers between devices: 5.21 us -> 6.44 us  [chip_swap(): return lax.ppermute(value, BOTH, pairs)]
    unnamed x14 -> x18, local copies, waits for them, and re-layouts: 3.4 us -> 3.98 us
    pallas_call x15 -> x14, Pallas kernels: 23.7 us -> 23.3 us  [call(): pl.pallas_call(kernel, out_shape=shapes, in_specs=specs, out_specs=[pl.Bl...]
  transfers between devices with their start and end apart: 15 -> 15, of which waited for: 5 -> 7; matrix products, arithmetic and copies ran while one was open for 0% -> 0% of each run, Pallas kernels for 24% -> 24%
where the time goes in v6:
time: 65.1 us; the launch traced here: 64.9 us
  starting transfers between devices  26.8 us (41%)
  Pallas kernels  23.3 us (36%)
  waiting for transfers between devices  8.73 us (13%)
  local copies, waits for them, and re-layouts  3.98 us (6%)
  other arithmetic  1.24 us (2%)
  between operations  0.86 us (1%)
    pallas_call x14, Pallas kernels, call(): pl.pallas_call(kernel, out_shape=shapes, in_specs=specs, out_specs=[pl.Bl...  23.3 us
    ppermute x5, starting transfers between devices, swap_cores(): return lax.ppermute(value, 'src', [(at, at ^ 1) for at in range(8)])  8.47 us
    ppermute x4, starting transfers between devices, tile_swap(): lax.ppermute(value, 'tile', [(at, partner(at)) for at in range(TROWS * TC...  6.65 us
    ppermute x2, starting transfers between devices, chip_swap(): return lax.ppermute(value, BOTH, pairs)  6.44 us
    ppermute x4, starting transfers between devices, tile_move(): return lax.ppermute(value, BOTH, pairs)  5.25 us
    ppermute x4, waiting for transfers between devices, tile_move(): return lax.ppermute(value, BOTH, pairs)  4.99 us
    unnamed x18, local copies, waits for them, and re-layouts  3.98 us
    ppermute x5, waiting for transfers between devices, swap_cores(): return lax.ppermute(value, 'src', [(at, at ^ 1) for at in range(8)])  3.29 us
  transfers between devices with their start and end apart: 15, of which 7 were waited for; matrix products, arithmetic and copies ran while one was open for 0% of the time, Pallas kernels for 24%

profile of v6, /device:TPU:1, one launch (start us, length us, event | category | flops | bytes accessed | tf_op | source)
XLA Modules:
  0.0 64.9 jit_solution(16763692650914541534)
XLA Ops:
  0.6 0.0 copy-start
  0.7 1.1 %select_bitcast_fusion = f32[64,512]{1,0:T(8,128)S(1)} fusion(f32[1,512,512]{2,1,0:T(8,128)} %tile_ref.1, pred[]{:T(512)S(6)} %eq.14), kind=kLoop, calls=%fused_computation | loop fusion | flops 32768 | bytes 393217 | tf_op jit(solution)/shard_map/jit(_where)/select_n | solution.py:482
  1.8 3.3 %collective-permute-start.2 = (f32[64,512]{1,0:T(8,128)S(1)}, f32[64,512]{1,0:T(8,128)S(1)}, u32[]{:S(2)}, u32[]{:S(2)}) collective-permute-start(f32[64,512]{1,0:T(8,128)S(1)} %select_bitcast_fusion), channel_id=1, source_target_pairs={{0,8},{1,9},{2,10},{3,11},{4,12},{5,13},{6,14},{7,15},{8,16},{9,17... | collective-permute-start | bytes 393224 | tf_op jit(solution)/shard_map/ppermute | solution.py:459
  5.1 1.4 %copy-done.1 = bf16[44,64,256]{2,1,0:T(8,128)(2,1)S(1)} copy-done((bf16[44,64,256]{2,1,0:T(8,128)(2,1)S(1)}, bf16[44,64,256]{2,1,0:T(8,128)(2,1)}, u32[]{:S(2)}) %copy-start.1) | copy-done | bytes 1441816
  6.4 1.2 %copy-done.4 = f32[1,512,512]{2,1,0:T(8,128)S(1)} copy-done((f32[1,512,512]{2,1,0:T(8,128)S(1)}, f32[1,512,512]{2,1,0:T(8,128)}, u32[]{:S(2)}) %copy-start.4) | copy-done | bytes 1048600
  7.6 0.6 own.1
  8.2 0.0 collective-permute-done.2.mine_ref
  8.2 0.1 collective-permute-start.3
  8.4 1.3 %collective-permute-done.3.other_ref = f32[64,512]{1,0:T(8,128)S(1)} collective-permute-done((f32[64,512]{1,0:T(8,128)S(1)}, f32[64,512]{1,0:T(8,128)S(1)}, u32[]{:S(2)}, u32[]{:S(2)}) %collective-permute-start.3) | collective-permute-done | bytes 131104 | tf_op jit(solution)/shard_map/ppermute | solution.py:434
  9.7 0.4 rows.1
  10.1 0.2 collective-permute-start.4
  10.4 0.1 convert_select_fusion.info_ref
  10.4 5.7 %collective-permute-start = (f32[4,2,128]{2,1,0:T(2,128)S(1)}, f32[4,2,128]{2,1,0:T(2,128)S(1)}, u32[]{:S(2)}, u32[]{:S(2)}) collective-permute-start(f32[4,2,128]{2,1,0:T(2,128)S(1)} %convert_select_fusion.info_ref), channel_id=1, source_target_pairs={{0,193},{1,64},{2,195},{3,66},{4,197},{5,68},{6,199},{7,70},{8,201... | collective-permute-start | bytes 12296 | tf_op jit(solution)/shard_map/ppermute | solution.py:444
  16.1 1.4 %copy-done.2 = bf16[44,64,256]{2,1,0:T(8,128)(2,1)S(1)} copy-done((bf16[44,64,256]{2,1,0:T(8,128)(2,1)S(1)}, bf16[44,64,256]{2,1,0:T(8,128)(2,1)}, u32[]{:S(2)}) %copy-start.2) | copy-done | bytes 1441816
  17.5 0.4 columns.1.basis_ref
  17.8 0.0 collective-permute-done.4.mine_ref
  17.8 1.9 %collective-permute-start.5 = (f32[128,128]{1,0:T(8,128)S(1)}, f32[128,128]{1,0:T(8,128)S(1)}, u32[]{:S(2)}, u32[]{:S(2)}) collective-permute-start(f32[128,128]{1,0:T(8,128)S(1)} %collective-permute-done.4.mine_ref), channel_id=1, source_target_pairs={{0,32},{32,0},{64,96},{96,64},{128,160},{160,128},{192,224},{224,1... | collective-permute-start | bytes 196616 | tf_op jit(solution)/shard_map/ppermute | solution.py:434
  19.8 0.0 collective-permute-done.near_ref.info_ref
  19.8 0.8 %collective-permute-start.1 = (f32[8,2,128]{2,1,0:T(2,128)S(1)}, f32[8,2,128]{2,1,0:T(2,128)S(1)}, u32[]{:S(2)}, u32[]{:S(2)}) collective-permute-start(f32[8,2,128]{2,1,0:T(2,128)S(1)} %pad_maximum_fusion), channel_id=1, source_target_pairs={{0,65},{1,192},{2,67},{3,194},{4,69},{5,196},{6,71},{7,198},{8,73}... | collective-permute-start | bytes 24584 | tf_op jit(solution)/shard_map/ppermute | solution.py:444
  20.6 0.1 collective-permute-done.5.other_ref
  20.7 3.1 %image.1 = (f32[4,256,512]{2,1,0:T(8,128)S(1)}, f32[256,256]{1,0:T(8,128)S(1)}, f32[2,256,128]{2,1,0:T(8,128)S(1)}, f32[2,256,128]{2,1,0:T(8,128)S(1)}) custom-call(f32[4,2,128]{2,1,0:T(2,128)S(1)} %convert_select_fusion.info_ref, f32[256,256]{1,0:T(8,128)S(1)} %columns.1.basis_ref, f32[128,128]{1,0:T(8,128)S(1)} %collective-permute-done.4.mine_ref, ...), custom_call_target="tpu_custom_call" | custom-call | flops 2000000000 | bytes 7409664 | tf_op jit(solution)/shard_map/image/pallas_call | solution.py:161
  23.7 0.4 collective-permute-done.1.far_ref.info_ref
  24.2 5.1 %others.1 = (f32[12,256,512]{2,1,0:T(8,128)S(1)}, f32[256,256]{1,0:T(8,128)S(1)}) custom-call(f32[4,2,128]{2,1,0:T(2,128)S(1)} %collective-permute-done.near_ref.info_ref, f32[8,2,128]{2,1,0:T(2,128)S(1)} %collective-permute-done.1.far_ref.info_ref, f32[128,128]{1,0:T(8,128)S(1)} %copy-done.5, bf16[80,64,256]{2,1,0:T(8,128)(2,1)S(1)} %copy-done, ...), custom_call_target="tpu_custom_call" | custom-call | flops 5000000000 | bytes 10039296 | tf_op jit(solution)/shard_map/others/pallas_call | solution.py:161
  29.3 1.3 %collective-permute-start.6 = (f32[256,256]{1,0:T(8,128)S(1)}, f32[256,256]{1,0:T(8,128)S(1)}, u32[]{:S(2)}, u32[]{:S(2)}) collective-permute-start(f32[256,256]{1,0:T(8,128)S(1)} %get-tuple-element.59.mine_ref), channel_id=1, source_target_pairs={{0,32},{32,0},{64,96},{96,64},{128,160},{160,128},{192,224},{224,1... | collective-permute-start | bytes 786440 | tf_op jit(solution)/shard_map/ppermute | solution.py:434
  30.5 1.3 %wanted.1.wanted_ref = f32[256,256]{1,0:T(8,128)S(1)} custom-call(f32[1,512,512]{2,1,0:T(8,128)S(1)} %copy-done.6, bf16[80,64,256]{2,1,0:T(8,128)(2,1)S(1)} %copy-done), custom_call_target="tpu_custom_call" | custom-call | flops 600000000 | bytes 3932160 | tf_op jit(solution)/shard_map/wanted/pallas_call | solution.py:161
  31.8 0.0 collective-permute-done.6.other_ref
  31.8 0.8 %residual.1 = (f32[256,256]{1,0:T(8,128)S(1)}, f32[8,128]{1,0:T(8,128)S(1)}) custom-call(f32[256,256]{1,0:T(8,128)S(1)} %get-tuple-element.59.mine_ref, f32[256,256]{1,0:T(8,128)S(1)} %collective-permute-done.6.other_ref, f32[256,256]{1,0:T(8,128)S(1)} %wanted.1.wanted_ref, f32[4,256,512]{2,1,0:T(8,128)S(1)} %get-tuple-element.62.field_ref, ...), custom_call_target="tpu_custom_call" | custom-call | flops 300000000 | bytes 5771264 | tf_op jit(solution)/shard_map/residual/pallas_call | solution.py:161
  32.6 1.7 %collective-permute-start.7 = (f32[8,128]{1,0:T(8,128)S(1)}, f32[8,128]{1,0:T(8,128)S(1)}, u32[]{:S(2)}, u32[]{:S(2)}) collective-permute-start(f32[8,128]{1,0:T(8,128)S(1)} %get-tuple-element.67), channel_id=1, source_target_pairs={{0,8},{1,9},{2,10},{3,11},{4,12},{5,13},{6,14},{7,15},{8,0},{9,1},... | collective-permute-start | bytes 12296 | tf_op jit(solution)/shard_map/ppermute | solution.py:473
  34.3 2.2 %adjoint.4 = (f32[2,256,128]{2,1,0:T(8,128)S(1)}, f32[2,256,128]{2,1,0:T(8,128)S(1)}) custom-call(f32[4,2,128]{2,1,0:T(2,128)S(1)} %convert_select_fusion.info_ref, f32[256,256]{1,0:T(8,128)S(1)} %get-tuple-element.63.residual_ref, f32[4,256,512]{2,1,0:T(8,128)S(1)} %get-tuple-element.62.field_ref, f32[128,128]{1,0:T(8,128)S(1)} %copy-done.5, ...), custom_call_target="tpu_custom_call" | custom-call | flops 1500000000 | bytes 7024640 | tf_op jit(solution)/shard_map/adjoint/pallas_call | solution.py:161
  36.6 1.3 %collective-permute-start.8 = (f32[8,128]{1,0:T(8,128)S(1)}, f32[8,128]{1,0:T(8,128)S(1)}, u32[]{:S(2)}, u32[]{:S(2)}) collective-permute-start(f32[8,128]{1,0:T(8,128)S(1)} %add.17), channel_id=1, source_target_pairs={{0,2},{1,3},{2,0},{3,1},{4,6},{5,7},{6,4},{7,5},{8,10},{9,11},{10,... | collective-permute-start | bytes 12296 | tf_op jit(solution)/shard_map/ppermute | solution.py:473
  37.9 2.2 %adjoint.5 = (f32[2,256,128]{2,1,0:T(8,128)S(1)}, f32[2,256,128]{2,1,0:T(8,128)S(1)}) custom-call(f32[4,2,128]{2,1,0:T(2,128)S(1)} %collective-permute-done.near_ref.info_ref, f32[256,256]{1,0:T(8,128)S(1)} %get-tuple-element.63.residual_ref, f32[12,256,512]{2,1,0:T(8,128)S(1)} %get-tuple-element.64.field_ref, f32[128,128]{1,0:T(8,128)S(1)} %copy-done.5, ...), custom_call_target="tpu_custom_call" | custom-call | flops 1500000000 | bytes 11735040 | tf_op jit(solution)/shard_map/adjoint/pallas_call | solution.py:161
  40.2 2.0 %collective-permute-start.9 = (f32[8,128]{1,0:T(8,128)S(1)}, f32[8,128]{1,0:T(8,128)S(1)}, u32[]{:S(2)}, u32[]{:S(2)}) collective-permute-start(f32[8,128]{1,0:T(8,128)S(1)} %add.18), channel_id=1, source_target_pairs={{0,24},{1,25},{2,26},{3,27},{4,28},{5,29},{6,30},{7,31},{8,16},{9,... | collective-permute-start | bytes 12296 | tf_op jit(solution)/shard_map/ppermute | solution.py:473
  42.2 2.3 %adjoint.6 = (f32[2,256,128]{2,1,0:T(8,128)S(1)}, f32[2,256,128]{2,1,0:T(8,128)S(1)}) custom-call(f32[8,2,128]{2,1,0:T(2,128)S(1)} %collective-permute-done.1.far_ref.info_ref, f32[256,256]{1,0:T(8,128)S(1)} %get-tuple-element.63.residual_ref, f32[12,256,512]{2,1,0:T(8,128)S(1)} %get-tuple-element.64.field_ref, f32[128,128]{1,0:T(8,128)S(1)} %copy-done.5, ...), custom_call_target="tpu_custom_call" | custom-call | flops 1500000000 | bytes 11739136 | tf_op jit(solution)/shard_map/adjoint/pallas_call | solution.py:161
  44.5 0.0 collective-permute-done.9
  44.5 0.0 copy-start.3
  44.5 1.7 %collective-permute-start.10 = (f32[8,128]{1,0:T(8,128)S(1)}, f32[8,128]{1,0:T(8,128)S(1)}, u32[]{:S(2)}, u32[]{:S(2)}) collective-permute-start(f32[8,128]{1,0:T(8,128)S(1)} %add.19), channel_id=1, source_target_pairs={{0,6},{1,7},{2,4},{3,5},{4,2},{5,3},{6,0},{7,1},{8,14},{9,15},{10,... | collective-permute-start | bytes 12296 | tf_op jit(solution)/shard_map/ppermute | solution.py:473
  46.2 3.7 %adjoint.7 = (f32[128,256]{1,0:T(8,128)S(1)}, f32[64,256]{1,0:T(8,128)S(1)}) custom-call(f32[8,2,128]{2,1,0:T(2,128)S(1)} %collective-permute-done.1.far_ref.info_ref, f32[256,256]{1,0:T(8,128)S(1)} %get-tuple-element.63.residual_ref, f32[12,256,512]{2,1,0:T(8,128)S(1)} %get-tuple-element.64.field_ref, f32[128,128]{1,0:T(8,128)S(1)} %copy-done.5, ...), custom_call_target="tpu_custom_call" | custom-call | flops 1500000000 | bytes 11411456 | tf_op jit(solution)/shard_map/adjoint/pallas_call | solution.py:161
  49.9 0.0 collective-permute-done.10
  49.9 0.5 collective-permute-start.11
  50.4 3.9 %collective-permute-done.11.rim_ref = f32[64,256]{1,0:T(8,128)S(1)} collective-permute-done((f32[64,256]{1,0:T(8,128)S(1)}, f32[64,256]{1,0:T(8,128)S(1)}, u32[]{:S(2)}, u32[]{:S(2)}) %collective-permute-start.11) | collective-permute-done | bytes 65568 | tf_op jit(solution)/shard_map/ppermute | solution.py:459
  54.3 3.1 %collective-permute-start.12 = (f32[136,256]{1,0:T(8,128)S(1)}, f32[136,256]{1,0:T(8,128)S(1)}, u32[]{:S(2)}, u32[]{:S(2)}) collective-permute-start(f32[136,256]{1,0:T(8,128)S(1)} %rim.1.mine_ref), channel_id=1, source_target_pairs={{0,32},{32,0},{64,96},{96,64},{128,160},{160,128},{192,224},{224,1... | collective-permute-start | bytes 417800 | tf_op jit(solution)/shard_map/ppermute | solution.py:434
  57.4 1.0 %collective-permute-done.12.other_ref = f32[136,256]{1,0:T(8,128)S(1)} collective-permute-done((f32[136,256]{1,0:T(8,128)S(1)}, f32[136,256]{1,0:T(8,128)S(1)}, u32[]{:S(2)}, u32[]{:S(2)}) %collective-permute-start.12) | collective-permute-done | bytes 139296 | tf_op jit(solution)/shard_map/ppermute | solution.py:434
  58.4 0.4 pixels.1
  58.8 1.3 %collective-permute-start.13 = (f32[72,128]{1,0:T(8,128)S(1)}, f32[72,128]{1,0:T(8,128)S(1)}, u32[]{:S(2)}, u32[]{:S(2)}) collective-permute-start(f32[72,128]{1,0:T(8,128)S(1)} %get-tuple-element.87.before_ref), channel_id=1, source_target_pairs={{0,32},{1,0},{2,1},{3,2},{4,3},{5,4},{6,5},{7,6},{8,40},{9,8},{10,... | collective-permute-start | bytes 110600 | tf_op jit(solution)/shard_map/ppermute | solution.py:459
  60.1 1.1 %collective-permute-done.13.mine_ref = f32[72,128]{1,0:T(8,128)S(1)} collective-permute-done((f32[72,128]{1,0:T(8,128)S(1)}, f32[72,128]{1,0:T(8,128)S(1)}, u32[]{:S(2)}, u32[]{:S(2)}) %collective-permute-start.13) | collective-permute-done | bytes 36896 | tf_op jit(solution)/shard_map/ppermute | solution.py:459
  61.2 2.1 %collective-permute-start.14 = (f32[72,128]{1,0:T(8,128)S(1)}, f32[72,128]{1,0:T(8,128)S(1)}, u32[]{:S(2)}, u32[]{:S(2)}) collective-permute-start(f32[72,128]{1,0:T(8,128)S(1)} %collective-permute-done.13.mine_ref), channel_id=1, source_target_pairs={{0,32},{32,0},{64,96},{96,64},{128,160},{160,128},{192,224},{224,1... | collective-permute-start | bytes 110600 | tf_op jit(solution)/shard_map/ppermute | solution.py:434
  63.3 0.9 %collective-permute-done.14.other_ref = f32[72,128]{1,0:T(8,128)S(1)} collective-permute-done((f32[72,128]{1,0:T(8,128)S(1)}, f32[72,128]{1,0:T(8,128)S(1)}, u32[]{:S(2)}, u32[]{:S(2)}) %collective-permute-start.14) | collective-permute-done | bytes 36896 | tf_op jit(solution)/shard_map/ppermute | solution.py:434
  64.1 0.8 %join.1 = (f32[1,64,512]{2,1,0:T(8,128)}, f32[4]{0:T(128)}) custom-call(f32[64,512]{1,0:T(8,128)S(1)} %get-tuple-element.86.inner_ref, f32[72,128]{1,0:T(8,128)S(1)} %get-tuple-element.87.before_ref, f32[72,128]{1,0:T(8,128)S(1)} %collective-permute-done.13.mine_ref, f32[72,128]{1,0:T(8,128)S(1)} %collective-permute-done.14.other_ref), custom_call_target="tpu_custom_call" | custom-call | flops 32768 | bytes 372752 | tf_op jit(solution)/shard_map/join/pallas_call | solution.py:161
  (23 shorter events, 0.1 us)
Async XLA Ops:
  0.6 15.5 %copy-start = (bf16[80,64,256]{2,1,0:T(8,128)(2,1)S(1)}, bf16[80,64,256]{2,1,0:T(8,128)(2,1)}, u32[]{:S(2)}) copy-start(bf16[80,64,256]{2,1,0:T(8,128)(2,1)} %constant.28.clone._.table_ref) | copy-start | bytes 7864324
  1.8 6.4 %collective-permute-start.2 = (f32[64,512]{1,0:T(8,128)S(1)}, f32[64,512]{1,0:T(8,128)S(1)}, u32[]{:S(2)}, u32[]{:S(2)}) collective-permute-start(f32[64,512]{1,0:T(8,128)S(1)} %select_bitcast_fusion), channel_id=1, source_target_pairs={{0,8},{1,9},{2,10},{3,11},{4,12},{5,13},{6,14},{7,15},{8,16},{9,17... | collective-permute-start | bytes 393224 | tf_op jit(solution)/shard_map/ppermute | solution.py:459
  5.1 1.4 %copy-start.1 = (bf16[44,64,256]{2,1,0:T(8,128)(2,1)S(1)}, bf16[44,64,256]{2,1,0:T(8,128)(2,1)}, u32[]{:S(2)}) copy-start(bf16[44,64,256]{2,1,0:T(8,128)(2,1)} %constant.27.clone.table_ref.early_ref) | copy-start | bytes 4325380
  6.4 1.2 %copy-start.4 = (f32[1,512,512]{2,1,0:T(8,128)S(1)}, f32[1,512,512]{2,1,0:T(8,128)}, u32[]{:S(2)}) copy-start(f32[1,512,512]{2,1,0:T(8,128)} %tile_ref.1) | copy-start | bytes 3145732
  7.6 2.7 %copy-start.7 = (s32[4,2,128]{2,1,0:T(2,128)S(1)}, s32[4,2,128]{2,1,0:T(2,128)}, u32[]{:S(2)}) copy-start(s32[4,2,128]{2,1,0:T(2,128)} %param.11) | copy-start | bytes 12292
  7.6 2.7 %copy-start.8 = (f32[4]{0:T(128)S(1)}, f32[4]{0:T(128)}, u32[]{:S(2)}) copy-start(f32[4]{0:T(128)} %param.10) | copy-start | bytes 52
  8.2 1.4 %collective-permute-start.3 = (f32[64,512]{1,0:T(8,128)S(1)}, f32[64,512]{1,0:T(8,128)S(1)}, u32[]{:S(2)}, u32[]{:S(2)}) collective-permute-start(f32[64,512]{1,0:T(8,128)S(1)} %collective-permute-done.2.mine_ref), channel_id=1, source_target_pairs={{0,32},{32,0},{64,96},{96,64},{128,160},{160,128},{192,224},{224,1... | collective-permute-start | bytes 393224 | tf_op jit(solution)/shard_map/ppermute | solution.py:434
  9.7 11.0 %copy-start.5 = (f32[128,128]{1,0:T(8,128)S(1)}, f32[128,128]{1,0:T(8,128)}, u32[]{:S(2)}) copy-start(f32[128,128]{1,0:T(8,128)} %gain_ref.11) | copy-start | bytes 196612
  10.1 7.7 %collective-permute-start.4 = (f32[128,128]{1,0:T(8,128)S(1)}, f32[128,128]{1,0:T(8,128)S(1)}, u32[]{:S(2)}, u32[]{:S(2)}) collective-permute-start(f32[128,128]{1,0:T(8,128)S(1)} %get-tuple-element.52), channel_id=1, source_target_pairs={{0,1},{1,2},{2,3},{3,4},{4,5},{5,6},{6,7},{7,39},{8,9},{9,10},{10,... | collective-permute-start | bytes 196616 | tf_op jit(solution)/shard_map/ppermute | solution.py:459
  10.4 9.3 %collective-permute-start = (f32[4,2,128]{2,1,0:T(2,128)S(1)}, f32[4,2,128]{2,1,0:T(2,128)S(1)}, u32[]{:S(2)}, u32[]{:S(2)}) collective-permute-start(f32[4,2,128]{2,1,0:T(2,128)S(1)} %convert_select_fusion.info_ref), channel_id=1, source_target_pairs={{0,193},{1,64},{2,195},{3,66},{4,197},{5,68},{6,199},{7,70},{8,201... | collective-permute-start | bytes 12296 | tf_op jit(solution)/shard_map/ppermute | solution.py:444
  16.1 1.4 %copy-start.2 = (bf16[44,64,256]{2,1,0:T(8,128)(2,1)S(1)}, bf16[44,64,256]{2,1,0:T(8,128)(2,1)}, u32[]{:S(2)}) copy-start(bf16[44,64,256]{2,1,0:T(8,128)(2,1)} %constant.27.clone.table_ref.early_ref) | copy-start | bytes 4325380
  17.8 2.8 %collective-permute-start.5 = (f32[128,128]{1,0:T(8,128)S(1)}, f32[128,128]{1,0:T(8,128)S(1)}, u32[]{:S(2)}, u32[]{:S(2)}) collective-permute-start(f32[128,128]{1,0:T(8,128)S(1)} %collective-permute-done.4.mine_ref), channel_id=1, source_target_pairs={{0,32},{32,0},{64,96},{96,64},{128,160},{160,128},{192,224},{224,1... | collective-permute-start | bytes 196616 | tf_op jit(solution)/shard_map/ppermute | solution.py:434
  19.8 4.4 %collective-permute-start.1 = (f32[8,2,128]{2,1,0:T(2,128)S(1)}, f32[8,2,128]{2,1,0:T(2,128)S(1)}, u32[]{:S(2)}, u32[]{:S(2)}) collective-permute-start(f32[8,2,128]{2,1,0:T(2,128)S(1)} %pad_maximum_fusion), channel_id=1, source_target_pairs={{0,65},{1,192},{2,67},{3,194},{4,69},{5,196},{6,71},{7,198},{8,73}... | collective-permute-start | bytes 24584 | tf_op jit(solution)/shard_map/ppermute | solution.py:444
  24.2 6.4 %copy-start.6 = (f32[1,512,512]{2,1,0:T(8,128)S(1)}, f32[1,512,512]{2,1,0:T(8,128)}, u32[]{:S(2)}) copy-start(f32[1,512,512]{2,1,0:T(8,128)} %target_ref.1) | copy-start | bytes 3145732
  29.3 2.6 %collective-permute-start.6 = (f32[256,256]{1,0:T(8,128)S(1)}, f32[256,256]{1,0:T(8,128)S(1)}, u32[]{:S(2)}, u32[]{:S(2)}) collective-permute-start(f32[256,256]{1,0:T(8,128)S(1)} %get-tuple-element.59.mine_ref), channel_id=1, source_target_pairs={{0,32},{32,0},{64,96},{96,64},{128,160},{160,128},{192,224},{224,1... | collective-permute-start | bytes 786440 | tf_op jit(solution)/shard_map/ppermute | solution.py:434
  32.6 3.9 %collective-permute-start.7 = (f32[8,128]{1,0:T(8,128)S(1)}, f32[8,128]{1,0:T(8,128)S(1)}, u32[]{:S(2)}, u32[]{:S(2)}) collective-permute-start(f32[8,128]{1,0:T(8,128)S(1)} %get-tuple-element.67), channel_id=1, source_target_pairs={{0,8},{1,9},{2,10},{3,11},{4,12},{5,13},{6,14},{7,15},{8,0},{9,1},... | collective-permute-start | bytes 12296 | tf_op jit(solution)/shard_map/ppermute | solution.py:473
  36.6 3.6 %collective-permute-start.8 = (f32[8,128]{1,0:T(8,128)S(1)}, f32[8,128]{1,0:T(8,128)S(1)}, u32[]{:S(2)}, u32[]{:S(2)}) collective-permute-start(f32[8,128]{1,0:T(8,128)S(1)} %add.17), channel_id=1, source_target_pairs={{0,2},{1,3},{2,0},{3,1},{4,6},{5,7},{6,4},{7,5},{8,10},{9,11},{10,... | collective-permute-start | bytes 12296 | tf_op jit(solution)/shard_map/ppermute | solution.py:473
  40.2 4.3 %collective-permute-start.9 = (f32[8,128]{1,0:T(8,128)S(1)}, f32[8,128]{1,0:T(8,128)S(1)}, u32[]{:S(2)}, u32[]{:S(2)}) collective-permute-start(f32[8,128]{1,0:T(8,128)S(1)} %add.18), channel_id=1, source_target_pairs={{0,24},{1,25},{2,26},{3,27},{4,28},{5,29},{6,30},{7,31},{8,16},{9,... | collective-permute-start | bytes 12296 | tf_op jit(solution)/shard_map/ppermute | solution.py:473
  44.5 14.0 %copy-start.3 = (bf16[44,64,256]{2,1,0:T(8,128)(2,1)S(1)}, bf16[44,64,256]{2,1,0:T(8,128)(2,1)}, u32[]{:S(2)}) copy-start(bf16[44,64,256]{2,1,0:T(8,128)(2,1)} %constant.27.clone.table_ref.early_ref) | copy-start | bytes 4325380
  44.5 5.4 %collective-permute-start.10 = (f32[8,128]{1,0:T(8,128)S(1)}, f32[8,128]{1,0:T(8,128)S(1)}, u32[]{:S(2)}, u32[]{:S(2)}) collective-permute-start(f32[8,128]{1,0:T(8,128)S(1)} %add.19), channel_id=1, source_target_pairs={{0,6},{1,7},{2,4},{3,5},{4,2},{5,3},{6,0},{7,1},{8,14},{9,15},{10,... | collective-permute-start | bytes 12296 | tf_op jit(solution)/shard_map/ppermute | solution.py:473
  49.9 4.4 %collective-permute-start.11 = (f32[64,256]{1,0:T(8,128)S(1)}, f32[64,256]{1,0:T(8,128)S(1)}, u32[]{:S(2)}, u32[]{:S(2)}) collective-permute-start(f32[64,256]{1,0:T(8,128)S(1)} %get-tuple-element.84), channel_id=1, source_target_pairs={{0,8},{1,9},{2,10},{3,11},{4,12},{5,13},{6,14},{7,15},{8,16},{9,17... | collective-permute-start | bytes 196616 | tf_op jit(solution)/shard_map/ppermute | solution.py:459
  54.3 4.1 %collective-permute-start.12 = (f32[136,256]{1,0:T(8,128)S(1)}, f32[136,256]{1,0:T(8,128)S(1)}, u32[]{:S(2)}, u32[]{:S(2)}) collective-permute-start(f32[136,256]{1,0:T(8,128)S(1)} %rim.1.mine_ref), channel_id=1, source_target_pairs={{0,32},{32,0},{64,96},{96,64},{128,160},{160,128},{192,224},{224,1... | collective-permute-start | bytes 417800 | tf_op jit(solution)/shard_map/ppermute | solution.py:434
  58.8 2.3 %collective-permute-start.13 = (f32[72,128]{1,0:T(8,128)S(1)}, f32[72,128]{1,0:T(8,128)S(1)}, u32[]{:S(2)}, u32[]{:S(2)}) collective-permute-start(f32[72,128]{1,0:T(8,128)S(1)} %get-tuple-element.87.before_ref), channel_id=1, source_target_pairs={{0,32},{1,0},{2,1},{3,2},{4,3},{5,4},{6,5},{7,6},{8,40},{9,8},{10,... | collective-permute-start | bytes 110600 | tf_op jit(solution)/shard_map/ppermute | solution.py:459
  61.2 2.9 %collective-permute-start.14 = (f32[72,128]{1,0:T(8,128)S(1)}, f32[72,128]{1,0:T(8,128)S(1)}, u32[]{:S(2)}, u32[]{:S(2)}) collective-permute-start(f32[72,128]{1,0:T(8,128)S(1)} %collective-permute-done.13.mine_ref), channel_id=1, source_target_pairs={{0,32},{32,0},{64,96},{96,64},{128,160},{160,128},{192,224},{224,1... | collective-permute-start | bytes 110600 | tf_op jit(solution)/shard_map/ppermute | solution.py:434

commit v7 on v6

--- a/solution.py
+++ b/solution.py
@@ -459,6 +459,17 @@
     return lax.ppermute(value, BOTH, pairs)
 
 
+def line_move(value):
+    pairs = []
+    for source in range(2 * CHIPS):
+        down = 1 if source // 2 % 2 == 0 else -1
+        for tile in range(TROWS * TCOLS):
+            to = tile + down * TCOLS
+            inside = 0 <= to < TROWS * TCOLS
+            pairs.append((source * 32 + tile, source * 32 + to if inside else (source ^ 2) * 32 + tile))
+    return lax.ppermute(value, BOTH, pairs)
+
+
 def tile_swap(value, step):
     def partner(at):
         y, x, z = at // TCOLS, at // 2 % 4, at % 2
@@ -521,7 +532,7 @@
     plane = pltpu.VMEM((2, W, K), F32)
     planes = (jnp.zeros((8, K), F32),) * 2
     for chip in range(CHIPS):
-        arrived = tile_swap(energies, (3, 1, 4, 2)[chip])
+        arrived = tile_swap(energies, (4, 2, 3, 1)[chip])
         last = chip == CHIPS - 1
         outs = call(
             functools.partial(adjoint_kernel, chip),
@@ -535,7 +546,7 @@
         planes = outs
         *planes, energies = tied(*planes, energies + arrived)
     lines, rim = planes
-    from_rows = tile_move(rim, lambda source: (1, 0) if source < CHIPS else (-1, 0))
+    from_rows = line_move(rim)
     (mine,) = call(rim_kernel, [(K + 8, W)], [lines, from_rows, energies], "rim", K * K)
     other = swap_cores(mine)
     inner, side = call(

time: 65.1 us -> 64.9 us (level)
    ppermute x4 -> x3, waiting for transfers between devices: 4.99 us -> 1.08 us  [tile_move(): return lax.ppermute(value, BOTH, pairs)]
    ppermute x0 -> x1, waiting for transfers between devices: none -> 3.28 us  [line_move(): return lax.ppermute(value, BOTH, pairs)]
    ppermute x5, starting transfers between devices: 8.47 us -> 10 us  [swap_cores(): return lax.ppermute(value, 'src', [(at, at ^ 1) for at in range(8)])]
    ppermute x4 -> x3, starting transfers between devices: 5.25 us -> 3.71 us  [tile_move(): return lax.ppermute(value, BOTH, pairs)]
    ppermute x0 -> x1, starting transfers between devices: none -> 1.52 us  [line_move(): return lax.ppermute(value, BOTH, pairs)]
    ppermute x4, starting transfers between devices: 6.65 us -> 5.2 us  [tile_swap(): lax.ppermute(value, 'tile', [(at, partner(at)) for at in range(TROWS * TC...]
  transfers between devices with their start and end apart: 15 -> 15, of which waited for: 7 -> 9; matrix products, arithmetic and copies ran while one was open for 0% -> 0% of each run, Pallas kernels for 24% -> 24%
where the time goes in v7:
time: 64.9 us; the launch traced here: 64.8 us
  starting transfers between devices  26.9 us (41%)
  Pallas kernels  23.3 us (36%)
  waiting for transfers between devices  8.54 us (13%)
  local copies, waits for them, and re-layouts  3.97 us (6%)
  other arithmetic  1.24 us (2%)
  between operations  0.82 us (1%)
    pallas_call x14, Pallas kernels, call(): pl.pallas_call(kernel, out_shape=shapes, in_specs=specs, out_specs=[pl.Bl...  23.3 us
    ppermute x5, starting transfers between devices, swap_cores(): return lax.ppermute(value, 'src', [(at, at ^ 1) for at in range(8)])  10 us
    ppermute x2, starting transfers between devices, chip_swap(): return lax.ppermute(value, BOTH, pairs)  6.44 us
    ppermute x4, starting transfers between devices, tile_swap(): lax.ppermute(value, 'tile', [(at, partner(at)) for at in range(TROWS * TC...  5.2 us
    unnamed x18, local copies, waits for them, and re-layouts  3.97 us
    ppermute x3, starting transfers between devices, tile_move(): return lax.ppermute(value, BOTH, pairs)  3.71 us
    ppermute x5, waiting for transfers between devices, swap_cores(): return lax.ppermute(value, 'src', [(at, at ^ 1) for at in range(8)])  3.29 us
    ppermute x1, waiting for transfers between devices, line_move(): return lax.ppermute(value, BOTH, pairs)  3.28 us
  transfers between devices with their start and end apart: 15, of which 9 were waited for; matrix products, arithmetic and copies ran while one was open for 0% of the time, Pallas kernels for 24%

profile of v7, /device:TPU:1, one launch (start us, length us, event | category | flops | bytes accessed | tf_op | source)
XLA Modules:
  0.0 64.8 jit_solution(16576086417170598775)
XLA Ops:
  0.6 0.0 copy-start
  0.7 1.1 %select_bitcast_fusion = f32[64,512]{1,0:T(8,128)S(1)} fusion(f32[1,512,512]{2,1,0:T(8,128)} %tile_ref.1, pred[]{:T(512)S(6)} %eq.14), kind=kLoop, calls=%fused_computation | loop fusion | flops 32768 | bytes 393217 | tf_op jit(solution)/shard_map/jit(_where)/select_n | solution.py:493
  1.8 3.3 %collective-permute-start.2 = (f32[64,512]{1,0:T(8,128)S(1)}, f32[64,512]{1,0:T(8,128)S(1)}, u32[]{:S(2)}, u32[]{:S(2)}) collective-permute-start(f32[64,512]{1,0:T(8,128)S(1)} %select_bitcast_fusion), channel_id=1, source_target_pairs={{0,8},{1,9},{2,10},{3,11},{4,12},{5,13},{6,14},{7,15},{8,16},{9,17... | collective-permute-start | bytes 393224 | tf_op jit(solution)/shard_map/ppermute | solution.py:459
  5.1 1.4 %copy-done.1 = bf16[44,64,256]{2,1,0:T(8,128)(2,1)S(1)} copy-done((bf16[44,64,256]{2,1,0:T(8,128)(2,1)S(1)}, bf16[44,64,256]{2,1,0:T(8,128)(2,1)}, u32[]{:S(2)}) %copy-start.1) | copy-done | bytes 1441816
  6.4 1.2 %copy-done.4 = f32[1,512,512]{2,1,0:T(8,128)S(1)} copy-done((f32[1,512,512]{2,1,0:T(8,128)S(1)}, f32[1,512,512]{2,1,0:T(8,128)}, u32[]{:S(2)}) %copy-start.4) | copy-done | bytes 1048600
  7.6 0.6 own.1
  8.2 0.0 collective-permute-done.2.mine_ref
  8.2 0.1 collective-permute-start.3
  8.4 1.3 %collective-permute-done.3.other_ref = f32[64,512]{1,0:T(8,128)S(1)} collective-permute-done((f32[64,512]{1,0:T(8,128)S(1)}, f32[64,512]{1,0:T(8,128)S(1)}, u32[]{:S(2)}, u32[]{:S(2)}) %collective-permute-start.3) | collective-permute-done | bytes 131104 | tf_op jit(solution)/shard_map/ppermute | solution.py:434
  9.7 0.4 rows.1
  10.1 0.2 collective-permute-start.4
  10.4 0.1 convert_select_fusion.info_ref
  10.4 5.7 %collective-permute-start = (f32[4,2,128]{2,1,0:T(2,128)S(1)}, f32[4,2,128]{2,1,0:T(2,128)S(1)}, u32[]{:S(2)}, u32[]{:S(2)}) collective-permute-start(f32[4,2,128]{2,1,0:T(2,128)S(1)} %convert_select_fusion.info_ref), channel_id=1, source_target_pairs={{0,193},{1,64},{2,195},{3,66},{4,197},{5,68},{6,199},{7,70},{8,201... | collective-permute-start | bytes 12296 | tf_op jit(solution)/shard_map/ppermute | solution.py:444
  16.1 1.4 %copy-done.2 = bf16[44,64,256]{2,1,0:T(8,128)(2,1)S(1)} copy-done((bf16[44,64,256]{2,1,0:T(8,128)(2,1)S(1)}, bf16[44,64,256]{2,1,0:T(8,128)(2,1)}, u32[]{:S(2)}) %copy-start.2) | copy-done | bytes 1441816
  17.5 0.4 columns.1.basis_ref
  17.8 1.9 %collective-permute-start.5 = (f32[128,128]{1,0:T(8,128)S(1)}, f32[128,128]{1,0:T(8,128)S(1)}, u32[]{:S(2)}, u32[]{:S(2)}) collective-permute-start(f32[128,128]{1,0:T(8,128)S(1)} %collective-permute-done.4.mine_ref), channel_id=1, source_target_pairs={{0,32},{32,0},{64,96},{96,64},{128,160},{160,128},{192,224},{224,1... | collective-permute-start | bytes 196616 | tf_op jit(solution)/shard_map/ppermute | solution.py:434
  19.8 0.0 collective-permute-done.near_ref.info_ref
  19.8 0.8 %collective-permute-start.1 = (f32[8,2,128]{2,1,0:T(2,128)S(1)}, f32[8,2,128]{2,1,0:T(2,128)S(1)}, u32[]{:S(2)}, u32[]{:S(2)}) collective-permute-start(f32[8,2,128]{2,1,0:T(2,128)S(1)} %pad_maximum_fusion), channel_id=1, source_target_pairs={{0,65},{1,192},{2,67},{3,194},{4,69},{5,196},{6,71},{7,198},{8,73}... | collective-permute-start | bytes 24584 | tf_op jit(solution)/shard_map/ppermute | solution.py:444
  20.6 0.1 collective-permute-done.5.other_ref
  20.7 3.0 %image.1 = (f32[4,256,512]{2,1,0:T(8,128)S(1)}, f32[256,256]{1,0:T(8,128)S(1)}, f32[2,256,128]{2,1,0:T(8,128)S(1)}, f32[2,256,128]{2,1,0:T(8,128)S(1)}) custom-call(f32[4,2,128]{2,1,0:T(2,128)S(1)} %convert_select_fusion.info_ref, f32[256,256]{1,0:T(8,128)S(1)} %columns.1.basis_ref, f32[128,128]{1,0:T(8,128)S(1)} %collective-permute-done.4.mine_ref, ...), custom_call_target="tpu_custom_call" | custom-call | flops 2000000000 | bytes 7409664 | tf_op jit(solution)/shard_map/image/pallas_call | solution.py:161
  23.7 0.4 collective-permute-done.1.far_ref.info_ref
  24.2 5.1 %others.1 = (f32[12,256,512]{2,1,0:T(8,128)S(1)}, f32[256,256]{1,0:T(8,128)S(1)}) custom-call(f32[4,2,128]{2,1,0:T(2,128)S(1)} %collective-permute-done.near_ref.info_ref, f32[8,2,128]{2,1,0:T(2,128)S(1)} %collective-permute-done.1.far_ref.info_ref, f32[128,128]{1,0:T(8,128)S(1)} %copy-done.5, bf16[80,64,256]{2,1,0:T(8,128)(2,1)S(1)} %copy-done, ...), custom_call_target="tpu_custom_call" | custom-call | flops 5000000000 | bytes 10039296 | tf_op jit(solution)/shard_map/others/pallas_call | solution.py:161
  29.3 1.3 %collective-permute-start.6 = (f32[256,256]{1,0:T(8,128)S(1)}, f32[256,256]{1,0:T(8,128)S(1)}, u32[]{:S(2)}, u32[]{:S(2)}) collective-permute-start(f32[256,256]{1,0:T(8,128)S(1)} %get-tuple-element.59.mine_ref), channel_id=1, source_target_pairs={{0,32},{32,0},{64,96},{96,64},{128,160},{160,128},{192,224},{224,1... | collective-permute-start | bytes 786440 | tf_op jit(solution)/shard_map/ppermute | solution.py:434
  30.5 1.3 %wanted.1.wanted_ref = f32[256,256]{1,0:T(8,128)S(1)} custom-call(f32[1,512,512]{2,1,0:T(8,128)S(1)} %copy-done.6, bf16[80,64,256]{2,1,0:T(8,128)(2,1)S(1)} %copy-done), custom_call_target="tpu_custom_call" | custom-call | flops 600000000 | bytes 3932160 | tf_op jit(solution)/shard_map/wanted/pallas_call | solution.py:161
  31.8 0.0 collective-permute-done.6.other_ref
  31.8 0.8 %residual.1 = (f32[256,256]{1,0:T(8,128)S(1)}, f32[8,128]{1,0:T(8,128)S(1)}) custom-call(f32[256,256]{1,0:T(8,128)S(1)} %get-tuple-element.59.mine_ref, f32[256,256]{1,0:T(8,128)S(1)} %collective-permute-done.6.other_ref, f32[256,256]{1,0:T(8,128)S(1)} %wanted.1.wanted_ref, f32[4,256,512]{2,1,0:T(8,128)S(1)} %get-tuple-element.62.field_ref, ...), custom_call_target="tpu_custom_call" | custom-call | flops 300000000 | bytes 5771264 | tf_op jit(solution)/shard_map/residual/pallas_call | solution.py:161
  32.6 3.1 %collective-permute-start.7 = (f32[8,128]{1,0:T(8,128)S(1)}, f32[8,128]{1,0:T(8,128)S(1)}, u32[]{:S(2)}, u32[]{:S(2)}) collective-permute-start(f32[8,128]{1,0:T(8,128)S(1)} %get-tuple-element.67), channel_id=1, source_target_pairs={{0,24},{1,25},{2,26},{3,27},{4,28},{5,29},{6,30},{7,31},{8,16},{9,... | collective-permute-start | bytes 12296 | tf_op jit(solution)/shard_map/ppermute | solution.py:484
  35.8 2.2 %adjoint.4 = (f32[2,256,128]{2,1,0:T(8,128)S(1)}, f32[2,256,128]{2,1,0:T(8,128)S(1)}) custom-call(f32[4,2,128]{2,1,0:T(2,128)S(1)} %convert_select_fusion.info_ref, f32[256,256]{1,0:T(8,128)S(1)} %get-tuple-element.63.residual_ref, f32[4,256,512]{2,1,0:T(8,128)S(1)} %get-tuple-element.62.field_ref, f32[128,128]{1,0:T(8,128)S(1)} %copy-done.5, ...), custom_call_target="tpu_custom_call" | custom-call | flops 1500000000 | bytes 7024640 | tf_op jit(solution)/shard_map/adjoint/pallas_call | solution.py:161
  38.0 0.0 collective-permute-done.7
  38.0 1.2 %collective-permute-start.8 = (f32[8,128]{1,0:T(8,128)S(1)}, f32[8,128]{1,0:T(8,128)S(1)}, u32[]{:S(2)}, u32[]{:S(2)}) collective-permute-start(f32[8,128]{1,0:T(8,128)S(1)} %add.17), channel_id=1, source_target_pairs={{0,6},{1,7},{2,4},{3,5},{4,2},{5,3},{6,0},{7,1},{8,14},{9,15},{10,... | collective-permute-start | bytes 12296 | tf_op jit(solution)/shard_map/ppermute | solution.py:484
  39.2 2.2 %adjoint.5 = (f32[2,256,128]{2,1,0:T(8,128)S(1)}, f32[2,256,128]{2,1,0:T(8,128)S(1)}) custom-call(f32[4,2,128]{2,1,0:T(2,128)S(1)} %collective-permute-done.near_ref.info_ref, f32[256,256]{1,0:T(8,128)S(1)} %get-tuple-element.63.residual_ref, f32[12,256,512]{2,1,0:T(8,128)S(1)} %get-tuple-element.64.field_ref, f32[128,128]{1,0:T(8,128)S(1)} %copy-done.5, ...), custom_call_target="tpu_custom_call" | custom-call | flops 1500000000 | bytes 11735040 | tf_op jit(solution)/shard_map/adjoint/pallas_call | solution.py:161
  41.5 0.3 collective-permute-done.8
  41.8 0.0 collective-permute-start.9
  41.8 2.3 %adjoint.6 = (f32[2,256,128]{2,1,0:T(8,128)S(1)}, f32[2,256,128]{2,1,0:T(8,128)S(1)}) custom-call(f32[8,2,128]{2,1,0:T(2,128)S(1)} %collective-permute-done.1.far_ref.info_ref, f32[256,256]{1,0:T(8,128)S(1)} %get-tuple-element.63.residual_ref, f32[12,256,512]{2,1,0:T(8,128)S(1)} %get-tuple-element.64.field_ref, f32[128,128]{1,0:T(8,128)S(1)} %copy-done.5, ...), custom_call_target="tpu_custom_call" | custom-call | flops 1500000000 | bytes 11739136 | tf_op jit(solution)/shard_map/adjoint/pallas_call | solution.py:161
  44.1 0.1 collective-permute-done.9
  44.3 0.9 %collective-permute-start.10 = (f32[8,128]{1,0:T(8,128)S(1)}, f32[8,128]{1,0:T(8,128)S(1)}, u32[]{:S(2)}, u32[]{:S(2)}) collective-permute-start(f32[8,128]{1,0:T(8,128)S(1)} %add.19), channel_id=1, source_target_pairs={{0,2},{1,3},{2,0},{3,1},{4,6},{5,7},{6,4},{7,5},{8,10},{9,11},{10,... | collective-permute-start | bytes 12296 | tf_op jit(solution)/shard_map/ppermute | solution.py:484
  45.1 3.7 %adjoint.7 = (f32[128,256]{1,0:T(8,128)S(1)}, f32[64,256]{1,0:T(8,128)S(1)}) custom-call(f32[8,2,128]{2,1,0:T(2,128)S(1)} %collective-permute-done.1.far_ref.info_ref, f32[256,256]{1,0:T(8,128)S(1)} %get-tuple-element.63.residual_ref, f32[12,256,512]{2,1,0:T(8,128)S(1)} %get-tuple-element.64.field_ref, f32[128,128]{1,0:T(8,128)S(1)} %copy-done.5, ...), custom_call_target="tpu_custom_call" | custom-call | flops 1500000000 | bytes 11411456 | tf_op jit(solution)/shard_map/adjoint/pallas_call | solution.py:161
  48.9 0.0 collective-permute-done.10
  48.9 1.5 %collective-permute-start.11 = (f32[64,256]{1,0:T(8,128)S(1)}, f32[64,256]{1,0:T(8,128)S(1)}, u32[]{:S(2)}, u32[]{:S(2)}) collective-permute-start(f32[64,256]{1,0:T(8,128)S(1)} %get-tuple-element.84), channel_id=1, source_target_pairs={{0,8},{1,9},{2,10},{3,11},{4,12},{5,13},{6,14},{7,15},{8,16},{9,17... | collective-permute-start | bytes 196616 | tf_op jit(solution)/shard_map/ppermute | solution.py:470
  50.4 3.3 %collective-permute-done.11.rim_ref = f32[64,256]{1,0:T(8,128)S(1)} collective-permute-done((f32[64,256]{1,0:T(8,128)S(1)}, f32[64,256]{1,0:T(8,128)S(1)}, u32[]{:S(2)}, u32[]{:S(2)}) %collective-permute-start.11) | collective-permute-done | bytes 65568 | tf_op jit(solution)/shard_map/ppermute | solution.py:470
  53.7 3.5 %collective-permute-start.12 = (f32[136,256]{1,0:T(8,128)S(1)}, f32[136,256]{1,0:T(8,128)S(1)}, u32[]{:S(2)}, u32[]{:S(2)}) collective-permute-start(f32[136,256]{1,0:T(8,128)S(1)} %rim.1.mine_ref), channel_id=1, source_target_pairs={{0,32},{32,0},{64,96},{96,64},{128,160},{160,128},{192,224},{224,1... | collective-permute-start | bytes 417800 | tf_op jit(solution)/shard_map/ppermute | solution.py:434
  57.2 1.0 %collective-permute-done.12.other_ref = f32[136,256]{1,0:T(8,128)S(1)} collective-permute-done((f32[136,256]{1,0:T(8,128)S(1)}, f32[136,256]{1,0:T(8,128)S(1)}, u32[]{:S(2)}, u32[]{:S(2)}) %collective-permute-start.12) | collective-permute-done | bytes 139296 | tf_op jit(solution)/shard_map/ppermute | solution.py:434
  58.2 0.4 pixels.1
  58.6 0.2 collective-permute-start.13
  58.8 1.1 %collective-permute-done.13.mine_ref = f32[72,128]{1,0:T(8,128)S(1)} collective-permute-done((f32[72,128]{1,0:T(8,128)S(1)}, f32[72,128]{1,0:T(8,128)S(1)}, u32[]{:S(2)}, u32[]{:S(2)}) %collective-permute-start.13) | collective-permute-done | bytes 36896 | tf_op jit(solution)/shard_map/ppermute | solution.py:459
  59.9 3.2 %collective-permute-start.14 = (f32[72,128]{1,0:T(8,128)S(1)}, f32[72,128]{1,0:T(8,128)S(1)}, u32[]{:S(2)}, u32[]{:S(2)}) collective-permute-start(f32[72,128]{1,0:T(8,128)S(1)} %collective-permute-done.13.mine_ref), channel_id=1, source_target_pairs={{0,32},{32,0},{64,96},{96,64},{128,160},{160,128},{192,224},{224,1... | collective-permute-start | bytes 110600 | tf_op jit(solution)/shard_map/ppermute | solution.py:434
  63.1 0.9 %collective-permute-done.14.other_ref = f32[72,128]{1,0:T(8,128)S(1)} collective-permute-done((f32[72,128]{1,0:T(8,128)S(1)}, f32[72,128]{1,0:T(8,128)S(1)}, u32[]{:S(2)}, u32[]{:S(2)}) %collective-permute-start.14) | collective-permute-done | bytes 36896 | tf_op jit(solution)/shard_map/ppermute | solution.py:434
  64.0 0.8 %join.1 = (f32[1,64,512]{2,1,0:T(8,128)}, f32[4]{0:T(128)}) custom-call(f32[64,512]{1,0:T(8,128)S(1)} %get-tuple-element.86.inner_ref, f32[72,128]{1,0:T(8,128)S(1)} %get-tuple-element.87.before_ref, f32[72,128]{1,0:T(8,128)S(1)} %collective-permute-done.13.mine_ref, f32[72,128]{1,0:T(8,128)S(1)} %collective-permute-done.14.other_ref), custom_call_target="tpu_custom_call" | custom-call | flops 32768 | bytes 372752 | tf_op jit(solution)/shard_map/join/pallas_call | solution.py:161
  (23 shorter events, 0.1 us)
Async XLA Ops:
  0.6 15.5 %copy-start = (bf16[80,64,256]{2,1,0:T(8,128)(2,1)S(1)}, bf16[80,64,256]{2,1,0:T(8,128)(2,1)}, u32[]{:S(2)}) copy-start(bf16[80,64,256]{2,1,0:T(8,128)(2,1)} %constant.28.clone._.table_ref) | copy-start | bytes 7864324
  1.8 6.4 %collective-permute-start.2 = (f32[64,512]{1,0:T(8,128)S(1)}, f32[64,512]{1,0:T(8,128)S(1)}, u32[]{:S(2)}, u32[]{:S(2)}) collective-permute-start(f32[64,512]{1,0:T(8,128)S(1)} %select_bitcast_fusion), channel_id=1, source_target_pairs={{0,8},{1,9},{2,10},{3,11},{4,12},{5,13},{6,14},{7,15},{8,16},{9,17... | collective-permute-start | bytes 393224 | tf_op jit(solution)/shard_map/ppermute | solution.py:459
  5.1 1.4 %copy-start.1 = (bf16[44,64,256]{2,1,0:T(8,128)(2,1)S(1)}, bf16[44,64,256]{2,1,0:T(8,128)(2,1)}, u32[]{:S(2)}) copy-start(bf16[44,64,256]{2,1,0:T(8,128)(2,1)} %constant.27.clone.table_ref.early_ref) | copy-start | bytes 4325380
  6.4 1.2 %copy-start.4 = (f32[1,512,512]{2,1,0:T(8,128)S(1)}, f32[1,512,512]{2,1,0:T(8,128)}, u32[]{:S(2)}) copy-start(f32[1,512,512]{2,1,0:T(8,128)} %tile_ref.1) | copy-start | bytes 3145732
  7.6 2.7 %copy-start.7 = (s32[4,2,128]{2,1,0:T(2,128)S(1)}, s32[4,2,128]{2,1,0:T(2,128)}, u32[]{:S(2)}) copy-start(s32[4,2,128]{2,1,0:T(2,128)} %param.11) | copy-start | bytes 12292
  7.6 2.7 %copy-start.8 = (f32[4]{0:T(128)S(1)}, f32[4]{0:T(128)}, u32[]{:S(2)}) copy-start(f32[4]{0:T(128)} %param.10) | copy-start | bytes 52
  8.2 1.4 %collective-permute-start.3 = (f32[64,512]{1,0:T(8,128)S(1)}, f32[64,512]{1,0:T(8,128)S(1)}, u32[]{:S(2)}, u32[]{:S(2)}) collective-permute-start(f32[64,512]{1,0:T(8,128)S(1)} %collective-permute-done.2.mine_ref), channel_id=1, source_target_pairs={{0,32},{32,0},{64,96},{96,64},{128,160},{160,128},{192,224},{224,1... | collective-permute-start | bytes 393224 | tf_op jit(solution)/shard_map/ppermute | solution.py:434
  9.7 11.0 %copy-start.5 = (f32[128,128]{1,0:T(8,128)S(1)}, f32[128,128]{1,0:T(8,128)}, u32[]{:S(2)}) copy-start(f32[128,128]{1,0:T(8,128)} %gain_ref.11) | copy-start | bytes 196612
  10.1 7.7 %collective-permute-start.4 = (f32[128,128]{1,0:T(8,128)S(1)}, f32[128,128]{1,0:T(8,128)S(1)}, u32[]{:S(2)}, u32[]{:S(2)}) collective-permute-start(f32[128,128]{1,0:T(8,128)S(1)} %get-tuple-element.52), channel_id=1, source_target_pairs={{0,1},{1,2},{2,3},{3,4},{4,5},{5,6},{6,7},{7,39},{8,9},{9,10},{10,... | collective-permute-start | bytes 196616 | tf_op jit(solution)/shard_map/ppermute | solution.py:459
  10.4 9.3 %collective-permute-start = (f32[4,2,128]{2,1,0:T(2,128)S(1)}, f32[4,2,128]{2,1,0:T(2,128)S(1)}, u32[]{:S(2)}, u32[]{:S(2)}) collective-permute-start(f32[4,2,128]{2,1,0:T(2,128)S(1)} %convert_select_fusion.info_ref), channel_id=1, source_target_pairs={{0,193},{1,64},{2,195},{3,66},{4,197},{5,68},{6,199},{7,70},{8,201... | collective-permute-start | bytes 12296 | tf_op jit(solution)/shard_map/ppermute | solution.py:444
  16.1 1.4 %copy-start.2 = (bf16[44,64,256]{2,1,0:T(8,128)(2,1)S(1)}, bf16[44,64,256]{2,1,0:T(8,128)(2,1)}, u32[]{:S(2)}) copy-start(bf16[44,64,256]{2,1,0:T(8,128)(2,1)} %constant.27.clone.table_ref.early_ref) | copy-start | bytes 4325380
  17.8 2.8 %collective-permute-start.5 = (f32[128,128]{1,0:T(8,128)S(1)}, f32[128,128]{1,0:T(8,128)S(1)}, u32[]{:S(2)}, u32[]{:S(2)}) collective-permute-start(f32[128,128]{1,0:T(8,128)S(1)} %collective-permute-done.4.mine_ref), channel_id=1, source_target_pairs={{0,32},{32,0},{64,96},{96,64},{128,160},{160,128},{192,224},{224,1... | collective-permute-start | bytes 196616 | tf_op jit(solution)/shard_map/ppermute | solution.py:434
  19.8 4.4 %collective-permute-start.1 = (f32[8,2,128]{2,1,0:T(2,128)S(1)}, f32[8,2,128]{2,1,0:T(2,128)S(1)}, u32[]{:S(2)}, u32[]{:S(2)}) collective-permute-start(f32[8,2,128]{2,1,0:T(2,128)S(1)} %pad_maximum_fusion), channel_id=1, source_target_pairs={{0,65},{1,192},{2,67},{3,194},{4,69},{5,196},{6,71},{7,198},{8,73}... | collective-permute-start | bytes 24584 | tf_op jit(solution)/shard_map/ppermute | solution.py:444
  24.2 6.4 %copy-start.6 = (f32[1,512,512]{2,1,0:T(8,128)S(1)}, f32[1,512,512]{2,1,0:T(8,128)}, u32[]{:S(2)}) copy-start(f32[1,512,512]{2,1,0:T(8,128)} %target_ref.1) | copy-start | bytes 3145732
  29.3 2.6 %collective-permute-start.6 = (f32[256,256]{1,0:T(8,128)S(1)}, f32[256,256]{1,0:T(8,128)S(1)}, u32[]{:S(2)}, u32[]{:S(2)}) collective-permute-start(f32[256,256]{1,0:T(8,128)S(1)} %get-tuple-element.59.mine_ref), channel_id=1, source_target_pairs={{0,32},{32,0},{64,96},{96,64},{128,160},{160,128},{192,224},{224,1... | collective-permute-start | bytes 786440 | tf_op jit(solution)/shard_map/ppermute | solution.py:434
  32.6 5.4 %collective-permute-start.7 = (f32[8,128]{1,0:T(8,128)S(1)}, f32[8,128]{1,0:T(8,128)S(1)}, u32[]{:S(2)}, u32[]{:S(2)}) collective-permute-start(f32[8,128]{1,0:T(8,128)S(1)} %get-tuple-element.67), channel_id=1, source_target_pairs={{0,24},{1,25},{2,26},{3,27},{4,28},{5,29},{6,30},{7,31},{8,16},{9,... | collective-permute-start | bytes 12296 | tf_op jit(solution)/shard_map/ppermute | solution.py:484
  38.0 3.8 %collective-permute-start.8 = (f32[8,128]{1,0:T(8,128)S(1)}, f32[8,128]{1,0:T(8,128)S(1)}, u32[]{:S(2)}, u32[]{:S(2)}) collective-permute-start(f32[8,128]{1,0:T(8,128)S(1)} %add.17), channel_id=1, source_target_pairs={{0,6},{1,7},{2,4},{3,5},{4,2},{5,3},{6,0},{7,1},{8,14},{9,15},{10,... | collective-permute-start | bytes 12296 | tf_op jit(solution)/shard_map/ppermute | solution.py:484
  41.8 2.5 %collective-permute-start.9 = (f32[8,128]{1,0:T(8,128)S(1)}, f32[8,128]{1,0:T(8,128)S(1)}, u32[]{:S(2)}, u32[]{:S(2)}) collective-permute-start(f32[8,128]{1,0:T(8,128)S(1)} %add.18), channel_id=1, source_target_pairs={{0,8},{1,9},{2,10},{3,11},{4,12},{5,13},{6,14},{7,15},{8,0},{9,1},... | collective-permute-start | bytes 12296 | tf_op jit(solution)/shard_map/ppermute | solution.py:484
  44.3 13.9 %copy-start.3 = (bf16[44,64,256]{2,1,0:T(8,128)(2,1)S(1)}, bf16[44,64,256]{2,1,0:T(8,128)(2,1)}, u32[]{:S(2)}) copy-start(bf16[44,64,256]{2,1,0:T(8,128)(2,1)} %constant.27.clone.table_ref.early_ref) | copy-start | bytes 4325380
  44.3 4.6 %collective-permute-start.10 = (f32[8,128]{1,0:T(8,128)S(1)}, f32[8,128]{1,0:T(8,128)S(1)}, u32[]{:S(2)}, u32[]{:S(2)}) collective-permute-start(f32[8,128]{1,0:T(8,128)S(1)} %add.19), channel_id=1, source_target_pairs={{0,2},{1,3},{2,0},{3,1},{4,6},{5,7},{6,4},{7,5},{8,10},{9,11},{10,... | collective-permute-start | bytes 12296 | tf_op jit(solution)/shard_map/ppermute | solution.py:484
  48.9 4.8 %collective-permute-start.11 = (f32[64,256]{1,0:T(8,128)S(1)}, f32[64,256]{1,0:T(8,128)S(1)}, u32[]{:S(2)}, u32[]{:S(2)}) collective-permute-start(f32[64,256]{1,0:T(8,128)S(1)} %get-tuple-element.84), channel_id=1, source_target_pairs={{0,8},{1,9},{2,10},{3,11},{4,12},{5,13},{6,14},{7,15},{8,16},{9,17... | collective-permute-start | bytes 196616 | tf_op jit(solution)/shard_map/ppermute | solution.py:470
  53.7 4.5 %collective-permute-start.12 = (f32[136,256]{1,0:T(8,128)S(1)}, f32[136,256]{1,0:T(8,128)S(1)}, u32[]{:S(2)}, u32[]{:S(2)}) collective-permute-start(f32[136,256]{1,0:T(8,128)S(1)} %rim.1.mine_ref), channel_id=1, source_target_pairs={{0,32},{32,0},{64,96},{96,64},{128,160},{160,128},{192,224},{224,1... | collective-permute-start | bytes 417800 | tf_op jit(solution)/shard_map/ppermute | solution.py:434
  58.6 1.3 %collective-permute-start.13 = (f32[72,128]{1,0:T(8,128)S(1)}, f32[72,128]{1,0:T(8,128)S(1)}, u32[]{:S(2)}, u32[]{:S(2)}) collective-permute-start(f32[72,128]{1,0:T(8,128)S(1)} %get-tuple-element.87.before_ref), channel_id=1, source_target_pairs={{0,32},{1,0},{2,1},{3,2},{4,3},{5,4},{6,5},{7,6},{8,40},{9,8},{10,... | collective-permute-start | bytes 110600 | tf_op jit(solution)/shard_map/ppermute | solution.py:459
  59.9 4.1 %collective-permute-start.14 = (f32[72,128]{1,0:T(8,128)S(1)}, f32[72,128]{1,0:T(8,128)S(1)}, u32[]{:S(2)}, u32[]{:S(2)}) collective-permute-start(f32[72,128]{1,0:T(8,128)S(1)} %collective-permute-done.13.mine_ref), channel_id=1, source_target_pairs={{0,32},{32,0},{64,96},{96,64},{128,160},{160,128},{192,224},{224,1... | collective-permute-start | bytes 110600 | tf_op jit(solution)/shard_map/ppermute | solution.py:434

commit v8 on v6

--- a/solution.py
+++ b/solution.py
@@ -521,7 +521,7 @@
     plane = pltpu.VMEM((2, W, K), F32)
     planes = (jnp.zeros((8, K), F32),) * 2
     for chip in range(CHIPS):
-        arrived = tile_swap(energies, (3, 1, 4, 2)[chip])
+        arrived = tile_swap(energies, (4, 2, 3, 1)[chip])
         last = chip == CHIPS - 1
         outs = call(
             functools.partial(adjoint_kernel, chip),

time: 65.1 us -> 64.5 us (level)
    ppermute x4, starting transfers between devices: 6.65 us -> 5.21 us  [tile_swap(): lax.ppermute(value, 'tile', [(at, partner(at)) for at in range(TROWS * TC...]
    ppermute x4, waiting for transfers between devices: 4.99 us -> 3.95 us  [tile_move(): return lax.ppermute(value, BOTH, pairs)]
    ppermute x5, starting transfers between devices: 8.47 us -> 9.34 us  [swap_cores(): return lax.ppermute(value, 'src', [(at, at ^ 1) for at in range(8)])]
  transfers between devices with their start and end apart: 15 -> 15, of which waited for: 7 -> 9; matrix products, arithmetic and copies ran while one was open for 0% -> 0% of each run, Pallas kernels for 24% -> 25%
where the time goes in v8:
time: 64.5 us; the launch traced here: 64.3 us
  starting transfers between devices  26.8 us (42%)
  Pallas kernels  23.3 us (36%)
  waiting for transfers between devices  8.14 us (13%)
  local copies, waits for them, and re-layouts  3.97 us (6%)
  other arithmetic  1.24 us (2%)
  between operations  0.82 us (1%)
    pallas_call x14, Pallas kernels, call(): pl.pallas_call(kernel, out_shape=shapes, in_specs=specs, out_specs=[pl.Bl...  23.3 us
    ppermute x5, starting transfers between devices, swap_cores(): return lax.ppermute(value, 'src', [(at, at ^ 1) for at in range(8)])  9.34 us
    ppermute x2, starting transfers between devices, chip_swap(): return lax.ppermute(value, BOTH, pairs)  6.44 us
    ppermute x4, starting transfers between devices, tile_move(): return lax.ppermute(value, BOTH, pairs)  5.82 us
    ppermute x4, starting transfers between devices, tile_swap(): lax.ppermute(value, 'tile', [(at, partner(at)) for at in range(TROWS * TC...  5.21 us
    unnamed x18, local copies, waits for them, and re-layouts  3.97 us
    ppermute x4, waiting for transfers between devices, tile_move(): return lax.ppermute(value, BOTH, pairs)  3.95 us
    ppermute x5, waiting for transfers between devices, swap_cores(): return lax.ppermute(value, 'src', [(at, at ^ 1) for at in range(8)])  3.29 us
  transfers between devices with their start and end apart: 15, of which 9 were waited for; matrix products, arithmetic and copies ran while one was open for 0% of the time, Pallas kernels for 25%

profile of v8, /device:TPU:1, one launch (start us, length us, event | category | flops | bytes accessed | tf_op | source)
XLA Modules:
  0.0 64.3 jit_solution(2074614333779543521)
XLA Ops:
  0.6 0.0 copy-start
  0.7 1.1 %select_bitcast_fusion = f32[64,512]{1,0:T(8,128)S(1)} fusion(f32[1,512,512]{2,1,0:T(8,128)} %tile_ref.1, pred[]{:T(512)S(6)} %eq.14), kind=kLoop, calls=%fused_computation | loop fusion | flops 32768 | bytes 393217 | tf_op jit(solution)/shard_map/jit(_where)/select_n | solution.py:482
  1.8 3.3 %collective-permute-start.2 = (f32[64,512]{1,0:T(8,128)S(1)}, f32[64,512]{1,0:T(8,128)S(1)}, u32[]{:S(2)}, u32[]{:S(2)}) collective-permute-start(f32[64,512]{1,0:T(8,128)S(1)} %select_bitcast_fusion), channel_id=1, source_target_pairs={{0,8},{1,9},{2,10},{3,11},{4,12},{5,13},{6,14},{7,15},{8,16},{9,17... | collective-permute-start | bytes 393224 | tf_op jit(solution)/shard_map/ppermute | solution.py:459
  5.1 1.4 %copy-done.1 = bf16[44,64,256]{2,1,0:T(8,128)(2,1)S(1)} copy-done((bf16[44,64,256]{2,1,0:T(8,128)(2,1)S(1)}, bf16[44,64,256]{2,1,0:T(8,128)(2,1)}, u32[]{:S(2)}) %copy-start.1) | copy-done | bytes 1441816
  6.4 1.2 %copy-done.4 = f32[1,512,512]{2,1,0:T(8,128)S(1)} copy-done((f32[1,512,512]{2,1,0:T(8,128)S(1)}, f32[1,512,512]{2,1,0:T(8,128)}, u32[]{:S(2)}) %copy-start.4) | copy-done | bytes 1048600
  7.6 0.6 own.1
  8.2 0.0 collective-permute-done.2.mine_ref
  8.2 0.1 collective-permute-start.3
  8.4 1.3 %collective-permute-done.3.other_ref = f32[64,512]{1,0:T(8,128)S(1)} collective-permute-done((f32[64,512]{1,0:T(8,128)S(1)}, f32[64,512]{1,0:T(8,128)S(1)}, u32[]{:S(2)}, u32[]{:S(2)}) %collective-permute-start.3) | collective-permute-done | bytes 131104 | tf_op jit(solution)/shard_map/ppermute | solution.py:434
  9.7 0.4 rows.1
  10.1 0.2 collective-permute-start.4
  10.4 0.1 convert_select_fusion.info_ref
  10.4 5.7 %collective-permute-start = (f32[4,2,128]{2,1,0:T(2,128)S(1)}, f32[4,2,128]{2,1,0:T(2,128)S(1)}, u32[]{:S(2)}, u32[]{:S(2)}) collective-permute-start(f32[4,2,128]{2,1,0:T(2,128)S(1)} %convert_select_fusion.info_ref), channel_id=1, source_target_pairs={{0,193},{1,64},{2,195},{3,66},{4,197},{5,68},{6,199},{7,70},{8,201... | collective-permute-start | bytes 12296 | tf_op jit(solution)/shard_map/ppermute | solution.py:444
  16.1 1.4 %copy-done.2 = bf16[44,64,256]{2,1,0:T(8,128)(2,1)S(1)} copy-done((bf16[44,64,256]{2,1,0:T(8,128)(2,1)S(1)}, bf16[44,64,256]{2,1,0:T(8,128)(2,1)}, u32[]{:S(2)}) %copy-start.2) | copy-done | bytes 1441816
  17.5 0.4 columns.1.basis_ref
  17.8 0.0 collective-permute-done.4.mine_ref
  17.8 1.9 %collective-permute-start.5 = (f32[128,128]{1,0:T(8,128)S(1)}, f32[128,128]{1,0:T(8,128)S(1)}, u32[]{:S(2)}, u32[]{:S(2)}) collective-permute-start(f32[128,128]{1,0:T(8,128)S(1)} %collective-permute-done.4.mine_ref), channel_id=1, source_target_pairs={{0,32},{32,0},{64,96},{96,64},{128,160},{160,128},{192,224},{224,1... | collective-permute-start | bytes 196616 | tf_op jit(solution)/shard_map/ppermute | solution.py:434
  19.8 0.0 collective-permute-done.near_ref.info_ref
  19.8 0.8 %collective-permute-start.1 = (f32[8,2,128]{2,1,0:T(2,128)S(1)}, f32[8,2,128]{2,1,0:T(2,128)S(1)}, u32[]{:S(2)}, u32[]{:S(2)}) collective-permute-start(f32[8,2,128]{2,1,0:T(2,128)S(1)} %pad_maximum_fusion), channel_id=1, source_target_pairs={{0,65},{1,192},{2,67},{3,194},{4,69},{5,196},{6,71},{7,198},{8,73}... | collective-permute-start | bytes 24584 | tf_op jit(solution)/shard_map/ppermute | solution.py:444
  20.6 0.1 collective-permute-done.5.other_ref
  20.7 3.0 %image.1 = (f32[4,256,512]{2,1,0:T(8,128)S(1)}, f32[256,256]{1,0:T(8,128)S(1)}, f32[2,256,128]{2,1,0:T(8,128)S(1)}, f32[2,256,128]{2,1,0:T(8,128)S(1)}) custom-call(f32[4,2,128]{2,1,0:T(2,128)S(1)} %convert_select_fusion.info_ref, f32[256,256]{1,0:T(8,128)S(1)} %columns.1.basis_ref, f32[128,128]{1,0:T(8,128)S(1)} %collective-permute-done.4.mine_ref, ...), custom_call_target="tpu_custom_call" | custom-call | flops 2000000000 | bytes 7409664 | tf_op jit(solution)/shard_map/image/pallas_call | solution.py:161
  23.7 0.4 collective-permute-done.1.far_ref.info_ref
  24.2 5.1 %others.1 = (f32[12,256,512]{2,1,0:T(8,128)S(1)}, f32[256,256]{1,0:T(8,128)S(1)}) custom-call(f32[4,2,128]{2,1,0:T(2,128)S(1)} %collective-permute-done.near_ref.info_ref, f32[8,2,128]{2,1,0:T(2,128)S(1)} %collective-permute-done.1.far_ref.info_ref, f32[128,128]{1,0:T(8,128)S(1)} %copy-done.5, bf16[80,64,256]{2,1,0:T(8,128)(2,1)S(1)} %copy-done, ...), custom_call_target="tpu_custom_call" | custom-call | flops 5000000000 | bytes 10039296 | tf_op jit(solution)/shard_map/others/pallas_call | solution.py:161
  29.3 1.3 %collective-permute-start.6 = (f32[256,256]{1,0:T(8,128)S(1)}, f32[256,256]{1,0:T(8,128)S(1)}, u32[]{:S(2)}, u32[]{:S(2)}) collective-permute-start(f32[256,256]{1,0:T(8,128)S(1)} %get-tuple-element.59.mine_ref), channel_id=1, source_target_pairs={{0,32},{32,0},{64,96},{96,64},{128,160},{160,128},{192,224},{224,1... | collective-permute-start | bytes 786440 | tf_op jit(solution)/shard_map/ppermute | solution.py:434
  30.6 1.3 %wanted.1.wanted_ref = f32[256,256]{1,0:T(8,128)S(1)} custom-call(f32[1,512,512]{2,1,0:T(8,128)S(1)} %copy-done.6, bf16[80,64,256]{2,1,0:T(8,128)(2,1)S(1)} %copy-done), custom_call_target="tpu_custom_call" | custom-call | flops 600000000 | bytes 3932160 | tf_op jit(solution)/shard_map/wanted/pallas_call | solution.py:161
  31.8 0.0 collective-permute-done.6.other_ref
  31.9 0.8 %residual.1 = (f32[256,256]{1,0:T(8,128)S(1)}, f32[8,128]{1,0:T(8,128)S(1)}) custom-call(f32[256,256]{1,0:T(8,128)S(1)} %get-tuple-element.59.mine_ref, f32[256,256]{1,0:T(8,128)S(1)} %collective-permute-done.6.other_ref, f32[256,256]{1,0:T(8,128)S(1)} %wanted.1.wanted_ref, f32[4,256,512]{2,1,0:T(8,128)S(1)} %get-tuple-element.62.field_ref, ...), custom_call_target="tpu_custom_call" | custom-call | flops 300000000 | bytes 5771264 | tf_op jit(solution)/shard_map/residual/pallas_call | solution.py:161
  32.6 3.1 %collective-permute-start.7 = (f32[8,128]{1,0:T(8,128)S(1)}, f32[8,128]{1,0:T(8,128)S(1)}, u32[]{:S(2)}, u32[]{:S(2)}) collective-permute-start(f32[8,128]{1,0:T(8,128)S(1)} %get-tuple-element.67), channel_id=1, source_target_pairs={{0,24},{1,25},{2,26},{3,27},{4,28},{5,29},{6,30},{7,31},{8,16},{9,... | collective-permute-start | bytes 12296 | tf_op jit(solution)/shard_map/ppermute | solution.py:473
  35.8 2.2 %adjoint.4 = (f32[2,256,128]{2,1,0:T(8,128)S(1)}, f32[2,256,128]{2,1,0:T(8,128)S(1)}) custom-call(f32[4,2,128]{2,1,0:T(2,128)S(1)} %convert_select_fusion.info_ref, f32[256,256]{1,0:T(8,128)S(1)} %get-tuple-element.63.residual_ref, f32[4,256,512]{2,1,0:T(8,128)S(1)} %get-tuple-element.62.field_ref, f32[128,128]{1,0:T(8,128)S(1)} %copy-done.5, ...), custom_call_target="tpu_custom_call" | custom-call | flops 1500000000 | bytes 7024640 | tf_op jit(solution)/shard_map/adjoint/pallas_call | solution.py:161
  38.0 0.0 collective-permute-done.7
  38.0 1.2 %collective-permute-start.8 = (f32[8,128]{1,0:T(8,128)S(1)}, f32[8,128]{1,0:T(8,128)S(1)}, u32[]{:S(2)}, u32[]{:S(2)}) collective-permute-start(f32[8,128]{1,0:T(8,128)S(1)} %add.17), channel_id=1, source_target_pairs={{0,6},{1,7},{2,4},{3,5},{4,2},{5,3},{6,0},{7,1},{8,14},{9,15},{10,... | collective-permute-start | bytes 12296 | tf_op jit(solution)/shard_map/ppermute | solution.py:473
  39.2 2.2 %adjoint.5 = (f32[2,256,128]{2,1,0:T(8,128)S(1)}, f32[2,256,128]{2,1,0:T(8,128)S(1)}) custom-call(f32[4,2,128]{2,1,0:T(2,128)S(1)} %collective-permute-done.near_ref.info_ref, f32[256,256]{1,0:T(8,128)S(1)} %get-tuple-element.63.residual_ref, f32[12,256,512]{2,1,0:T(8,128)S(1)} %get-tuple-element.64.field_ref, f32[128,128]{1,0:T(8,128)S(1)} %copy-done.5, ...), custom_call_target="tpu_custom_call" | custom-call | flops 1500000000 | bytes 11735040 | tf_op jit(solution)/shard_map/adjoint/pallas_call | solution.py:161
  41.5 0.3 collective-permute-done.8
  41.8 0.0 collective-permute-start.9
  41.8 2.3 %adjoint.6 = (f32[2,256,128]{2,1,0:T(8,128)S(1)}, f32[2,256,128]{2,1,0:T(8,128)S(1)}) custom-call(f32[8,2,128]{2,1,0:T(2,128)S(1)} %collective-permute-done.1.far_ref.info_ref, f32[256,256]{1,0:T(8,128)S(1)} %get-tuple-element.63.residual_ref, f32[12,256,512]{2,1,0:T(8,128)S(1)} %get-tuple-element.64.field_ref, f32[128,128]{1,0:T(8,128)S(1)} %copy-done.5, ...), custom_call_target="tpu_custom_call" | custom-call | flops 1500000000 | bytes 11739136 | tf_op jit(solution)/shard_map/adjoint/pallas_call | solution.py:161
  44.1 0.1 collective-permute-done.9
  44.3 0.9 %collective-permute-start.10 = (f32[8,128]{1,0:T(8,128)S(1)}, f32[8,128]{1,0:T(8,128)S(1)}, u32[]{:S(2)}, u32[]{:S(2)}) collective-permute-start(f32[8,128]{1,0:T(8,128)S(1)} %add.19), channel_id=1, source_target_pairs={{0,2},{1,3},{2,0},{3,1},{4,6},{5,7},{6,4},{7,5},{8,10},{9,11},{10,... | collective-permute-start | bytes 12296 | tf_op jit(solution)/shard_map/ppermute | solution.py:473
  45.1 3.7 %adjoint.7 = (f32[128,256]{1,0:T(8,128)S(1)}, f32[64,256]{1,0:T(8,128)S(1)}) custom-call(f32[8,2,128]{2,1,0:T(2,128)S(1)} %collective-permute-done.1.far_ref.info_ref, f32[256,256]{1,0:T(8,128)S(1)} %get-tuple-element.63.residual_ref, f32[12,256,512]{2,1,0:T(8,128)S(1)} %get-tuple-element.64.field_ref, f32[128,128]{1,0:T(8,128)S(1)} %copy-done.5, ...), custom_call_target="tpu_custom_call" | custom-call | flops 1500000000 | bytes 11411456 | tf_op jit(solution)/shard_map/adjoint/pallas_call | solution.py:161
  48.9 1.5 %collective-permute-start.11 = (f32[64,256]{1,0:T(8,128)S(1)}, f32[64,256]{1,0:T(8,128)S(1)}, u32[]{:S(2)}, u32[]{:S(2)}) collective-permute-start(f32[64,256]{1,0:T(8,128)S(1)} %get-tuple-element.84), channel_id=1, source_target_pairs={{0,8},{1,9},{2,10},{3,11},{4,12},{5,13},{6,14},{7,15},{8,16},{9,17... | collective-permute-start | bytes 196616 | tf_op jit(solution)/shard_map/ppermute | solution.py:459
  50.4 2.9 %collective-permute-done.11.rim_ref = f32[64,256]{1,0:T(8,128)S(1)} collective-permute-done((f32[64,256]{1,0:T(8,128)S(1)}, f32[64,256]{1,0:T(8,128)S(1)}, u32[]{:S(2)}, u32[]{:S(2)}) %collective-permute-start.11) | collective-permute-done | bytes 65568 | tf_op jit(solution)/shard_map/ppermute | solution.py:459
  53.3 3.5 %collective-permute-start.12 = (f32[136,256]{1,0:T(8,128)S(1)}, f32[136,256]{1,0:T(8,128)S(1)}, u32[]{:S(2)}, u32[]{:S(2)}) collective-permute-start(f32[136,256]{1,0:T(8,128)S(1)} %rim.1.mine_ref), channel_id=1, source_target_pairs={{0,32},{32,0},{64,96},{96,64},{128,160},{160,128},{192,224},{224,1... | collective-permute-start | bytes 417800 | tf_op jit(solution)/shard_map/ppermute | solution.py:434
  56.8 1.0 %collective-permute-done.12.other_ref = f32[136,256]{1,0:T(8,128)S(1)} collective-permute-done((f32[136,256]{1,0:T(8,128)S(1)}, f32[136,256]{1,0:T(8,128)S(1)}, u32[]{:S(2)}, u32[]{:S(2)}) %collective-permute-start.12) | collective-permute-done | bytes 139296 | tf_op jit(solution)/shard_map/ppermute | solution.py:434
  57.8 0.4 pixels.1
  58.2 0.8 %collective-permute-start.13 = (f32[72,128]{1,0:T(8,128)S(1)}, f32[72,128]{1,0:T(8,128)S(1)}, u32[]{:S(2)}, u32[]{:S(2)}) collective-permute-start(f32[72,128]{1,0:T(8,128)S(1)} %get-tuple-element.87.before_ref), channel_id=1, source_target_pairs={{0,32},{1,0},{2,1},{3,2},{4,3},{5,4},{6,5},{7,6},{8,40},{9,8},{10,... | collective-permute-start | bytes 110600 | tf_op jit(solution)/shard_map/ppermute | solution.py:459
  59.0 1.1 %collective-permute-done.13.mine_ref = f32[72,128]{1,0:T(8,128)S(1)} collective-permute-done((f32[72,128]{1,0:T(8,128)S(1)}, f32[72,128]{1,0:T(8,128)S(1)}, u32[]{:S(2)}, u32[]{:S(2)}) %collective-permute-start.13) | collective-permute-done | bytes 36896 | tf_op jit(solution)/shard_map/ppermute | solution.py:459
  60.0 2.6 %collective-permute-start.14 = (f32[72,128]{1,0:T(8,128)S(1)}, f32[72,128]{1,0:T(8,128)S(1)}, u32[]{:S(2)}, u32[]{:S(2)}) collective-permute-start(f32[72,128]{1,0:T(8,128)S(1)} %collective-permute-done.13.mine_ref), channel_id=1, source_target_pairs={{0,32},{32,0},{64,96},{96,64},{128,160},{160,128},{192,224},{224,1... | collective-permute-start | bytes 110600 | tf_op jit(solution)/shard_map/ppermute | solution.py:434
  62.6 0.9 %collective-permute-done.14.other_ref = f32[72,128]{1,0:T(8,128)S(1)} collective-permute-done((f32[72,128]{1,0:T(8,128)S(1)}, f32[72,128]{1,0:T(8,128)S(1)}, u32[]{:S(2)}, u32[]{:S(2)}) %collective-permute-start.14) | collective-permute-done | bytes 36896 | tf_op jit(solution)/shard_map/ppermute | solution.py:434
  63.5 0.8 %join.1 = (f32[1,64,512]{2,1,0:T(8,128)}, f32[4]{0:T(128)}) custom-call(f32[64,512]{1,0:T(8,128)S(1)} %get-tuple-element.86.inner_ref, f32[72,128]{1,0:T(8,128)S(1)} %get-tuple-element.87.before_ref, f32[72,128]{1,0:T(8,128)S(1)} %collective-permute-done.13.mine_ref, f32[72,128]{1,0:T(8,128)S(1)} %collective-permute-done.14.other_ref), custom_call_target="tpu_custom_call" | custom-call | flops 32768 | bytes 372752 | tf_op jit(solution)/shard_map/join/pallas_call | solution.py:161
  (23 shorter events, 0.1 us)
Async XLA Ops:
  0.6 15.5 %copy-start = (bf16[80,64,256]{2,1,0:T(8,128)(2,1)S(1)}, bf16[80,64,256]{2,1,0:T(8,128)(2,1)}, u32[]{:S(2)}) copy-start(bf16[80,64,256]{2,1,0:T(8,128)(2,1)} %constant.28.clone._.table_ref) | copy-start | bytes 7864324
  1.8 6.4 %collective-permute-start.2 = (f32[64,512]{1,0:T(8,128)S(1)}, f32[64,512]{1,0:T(8,128)S(1)}, u32[]{:S(2)}, u32[]{:S(2)}) collective-permute-start(f32[64,512]{1,0:T(8,128)S(1)} %select_bitcast_fusion), channel_id=1, source_target_pairs={{0,8},{1,9},{2,10},{3,11},{4,12},{5,13},{6,14},{7,15},{8,16},{9,17... | collective-permute-start | bytes 393224 | tf_op jit(solution)/shard_map/ppermute | solution.py:459
  5.1 1.4 %copy-start.1 = (bf16[44,64,256]{2,1,0:T(8,128)(2,1)S(1)}, bf16[44,64,256]{2,1,0:T(8,128)(2,1)}, u32[]{:S(2)}) copy-start(bf16[44,64,256]{2,1,0:T(8,128)(2,1)} %constant.27.clone.table_ref.early_ref) | copy-start | bytes 4325380
  6.4 1.2 %copy-start.4 = (f32[1,512,512]{2,1,0:T(8,128)S(1)}, f32[1,512,512]{2,1,0:T(8,128)}, u32[]{:S(2)}) copy-start(f32[1,512,512]{2,1,0:T(8,128)} %tile_ref.1) | copy-start | bytes 3145732
  7.6 2.7 %copy-start.7 = (s32[4,2,128]{2,1,0:T(2,128)S(1)}, s32[4,2,128]{2,1,0:T(2,128)}, u32[]{:S(2)}) copy-start(s32[4,2,128]{2,1,0:T(2,128)} %param.11) | copy-start | bytes 12292
  7.6 2.7 %copy-start.8 = (f32[4]{0:T(128)S(1)}, f32[4]{0:T(128)}, u32[]{:S(2)}) copy-start(f32[4]{0:T(128)} %param.10) | copy-start | bytes 52
  8.2 1.4 %collective-permute-start.3 = (f32[64,512]{1,0:T(8,128)S(1)}, f32[64,512]{1,0:T(8,128)S(1)}, u32[]{:S(2)}, u32[]{:S(2)}) collective-permute-start(f32[64,512]{1,0:T(8,128)S(1)} %collective-permute-done.2.mine_ref), channel_id=1, source_target_pairs={{0,32},{32,0},{64,96},{96,64},{128,160},{160,128},{192,224},{224,1... | collective-permute-start | bytes 393224 | tf_op jit(solution)/shard_map/ppermute | solution.py:434
  9.7 11.0 %copy-start.5 = (f32[128,128]{1,0:T(8,128)S(1)}, f32[128,128]{1,0:T(8,128)}, u32[]{:S(2)}) copy-start(f32[128,128]{1,0:T(8,128)} %gain_ref.11) | copy-start | bytes 196612
  10.1 7.7 %collective-permute-start.4 = (f32[128,128]{1,0:T(8,128)S(1)}, f32[128,128]{1,0:T(8,128)S(1)}, u32[]{:S(2)}, u32[]{:S(2)}) collective-permute-start(f32[128,128]{1,0:T(8,128)S(1)} %get-tuple-element.52), channel_id=1, source_target_pairs={{0,1},{1,2},{2,3},{3,4},{4,5},{5,6},{6,7},{7,39},{8,9},{9,10},{10,... | collective-permute-start | bytes 196616 | tf_op jit(solution)/shard_map/ppermute | solution.py:459
  10.4 9.3 %collective-permute-start = (f32[4,2,128]{2,1,0:T(2,128)S(1)}, f32[4,2,128]{2,1,0:T(2,128)S(1)}, u32[]{:S(2)}, u32[]{:S(2)}) collective-permute-start(f32[4,2,128]{2,1,0:T(2,128)S(1)} %convert_select_fusion.info_ref), channel_id=1, source_target_pairs={{0,193},{1,64},{2,195},{3,66},{4,197},{5,68},{6,199},{7,70},{8,201... | collective-permute-start | bytes 12296 | tf_op jit(solution)/shard_map/ppermute | solution.py:444
  16.1 1.4 %copy-start.2 = (bf16[44,64,256]{2,1,0:T(8,128)(2,1)S(1)}, bf16[44,64,256]{2,1,0:T(8,128)(2,1)}, u32[]{:S(2)}) copy-start(bf16[44,64,256]{2,1,0:T(8,128)(2,1)} %constant.27.clone.table_ref.early_ref) | copy-start | bytes 4325380
  17.8 2.8 %collective-permute-start.5 = (f32[128,128]{1,0:T(8,128)S(1)}, f32[128,128]{1,0:T(8,128)S(1)}, u32[]{:S(2)}, u32[]{:S(2)}) collective-permute-start(f32[128,128]{1,0:T(8,128)S(1)} %collective-permute-done.4.mine_ref), channel_id=1, source_target_pairs={{0,32},{32,0},{64,96},{96,64},{128,160},{160,128},{192,224},{224,1... | collective-permute-start | bytes 196616 | tf_op jit(solution)/shard_map/ppermute | solution.py:434
  19.8 4.4 %collective-permute-start.1 = (f32[8,2,128]{2,1,0:T(2,128)S(1)}, f32[8,2,128]{2,1,0:T(2,128)S(1)}, u32[]{:S(2)}, u32[]{:S(2)}) collective-permute-start(f32[8,2,128]{2,1,0:T(2,128)S(1)} %pad_maximum_fusion), channel_id=1, source_target_pairs={{0,65},{1,192},{2,67},{3,194},{4,69},{5,196},{6,71},{7,198},{8,73}... | collective-permute-start | bytes 24584 | tf_op jit(solution)/shard_map/ppermute | solution.py:444
  24.2 6.4 %copy-start.6 = (f32[1,512,512]{2,1,0:T(8,128)S(1)}, f32[1,512,512]{2,1,0:T(8,128)}, u32[]{:S(2)}) copy-start(f32[1,512,512]{2,1,0:T(8,128)} %target_ref.1) | copy-start | bytes 3145732
  29.3 2.6 %collective-permute-start.6 = (f32[256,256]{1,0:T(8,128)S(1)}, f32[256,256]{1,0:T(8,128)S(1)}, u32[]{:S(2)}, u32[]{:S(2)}) collective-permute-start(f32[256,256]{1,0:T(8,128)S(1)} %get-tuple-element.59.mine_ref), channel_id=1, source_target_pairs={{0,32},{32,0},{64,96},{96,64},{128,160},{160,128},{192,224},{224,1... | collective-permute-start | bytes 786440 | tf_op jit(solution)/shard_map/ppermute | solution.py:434
  32.6 5.4 %collective-permute-start.7 = (f32[8,128]{1,0:T(8,128)S(1)}, f32[8,128]{1,0:T(8,128)S(1)}, u32[]{:S(2)}, u32[]{:S(2)}) collective-permute-start(f32[8,128]{1,0:T(8,128)S(1)} %get-tuple-element.67), channel_id=1, source_target_pairs={{0,24},{1,25},{2,26},{3,27},{4,28},{5,29},{6,30},{7,31},{8,16},{9,... | collective-permute-start | bytes 12296 | tf_op jit(solution)/shard_map/ppermute | solution.py:473
  38.0 3.8 %collective-permute-start.8 = (f32[8,128]{1,0:T(8,128)S(1)}, f32[8,128]{1,0:T(8,128)S(1)}, u32[]{:S(2)}, u32[]{:S(2)}) collective-permute-start(f32[8,128]{1,0:T(8,128)S(1)} %add.17), channel_id=1, source_target_pairs={{0,6},{1,7},{2,4},{3,5},{4,2},{5,3},{6,0},{7,1},{8,14},{9,15},{10,... | collective-permute-start | bytes 12296 | tf_op jit(solution)/shard_map/ppermute | solution.py:473
  41.8 2.5 %collective-permute-start.9 = (f32[8,128]{1,0:T(8,128)S(1)}, f32[8,128]{1,0:T(8,128)S(1)}, u32[]{:S(2)}, u32[]{:S(2)}) collective-permute-start(f32[8,128]{1,0:T(8,128)S(1)} %add.18), channel_id=1, source_target_pairs={{0,8},{1,9},{2,10},{3,11},{4,12},{5,13},{6,14},{7,15},{8,0},{9,1},... | collective-permute-start | bytes 12296 | tf_op jit(solution)/shard_map/ppermute | solution.py:473
  44.3 13.5 %copy-start.3 = (bf16[44,64,256]{2,1,0:T(8,128)(2,1)S(1)}, bf16[44,64,256]{2,1,0:T(8,128)(2,1)}, u32[]{:S(2)}) copy-start(bf16[44,64,256]{2,1,0:T(8,128)(2,1)} %constant.27.clone.table_ref.early_ref) | copy-start | bytes 4325380
  44.3 4.6 %collective-permute-start.10 = (f32[8,128]{1,0:T(8,128)S(1)}, f32[8,128]{1,0:T(8,128)S(1)}, u32[]{:S(2)}, u32[]{:S(2)}) collective-permute-start(f32[8,128]{1,0:T(8,128)S(1)} %add.19), channel_id=1, source_target_pairs={{0,2},{1,3},{2,0},{3,1},{4,6},{5,7},{6,4},{7,5},{8,10},{9,11},{10,... | collective-permute-start | bytes 12296 | tf_op jit(solution)/shard_map/ppermute | solution.py:473
  48.9 4.4 %collective-permute-start.11 = (f32[64,256]{1,0:T(8,128)S(1)}, f32[64,256]{1,0:T(8,128)S(1)}, u32[]{:S(2)}, u32[]{:S(2)}) collective-permute-start(f32[64,256]{1,0:T(8,128)S(1)} %get-tuple-element.84), channel_id=1, source_target_pairs={{0,8},{1,9},{2,10},{3,11},{4,12},{5,13},{6,14},{7,15},{8,16},{9,17... | collective-permute-start | bytes 196616 | tf_op jit(solution)/shard_map/ppermute | solution.py:459
  53.3 4.5 %collective-permute-start.12 = (f32[136,256]{1,0:T(8,128)S(1)}, f32[136,256]{1,0:T(8,128)S(1)}, u32[]{:S(2)}, u32[]{:S(2)}) collective-permute-start(f32[136,256]{1,0:T(8,128)S(1)} %rim.1.mine_ref), channel_id=1, source_target_pairs={{0,32},{32,0},{64,96},{96,64},{128,160},{160,128},{192,224},{224,1... | collective-permute-start | bytes 417800 | tf_op jit(solution)/shard_map/ppermute | solution.py:434
  58.2 1.9 %collective-permute-start.13 = (f32[72,128]{1,0:T(8,128)S(1)}, f32[72,128]{1,0:T(8,128)S(1)}, u32[]{:S(2)}, u32[]{:S(2)}) collective-permute-start(f32[72,128]{1,0:T(8,128)S(1)} %get-tuple-element.87.before_ref), channel_id=1, source_target_pairs={{0,32},{1,0},{2,1},{3,2},{4,3},{5,4},{6,5},{7,6},{8,40},{9,8},{10,... | collective-permute-start | bytes 110600 | tf_op jit(solution)/shard_map/ppermute | solution.py:459
  60.0 3.4 %collective-permute-start.14 = (f32[72,128]{1,0:T(8,128)S(1)}, f32[72,128]{1,0:T(8,128)S(1)}, u32[]{:S(2)}, u32[]{:S(2)}) collective-permute-start(f32[72,128]{1,0:T(8,128)S(1)} %collective-permute-done.13.mine_ref), channel_id=1, source_target_pairs={{0,32},{32,0},{64,96},{96,64},{128,160},{160,128},{192,224},{224,1... | collective-permute-start | bytes 110600 | tf_op jit(solution)/shard_map/ppermute | solution.py:434

commit v9 on v8

--- a/solution.py
+++ b/solution.py
@@ -521,7 +521,7 @@
     plane = pltpu.VMEM((2, W, K), F32)
     planes = (jnp.zeros((8, K), F32),) * 2
     for chip in range(CHIPS):
-        arrived = tile_swap(energies, (4, 2, 3, 1)[chip])
+        arrived = tile_swap(energies, (2, 4, 1, 3)[chip])
         last = chip == CHIPS - 1
         outs = call(
             functools.partial(adjoint_kernel, chip),

time: 64.5 us -> 64.3 us (level)
  transfers between devices with their start and end apart: 15 -> 15, of which waited for: 9 -> 8; matrix products, arithmetic and copies ran while one was open for 0% -> 0% of each run, Pallas kernels for 25% -> 25%
where the time goes in v9:
time: 64.3 us; the launch traced here: 64.1 us
  starting transfers between devices  26.7 us (42%)
  Pallas kernels  23.3 us (36%)
  waiting for transfers between devices  8 us (12%)
  local copies, waits for them, and re-layouts  3.98 us (6%)
  other arithmetic  1.24 us (2%)
  between operations  0.85 us (1%)
    pallas_call x14, Pallas kernels, call(): pl.pallas_call(kernel, out_shape=shapes, in_specs=specs, out_specs=[pl.Bl...  23.3 us
    ppermute x5, starting transfers between devices, swap_cores(): return lax.ppermute(value, 'src', [(at, at ^ 1) for at in range(8)])  9.07 us
    ppermute x2, starting transfers between devices, chip_swap(): return lax.ppermute(value, BOTH, pairs)  6.44 us
    ppermute x4, starting transfers between devices, tile_move(): return lax.ppermute(value, BOTH, pairs)  5.91 us
    ppermute x4, starting transfers between devices, tile_swap(): lax.ppermute(value, 'tile', [(at, partner(at)) for at in range(TROWS * TC...  5.29 us
    unnamed x18, local copies, waits for them, and re-layouts  3.98 us
    ppermute x4, waiting for transfers between devices, tile_move(): return lax.ppermute(value, BOTH, pairs)  3.95 us
    ppermute x5, waiting for transfers between devices, swap_cores(): return lax.ppermute(value, 'src', [(at, at ^ 1) for at in range(8)])  3.29 us
  transfers between devices with their start and end apart: 15, of which 8 were waited for; matrix products, arithmetic and copies ran while one was open for 0% of the time, Pallas kernels for 25%

profile of v9, /device:TPU:1, one launch (start us, length us, event | category | flops | bytes accessed | tf_op | source)
XLA Modules:
  0.0 64.1 jit_solution(945464006786966582)
XLA Ops:
  0.6 0.0 copy-start
  0.7 1.1 %select_bitcast_fusion = f32[64,512]{1,0:T(8,128)S(1)} fusion(f32[1,512,512]{2,1,0:T(8,128)} %tile_ref.1, pred[]{:T(512)S(6)} %eq.14), kind=kLoop, calls=%fused_computation | loop fusion | flops 32768 | bytes 393217 | tf_op jit(solution)/shard_map/jit(_where)/select_n | solution.py:482
  1.8 3.3 %collective-permute-start.2 = (f32[64,512]{1,0:T(8,128)S(1)}, f32[64,512]{1,0:T(8,128)S(1)}, u32[]{:S(2)}, u32[]{:S(2)}) collective-permute-start(f32[64,512]{1,0:T(8,128)S(1)} %select_bitcast_fusion), channel_id=1, source_target_pairs={{0,8},{1,9},{2,10},{3,11},{4,12},{5,13},{6,14},{7,15},{8,16},{9,17... | collective-permute-start | bytes 393224 | tf_op jit(solution)/shard_map/ppermute | solution.py:459
  5.1 1.4 %copy-done.1 = bf16[44,64,256]{2,1,0:T(8,128)(2,1)S(1)} copy-done((bf16[44,64,256]{2,1,0:T(8,128)(2,1)S(1)}, bf16[44,64,256]{2,1,0:T(8,128)(2,1)}, u32[]{:S(2)}) %copy-start.1) | copy-done | bytes 1441816
  6.4 1.2 %copy-done.4 = f32[1,512,512]{2,1,0:T(8,128)S(1)} copy-done((f32[1,512,512]{2,1,0:T(8,128)S(1)}, f32[1,512,512]{2,1,0:T(8,128)}, u32[]{:S(2)}) %copy-start.4) | copy-done | bytes 1048600
  7.6 0.6 own.1
  8.2 0.0 collective-permute-done.2.mine_ref
  8.2 0.1 collective-permute-start.3
  8.4 1.3 %collective-permute-done.3.other_ref = f32[64,512]{1,0:T(8,128)S(1)} collective-permute-done((f32[64,512]{1,0:T(8,128)S(1)}, f32[64,512]{1,0:T(8,128)S(1)}, u32[]{:S(2)}, u32[]{:S(2)}) %collective-permute-start.3) | collective-permute-done | bytes 131104 | tf_op jit(solution)/shard_map/ppermute | solution.py:434
  9.7 0.4 rows.1
  10.1 0.2 collective-permute-start.4
  10.4 0.1 convert_select_fusion.info_ref
  10.4 5.7 %collective-permute-start = (f32[4,2,128]{2,1,0:T(2,128)S(1)}, f32[4,2,128]{2,1,0:T(2,128)S(1)}, u32[]{:S(2)}, u32[]{:S(2)}) collective-permute-start(f32[4,2,128]{2,1,0:T(2,128)S(1)} %convert_select_fusion.info_ref), channel_id=1, source_target_pairs={{0,193},{1,64},{2,195},{3,66},{4,197},{5,68},{6,199},{7,70},{8,201... | collective-permute-start | bytes 12296 | tf_op jit(solution)/shard_map/ppermute | solution.py:444
  16.1 1.4 %copy-done.2 = bf16[44,64,256]{2,1,0:T(8,128)(2,1)S(1)} copy-done((bf16[44,64,256]{2,1,0:T(8,128)(2,1)S(1)}, bf16[44,64,256]{2,1,0:T(8,128)(2,1)}, u32[]{:S(2)}) %copy-start.2) | copy-done | bytes 1441816
  17.5 0.4 columns.1.basis_ref
  17.8 0.0 collective-permute-done.4.mine_ref
  17.8 1.9 %collective-permute-start.5 = (f32[128,128]{1,0:T(8,128)S(1)}, f32[128,128]{1,0:T(8,128)S(1)}, u32[]{:S(2)}, u32[]{:S(2)}) collective-permute-start(f32[128,128]{1,0:T(8,128)S(1)} %collective-permute-done.4.mine_ref), channel_id=1, source_target_pairs={{0,32},{32,0},{64,96},{96,64},{128,160},{160,128},{192,224},{224,1... | collective-permute-start | bytes 196616 | tf_op jit(solution)/shard_map/ppermute | solution.py:434
  19.8 0.0 collective-permute-done.near_ref.info_ref
  19.8 0.8 %collective-permute-start.1 = (f32[8,2,128]{2,1,0:T(2,128)S(1)}, f32[8,2,128]{2,1,0:T(2,128)S(1)}, u32[]{:S(2)}, u32[]{:S(2)}) collective-permute-start(f32[8,2,128]{2,1,0:T(2,128)S(1)} %pad_maximum_fusion), channel_id=1, source_target_pairs={{0,65},{1,192},{2,67},{3,194},{4,69},{5,196},{6,71},{7,198},{8,73}... | collective-permute-start | bytes 24584 | tf_op jit(solution)/shard_map/ppermute | solution.py:444
  20.6 0.1 collective-permute-done.5.other_ref
  20.7 3.0 %image.1 = (f32[4,256,512]{2,1,0:T(8,128)S(1)}, f32[256,256]{1,0:T(8,128)S(1)}, f32[2,256,128]{2,1,0:T(8,128)S(1)}, f32[2,256,128]{2,1,0:T(8,128)S(1)}) custom-call(f32[4,2,128]{2,1,0:T(2,128)S(1)} %convert_select_fusion.info_ref, f32[256,256]{1,0:T(8,128)S(1)} %columns.1.basis_ref, f32[128,128]{1,0:T(8,128)S(1)} %collective-permute-done.4.mine_ref, ...), custom_call_target="tpu_custom_call" | custom-call | flops 2000000000 | bytes 7409664 | tf_op jit(solution)/shard_map/image/pallas_call | solution.py:161
  23.7 0.5 collective-permute-done.1.far_ref.info_ref
  24.2 5.1 %others.1 = (f32[12,256,512]{2,1,0:T(8,128)S(1)}, f32[256,256]{1,0:T(8,128)S(1)}) custom-call(f32[4,2,128]{2,1,0:T(2,128)S(1)} %collective-permute-done.near_ref.info_ref, f32[8,2,128]{2,1,0:T(2,128)S(1)} %collective-permute-done.1.far_ref.info_ref, f32[128,128]{1,0:T(8,128)S(1)} %copy-done.5, bf16[80,64,256]{2,1,0:T(8,128)(2,1)S(1)} %copy-done, ...), custom_call_target="tpu_custom_call" | custom-call | flops 5000000000 | bytes 10039296 | tf_op jit(solution)/shard_map/others/pallas_call | solution.py:161
  29.3 1.3 %collective-permute-start.6 = (f32[256,256]{1,0:T(8,128)S(1)}, f32[256,256]{1,0:T(8,128)S(1)}, u32[]{:S(2)}, u32[]{:S(2)}) collective-permute-start(f32[256,256]{1,0:T(8,128)S(1)} %get-tuple-element.59.mine_ref), channel_id=1, source_target_pairs={{0,32},{32,0},{64,96},{96,64},{128,160},{160,128},{192,224},{224,1... | collective-permute-start | bytes 786440 | tf_op jit(solution)/shard_map/ppermute | solution.py:434
  30.5 1.3 %wanted.1.wanted_ref = f32[256,256]{1,0:T(8,128)S(1)} custom-call(f32[1,512,512]{2,1,0:T(8,128)S(1)} %copy-done.6, bf16[80,64,256]{2,1,0:T(8,128)(2,1)S(1)} %copy-done), custom_call_target="tpu_custom_call" | custom-call | flops 600000000 | bytes 3932160 | tf_op jit(solution)/shard_map/wanted/pallas_call | solution.py:161
  31.8 0.0 collective-permute-done.6.other_ref
  31.8 0.8 %residual.1 = (f32[256,256]{1,0:T(8,128)S(1)}, f32[8,128]{1,0:T(8,128)S(1)}) custom-call(f32[256,256]{1,0:T(8,128)S(1)} %get-tuple-element.59.mine_ref, f32[256,256]{1,0:T(8,128)S(1)} %collective-permute-done.6.other_ref, f32[256,256]{1,0:T(8,128)S(1)} %wanted.1.wanted_ref, f32[4,256,512]{2,1,0:T(8,128)S(1)} %get-tuple-element.62.field_ref, ...), custom_call_target="tpu_custom_call" | custom-call | flops 300000000 | bytes 5771264 | tf_op jit(solution)/shard_map/residual/pallas_call | solution.py:161
  32.6 1.4 %collective-permute-start.7 = (f32[8,128]{1,0:T(8,128)S(1)}, f32[8,128]{1,0:T(8,128)S(1)}, u32[]{:S(2)}, u32[]{:S(2)}) collective-permute-start(f32[8,128]{1,0:T(8,128)S(1)} %get-tuple-element.67), channel_id=1, source_target_pairs={{0,6},{1,7},{2,4},{3,5},{4,2},{5,3},{6,0},{7,1},{8,14},{9,15},{10,... | collective-permute-start | bytes 12296 | tf_op jit(solution)/shard_map/ppermute | solution.py:473
  34.0 2.2 %adjoint.4 = (f32[2,256,128]{2,1,0:T(8,128)S(1)}, f32[2,256,128]{2,1,0:T(8,128)S(1)}) custom-call(f32[4,2,128]{2,1,0:T(2,128)S(1)} %convert_select_fusion.info_ref, f32[256,256]{1,0:T(8,128)S(1)} %get-tuple-element.63.residual_ref, f32[4,256,512]{2,1,0:T(8,128)S(1)} %get-tuple-element.62.field_ref, f32[128,128]{1,0:T(8,128)S(1)} %copy-done.5, ...), custom_call_target="tpu_custom_call" | custom-call | flops 1500000000 | bytes 7024640 | tf_op jit(solution)/shard_map/adjoint/pallas_call | solution.py:161
  36.3 0.3 collective-permute-done.7
  36.6 2.9 %collective-permute-start.8 = (f32[8,128]{1,0:T(8,128)S(1)}, f32[8,128]{1,0:T(8,128)S(1)}, u32[]{:S(2)}, u32[]{:S(2)}) collective-permute-start(f32[8,128]{1,0:T(8,128)S(1)} %add.17), channel_id=1, source_target_pairs={{0,24},{1,25},{2,26},{3,27},{4,28},{5,29},{6,30},{7,31},{8,16},{9,... | collective-permute-start | bytes 12296 | tf_op jit(solution)/shard_map/ppermute | solution.py:473
  39.4 2.2 %adjoint.5 = (f32[2,256,128]{2,1,0:T(8,128)S(1)}, f32[2,256,128]{2,1,0:T(8,128)S(1)}) custom-call(f32[4,2,128]{2,1,0:T(2,128)S(1)} %collective-permute-done.near_ref.info_ref, f32[256,256]{1,0:T(8,128)S(1)} %get-tuple-element.63.residual_ref, f32[12,256,512]{2,1,0:T(8,128)S(1)} %get-tuple-element.64.field_ref, f32[128,128]{1,0:T(8,128)S(1)} %copy-done.5, ...), custom_call_target="tpu_custom_call" | custom-call | flops 1500000000 | bytes 11735040 | tf_op jit(solution)/shard_map/adjoint/pallas_call | solution.py:161
  41.7 0.0 collective-permute-done.8
  41.7 1.0 %collective-permute-start.9 = (f32[8,128]{1,0:T(8,128)S(1)}, f32[8,128]{1,0:T(8,128)S(1)}, u32[]{:S(2)}, u32[]{:S(2)}) collective-permute-start(f32[8,128]{1,0:T(8,128)S(1)} %add.18), channel_id=1, source_target_pairs={{0,2},{1,3},{2,0},{3,1},{4,6},{5,7},{6,4},{7,5},{8,10},{9,11},{10,... | collective-permute-start | bytes 12296 | tf_op jit(solution)/shard_map/ppermute | solution.py:473
  42.7 2.3 %adjoint.6 = (f32[2,256,128]{2,1,0:T(8,128)S(1)}, f32[2,256,128]{2,1,0:T(8,128)S(1)}) custom-call(f32[8,2,128]{2,1,0:T(2,128)S(1)} %collective-permute-done.1.far_ref.info_ref, f32[256,256]{1,0:T(8,128)S(1)} %get-tuple-element.63.residual_ref, f32[12,256,512]{2,1,0:T(8,128)S(1)} %get-tuple-element.64.field_ref, f32[128,128]{1,0:T(8,128)S(1)} %copy-done.5, ...), custom_call_target="tpu_custom_call" | custom-call | flops 1500000000 | bytes 11739136 | tf_op jit(solution)/shard_map/adjoint/pallas_call | solution.py:161
  45.0 0.0 copy-start.3
  45.0 0.1 collective-permute-start.10
  45.1 3.7 %adjoint.7 = (f32[128,256]{1,0:T(8,128)S(1)}, f32[64,256]{1,0:T(8,128)S(1)}) custom-call(f32[8,2,128]{2,1,0:T(2,128)S(1)} %collective-permute-done.1.far_ref.info_ref, f32[256,256]{1,0:T(8,128)S(1)} %get-tuple-element.63.residual_ref, f32[12,256,512]{2,1,0:T(8,128)S(1)} %get-tuple-element.64.field_ref, f32[128,128]{1,0:T(8,128)S(1)} %copy-done.5, ...), custom_call_target="tpu_custom_call" | custom-call | flops 1500000000 | bytes 11411456 | tf_op jit(solution)/shard_map/adjoint/pallas_call | solution.py:161
  48.9 1.5 %collective-permute-start.11 = (f32[64,256]{1,0:T(8,128)S(1)}, f32[64,256]{1,0:T(8,128)S(1)}, u32[]{:S(2)}, u32[]{:S(2)}) collective-permute-start(f32[64,256]{1,0:T(8,128)S(1)} %get-tuple-element.84), channel_id=1, source_target_pairs={{0,8},{1,9},{2,10},{3,11},{4,12},{5,13},{6,14},{7,15},{8,16},{9,17... | collective-permute-start | bytes 196616 | tf_op jit(solution)/shard_map/ppermute | solution.py:459
  50.4 2.9 %collective-permute-done.11.rim_ref = f32[64,256]{1,0:T(8,128)S(1)} collective-permute-done((f32[64,256]{1,0:T(8,128)S(1)}, f32[64,256]{1,0:T(8,128)S(1)}, u32[]{:S(2)}, u32[]{:S(2)}) %collective-permute-start.11) | collective-permute-done | bytes 65568 | tf_op jit(solution)/shard_map/ppermute | solution.py:459
  53.3 3.3 %collective-permute-start.12 = (f32[136,256]{1,0:T(8,128)S(1)}, f32[136,256]{1,0:T(8,128)S(1)}, u32[]{:S(2)}, u32[]{:S(2)}) collective-permute-start(f32[136,256]{1,0:T(8,128)S(1)} %rim.1.mine_ref), channel_id=1, source_target_pairs={{0,32},{32,0},{64,96},{96,64},{128,160},{160,128},{192,224},{224,1... | collective-permute-start | bytes 417800 | tf_op jit(solution)/shard_map/ppermute | solution.py:434
  56.6 1.0 %collective-permute-done.12.other_ref = f32[136,256]{1,0:T(8,128)S(1)} collective-permute-done((f32[136,256]{1,0:T(8,128)S(1)}, f32[136,256]{1,0:T(8,128)S(1)}, u32[]{:S(2)}, u32[]{:S(2)}) %collective-permute-start.12) | collective-permute-done | bytes 139296 | tf_op jit(solution)/shard_map/ppermute | solution.py:434
  57.6 0.4 pixels.1
  58.0 0.9 %collective-permute-start.13 = (f32[72,128]{1,0:T(8,128)S(1)}, f32[72,128]{1,0:T(8,128)S(1)}, u32[]{:S(2)}, u32[]{:S(2)}) collective-permute-start(f32[72,128]{1,0:T(8,128)S(1)} %get-tuple-element.87.before_ref), channel_id=1, source_target_pairs={{0,32},{1,0},{2,1},{3,2},{4,3},{5,4},{6,5},{7,6},{8,40},{9,8},{10,... | collective-permute-start | bytes 110600 | tf_op jit(solution)/shard_map/ppermute | solution.py:459
  58.9 1.1 %collective-permute-done.13.mine_ref = f32[72,128]{1,0:T(8,128)S(1)} collective-permute-done((f32[72,128]{1,0:T(8,128)S(1)}, f32[72,128]{1,0:T(8,128)S(1)}, u32[]{:S(2)}, u32[]{:S(2)}) %collective-permute-start.13) | collective-permute-done | bytes 36896 | tf_op jit(solution)/shard_map/ppermute | solution.py:459
  60.0 2.4 %collective-permute-start.14 = (f32[72,128]{1,0:T(8,128)S(1)}, f32[72,128]{1,0:T(8,128)S(1)}, u32[]{:S(2)}, u32[]{:S(2)}) collective-permute-start(f32[72,128]{1,0:T(8,128)S(1)} %collective-permute-done.13.mine_ref), channel_id=1, source_target_pairs={{0,32},{32,0},{64,96},{96,64},{128,160},{160,128},{192,224},{224,1... | collective-permute-start | bytes 110600 | tf_op jit(solution)/shard_map/ppermute | solution.py:434
  62.4 0.9 %collective-permute-done.14.other_ref = f32[72,128]{1,0:T(8,128)S(1)} collective-permute-done((f32[72,128]{1,0:T(8,128)S(1)}, f32[72,128]{1,0:T(8,128)S(1)}, u32[]{:S(2)}, u32[]{:S(2)}) %collective-permute-start.14) | collective-permute-done | bytes 36896 | tf_op jit(solution)/shard_map/ppermute | solution.py:434
  63.3 0.8 %join.1 = (f32[1,64,512]{2,1,0:T(8,128)}, f32[4]{0:T(128)}) custom-call(f32[64,512]{1,0:T(8,128)S(1)} %get-tuple-element.86.inner_ref, f32[72,128]{1,0:T(8,128)S(1)} %get-tuple-element.87.before_ref, f32[72,128]{1,0:T(8,128)S(1)} %collective-permute-done.13.mine_ref, f32[72,128]{1,0:T(8,128)S(1)} %collective-permute-done.14.other_ref), custom_call_target="tpu_custom_call" | custom-call | flops 32768 | bytes 372752 | tf_op jit(solution)/shard_map/join/pallas_call | solution.py:161
  (23 shorter events, 0.1 us)
Async XLA Ops:
  0.6 15.5 %copy-start = (bf16[80,64,256]{2,1,0:T(8,128)(2,1)S(1)}, bf16[80,64,256]{2,1,0:T(8,128)(2,1)}, u32[]{:S(2)}) copy-start(bf16[80,64,256]{2,1,0:T(8,128)(2,1)} %constant.28.clone._.table_ref) | copy-start | bytes 7864324
  1.8 6.4 %collective-permute-start.2 = (f32[64,512]{1,0:T(8,128)S(1)}, f32[64,512]{1,0:T(8,128)S(1)}, u32[]{:S(2)}, u32[]{:S(2)}) collective-permute-start(f32[64,512]{1,0:T(8,128)S(1)} %select_bitcast_fusion), channel_id=1, source_target_pairs={{0,8},{1,9},{2,10},{3,11},{4,12},{5,13},{6,14},{7,15},{8,16},{9,17... | collective-permute-start | bytes 393224 | tf_op jit(solution)/shard_map/ppermute | solution.py:459
  5.1 1.4 %copy-start.1 = (bf16[44,64,256]{2,1,0:T(8,128)(2,1)S(1)}, bf16[44,64,256]{2,1,0:T(8,128)(2,1)}, u32[]{:S(2)}) copy-start(bf16[44,64,256]{2,1,0:T(8,128)(2,1)} %constant.27.clone.table_ref.early_ref) | copy-start | bytes 4325380
  6.4 1.2 %copy-start.4 = (f32[1,512,512]{2,1,0:T(8,128)S(1)}, f32[1,512,512]{2,1,0:T(8,128)}, u32[]{:S(2)}) copy-start(f32[1,512,512]{2,1,0:T(8,128)} %tile_ref.1) | copy-start | bytes 3145732
  7.6 2.7 %copy-start.7 = (s32[4,2,128]{2,1,0:T(2,128)S(1)}, s32[4,2,128]{2,1,0:T(2,128)}, u32[]{:S(2)}) copy-start(s32[4,2,128]{2,1,0:T(2,128)} %param.11) | copy-start | bytes 12292
  7.6 2.7 %copy-start.8 = (f32[4]{0:T(128)S(1)}, f32[4]{0:T(128)}, u32[]{:S(2)}) copy-start(f32[4]{0:T(128)} %param.10) | copy-start | bytes 52
  8.2 1.4 %collective-permute-start.3 = (f32[64,512]{1,0:T(8,128)S(1)}, f32[64,512]{1,0:T(8,128)S(1)}, u32[]{:S(2)}, u32[]{:S(2)}) collective-permute-start(f32[64,512]{1,0:T(8,128)S(1)} %collective-permute-done.2.mine_ref), channel_id=1, source_target_pairs={{0,32},{32,0},{64,96},{96,64},{128,160},{160,128},{192,224},{224,1... | collective-permute-start | bytes 393224 | tf_op jit(solution)/shard_map/ppermute | solution.py:434
  9.7 11.0 %copy-start.5 = (f32[128,128]{1,0:T(8,128)S(1)}, f32[128,128]{1,0:T(8,128)}, u32[]{:S(2)}) copy-start(f32[128,128]{1,0:T(8,128)} %gain_ref.11) | copy-start | bytes 196612
  10.1 7.7 %collective-permute-start.4 = (f32[128,128]{1,0:T(8,128)S(1)}, f32[128,128]{1,0:T(8,128)S(1)}, u32[]{:S(2)}, u32[]{:S(2)}) collective-permute-start(f32[128,128]{1,0:T(8,128)S(1)} %get-tuple-element.52), channel_id=1, source_target_pairs={{0,1},{1,2},{2,3},{3,4},{4,5},{5,6},{6,7},{7,39},{8,9},{9,10},{10,... | collective-permute-start | bytes 196616 | tf_op jit(solution)/shard_map/ppermute | solution.py:459
  10.4 9.3 %collective-permute-start = (f32[4,2,128]{2,1,0:T(2,128)S(1)}, f32[4,2,128]{2,1,0:T(2,128)S(1)}, u32[]{:S(2)}, u32[]{:S(2)}) collective-permute-start(f32[4,2,128]{2,1,0:T(2,128)S(1)} %convert_select_fusion.info_ref), channel_id=1, source_target_pairs={{0,193},{1,64},{2,195},{3,66},{4,197},{5,68},{6,199},{7,70},{8,201... | collective-permute-start | bytes 12296 | tf_op jit(solution)/shard_map/ppermute | solution.py:444
  16.1 1.4 %copy-start.2 = (bf16[44,64,256]{2,1,0:T(8,128)(2,1)S(1)}, bf16[44,64,256]{2,1,0:T(8,128)(2,1)}, u32[]{:S(2)}) copy-start(bf16[44,64,256]{2,1,0:T(8,128)(2,1)} %constant.27.clone.table_ref.early_ref) | copy-start | bytes 4325380
  17.8 2.8 %collective-permute-start.5 = (f32[128,128]{1,0:T(8,128)S(1)}, f32[128,128]{1,0:T(8,128)S(1)}, u32[]{:S(2)}, u32[]{:S(2)}) collective-permute-start(f32[128,128]{1,0:T(8,128)S(1)} %collective-permute-done.4.mine_ref), channel_id=1, source_target_pairs={{0,32},{32,0},{64,96},{96,64},{128,160},{160,128},{192,224},{224,1... | collective-permute-start | bytes 196616 | tf_op jit(solution)/shard_map/ppermute | solution.py:434
  19.8 4.4 %collective-permute-start.1 = (f32[8,2,128]{2,1,0:T(2,128)S(1)}, f32[8,2,128]{2,1,0:T(2,128)S(1)}, u32[]{:S(2)}, u32[]{:S(2)}) collective-permute-start(f32[8,2,128]{2,1,0:T(2,128)S(1)} %pad_maximum_fusion), channel_id=1, source_target_pairs={{0,65},{1,192},{2,67},{3,194},{4,69},{5,196},{6,71},{7,198},{8,73}... | collective-permute-start | bytes 24584 | tf_op jit(solution)/shard_map/ppermute | solution.py:444
  24.2 6.4 %copy-start.6 = (f32[1,512,512]{2,1,0:T(8,128)S(1)}, f32[1,512,512]{2,1,0:T(8,128)}, u32[]{:S(2)}) copy-start(f32[1,512,512]{2,1,0:T(8,128)} %target_ref.1) | copy-start | bytes 3145732
  29.3 2.6 %collective-permute-start.6 = (f32[256,256]{1,0:T(8,128)S(1)}, f32[256,256]{1,0:T(8,128)S(1)}, u32[]{:S(2)}, u32[]{:S(2)}) collective-permute-start(f32[256,256]{1,0:T(8,128)S(1)} %get-tuple-element.59.mine_ref), channel_id=1, source_target_pairs={{0,32},{32,0},{64,96},{96,64},{128,160},{160,128},{192,224},{224,1... | collective-permute-start | bytes 786440 | tf_op jit(solution)/shard_map/ppermute | solution.py:434
  32.6 3.9 %collective-permute-start.7 = (f32[8,128]{1,0:T(8,128)S(1)}, f32[8,128]{1,0:T(8,128)S(1)}, u32[]{:S(2)}, u32[]{:S(2)}) collective-permute-start(f32[8,128]{1,0:T(8,128)S(1)} %get-tuple-element.67), channel_id=1, source_target_pairs={{0,6},{1,7},{2,4},{3,5},{4,2},{5,3},{6,0},{7,1},{8,14},{9,15},{10,... | collective-permute-start | bytes 12296 | tf_op jit(solution)/shard_map/ppermute | solution.py:473
  36.6 5.1 %collective-permute-start.8 = (f32[8,128]{1,0:T(8,128)S(1)}, f32[8,128]{1,0:T(8,128)S(1)}, u32[]{:S(2)}, u32[]{:S(2)}) collective-permute-start(f32[8,128]{1,0:T(8,128)S(1)} %add.17), channel_id=1, source_target_pairs={{0,24},{1,25},{2,26},{3,27},{4,28},{5,29},{6,30},{7,31},{8,16},{9,... | collective-permute-start | bytes 12296 | tf_op jit(solution)/shard_map/ppermute | solution.py:473
  41.7 3.3 %collective-permute-start.9 = (f32[8,128]{1,0:T(8,128)S(1)}, f32[8,128]{1,0:T(8,128)S(1)}, u32[]{:S(2)}, u32[]{:S(2)}) collective-permute-start(f32[8,128]{1,0:T(8,128)S(1)} %add.18), channel_id=1, source_target_pairs={{0,2},{1,3},{2,0},{3,1},{4,6},{5,7},{6,4},{7,5},{8,10},{9,11},{10,... | collective-permute-start | bytes 12296 | tf_op jit(solution)/shard_map/ppermute | solution.py:473
  45.0 12.6 %copy-start.3 = (bf16[44,64,256]{2,1,0:T(8,128)(2,1)S(1)}, bf16[44,64,256]{2,1,0:T(8,128)(2,1)}, u32[]{:S(2)}) copy-start(bf16[44,64,256]{2,1,0:T(8,128)(2,1)} %constant.27.clone.table_ref.early_ref) | copy-start | bytes 4325380
  45.0 3.8 %collective-permute-start.10 = (f32[8,128]{1,0:T(8,128)S(1)}, f32[8,128]{1,0:T(8,128)S(1)}, u32[]{:S(2)}, u32[]{:S(2)}) collective-permute-start(f32[8,128]{1,0:T(8,128)S(1)} %add.19), channel_id=1, source_target_pairs={{0,8},{1,9},{2,10},{3,11},{4,12},{5,13},{6,14},{7,15},{8,0},{9,1},... | collective-permute-start | bytes 12296 | tf_op jit(solution)/shard_map/ppermute | solution.py:473
  48.9 4.4 %collective-permute-start.11 = (f32[64,256]{1,0:T(8,128)S(1)}, f32[64,256]{1,0:T(8,128)S(1)}, u32[]{:S(2)}, u32[]{:S(2)}) collective-permute-start(f32[64,256]{1,0:T(8,128)S(1)} %get-tuple-element.84), channel_id=1, source_target_pairs={{0,8},{1,9},{2,10},{3,11},{4,12},{5,13},{6,14},{7,15},{8,16},{9,17... | collective-permute-start | bytes 196616 | tf_op jit(solution)/shard_map/ppermute | solution.py:459
  53.3 4.3 %collective-permute-start.12 = (f32[136,256]{1,0:T(8,128)S(1)}, f32[136,256]{1,0:T(8,128)S(1)}, u32[]{:S(2)}, u32[]{:S(2)}) collective-permute-start(f32[136,256]{1,0:T(8,128)S(1)} %rim.1.mine_ref), channel_id=1, source_target_pairs={{0,32},{32,0},{64,96},{96,64},{128,160},{160,128},{192,224},{224,1... | collective-permute-start | bytes 417800 | tf_op jit(solution)/shard_map/ppermute | solution.py:434
  58.0 2.0 %collective-permute-start.13 = (f32[72,128]{1,0:T(8,128)S(1)}, f32[72,128]{1,0:T(8,128)S(1)}, u32[]{:S(2)}, u32[]{:S(2)}) collective-permute-start(f32[72,128]{1,0:T(8,128)S(1)} %get-tuple-element.87.before_ref), channel_id=1, source_target_pairs={{0,32},{1,0},{2,1},{3,2},{4,3},{5,4},{6,5},{7,6},{8,40},{9,8},{10,... | collective-permute-start | bytes 110600 | tf_op jit(solution)/shard_map/ppermute | solution.py:459
  60.0 3.3 %collective-permute-start.14 = (f32[72,128]{1,0:T(8,128)S(1)}, f32[72,128]{1,0:T(8,128)S(1)}, u32[]{:S(2)}, u32[]{:S(2)}) collective-permute-start(f32[72,128]{1,0:T(8,128)S(1)} %collective-permute-done.13.mine_ref), channel_id=1, source_target_pairs={{0,32},{32,0},{64,96},{96,64},{128,160},{160,128},{192,224},{224,1... | collective-permute-start | bytes 110600 | tf_op jit(solution)/shard_map/ppermute | solution.py:434
